TPU v7x, 32 devices: a whole 2x2x4 slice. The times are simulated.
32 devices in a mesh: rows: 4 (over y, x), cols: 8 (over z, core).
Axes of the slice: x: 2, y: 2, z: 4, core: 2. Of those that a mesh axis runs over, the one named last changes fastest.
Arguments:
- tokens: bfloat16 [8, 1536, 1536], P('cols', 'rows'), may hold values from -6 to 6
- segment_ids: int32 [8, 1536], P('cols'), may hold values from 0 to 3, never falling along the last dimension, each value on 1 to 768 neighbouring positions
- expert_ids: int32 [8, 1536, 8], P('cols', 'rows'), may hold values from 0 to 31, all different within a row; in each aligned block of 384 rows (0 to 383, 384 to 767, ..., all dimensions but the last counted through in order) at most 120 rows name the same one
- w_query: bfloat16 [1536, 1536], P('cols', 'rows'), may hold values from -0.625 to 0.625
- key_matrix: bfloat16 [1536, 512], P('cols', 'rows'), may hold values from -0.625 to 0.625
- value_matrix: bfloat16 [1536, 512], P('cols', 'rows'), may hold values from -0.15625 to 0.15625
- w_out: bfloat16 [1536, 1536], P(('rows', 'cols')), may hold values from -1.75 to 1.75
- norm_attn: bfloat16 [1536], P(('rows', 'cols')), may hold values from 0.5 to 1.5
- norm_moe: bfloat16 [1536], P(('rows', 'cols')), may hold values from 0.5 to 1.5
- w_router: bfloat16 [1536, 32], P(('rows', 'cols')), may hold values from -0.078125 to 0.078125
- w_gate: bfloat16 [32, 1536, 512], P('cols', 'rows'), may hold values from -0.15625 to 0.15625
- w_up: bfloat16 [32, 1536, 512], P('cols', 'rows'), may hold values from -0.15625 to 0.15625
- w_down: bfloat16 [32, 512, 1536], P('cols', None, 'rows'), may hold values from -2 to 2
- cotangent: bfloat16 [8, 1536, 1536], P('cols', 'rows'), may hold values from -6 to 6
Outputs:
- block_out: float32 [8, 1536, 1536], P('cols', 'rows')
- grad_tokens: float32 [8, 1536, 1536], P('cols', 'rows')
- grad_w_query: float32 [1536, 1536], P('cols', 'rows')
- grad_w_key: float32 [1536, 512], P('cols', 'rows')
- grad_w_value: float32 [1536, 512], P('cols', 'rows')
- grad_w_out: float32 [1536, 1536], P(('rows', 'cols'))
- grad_norm_attn: float32 [1536], P(('rows', 'cols'))
- grad_norm_moe: float32 [1536], P(('rows', 'cols'))
- grad_w_router: float32 [1536, 32], P(('rows', 'cols'))
- grad_w_gate: float32 [32, 1536, 512], P('cols', 'rows')
- grad_w_up: float32 [32, 1536, 512], P('cols', 'rows')
- grad_w_down: float32 [32, 512, 1536], P('cols', None, 'rows')
Inputs may be any that keep to these rules, and one draw needn't show every extreme that they name: `segment_ids`: within a sequence the numbers never fall; each document has at most 768 tokens. `expert_ids`: each token names 8 different experts; among the rows of one device (aligned blocks of 384 tokens) no expert is named more than 120 times, a bound that some block reaches.
All inputs are finite; a program needn't handle non-finite values.
Results may differ from a plain program's by a relative error of at most 0.02.
Values may be sent and summed in bfloat16 or wider, within the bound.
No kernel may reach another device: no remote copies, remote signals or barrier semaphores. Data moves between devices by JAX's collectives and lax.ppermute only.
A program may use at most 320 MiB of HBM per device.

v0:
```python
from functools import partial

import jax
import jax.numpy as jnp
from jax import lax
from jax.sharding import PartitionSpec as P

HEAD_SIZE = 64


res_scale = 0.22
att_scale = 0.015625
norm_eps = 1e-06
rope_base = 10000.0
masked_score = -1e30
highest = lax.Precision.HIGHEST


def rms_scale(hidden_rows):
    return lax.rsqrt(jnp.mean(hidden_rows * hidden_rows, axis=-1, keepdims=True) + norm_eps)


def doc_positions(segments):
    seq_len = segments.shape[0]
    position_ids = jnp.arange(seq_len, dtype=jnp.int32)
    before = jnp.concatenate([jnp.full((1,), -1, jnp.int32), segments[:-1]])
    doc_starts = lax.cummax(jnp.where(segments != before, position_ids, 0), axis=0)
    return (position_ids - doc_starts).astype(jnp.float32)


def rope_tables(positions, head_dim):
    half_dim = head_dim // 2
    frequency = rope_base ** (-(2.0 * jnp.arange(half_dim, dtype=jnp.float32)) / head_dim)
    angles = positions[:, None] * frequency[None, :]
    return (jnp.cos(angles), jnp.sin(angles))


def rotate(hidden_rows, cosine, sine_part):
    half_dim = hidden_rows.shape[-1] // 2
    lower_portion = hidden_rows[..., :half_dim]
    upper_half = hidden_rows[..., half_dim:]
    cos_rows = cosine[:, None, :]
    sin_rows = sine_part[:, None, :]
    return jnp.concatenate(
        [
            lower_portion * cos_rows - upper_half * sin_rows,
            upper_half * cos_rows + lower_portion * sin_rows,
        ],
        axis=-1,
    )


def rotate_back(grad_rows, cosine, sine_part):
    half_dim = grad_rows.shape[-1] // 2
    lower_portion = grad_rows[..., :half_dim]
    upper_half = grad_rows[..., half_dim:]
    cos_rows = cosine[:, None, :]
    sin_rows = sine_part[:, None, :]
    return jnp.concatenate(
        [
            lower_portion * cos_rows + upper_half * sin_rows,
            upper_half * cos_rows - lower_portion * sin_rows,
        ],
        axis=-1,
    )


def visible_mask(segments, row_start, block_rows):
    seq_len = segments.shape[0]
    query_pos = row_start + jnp.arange(block_rows, dtype=jnp.int32)
    key_pos = jnp.arange(seq_len, dtype=jnp.int32)
    query_seg = lax.dynamic_slice_in_dim(segments, row_start, block_rows, 0)
    return (query_seg[:, None] == segments[None, :]) & (key_pos[None, :] <= query_pos[:, None])


def slot_tables(expert_rows, experts, capacity):
    tok_count, top_count = expert_rows.shape
    flat_ids = expert_rows.reshape(-1)
    one_hot = (flat_ids[:, None] == jnp.arange(experts, dtype=jnp.int32)[None, :]).astype(jnp.int32)
    running = jnp.cumsum(one_hot, axis=0)
    slot_ranks = jnp.sum((running - one_hot) * one_hot, axis=1)
    slot_index = flat_ids * capacity + slot_ranks
    pair_table = jnp.full((experts * capacity,), tok_count * top_count, jnp.int32)
    pair_table = pair_table.at[slot_index].set(jnp.arange(tok_count * top_count, dtype=jnp.int32))
    return (pair_table.reshape(experts, capacity), slot_index)


def attend_block(queries, key_rows, value_rows, segments, row_start, block_rows):
    query_block = lax.dynamic_slice_in_dim(queries, row_start, block_rows, 0)
    scores = (
        jnp.einsum("qkgd,tkd->kgqt", query_block, key_rows, preferred_element_type=jnp.float32)
        * att_scale
    )
    scores = jnp.where(
        visible_mask(segments, row_start, block_rows)[None, None], scores, masked_score
    )
    top_score = jnp.max(scores, axis=-1, keepdims=True)
    weights = jnp.exp(scores - top_score)
    totals = jnp.sum(weights, axis=-1, keepdims=True)
    probabilities = (weights / totals).astype(jnp.bfloat16)
    result = jnp.einsum(
        "kgqt,tkd->qkgd", probabilities, value_rows, preferred_element_type=jnp.float32
    )
    return (result, (top_score + jnp.log(totals))[..., 0])


def expert_hidden(expert_in, gate_full, up_full):
    gate_hidden = jnp.einsum(
        "erd,edf->erf", expert_in, gate_full, preferred_element_type=jnp.float32
    )
    up_hidden = jnp.einsum("erd,edf->erf", expert_in, up_full, preferred_element_type=jnp.float32)
    return (gate_hidden, up_hidden)


def per_device(
    tokens,
    segment_ids,
    expert_ids,
    w_query,
    key_matrix,
    value_matrix,
    w_out,
    norm_attn,
    norm_moe,
    w_router,
    w_gate,
    w_up,
    w_down,
    cotangent,
):
    own_tokens = tokens[0]
    tok_dev, model_width = own_tokens.shape
    seq_rows = lax.all_gather(own_tokens, "rows", axis=0, tiled=True)
    out_full, gain_attn, gain_moe, router_full = (
        lax.all_gather(w_out, ("rows", "cols"), axis=0, tiled=True),
        lax.all_gather(norm_attn, ("rows", "cols"), axis=0, tiled=True),
        lax.all_gather(norm_moe, ("rows", "cols"), axis=0, tiled=True),
        lax.all_gather(w_router, ("rows", "cols"), axis=0, tiled=True),
    )
    query_w, key_w, value_w = (
        lax.all_gather(w_query, "cols", axis=0, tiled=True),
        lax.all_gather(key_matrix, "cols", axis=0, tiled=True),
        lax.all_gather(value_matrix, "cols", axis=0, tiled=True),
    )
    gate_full, up_full, down_full = (
        lax.all_gather(w_gate, "rows", axis=1, tiled=True),
        lax.all_gather(w_up, "rows", axis=1, tiled=True),
        lax.all_gather(w_down, "rows", axis=2, tiled=True),
    )
    seq_len = seq_rows.shape[0]
    head_q = query_w.shape[1] // HEAD_SIZE
    head_kv = key_w.shape[1] // HEAD_SIZE
    group_size = head_q // head_kv
    gain_attn_f = gain_attn.astype(jnp.float32)
    gain_moe_f = gain_moe.astype(jnp.float32)
    seq_float = seq_rows.astype(jnp.float32)
    scale_attn = rms_scale(seq_float)
    unit_attn = seq_float * scale_attn
    normed = (unit_attn * gain_attn_f).astype(jnp.bfloat16)
    query_lin = jnp.dot(normed, query_w, preferred_element_type=jnp.float32)
    key_lin = jnp.dot(normed, key_w, preferred_element_type=jnp.float32)
    value_rows = (
        jnp.dot(normed, value_w, preferred_element_type=jnp.float32)
        .astype(jnp.bfloat16)
        .reshape(seq_len, head_kv, HEAD_SIZE)
    )
    segments = segment_ids[0]
    cosine, sine_part = rope_tables(doc_positions(segments), HEAD_SIZE)
    queries = (
        rotate(query_lin.reshape(seq_len, head_q, HEAD_SIZE), cosine, sine_part)
        .astype(jnp.bfloat16)
        .reshape(seq_len, head_kv, group_size, HEAD_SIZE)
    )
    key_rows = rotate(key_lin.reshape(seq_len, head_kv, HEAD_SIZE), cosine, sine_part).astype(
        jnp.bfloat16
    )
    block_rows = min(512, seq_len)
    starts = jnp.arange(seq_len // block_rows, dtype=jnp.int32) * block_rows
    attended, log_totals = lax.map(
        partial(attend_block, queries, key_rows, value_rows, segments, block_rows=block_rows),
        starts,
    )
    attended_low = attended.reshape(seq_len, head_q * HEAD_SIZE).astype(jnp.bfloat16)
    own_heads = lax.all_to_all(attended_low, "rows", split_axis=0, concat_axis=1, tiled=True)
    branch = jnp.dot(own_heads, out_full, preferred_element_type=jnp.float32)
    mixed_rows = own_tokens.astype(jnp.float32) + res_scale * branch
    scale_moe = rms_scale(mixed_rows)
    unit_moe = mixed_rows * scale_moe
    normed_moe = (unit_moe * gain_moe_f).astype(jnp.bfloat16)
    logits = jnp.dot(normed_moe, router_full, preferred_element_type=jnp.float32)
    expert_rows = expert_ids[0]
    top_count = expert_rows.shape[1]
    experts = w_gate.shape[0] * lax.axis_size("cols")
    capacity = 5 * tok_dev * top_count // (4 * experts)
    gate_weights = jax.nn.softmax(jnp.take_along_axis(logits, expert_rows, axis=1), axis=-1)
    pair_table, slot_index = slot_tables(expert_rows, experts, capacity)
    padded = jnp.concatenate([normed_moe, jnp.zeros((1, model_width), jnp.bfloat16)], axis=0)
    send_rows = padded[pair_table // top_count]
    received = lax.all_to_all(send_rows, "cols", split_axis=0, concat_axis=1, tiled=True)
    gate_hidden, up_hidden = expert_hidden(received, gate_full, up_full)
    active = (jax.nn.silu(gate_hidden) * up_hidden).astype(jnp.bfloat16)
    expert_out = jnp.einsum(
        "erf,efd->erd", active, down_full, preferred_element_type=jnp.float32
    ).astype(jnp.bfloat16)
    came_back = lax.all_to_all(expert_out, "cols", split_axis=1, concat_axis=0, tiled=True)
    picked = came_back.reshape(experts * capacity, model_width)[slot_index].reshape(
        tok_dev, top_count, model_width
    )
    moe_out = jnp.einsum("tk,tkd->td", gate_weights, picked, preferred_element_type=jnp.float32)
    block_out = mixed_rows + res_scale * moe_out
    grad_out = cotangent[0].astype(jnp.float32)
    grad_moe = res_scale * grad_out
    grad_gates = jnp.einsum("tkd,td->tk", picked, grad_moe, preferred_element_type=jnp.float32)
    grad_chosen = gate_weights * (
        grad_gates - jnp.sum(gate_weights * grad_gates, axis=-1, keepdims=True)
    )
    expert_range = jnp.arange(experts, dtype=jnp.int32)
    grad_logits = jnp.sum(
        (expert_rows[:, :, None] == expert_range[None, None, :]) * grad_chosen[:, :, None], axis=1
    )
    grad_normed_moe = jnp.dot(grad_logits, router_full.astype(jnp.float32).T, precision=highest)
    grad_router = jnp.dot(normed_moe.astype(jnp.float32).T, grad_logits, precision=highest)
    pair_grads = (
        (gate_weights[:, :, None] * grad_moe[:, None, :])
        .astype(jnp.bfloat16)
        .reshape(tok_dev * top_count, model_width)
    )
    pair_padded = jnp.concatenate([pair_grads, jnp.zeros((1, model_width), jnp.bfloat16)], axis=0)
    grad_send = pair_padded[pair_table]
    grad_received = lax.all_to_all(grad_send, "cols", split_axis=0, concat_axis=1, tiled=True)
    gate_again, up_again = expert_hidden(received, gate_full, up_full)
    sigmoid_gate = jax.nn.sigmoid(gate_again)
    silu_gate = gate_again * sigmoid_gate
    active_again = (silu_gate * up_again).astype(jnp.bfloat16)
    grad_down_w = jnp.einsum(
        "erf,erd->efd", active_again, grad_received, preferred_element_type=jnp.float32
    )
    grad_active = jnp.einsum(
        "erd,efd->erf", grad_received, down_full, preferred_element_type=jnp.float32
    )
    grad_gate_hidden = (
        grad_active * up_again * sigmoid_gate * (1.0 + gate_again * (1.0 - sigmoid_gate))
    ).astype(jnp.bfloat16)
    grad_up_hidden = (grad_active * silu_gate).astype(jnp.bfloat16)
    grad_gate_w = jnp.einsum(
        "erd,erf->edf", received, grad_gate_hidden, preferred_element_type=jnp.float32
    )
    grad_up_w = jnp.einsum(
        "erd,erf->edf", received, grad_up_hidden, preferred_element_type=jnp.float32
    )
    grad_inputs = (
        jnp.einsum("erf,edf->erd", grad_gate_hidden, gate_full, preferred_element_type=jnp.float32)
        + jnp.einsum("erf,edf->erd", grad_up_hidden, up_full, preferred_element_type=jnp.float32)
    ).astype(jnp.bfloat16)
    expert_sums = (
        lax.psum_scatter(
            grad_gate_w.astype(jnp.bfloat16), "rows", scatter_dimension=1, tiled=True
        ).astype(jnp.float32),
        lax.psum_scatter(
            grad_up_w.astype(jnp.bfloat16), "rows", scatter_dimension=1, tiled=True
        ).astype(jnp.float32),
        lax.psum_scatter(
            grad_down_w.astype(jnp.bfloat16), "rows", scatter_dimension=2, tiled=True
        ).astype(jnp.float32),
    )
    grad_back = lax.all_to_all(grad_inputs, "cols", split_axis=1, concat_axis=0, tiled=True)
    pair_back = grad_back.reshape(experts * capacity, model_width)[slot_index].reshape(
        tok_dev, top_count, model_width
    )
    grad_normed_moe = grad_normed_moe + jnp.sum(pair_back.astype(jnp.float32), axis=1)
    grad_unit_moe = grad_normed_moe * gain_moe_f
    grad_gain_moe = jnp.sum(grad_normed_moe * unit_moe, axis=0)
    grad_mixed = grad_out + scale_moe * (
        grad_unit_moe - unit_moe * jnp.mean(grad_unit_moe * unit_moe, axis=-1, keepdims=True)
    )
    grad_branch = (res_scale * grad_mixed).astype(jnp.bfloat16)
    grad_out_w = jnp.dot(own_heads.T, grad_branch, preferred_element_type=jnp.float32)
    grad_heads = jnp.dot(grad_branch, out_full.T, preferred_element_type=jnp.float32).astype(
        jnp.bfloat16
    )
    grad_attended = lax.all_to_all(
        grad_heads, "rows", split_axis=1, concat_axis=0, tiled=True
    ).reshape(seq_len, head_kv, group_size, HEAD_SIZE)

    def back_step(carried, scan_item):
        grad_keys, grad_values = carried
        row_start, log_block = scan_item
        query_block = lax.dynamic_slice_in_dim(queries, row_start, block_rows, 0)
        grad_block = lax.dynamic_slice_in_dim(grad_attended, row_start, block_rows, 0)
        scores = (
            jnp.einsum("qkgd,tkd->kgqt", query_block, key_rows, preferred_element_type=jnp.float32)
            * att_scale
        )
        scores = jnp.where(
            visible_mask(segments, row_start, block_rows)[None, None], scores, masked_score
        )
        probabilities = jnp.exp(scores - log_block[..., None])
        grad_probs = jnp.einsum(
            "qkgd,tkd->kgqt", grad_block, value_rows, preferred_element_type=jnp.float32
        )
        row_delta = jnp.sum(grad_probs * probabilities, axis=-1, keepdims=True)
        grad_scores = (probabilities * (grad_probs - row_delta)).astype(jnp.bfloat16)
        grad_query = (
            jnp.einsum("kgqt,tkd->qkgd", grad_scores, key_rows, preferred_element_type=jnp.float32)
            * att_scale
        )
        grad_keys = (
            grad_keys
            + jnp.einsum(
                "kgqt,qkgd->tkd", grad_scores, query_block, preferred_element_type=jnp.float32
            )
            * att_scale
        )
        grad_values = grad_values + jnp.einsum(
            "kgqt,qkgd->tkd",
            probabilities.astype(jnp.bfloat16),
            grad_block,
            preferred_element_type=jnp.float32,
        )
        return ((grad_keys, grad_values), grad_query)

    zero_keys = jnp.zeros((seq_len, head_kv, HEAD_SIZE), jnp.float32)
    (grad_keys, grad_values), grad_queries = lax.scan(
        back_step, (zero_keys, zero_keys), (starts, log_totals)
    )
    grad_query_lin = (
        rotate_back(grad_queries.reshape(seq_len, head_q, HEAD_SIZE), cosine, sine_part)
        .reshape(seq_len, head_q * HEAD_SIZE)
        .astype(jnp.bfloat16)
    )
    grad_key_lin = (
        rotate_back(grad_keys, cosine, sine_part)
        .reshape(seq_len, head_kv * HEAD_SIZE)
        .astype(jnp.bfloat16)
    )
    grad_value_lin = grad_values.reshape(seq_len, head_kv * HEAD_SIZE).astype(jnp.bfloat16)
    grad_normed = (
        jnp.dot(grad_query_lin, query_w.T, preferred_element_type=jnp.float32)
        + jnp.dot(grad_key_lin, key_w.T, preferred_element_type=jnp.float32)
        + jnp.dot(grad_value_lin, value_w.T, preferred_element_type=jnp.float32)
    )
    grad_query_w = jnp.dot(normed.T, grad_query_lin, preferred_element_type=jnp.float32)
    grad_key_w = jnp.dot(normed.T, grad_key_lin, preferred_element_type=jnp.float32)
    grad_value_w = jnp.dot(normed.T, grad_value_lin, preferred_element_type=jnp.float32)
    head_sums = (
        lax.psum_scatter(
            grad_query_w.astype(jnp.bfloat16), "cols", scatter_dimension=0, tiled=True
        ).astype(jnp.float32),
        lax.psum_scatter(
            grad_key_w.astype(jnp.bfloat16), "cols", scatter_dimension=0, tiled=True
        ).astype(jnp.float32),
        lax.psum_scatter(
            grad_value_w.astype(jnp.bfloat16), "cols", scatter_dimension=0, tiled=True
        ).astype(jnp.float32),
    )
    grad_gain_attn = jnp.sum(grad_normed * unit_attn, axis=0)
    grad_unit_attn = grad_normed * gain_attn_f
    input_part = lax.psum_scatter(
        (
            scale_attn
            * (
                grad_unit_attn
                - unit_attn * jnp.mean(grad_unit_attn * unit_attn, axis=-1, keepdims=True)
            )
        ).astype(jnp.bfloat16),
        "rows",
        scatter_dimension=0,
        tiled=True,
    ).astype(jnp.float32)
    grad_tokens = grad_mixed + input_part
    wide_sums = (
        lax.psum_scatter(grad_out_w, ("rows", "cols"), scatter_dimension=0, tiled=True),
        lax.psum_scatter(grad_gain_attn, ("rows", "cols"), scatter_dimension=0, tiled=True),
        lax.psum_scatter(grad_gain_moe, ("rows", "cols"), scatter_dimension=0, tiled=True),
        lax.psum_scatter(grad_router, ("rows", "cols"), scatter_dimension=0, tiled=True),
    )
    return (
        block_out[None],
        grad_tokens[None],
        head_sums[0],
        head_sums[1],
        head_sums[2],
        wide_sums[0],
        wide_sums[1],
        wide_sums[2],
        wide_sums[3],
        expert_sums[0],
        expert_sums[1],
        expert_sums[2],
    )


def solution(mesh):
    placed = (
        P("cols", "rows", None),
        P("cols", None),
        P("cols", "rows", None),
        P("cols", "rows"),
        P("cols", "rows"),
        P("cols", "rows"),
        P(("rows", "cols"), None),
        P(("rows", "cols")),
        P(("rows", "cols")),
        P(("rows", "cols"), None),
        P("cols", "rows", None),
        P("cols", "rows", None),
        P("cols", None, "rows"),
        P("cols", "rows", None),
    )
    return jax.shard_map(
        per_device,
        mesh=mesh,
        in_specs=placed,
        out_specs=(
            P("cols", "rows", None),
            P("cols", "rows", None),
            P("cols", "rows"),
            P("cols", "rows"),
            P("cols", "rows"),
            P(("rows", "cols"), None),
            P(("rows", "cols")),
            P(("rows", "cols")),
            P(("rows", "cols"), None),
            P("cols", "rows", None),
            P("cols", "rows", None),
            P("cols", None, "rows"),
        ),
        check_vma=False,
    )
```

profile of v0, /device:TPU:6, one launch (start us, length us, event | category | flops | bytes accessed | tf_op | source)
XLA Modules:
  0.0 2106.1 jit_solution(9172672634661453713)
XLA Ops:
  15.1 41.0 %all-reduce.7 = (bf16[1536]{0:T(1024)(128)(2,1)S(1)}, bf16[1536]{0:T(1024)(128)(2,1)S(1)}) all-reduce(bf16[1536]{0:T(1024)(128)(2,1)S(1)} %dynamic-update-slice, bf16[1536]{0:T(1024)(128)(2,1)S(1)} %dynamic-update-slice.1), channel_id=1, replica_groups=mesh['rows'=4,'cols'=8] {'rows','cols'}, use_global_device_ids=true, to_apply=%add.2 | all-reduce | flops 3072 | bytes 12288
  58.6 37.8 %all-gather.1 = bf16[32,48,32]{1,2,0:T(8,128)(2,1)S(1)} all-gather(bf16[1,48,32]{1,2,0:T(8,128)(2,1)} %bitcast.382), channel_id=1, replica_groups=mesh['rows'=4,'cols'=8] {'rows','cols'}, dimensions={0}, use_global_device_ids=true | all-gather | bytes 101376 | tf_op jit(solution)/shard_map/all_gather | solution.py:138
  97.5 9.2 reduce-window.19
  106.6 15.1 all_gather.36
  121.7 15.5 all_gather.37
  138.2 12.1 scatter_custom_fusion
  166.5 60.3 %while.27 = (s32[]{:T(128)}, bf16[3,512,2,3,64]{1,4,3,2,0:T(8,128)(2,1)}, f32[3,2,3,512]{3,2,1,0:T(4,128)}, s32[3]{0:T(128)S(1)}, s32[1536]{0:T(1024)S(1)}, /*in...) while((s32[]{:T(128)}, ...), condition=%wide.region_6.7_spmd, body=%wide.region_3.6_spmd.sunk | while | flops 1266939392 | bytes 61866176 | solution.py:179
  250.2 11.4 all-to-all-done
  269.3 24.9 %gather_fusion.4 = f32[3072]{0:T(1024)S(1)} fusion(f32[384,32]{0,1:T(8,128)S(1)} %fusion.91, s32[3072]{0:T(1024)S(1)} %copy-done.1), kind=kCustom, calls=%fused_computation.4 | custom fusion | bytes 49152 | tf_op jit(solution)/shard_map/jit(take_along_axis)/gather | solution.py:195
  309.6 28.7 %gather_fusion.2 = bf16[3840,1536]{1,0:T(8,128)(2,1)} fusion(bf16[3073,1536]{1,0:T(8,128)(2,1)} %concatenate.39, s32[4096]{0:T(1024)S(1)} %pad_clamp_fusion), kind=kCustom, calls=%fused_computation.2 | custom fusion | bytes 23608320 | tf_op jit(solution)/shard_map/gather | solution.py:229
  344.5 13.6 gather_fusion
  358.1 242.5 %all-to-all-done.3 = bf16[32,120,1536]{2,1,0:T(8,128)(2,1)} async-done(((bf16[32,120,1536]{2,1,0:T(8,128)(2,1)}), bf16[32,120,1536]{2,1,0:T(8,128)(2,1)}, u32[]{:S(2)}, u32[]{:S(2)}) %all-to-all-start.3) | async-done | bytes 11796512 | tf_op jit(solution)/shard_map/all_to_all | solution.py:230
  607.1 10.3 copy.100
  617.4 245.4 %all-to-all-done.1 = bf16[32,120,1536]{2,1,0:T(8,128)(2,1)} async-done(((bf16[32,120,1536]{2,1,0:T(8,128)(2,1)}), bf16[32,120,1536]{2,1,0:T(8,128)(2,1)}, u32[]{:S(2)}, u32[]{:S(2)}) %all-to-all-start.1) | async-done | bytes 11796512 | tf_op jit(solution)/shard_map/all_to_all | solution.py:199
  862.8 10.0 copy.95
  872.9 13.7 fusion.93
  886.6 13.7 fusion.92
  900.3 18.0 multiply_convert_fusion
  918.2 9.6 convolution_convert_fusion
  927.8 30.2 %copy.96 = bf16[4,960,1536]{2,0,1:T(4,128)(2,1)} copy(bf16[4,960,1536]{2,1,0:T(8,128)(2,1)S(1)} %convolution_convert_fusion) | data formatting | bytes 23592960 | tf_op jit(solution)/shard_map/convert_element_type | solution.py:204
  963.3 13.6 convolution_convert_fusion.1
  976.9 11.2 copy.120
  996.3 12.7 convolution_convert_fusion.2
  1009.0 15.0 fusion.94
  1024.0 18.6 add_convert_fusion
  1042.6 29.1 %copy.101 = bf16[4,960,1536]{2,0,1:T(4,128)(2,1)} copy(bf16[4,960,1536]{2,1,0:T(8,128)(2,1)} %add_convert_fusion) | data formatting | bytes 23592960 | tf_op jit(solution)/shard_map/convert_element_type | solution.py:254
  1071.8 148.5 %all-to-all-done.2 = bf16[4,960,1536]{2,0,1:T(4,128)(2,1)} async-done(((bf16[4,960,1536]{2,0,1:T(4,128)(2,1)}), bf16[4,960,1536]{2,0,1:T(4,128)(2,1)}, u32[]{:S(2)}, u32[]{:S(2)}) %all-to-all-start.2) | async-done | bytes 11796512 | tf_op jit(solution)/shard_map/all_to_all | solution.py:205
  1225.6 12.7 convolution_convert_fusion.3
  1239.8 12.1 copy.97
  1251.9 25.5 %gather_fusion.1 = bf16[3072,1536]{1,0:T(8,128)(2,1)} fusion(bf16[3840,1536]{1,0:T(8,128)(2,1)} %bitcast.348, s32[3072]{0:T(1024)S(1)} %broadcast_clamp_fusion), kind=kCustom, calls=%fused_computation.1 | custom fusion | bytes 18886656 | tf_op jit(solution)/shard_map/gather | solution.py:206
  1286.7 195.7 %all-to-all-done.4 = bf16[4,960,1536]{2,0,1:T(4,128)(2,1)} async-done(((bf16[4,960,1536]{2,0,1:T(4,128)(2,1)}), bf16[4,960,1536]{2,0,1:T(4,128)(2,1)}, u32[]{:S(2)}, u32[]{:S(2)}) %all-to-all-start.4) | async-done | bytes 11796512 | tf_op jit(solution)/shard_map/all_to_all | solution.py:266
  1482.5 12.0 copy.102
  1494.5 25.6 %gather_fusion.3 = bf16[3072,1536]{1,0:T(8,128)(2,1)} fusion(bf16[3840,1536]{1,0:T(8,128)(2,1)} %bitcast.347, s32[3072]{0:T(1024)S(1)} %broadcast_clamp_fusion), kind=kCustom, calls=%fused_computation.3 | custom fusion | bytes 18886656 | tf_op jit(solution)/shard_map/gather | solution.py:267
  1520.7 11.5 convert_reduce_fusion
  1565.9 10.1 all-to-all-done.5
  1582.7 207.4 %while.28 = (s32[]{:T(128)}, f32[1536,2,64]{0,2,1:T(8,128)S(1)}, f32[1536,2,64]{0,2,1:T(8,128)}, f32[3,512,2,3,64]{1,0,4,3,2:T(4,128)}, s32[3]{0:T(128)S(1)}, /*...) while((s32[]{:T(128)}, f32[1536,2,64]{0,2,1:T(8,128)S(1)}, ...), condition=%wide.region_20.21_spmd.clone, body=%wide.region_18.20_spmd.clone.sunk | while | flops 3094214144 | bytes 241164624 | solution.py:323
  1602.5 14.2 fusion.179
  1616.7 13.4 fusion.180
  1635.8 16.1 dynamic_update_slice.19
  1671.6 14.2 fusion.179
  1685.8 13.2 fusion.180
  1704.7 16.1 dynamic_update_slice.19
  1740.5 14.2 fusion.179
  1754.7 13.2 fusion.180
  1773.6 16.1 dynamic_update_slice.19
  1861.8 39.6 %all-reduce.6 = (f32[1536]{0:T(1024)S(1)}, f32[1536]{0:T(1024)S(1)}) all-reduce(f32[1536]{0:T(1024)S(1)} %get-tuple-element.180, f32[1536]{0:T(1024)S(1)} %copy-done.58), channel_id=8, replica_groups=mesh['rows'=4,'cols'=8] {'rows','cols'}, use_global_device_ids=true, to_apply=%region_28.29.clone | all-reduce | flops 3072 | bytes 24576
  1907.0 49.7 %reduce-scatter.14.cloned.1.call-done = bf16[384,1536]{1,0:T(8,128)(2,1)} async-done(((bf16[1536,1536]{1,0:T(8,128)(2,1)}), bf16[384,1536]{1,0:T(8,128)(2,1)}) %reduce-scatter.14.cloned.1.call-update) | async-done | bytes 1179664 | tf_op jit(solution)/shard_map/reduce_scatter | solution.py:358
  1959.8 139.7 %reduce-scatter.22.cloned.1.call-done = f32[48,1536]{1,0:T(8,128)} async-done(((f32[1536,1536]{1,0:T(8,128)}), f32[48,1536]{1,0:T(8,128)}) %reduce-scatter.22.cloned.1.call-update) | async-done | bytes 294928 | tf_op jit(solution)/shard_map/reduce_scatter | solution.py:372
  (375 shorter events, 361.7 us)
Async XLA Ops:
  7.2 99.5 %copy-start.52 = (bf16[192,128]{1,0:T(8,128)(2,1)S(1)}, bf16[192,128]{1,0:T(8,128)(2,1)}, u32[]{:S(2)}) copy-start(bf16[192,128]{1,0:T(8,128)(2,1)} %param.22) | copy-start | bytes 147460
  7.2 114.5 %copy-start.53 = (bf16[192,128]{1,0:T(8,128)(2,1)S(1)}, bf16[192,128]{1,0:T(8,128)(2,1)}, u32[]{:S(2)}) copy-start(bf16[192,128]{1,0:T(8,128)(2,1)} %param.23) | copy-start | bytes 147460
  7.2 144.6 %all-gather.19.cloned.1.call-start = ((), (), s32[]{:S(2)}) async-start(), calls=%async_computation.27 | async-start | bytes 5898240 | tf_op jit(solution)/shard_map/all_gather | solution.py:133
  7.9 153.1 %all-gather.9.cloned.1.call-start = ((), (), s32[]{:S(2)}) async-start(), calls=%async_computation.15 | async-start | bytes 1327104 | tf_op jit(solution)/shard_map/all_gather | solution.py:141
  8.7 253.0 %all-gather.11.cloned.1.call-start = ((), (), s32[]{:S(2)}) async-start(), calls=%async_computation.16 | async-start | bytes 4866048 | tf_op jit(solution)/shard_map/all_gather | solution.py:135
  13.1 142.2 %copy-start.18 = (s32[1,384,8]{2,1,0:T(8,128)}, s32[1,384,8]{2,1,0:T(8,128)S(1)}, u32[]{:S(2)}) copy-start(s32[1,384,8]{2,1,0:T(8,128)S(1)} %copy.87) | copy-start | bytes 36868
  13.3 142.1 %copy-start.49 = (s32[3072]{0:T(1024)}, s32[3072]{0:T(1024)S(1)}, u32[]{:S(2)}) copy-start(s32[3072]{0:T(1024)S(1)} %eq.76) | copy-start | bytes 36868
  56.2 99.2 %copy-start.43 = (f32[1536]{0:T(1024)}, f32[1536]{0:T(1024)S(1)}, u32[]{:S(2)}) copy-start(f32[1536]{0:T(1024)S(1)} %convert_element_type.157) | copy-start | bytes 18436
  121.7 36.9 %copy-start.27 = (bf16[1536,128]{1,0:T(8,128)(2,1)}, bf16[1536,128]{1,0:T(8,128)(2,1)S(1)}, u32[]{:S(2)}) copy-start(bf16[1536,128]{1,0:T(8,128)(2,1)S(1)} %all_gather.36) | copy-start | bytes 1179652
  137.3 19.7 copy-start.25
  138.2 18.7 copy-start.54
  151.8 14.1 copy-start.21
  151.8 14.1 copy-start.23
  226.8 20.2 copy-start.51
  237.9 23.8 %all-to-all-start = ((bf16[4,384,384]{1,2,0:T(8,128)(2,1)}), bf16[4,384,384]{1,2,0:T(8,128)(2,1)}, u32[]{:S(2)}, u32[]{:S(2)}) async-start(bf16[4,384,384]{1,2,0:T(8,128)(2,1)} %copy.86), calls=%async_computation | async-start | bytes 2359296 | tf_op jit(solution)/shard_map/all_to_all | solution.py:184
  268.7 75.6 %copy-start.13 = (bf16[384,1536]{1,0:T(8,128)(2,1)}, bf16[384,1536]{1,0:T(8,128)(2,1)S(1)}, u32[]{:S(2)}) copy-start(bf16[384,1536]{1,0:T(8,128)(2,1)S(1)} %multiply_convert_fusion.4) | copy-start | bytes 3538948
  269.2 25.1 %copy-start.19 = (s32[1,384,8]{2,1,0:T(8,128)S(1)}, s32[1,384,8]{2,1,0:T(8,128)}, u32[]{:S(2)}) copy-start(s32[1,384,8]{2,1,0:T(8,128)} %copy-done.18) | copy-start | bytes 36868
  269.2 26.0 %copy-start.50 = (s32[3072]{0:T(1024)S(1)}, s32[3072]{0:T(1024)}, u32[]{:S(2)}) copy-start(s32[3072]{0:T(1024)} %copy-done.49) | copy-start | bytes 36868
  338.3 262.3 %all-to-all-start.3 = ((bf16[32,120,1536]{2,1,0:T(8,128)(2,1)}), bf16[32,120,1536]{2,1,0:T(8,128)(2,1)}, u32[]{:S(2)}, u32[]{:S(2)}) async-start(bf16[32,120,1536]{2,1,0:T(8,128)(2,1)} %bitcast.350), calls=%async_computation.3 | async-start | bytes 23592960 | tf_op jit(solution)/shard_map/all_to_all | solution.py:230
  343.7 529.2 %all-gather.15.cloned.1.call-start = ((), (), s32[]{:S(2)}) async-start(), calls=%async_computation.18 | async-start | bytes 7864320 | tf_op jit(solution)/shard_map/all_gather | solution.py:147
  600.6 262.2 %all-to-all-start.1 = ((bf16[32,120,1536]{2,1,0:T(8,128)(2,1)}), bf16[32,120,1536]{2,1,0:T(8,128)(2,1)}, u32[]{:S(2)}, u32[]{:S(2)}) async-start(bf16[32,120,1536]{2,1,0:T(8,128)(2,1)} %bitcast.349), calls=%async_computation.1 | async-start | bytes 23592960 | tf_op jit(solution)/shard_map/all_to_all | solution.py:199
  605.9 280.7 %all-gather.13.cloned.1.call-start = ((), (), s32[]{:S(2)}) async-start(), calls=%async_computation.17 | async-start | bytes 7864320 | tf_op jit(solution)/shard_map/all_gather | solution.py:146
  606.5 293.8 %all-gather.17.cloned.1.call-start = ((), (), s32[]{:S(2)}) async-start(), calls=%async_computation.19 | async-start | bytes 7864320 | tf_op jit(solution)/shard_map/all_gather | solution.py:148
  958.0 262.2 %all-to-all-start.2 = ((bf16[4,960,1536]{2,0,1:T(4,128)(2,1)}), bf16[4,960,1536]{2,0,1:T(4,128)(2,1)}, u32[]{:S(2)}, u32[]{:S(2)}) async-start(bf16[4,960,1536]{2,0,1:T(4,128)(2,1)} %copy.96), calls=%async_computation.2 | async-start | bytes 23592960 | tf_op jit(solution)/shard_map/all_to_all | solution.py:205
  963.3 879.0 %reduce-scatter.30.cloned.1.call-start = ((), (), s32[]{:S(2)}) async-start(), calls=%async_computation.29 | async-start | bytes 7864320
  996.3 857.0 %reduce-scatter.26.cloned.1.call-start = ((), (), s32[]{:S(2)}) async-start(), calls=%async_computation.26 | async-start | bytes 7864320 | tf_op jit(solution)/shard_map/reduce_scatter | solution.py:259
  1220.2 262.3 %all-to-all-start.4 = ((bf16[4,960,1536]{2,0,1:T(4,128)(2,1)}), bf16[4,960,1536]{2,0,1:T(4,128)(2,1)}, u32[]{:S(2)}, u32[]{:S(2)}) async-start(bf16[4,960,1536]{2,0,1:T(4,128)(2,1)} %copy.101), calls=%async_computation.4 | async-start | bytes 23592960 | tf_op jit(solution)/shard_map/all_to_all | solution.py:266
  1225.6 631.3 %reduce-scatter.24.cloned.1.call-start = ((), (), s32[]{:S(2)}) async-start(), calls=%async_computation.25 | async-start | bytes 7864320 | tf_op jit(solution)/shard_map/reduce_scatter | solution.py:256
  1286.5 207.9 %copy-start.33 = (f32[384,8]{1,0:T(8,128)}, f32[384,8]{1,0:T(8,128)S(1)}, u32[]{:S(2)}) copy-start(f32[384,8]{1,0:T(8,128)S(1)} %get-tuple-element.231) | copy-start | bytes 36868
  1494.4 25.6 %copy-start.41 = (s32[1,384,8]{1,2,0:T(8,128)S(1)}, s32[1,384,8]{1,2,0:T(8,128)}, u32[]{:S(2)}) copy-start(s32[1,384,8]{1,2,0:T(8,128)} %param.20) | copy-start | bytes 36868
  1520.7 11.5 copy-start.10
  1520.7 11.5 copy-start.48
  1520.7 11.5 copy-start.60
  1556.5 26.2 %copy-start.5 = (bf16[1536,2,64]{0,2,1:T(8,128)(2,1)S(1)}, bf16[1536,2,64]{0,2,1:T(8,128)(2,1)}, u32[]{:S(2)}) copy-start(bf16[1536,2,64]{0,2,1:T(8,128)(2,1)} %copy-done.4) | copy-start | bytes 1179652
  1556.5 26.2 %copy-start.8 = (bf16[1536,2,3,64]{0,3,2,1:T(8,128)(2,1)S(1)}, bf16[1536,2,3,64]{0,3,2,1:T(8,128)(2,1)}, u32[]{:S(2)}) copy-start(bf16[1536,2,3,64]{0,3,2,1:T(8,128)(2,1)} %copy-done.7) | copy-start | bytes 3538948
  1556.5 26.2 %copy-start.15 = (bf16[1536,2,64]{0,2,1:T(8,128)(2,1)S(1)}, bf16[1536,2,64]{0,2,1:T(8,128)(2,1)}, u32[]{:S(2)}) copy-start(bf16[1536,2,64]{0,2,1:T(8,128)(2,1)} %copy-done.14) | copy-start | bytes 1179652
  1556.5 26.2 %copy-start.37 = (s32[1,1536]{1,0:T(1,128)S(1)}, s32[1,1536]{1,0:T(1,128)}, u32[]{:S(2)}) copy-start(s32[1,1536]{1,0:T(1,128)} %param.19) | copy-start | bytes 18436
  1556.5 26.2 %copy-start.64 = (s32[3]{0:T(128)S(1)}, s32[3]{0:T(128)}, u32[]{:S(2)}) copy-start(s32[3]{0:T(128)} %copy-done.63) | copy-start | bytes 40
  1556.5 19.6 all-to-all-start.5
  1562.3 298.0 %reduce-scatter.28.cloned.1.call-start = ((), (), s32[]{:S(2)}) async-start(), calls=%async_computation.28 | async-start | bytes 811008
  1565.9 336.6 %reduce-scatter.18.cloned.1.call-start = ((), (), s32[]{:S(2)}) async-start(), calls=%async_computation.22 | async-start | bytes 442368 | tf_op jit(solution)/shard_map/reduce_scatter | solution.py:349
  1602.5 14.3 copy-start.39
  1671.6 14.2 copy-start.39
  1740.5 14.2 copy-start.39
  1804.7 99.3 %reduce-scatter.20.cloned.1.call-start = ((), (), s32[]{:S(2)}) async-start(), calls=%async_computation.23 | async-start | bytes 442368 | tf_op jit(solution)/shard_map/reduce_scatter | solution.py:352
  1810.9 94.5 %reduce-scatter.16.cloned.1.call-start = ((), (), s32[]{:S(2)}) async-start(), calls=%async_computation.21 | async-start | bytes 1327104 | tf_op jit(solution)/shard_map/reduce_scatter | solution.py:346
  1820.1 136.6 %reduce-scatter.14.cloned.1.call-start = ((), (), s32[]{:S(2)}) async-start(), calls=%async_computation.20 | async-start | bytes 5898240 | tf_op jit(solution)/shard_map/reduce_scatter | solution.py:358
  1834.1 265.3 %reduce-scatter.22.cloned.1.call-start = ((), (), s32[]{:S(2)}) async-start(), calls=%async_computation.24 | async-start | bytes 9732096 | tf_op jit(solution)/shard_map/reduce_scatter | solution.py:372
  (46 other events, 285.7 us)
Sparse Core Ops, SparseCore 0:
  9.9 58.6 all-gather.18
  70.2 24.4 all-gather.8
  97.7 62.6 all-gather.10
  346.0 70.5 all-gather.14
  608.3 70.5 all-gather.12
  680.5 70.0 all-gather.16
  996.4 70.5 reduce-scatter.29
  1070.0 70.2 reduce-scatter.25
  1238.5 70.5 reduce-scatter.23
  1568.0 94.1 reduce-scatter.27
  1804.8 30.0 reduce-scatter.17
  1837.1 28.8 reduce-scatter.19
  1868.2 31.3 reduce-scatter.15
  1902.4 54.3 reduce-scatter.13
  1963.1 136.2 reduce-scatter.21
where the time goes:
time: 2120 us; the launch traced here: 2110 us
  waiting for transfers between devices  1050 us (50%)
  local copies, waits for them, and re-layouts  387 us (18%)
  matrix products  319 us (15%)
  blocking collectives  149 us (7%)
  other arithmetic  139 us (7%)
  starting transfers between devices  36.9 us (2%)
    all_to_all x1, waiting for transfers between devices, per_device(): lax.all_to_all(send_rows, 'cols', split_axis=0, concat_axis=1, tiled=True)  245 us
    all_to_all x1, waiting for transfers between devices, per_device(): lax.all_to_all(grad_send, 'cols', split_axis=0, concat_axis=1, tiled=True)  242 us
    all_to_all x1, waiting for transfers between devices, per_device(): lax.all_to_all(grad_inputs, 'cols', split_axis=1, concat_axis=0, tiled=True)  196 us
    all_to_all x1, waiting for transfers between devices, per_device(): lax.all_to_all(expert_out, 'cols', split_axis=1, concat_axis=0, tiled=True)  148 us
    reduce_scatter x1, waiting for transfers between devices, per_device(): lax.psum_scatter(grad_out_w, ('rows', 'cols'), scatter_dimension=0, tiled...  140 us
    unnamed x2, blocking collectives  80.6 us
    dynamic_update_slice x6, local copies, waits for them, and re-layouts, per_device(): lax.map(partial(attend_block, queries, key_rows, value_rows, segments, bl...  50.6 us
    reduce_scatter x1, waiting for transfers between devices, per_device(): lax.psum_scatter((scale_attn * (grad_unit_attn - unit_attn * jnp.mean(gra...  49.7 us
  transfers between devices with their start and end apart: 21, of which 8 were waited for; matrix products, arithmetic and copies ran while one was open for 33% of the time, Pallas kernels for 0%

commit v1 on v0

v1 whole, which is shorter than its diff:
```python
from functools import partial

import jax
import jax.numpy as jnp
from jax import lax
from jax.experimental import pallas as pl
from jax.experimental.pallas import tpu as pltpu
from jax.sharding import PartitionSpec as P

HEAD_SIZE = 64
LANES = 128
LONGEST_DOC = 768

res_scale = 0.22
att_scale = 0.015625
norm_eps = 1e-06
rope_base = 10000.0
masked_score = -1e30
log2_e = 1.4426950408889634
highest = lax.Precision.HIGHEST
bf16 = jnp.bfloat16
f32 = jnp.float32


def rms_scale(hidden_rows):
    return lax.rsqrt(jnp.mean(hidden_rows * hidden_rows, axis=-1, keepdims=True) + norm_eps)


def dot_nt(left, right):
    return lax.dot_general(left, right, (((1,), (1,)), ((), ())), preferred_element_type=f32)


def dot_tn(left, right):
    return lax.dot_general(left, right, (((0,), (0,)), ((), ())), preferred_element_type=f32)


def dot_nn(left, right):
    return jnp.dot(left, right, preferred_element_type=f32)


def rows_swap(array, distance):
    return lax.ppermute(array, "rows", [(i, i ^ distance) for i in range(4)])


def halves(array):
    axis = 0 if array.shape[0] % 2 == 0 else 1
    cut = array.shape[axis] // 2
    return (
        axis,
        lax.slice_in_dim(array, 0, cut, axis=axis),
        lax.slice_in_dim(array, cut, 2 * cut, axis=axis),
    )


def gather_near(array):
    return rows_swap(array, 1), rows_swap(array, 2)


def gather_far(array, from_x, from_y):
    axis, first_y, _ = halves(from_y)
    _, _, second_x = halves(from_x)
    far = jnp.concatenate([rows_swap(first_y, 1), rows_swap(second_x, 2)], axis=axis)
    return [array, from_x, from_y, far]


def rows_exchange(pieces):
    return [pieces[0]] + [rows_swap(pieces[j], j) for j in (1, 2, 3)]


def reduce_far(pieces):
    _, first, second = halves(pieces[3])
    return rows_swap(first, 1), rows_swap(second, 2)


def reduce_add(pieces, from_x, from_y):
    axis, first_x, second_x = halves(pieces[1])
    _, first_y, second_y = halves(pieces[2])
    return (
        jnp.concatenate([first_x, add_low(second_x, from_y)], axis=axis),
        jnp.concatenate([add_low(first_y, from_x), second_y], axis=axis),
    )


def reduce_near(to_x, to_y):
    return rows_swap(to_x, 1), rows_swap(to_y, 2)


def reduce_first(pieces):
    far = rows_swap(pieces[3][0], 1), rows_swap(pieces[3][1], 2)
    near = rows_swap(pieces[1][0], 1), rows_swap(pieces[2][1], 2)
    return far, near


def reduce_second(pieces, far):
    return add_low(pieces[1][1], far[1]), add_low(pieces[2][0], far[0])


def reduce_total(pieces, near, late):
    return [
        add_wide([pieces[0][0], near[0], late[1]]),
        add_wide([pieces[0][1], late[0], near[1]]),
    ]


def add_wide(arrays):
    return sum(array.astype(f32) for array in arrays)


def add_low_all(array):
    return jnp.sum(array.astype(f32), axis=0).astype(bf16)


def add_low(left, right):
    return (left.astype(f32) + right.astype(f32)).astype(bf16)


def chip_shift(array, distance):
    count = lax.axis_size("cols")
    return lax.ppermute(
        array, "cols", [(i, (i + 2 * distance) % count) for i in range(count)]
    )


def core_swap(array):
    count = lax.axis_size("cols")
    return lax.ppermute(array, "cols", [(i, i ^ 1) for i in range(count)])


def chips_exchange(array):
    count = lax.axis_size("cols")
    alike = [list(range(core, count, 2)) for core in range(2)]
    return lax.all_to_all(array, "cols", 0, 0, axis_index_groups=alike, tiled=True)


def chips_spread(array):
    chips = lax.axis_size("cols") // 2
    return chips_exchange(jnp.broadcast_to(array, (chips,) + array.shape))


def cores_in_order(mine, other, core, axis):
    return jnp.stack(
        [jnp.where(core == 0, mine, other), jnp.where(core == 0, other, mine)], axis=axis
    )


def call_params(mebibytes):
    return pltpu.CompilerParams(vmem_limit_bytes=mebibytes * 1024 * 1024)


def cost(micros):
    return pl.CostEstimate(flops=int(micros * 1.15e9), bytes_accessed=0, transcendentals=0)


def turn(rows, cosine, sine):
    lane = lax.broadcasted_iota(jnp.int32, rows.shape, 1)
    partner = jnp.where(
        (lane & (HEAD_SIZE - 1)) < HEAD_SIZE // 2,
        pltpu.roll(rows, LANES - HEAD_SIZE // 2, 1),
        pltpu.roll(rows, HEAD_SIZE // 2, 1),
    )
    return rows * cosine + partner * sine


def project_kernel(meta, *refs):
    parts, found, swapped, gain, cosine, sine = refs[:4], refs[4], refs[5], *refs[6:9]
    q_out, k_out, v_out, n_out, w_out = refs[9:]
    step = pl.program_id(0)
    chips, rows, _ = found.shape

    @pl.when(step == 0)
    def _():
        first_core = meta[2] == 0
        for chip in range(chips):
            mine, other = found[chip], swapped[chip]
            at = 2 * rows * chip
            w_out[at : at + rows, :] = jnp.where(first_core, mine, other)
            w_out[at + rows : at + 2 * rows, :] = jnp.where(first_core, other, mine)

    for index, part in enumerate(parts):

        @pl.when(step == index)
        def _(part=part):
            rows = part[...].astype(f32)
            n_out[0] = (rows * rms_scale(rows) * gain[...]).astype(bf16)

    linear = dot_nn(n_out[0], w_out[...])
    q_cols, k_cols = q_out.shape[1], k_out.shape[1]
    cos_rows, sin_rows = cosine[...], sine[...]
    turned = jnp.concatenate(
        [
            turn(linear[:, at : at + LANES], cos_rows, sin_rows)
            for at in range(0, q_cols + k_cols, LANES)
        ],
        axis=1,
    ).astype(bf16)
    q_out[...] = turned[:, :q_cols]
    k_out[...] = turned[:, q_cols:]
    v_out[...] = linear[:, q_cols + k_cols :].astype(bf16)


def project(meta, parts, found, swapped, gain, cosine, sine, q_cols, k_cols):
    tok, width = parts[0].shape
    length = 4 * tok
    whole = pl.BlockSpec(memory_space=pltpu.VMEM)

    def natural(step, meta):
        return (step ^ meta[0], 0)

    return pl.pallas_call(
        project_kernel,
        grid_spec=pltpu.PrefetchScalarGridSpec(
            num_scalar_prefetch=1,
            grid=(4,),
            in_specs=[whole] * 7
            + [pl.BlockSpec((tok, LANES), natural), pl.BlockSpec((tok, LANES), natural)],
            out_specs=[
                pl.BlockSpec((tok, q_cols), natural),
                pl.BlockSpec((tok, k_cols), natural),
                pl.BlockSpec((tok, k_cols), natural),
                pl.BlockSpec((1, tok, width), lambda step, meta: (step, 0, 0)),
                pl.BlockSpec((width, q_cols + 2 * k_cols), lambda step, meta: (0, 0)),
            ],
        ),
        out_shape=[
            jax.ShapeDtypeStruct((length, q_cols), bf16),
            jax.ShapeDtypeStruct((length, k_cols), bf16),
            jax.ShapeDtypeStruct((length, k_cols), bf16),
            jax.ShapeDtypeStruct((4, tok, width), bf16),
            jax.ShapeDtypeStruct((width, q_cols + 2 * k_cols), bf16),
        ],
        compiler_params=call_params(32),
        cost_estimate=cost(1),
        name="project",
    )(meta, *parts, found, swapped, gain, cosine, sine)


def attend_kernel(meta, queries, keys, values, starts, out, lse, *, bands):
    block = pl.program_id(0)
    rows = queries.shape[0]
    first = meta[3 + block]
    heads = queries.shape[1] // HEAD_SIZE
    group = queries.shape[1] // keys.shape[1]
    for band in range(1, bands + 1):

        @pl.when(block - first + 1 == band)
        def _(band=band):
            width = band * rows
            base = pl.multiple_of(first * rows, rows)
            key_band = keys[pl.ds(base, width), :]
            value_band = values[pl.ds(base, width), :]
            query_pos = block * rows + lax.broadcasted_iota(jnp.int32, (rows, width), 0)
            key_pos = base + lax.broadcasted_iota(jnp.int32, (rows, width), 1)
            allowed = (key_pos >= starts[...]) & (key_pos <= query_pos)
            results = []
            for head in range(heads):
                at = head // group * HEAD_SIZE
                scores = dot_nt(
                    queries[:, head * HEAD_SIZE : (head + 1) * HEAD_SIZE],
                    key_band[:, at : at + HEAD_SIZE],
                )
                scores = jnp.where(allowed, scores, masked_score)
                top = jnp.max(scores, axis=1, keepdims=True)
                weights = jnp.exp2((scores - top) * (att_scale * log2_e))
                total = jnp.sum(weights, axis=1, keepdims=True)
                result = dot_nn(weights.astype(bf16), value_band[:, at : at + HEAD_SIZE])
                results.append(result * (1.0 / total))
                lse[:, head : head + 1] = top * (att_scale * log2_e) + jnp.log2(total)
            out[0] = jnp.concatenate(results, axis=1).astype(bf16)


def attend(meta, queries, keys, values, starts, tok):
    length, q_cols = queries.shape
    k_cols = keys.shape[1]
    blocks = length // tok
    whole = pl.BlockSpec(memory_space=pltpu.VMEM)
    return pl.pallas_call(
        partial(attend_kernel, bands=min(blocks, LONGEST_DOC // tok + 1)),
        grid_spec=pltpu.PrefetchScalarGridSpec(
            num_scalar_prefetch=1,
            grid=(blocks,),
            in_specs=[
                pl.BlockSpec((tok, q_cols), lambda i, meta: (i, 0)),
                whole,
                whole,
                pl.BlockSpec((tok, 1), lambda i, meta: (i, 0)),
            ],
            out_specs=[
                pl.BlockSpec((1, tok, q_cols), lambda i, meta: (i, 0, 0)),
                pl.BlockSpec((tok, 8), lambda i, meta: (i, 0)),
            ],
        ),
        out_shape=[
            jax.ShapeDtypeStruct((blocks, tok, q_cols), bf16),
            jax.ShapeDtypeStruct((length, 8), f32),
        ],
        compiler_params=call_params(32),
        cost_estimate=cost(1),
        name="attend",
    )(meta, queries, keys, values, starts)


def attend_back_kernel(
    meta, queries, grads, lse, starts, keys, values, cosine, sine, out, key_sum, value_sum, *, bands
):
    block = pl.program_id(0)
    rows = queries.shape[0]
    first = meta[3 + block]
    q_cols, k_cols = queries.shape[1], keys.shape[1]
    heads = q_cols // HEAD_SIZE
    group = q_cols // k_cols

    @pl.when(block == 0)
    def _():
        key_sum[...] = jnp.zeros_like(key_sum)
        value_sum[...] = jnp.zeros_like(value_sum)

    for band in range(1, bands + 1):

        @pl.when(block - first + 1 == band)
        def _(band=band):
            width = band * rows
            base = pl.multiple_of(first * rows, rows)
            key_band = keys[pl.ds(base, width), :]
            value_band = values[pl.ds(base, width), :]
            key_pos = base + lax.broadcasted_iota(jnp.int32, (width, rows), 0)
            query_pos = block * rows + lax.broadcasted_iota(jnp.int32, (width, rows), 1)
            allowed = (key_pos >= starts[...]) & (key_pos <= query_pos)
            query_grads, key_parts, value_parts = [], [], []
            for kv_head in range(k_cols // HEAD_SIZE):
                at = kv_head * HEAD_SIZE
                key_rows = key_band[:, at : at + HEAD_SIZE]
                value_rows = value_band[:, at : at + HEAD_SIZE]
                key_part = jnp.zeros((width, HEAD_SIZE), f32)
                value_part = jnp.zeros((width, HEAD_SIZE), f32)
                for head in range(kv_head * group, (kv_head + 1) * group):
                    query_rows = queries[:, head * HEAD_SIZE : (head + 1) * HEAD_SIZE]
                    grad_rows = grads[0, :, head * HEAD_SIZE : (head + 1) * HEAD_SIZE]
                    scores = dot_nt(key_rows, query_rows)
                    probs = jnp.where(
                        allowed,
                        jnp.exp2(scores * (att_scale * log2_e) - lse[head : head + 1, :]),
                        0.0,
                    )
                    grad_probs = dot_nt(value_rows, grad_rows)
                    delta = jnp.sum(probs * grad_probs, axis=0, keepdims=True)
                    grad_scores = (probs * (grad_probs - delta)).astype(bf16)
                    value_part += dot_nn(probs.astype(bf16), grad_rows)
                    key_part += dot_nn(grad_scores, query_rows)
                    query_grads.append(dot_tn(grad_scores, key_rows))
                key_parts.append(key_part)
                value_parts.append(value_part)
            key_sum[pl.ds(base, width), :] += jnp.concatenate(key_parts, axis=1)
            value_sum[pl.ds(base, width), :] += jnp.concatenate(value_parts, axis=1)
            here = pl.ds(pl.multiple_of(block * rows, rows), rows)
            query_grad = jnp.concatenate(query_grads, axis=1) * att_scale
            turned = [
                turn(query_grad[:, c : c + LANES], cosine[here, :], -sine[here, :])
                for c in range(0, q_cols, LANES)
            ]
            out[block ^ meta[0], :, :q_cols] = jnp.concatenate(turned, axis=1).astype(bf16)

    @pl.when(block == pl.num_programs(0) - 1)
    def _():
        for part in range(4):
            here = pl.ds(pl.multiple_of((meta[0] ^ part) * rows, rows), rows)
            key_grad = key_sum[here, :] * att_scale
            turned = [
                turn(key_grad[:, c : c + LANES], cosine[here, :], -sine[here, :])
                for c in range(0, k_cols, LANES)
            ]
            out[part, :, q_cols : q_cols + k_cols] = jnp.concatenate(turned, axis=1).astype(bf16)
            out[part, :, q_cols + k_cols :] = value_sum[here, :].astype(bf16)


def attend_back(meta, queries, grads, lse, starts, keys, values, cosine, sine, tok):
    length, q_cols = queries.shape
    k_cols = keys.shape[1]
    blocks = length // tok
    whole = pl.BlockSpec(memory_space=pltpu.VMEM)
    return pl.pallas_call(
        partial(attend_back_kernel, bands=min(blocks, LONGEST_DOC // tok + 1)),
        grid_spec=pltpu.PrefetchScalarGridSpec(
            num_scalar_prefetch=1,
            grid=(blocks,),
            in_specs=[
                pl.BlockSpec((tok, q_cols), lambda i, meta: (i, 0)),
                pl.BlockSpec((1, tok, q_cols), lambda i, meta: (i, 0, 0)),
                pl.BlockSpec((8, tok), lambda i, meta: (0, i)),
                pl.BlockSpec((1, tok), lambda i, meta: (0, i)),
                whole,
                whole,
                whole,
                whole,
            ],
            out_specs=pl.BlockSpec(
                (blocks, tok, q_cols + 2 * k_cols), lambda i, meta: (0, 0, 0)
            ),
            scratch_shapes=[
                pltpu.VMEM((length, k_cols), f32),
                pltpu.VMEM((length, k_cols), f32),
            ],
        ),
        out_shape=jax.ShapeDtypeStruct((blocks, tok, q_cols + 2 * k_cols), bf16),
        compiler_params=call_params(40),
        cost_estimate=cost(29),
        name="attend_back",
    )(meta, queries, grads, lse, starts, keys, values, cosine, sine)


def low_pair(values):
    high = values.astype(bf16)
    return high, (values - high.astype(f32)).astype(bf16)


def mix_kernel(
    meta, heads, out_parts, tokens, member, gain, router, mixed_out, rows_out, gates_out, *, experts
):
    width = tokens.shape[1]
    branch = sum(dot_nn(heads[meta[0] ^ part], out_parts[part]) for part in range(4))
    mixed = tokens[...].astype(f32) + res_scale * branch
    mixed_out[...] = mixed
    normed = (mixed * rms_scale(mixed) * gain[...]).astype(bf16)
    logits = dot_nn(normed, router[...])
    named = member[...] > 0
    logits = jnp.where(named, logits, masked_score)
    lifted = jnp.exp(logits - jnp.max(logits, axis=1, keepdims=True))
    lifted = jnp.where(named, lifted, 0.0)
    gates = lifted * (1.0 / jnp.sum(lifted, axis=1, keepdims=True))
    gates_out[...] = gates
    high, low = low_pair(gates)
    low = pltpu.roll(low.astype(f32), experts, 1)
    rows_out[:, :width] = normed
    rows_out[:, width:] = (high.astype(f32) + low).astype(bf16)


def mix(meta, heads, out_parts, tokens, member, gain, router, experts):
    tok, width = tokens.shape
    whole = pl.BlockSpec(memory_space=pltpu.VMEM)
    return pl.pallas_call(
        partial(mix_kernel, experts=experts),
        in_specs=[pl.BlockSpec(memory_space=pltpu.SMEM)] + [whole] * 6,
        out_specs=[whole] * 3,
        out_shape=[
            jax.ShapeDtypeStruct((tok, width), f32),
            jax.ShapeDtypeStruct((tok, width + LANES), bf16),
            jax.ShapeDtypeStruct((tok, LANES), f32),
        ],
        compiler_params=call_params(40),
        cost_estimate=cost(6),
        name="mix",
    )(meta, heads, out_parts, tokens, member, gain, router)


def unmix_kernel(
    meta, came, last, mixed_in, cotangent, gates, gain, router, out_parts, heads,
    mixed_grad, heads_out, mine_out, other_out, *, experts
):
    width = cotangent.shape[1]
    summed = came[...].astype(f32) + last[...].astype(f32)
    beside = summed[:, width:]
    lane = lax.broadcasted_iota(jnp.int32, beside.shape, 1)
    weighted = jnp.where(lane < experts, beside + pltpu.roll(beside, LANES - experts, 1), 0.0)
    logit_grads = weighted - gates[...] * jnp.sum(weighted, axis=1, keepdims=True)
    high, low = low_pair(logit_grads)
    normed_grad = summed[:, :width] + dot_nt(high, router[...]) + dot_nt(low, router[...])
    mixed = mixed_in[...]
    scale = rms_scale(mixed)
    unit = mixed * scale
    normed = (unit * gain[...]).astype(bf16)
    one_lane = lax.broadcasted_iota(jnp.int32, (unit.shape[0], LANES), 1) == experts
    one_lane = one_lane.astype(f32).astype(bf16)
    gain_high, gain_low = low_pair(normed_grad * unit)
    shares = dot_tn(normed, high) + dot_tn(normed, low)
    shares = (shares + dot_tn(gain_high, one_lane) + dot_tn(gain_low, one_lane)).astype(bf16)
    unit_grad = normed_grad * gain[...]
    grad = cotangent[...].astype(f32) + scale * (
        unit_grad - unit * jnp.mean(unit_grad * unit, axis=-1, keepdims=True)
    )
    mixed_grad[...] = grad
    branch = (res_scale * grad).astype(bf16)
    for part in range(4):
        heads_out[meta[0] ^ part] = dot_nt(branch, out_parts[part]).astype(bf16)
    first_core = meta[2] == 0
    _, chips, sixth, _ = mine_out.shape
    tok = branch.shape[0]
    for part in range(4):
        wide = dot_tn(heads[part], branch).astype(bf16)
        wide = jnp.concatenate([wide, shares[part * tok : (part + 1) * tok]], axis=1)
        for chip in range(chips):
            at = 2 * chip * sixth
            even, odd = wide[at : at + sixth], wide[at + sixth : at + 2 * sixth]
            mine_out[part, chip] = jnp.where(first_core, even, odd)
            other_out[part, chip] = jnp.where(first_core, odd, even)


def unmix(meta, came, last, mixed, cotangent, gates, gain, router, out_parts, heads, experts, chips):
    tok, width = mixed.shape
    wide = (4, chips, tok // (2 * chips), width + LANES)
    whole = pl.BlockSpec(memory_space=pltpu.VMEM)
    return pl.pallas_call(
        partial(unmix_kernel, experts=experts),
        in_specs=[pl.BlockSpec(memory_space=pltpu.SMEM)] + [whole] * 9,
        out_specs=[whole] * 4,
        out_shape=[
            jax.ShapeDtypeStruct((tok, width), f32),
            jax.ShapeDtypeStruct((4, tok, out_parts.shape[1]), bf16),
            jax.ShapeDtypeStruct(wide, bf16),
            jax.ShapeDtypeStruct(wide, bf16),
        ],
        compiler_params=call_params(32),
        cost_estimate=cost(12),
        name="unmix",
    )(meta, came, last, mixed, cotangent, gates, gain, router, out_parts, heads)


def hidden_weights(parts, cut, ffe):
    tiles = 2 * ffe // LANES
    return jnp.concatenate(
        [
            jnp.concatenate([ref[0, t * cut : (t + 1) * cut, :] for t in range(tiles)], axis=1)
            for ref in parts
        ],
        axis=0,
    )


def down_weights(parts, cut, ffe):
    first = 2 * ffe // LANES * cut
    return jnp.concatenate(
        [
            ref[0, first + t * ffe : first + (t + 1) * ffe, :]
            for ref in parts
            for t in range(cut // LANES)
        ],
        axis=1,
    )


def experts_kernel(meta, *refs, experts, slots, local, final, earlier):
    blocks = 4
    x_refs, g_refs, refs = refs[:blocks], refs[blocks : 2 * blocks], refs[2 * blocks :]
    early, refs = refs[:earlier], refs[earlier:]
    parts, refs = refs[:4], refs[4:]
    returned_out, refs = refs[: blocks * final], refs[blocks * final :]
    x_out, g_out, active_out, grads_out, out_kept, dx_kept, t_kept, refs = *refs[:7], refs[7:]
    x_rows, g_rows, gate_kept, rows_sent, x_here, g_here, arrived, refs = *refs[:7], refs[7:]
    own = pl.program_id(0)
    own_count = x_rows.shape[0]
    tok = x_refs[0].shape[0]
    width = x_rows.shape[2]
    cut = width // 4
    ffe = active_out.shape[2]
    row, first_expert = meta[0], meta[1]
    loads = [
        (
            pltpu.make_async_copy(x_refs[block], x_here.at[block % 2], arrived.at[0, block % 2]),
            pltpu.make_async_copy(g_refs[block], g_here.at[block % 2], arrived.at[1, block % 2]),
        )
        for block in range(blocks)
    ]
    if final:
        ranks_kept, returned, sent, refs = *refs[:3], refs[3:]
    fetches = [
        [
            pltpu.make_async_copy(
                early[which].at[:, pl.ds(block * slots, slots), :],
                refs[which].at[block % 2],
                refs[3].at[which, block % 2],
            )
            for which in range(earlier)
        ]
        for block in range(blocks)
    ]
    row_copies = [
        pltpu.make_async_copy(x_rows, x_out, rows_sent.at[0]),
        pltpu.make_async_copy(g_rows, g_out, rows_sent.at[1]),
    ]

    def columns(part, start=0):
        return pl.ds(pl.multiple_of(start + (row ^ part) * cut, LANES), cut)

    @pl.when(own == 0)
    def _():
        for load in loads[0]:
            load.start()
        slot = lax.broadcasted_iota(jnp.int32, (slots, tok), 0).astype(f32)
        lower = (
            lax.broadcasted_iota(jnp.int32, (tok, tok), 0)
            > lax.broadcasted_iota(jnp.int32, (tok, tok), 1)
        ).astype(f32).astype(bf16)
        source = lax.broadcasted_iota(jnp.int32, (LANES, LANES), 1)
        target = lax.broadcasted_iota(jnp.int32, (LANES, LANES), 0)
        choose = (source == target + first_expert).astype(f32).astype(bf16)
        for block in range(blocks):
            for load in loads[block + 1] if block + 1 < blocks else ():
                load.start()
            for load in loads[block]:
                load.wait()
            x_block, g_block = x_here.at[block % 2], g_here.at[block % 2]
            member = g_block[:, width:]
            rank = jnp.where(member > 0, dot_nn(lower, member), -1.0).astype(bf16)
            if final:
                ranks_kept[block] = dot_nt(rank, choose)
            rank_rows = dot_nt(choose, rank)
            pick = jnp.concatenate(
                [
                    (rank_rows[index : index + 1, :] == slot).astype(f32).astype(bf16)
                    for index in range(local, local + own_count)
                ],
                axis=0,
            )
            beside = dot_nn(pick, x_block[:, width:])
            lane = lax.broadcasted_iota(jnp.int32, beside.shape, 1)
            named = lax.broadcasted_iota(jnp.int32, beside.shape, 0) // slots
            named = named + first_expert + local
            gates = jnp.sum(
                jnp.where((lane == named) | (lane == named + experts), beside, 0.0),
                axis=1,
                keepdims=True,
            )
            here = slice(block * slots, (block + 1) * slots)
            x_part = dot_nn(pick, x_block[:, :width]).astype(bf16)
            g_part = dot_nn(pick, g_block[:, :width]).astype(bf16)
            for index in range(own_count):
                rows = slice(index * slots, (index + 1) * slots)
                gate_kept[index, here, :] = gates[rows]
                for part in range(4):
                    there = slice(part * cut, (part + 1) * cut)
                    x_rows[index, here, columns(part)] = x_part[rows, there]
                    g_rows[index, here, columns(part)] = g_part[rows, there]
        for copy in row_copies:
            copy.start()

    @pl.when(own == own_count - 1)
    def _():
        for fetch in fetches[0] + fetches[1]:
            fetch.start()

    hidden_w = hidden_weights(parts, cut, ffe)
    down_w = down_weights(parts, cut, ffe)
    hidden = dot_nn(x_rows[own], hidden_w)
    hidden_gate, hidden_up = hidden[:, :ffe], hidden[:, ffe:]
    gates = gate_kept[own]
    grad_active = dot_nt(g_rows[own], down_w) * (res_scale * gates)
    sigmoid = jax.nn.sigmoid(hidden_gate)
    silu = hidden_gate * sigmoid
    active = silu * hidden_up
    gated = (active * gates).astype(bf16)
    grad_gate = grad_active * hidden_up * (sigmoid * (1.0 + hidden_gate * (1.0 - sigmoid)))
    grads = jnp.concatenate(
        [grad_gate.astype(bf16), (grad_active * silu).astype(bf16)], axis=1
    )
    weighted = jnp.sum(active * grad_active, axis=1, keepdims=True)
    active_out[0] = gated
    grads_out[0] = grads
    kept = own if final else 0
    out_kept[kept] = dot_nn(gated, down_w).astype(bf16)
    dx_kept[kept] = dot_nt(grads, hidden_w).astype(bf16)
    weighted_high = weighted.astype(bf16).astype(f32)
    lane = lax.broadcasted_iota(jnp.int32, (blocks * slots, LANES), 1)
    named = first_expert + local + own
    t_kept[kept] = jnp.where(
        lane == named,
        weighted_high,
        jnp.where(lane == named + experts, weighted - weighted_high, 0.0),
    ).astype(bf16)

    @pl.when(own == own_count - 1)
    def _():
        if final:
            slot = lax.broadcasted_iota(jnp.int32, (tok, slots), 1).astype(f32)
            gives = [
                pltpu.make_async_copy(
                    returned.at[block % 2], returned_out[block], sent.at[block]
                )
                for block in range(blocks)
            ]
            for block in range(blocks):
                here = slice(block * slots, (block + 1) * slots)
                put = jnp.concatenate(
                    [
                        (ranks_kept[block, :, index : index + 1] == slot).astype(f32).astype(bf16)
                        for index in range(local + own_count)
                    ],
                    axis=1,
                )

                def rows_of(which, here=here, block=block):
                    kept_rows = (out_kept, dx_kept, t_kept)[which]
                    found = [refs[which][block % 2, index] for index in range(local)]
                    found += [kept_rows[index, here, :] for index in range(own_count)]
                    return jnp.concatenate(found, axis=0)

                for fetch in fetches[block]:
                    fetch.wait()
                if block >= 2:
                    gives[block - 2].wait()
                out = dot_nn(put, rows_of(0)).astype(bf16)
                dx = dot_nn(put, rows_of(1)).astype(bf16)
                for part in range(4):
                    there = slice(part * cut, (part + 1) * cut)
                    returned[block % 2, :, columns(part)] = out[:, there]
                    returned[block % 2, :, columns(part, width)] = dx[:, there]
                returned[block % 2, :, 2 * width :] = dot_nn(put, rows_of(2)).astype(bf16)
                gives[block].start()
                for fetch in fetches[block + 2] if block + 2 < blocks else ():
                    fetch.start()
            for give in gives[-2:]:
                give.wait()
        for copy in row_copies:
            copy.wait()


def run_experts(meta, x_blocks, g_blocks, early, parts, ffe, experts, slots, local, final):
    blocks = len(x_blocks)
    tok, padded = x_blocks[0].shape
    width = padded - LANES
    own, packed, _ = parts[0].shape
    rows = blocks * slots
    anywhere = pl.BlockSpec(memory_space=pl.ANY)
    back = 2 * width + LANES
    kept_shapes = [(own, rows, width), (own, rows, width), (own, rows, LANES)]
    row_shapes = [(own, rows, width), (own, rows, width), (own, rows, ffe), (own, rows, 2 * ffe)]

    def one(*shape):
        return pl.BlockSpec((1,) + shape, lambda e, meta: (e, 0, 0))

    out_specs = [anywhere] * 2 + [one(rows, ffe), one(rows, 2 * ffe)]
    out_shapes = [jax.ShapeDtypeStruct(shape, bf16) for shape in row_shapes]
    scratch = []
    if final:
        out_specs = [anywhere] * blocks + out_specs
        out_shapes = [jax.ShapeDtypeStruct((tok, back), bf16)] * blocks + out_shapes
        scratch += [pltpu.VMEM(shape, bf16) for shape in kept_shapes]
    else:
        out_specs += [one(*shape[1:]) for shape in kept_shapes]
        out_shapes += [jax.ShapeDtypeStruct(shape, bf16) for shape in kept_shapes]
    scratch += [
        pltpu.VMEM((own, rows, width), bf16),
        pltpu.VMEM((own, rows, width), bf16),
        pltpu.VMEM((own, rows, 1), f32),
        pltpu.SemaphoreType.DMA((2,)),
        pltpu.VMEM((2, tok, padded), bf16),
        pltpu.VMEM((2, tok, padded), bf16),
        pltpu.SemaphoreType.DMA((2, 2)),
    ]
    if final:
        scratch += [
            pltpu.VMEM((blocks, tok, LANES), f32),
            pltpu.VMEM((2, tok, back), bf16),
            pltpu.SemaphoreType.DMA((blocks,)),
        ]
    if early:
        scratch += [
            pltpu.VMEM((2, array.shape[0], slots, array.shape[2]), bf16) for array in early
        ] + [pltpu.SemaphoreType.DMA((3, 2))]
    return pl.pallas_call(
        partial(
            experts_kernel,
            experts=experts,
            slots=slots,
            local=local,
            final=final,
            earlier=len(early),
        ),
        grid_spec=pltpu.PrefetchScalarGridSpec(
            num_scalar_prefetch=1,
            grid=(own,),
            in_specs=[anywhere] * (2 * blocks + len(early)) + [one(packed, LANES)] * 4,
            out_specs=out_specs,
            scratch_shapes=scratch,
        ),
        out_shape=out_shapes,
        compiler_params=call_params(60),
        cost_estimate=cost(26),
        name="experts",
    )(meta, *x_blocks, *g_blocks, *early, *parts)


def weight_grad_kernel(*refs, chunks, own_count):
    x_refs, grad_refs, active_refs, g_refs = (
        refs[chunks * index : chunks * (index + 1)] for index in range(4)
    )
    refs = refs[4 * chunks :]
    outs, (made, sent) = refs[: 4 * own_count], refs[4 * own_count :]
    x_rows = jnp.concatenate([ref[0] for ref in x_refs], axis=0)
    grads = jnp.concatenate([ref[0] for ref in grad_refs], axis=0)
    active = jnp.concatenate([ref[0] for ref in active_refs], axis=0)
    g_rows = jnp.concatenate([ref[0] for ref in g_refs], axis=0)
    cut = x_rows.shape[1] // 4
    ffe = grads.shape[1] // 2
    first = 2 * ffe // LANES * cut
    own = pl.program_id(0)
    for part in range(4):
        hidden = dot_tn(x_rows[:, part * cut : (part + 1) * cut], grads).astype(bf16)
        for t in range(2 * ffe // LANES):
            made[own, part, t * cut : (t + 1) * cut, :] = hidden[:, t * LANES : (t + 1) * LANES]
    down = (dot_tn(active, g_rows) * res_scale).astype(bf16)
    for part in range(4):
        for t in range(cut // LANES):
            at = part * cut + t * LANES
            here = slice(first + t * ffe, first + (t + 1) * ffe)
            made[own, part, here, :] = down[:, at : at + LANES]
    copies = [
        [
            pltpu.make_async_copy(
                made.at[expert, part], outs[part * own_count + expert].at[0], sent.at[expert, part]
            )
            for part in range(4)
        ]
        for expert in range(own_count)
    ]
    for expert in range(own_count):

        @pl.when(own == expert)
        def _(expert=expert):
            for copy in copies[expert]:
                copy.start()

    @pl.when(own == own_count - 1)
    def _():
        for group in copies:
            for copy in group:
                copy.wait()


def weight_grads(x_chunks, grad_chunks, active_chunks, g_chunks):
    own, rows, width = x_chunks[0].shape
    ffe = active_chunks[0].shape[2]
    chunks = len(x_chunks)
    packed = 3 * ffe * (width // 4) // LANES

    def one(*shape):
        return pl.BlockSpec((1,) + shape, lambda e: (e, 0, 0))

    outs = pl.pallas_call(
        partial(weight_grad_kernel, chunks=chunks, own_count=own),
        grid=(own,),
        in_specs=[one(rows, width)] * chunks
        + [one(rows, 2 * ffe)] * chunks
        + [one(rows, ffe)] * chunks
        + [one(rows, width)] * chunks,
        out_specs=[pl.BlockSpec(memory_space=pl.ANY)] * (4 * own),
        out_shape=[jax.ShapeDtypeStruct((1, packed, LANES), bf16)] * (4 * own),
        scratch_shapes=[
            pltpu.VMEM((own, 4, packed, LANES), bf16),
            pltpu.SemaphoreType.DMA((own, 4)),
        ],
        compiler_params=call_params(60),
        cost_estimate=cost(13),
        name="weight_grads",
    )(*x_chunks, *grad_chunks, *active_chunks, *g_chunks)
    return [list(outs[part * own : (part + 1) * own]) for part in range(4)]


def two_halves(arrays):
    return arrays if len(arrays) == 2 else list(halves(arrays[0])[1:])


def join_halves(arrays, own):
    return arrays if own == 2 else [jnp.concatenate(arrays, axis=1)]


def pack_weights(gate, up, down):
    return jnp.concatenate(
        [
            lax.slice_in_dim(array, at, at + LANES, axis=2)
            for array in (gate, up, down)
            for at in range(0, array.shape[2], LANES)
        ],
        axis=1,
    )


def unpack_weights(packed, cut, ffe):
    tiles = ffe // LANES

    def beside(first, rows, count):
        return jnp.concatenate(
            [packed[:, first + t * rows : first + (t + 1) * rows, :] for t in range(count)], axis=2
        )

    return (
        beside(0, cut, tiles),
        beside(tiles * cut, cut, tiles),
        beside(2 * tiles * cut, ffe, cut // LANES),
    )


def after(array, *earlier):
    return lax.optimization_barrier((array, earlier))[0]


def per_device(
    tokens,
    segment_ids,
    expert_ids,
    w_query,
    key_matrix,
    value_matrix,
    w_out,
    norm_attn,
    norm_moe,
    w_router,
    w_gate,
    w_up,
    w_down,
    cotangent,
):
    row = lax.axis_index("rows")
    column = lax.axis_index("cols")
    columns = lax.axis_size("cols")
    chips = columns // 2
    chip, core = column // 2, column % 2
    own_tokens = tokens[0]
    tok, width = own_tokens.shape
    own_experts = w_gate.shape[0]
    experts = own_experts * columns
    top_count = expert_ids.shape[2]
    capacity = 5 * tok * top_count // (4 * experts)
    slots = -(-capacity // LANES) * LANES
    q_cols, k_cols = w_query.shape[1], key_matrix.shape[1]

    token_near = gather_near(own_tokens)
    project_rows = jnp.concatenate([w_query, key_matrix, value_matrix], axis=1)
    project_found = chips_spread(project_rows)
    project_swapped = core_swap(project_found)
    sixth = w_out.shape[0]
    out_half = chips_spread(after(w_out, project_found)).reshape(chips * sixth, width)
    small = jnp.concatenate(
        [
            w_router,
            norm_attn[:, None],
            norm_moe[:, None],
            jnp.zeros((w_router.shape[0], LANES - experts - 2), bf16),
        ],
        axis=1,
    )
    small_full = lax.all_to_all(
        jnp.tile(after(small, out_half), (4 * columns, 1)), ("rows", "cols"), 0, 0, tiled=True
    )
    gain_attn = small_full[:, experts].astype(f32)[None, :]
    gain_moe = small_full[:, experts + 1].astype(f32)[None, :]
    router_full = jnp.where(jnp.arange(LANES) < experts, small_full, 0)
    token_parts = gather_far(own_tokens, *token_near)
    qkv_cols = q_cols + 2 * k_cols
    out_near = gather_near(after(out_half, token_near))

    expert_rows = expert_ids[0]
    lane_range = jnp.arange(LANES, dtype=jnp.int32)
    member = jnp.any(expert_rows[:, :, None] == lane_range[None, None, :], axis=1).astype(bf16)
    cot_rows = jnp.concatenate([cotangent[0], member], axis=1)
    cot_same = [cot_rows, chip_shift(after(cot_rows, out_half), 1)]

    groups = 2 if own_experts % 2 == 0 else 1
    group_size = own_experts // groups
    packed = []
    for group in range(groups):
        here = slice(group * group_size, (group + 1) * group_size)
        packed.append(pack_weights(after(w_gate[here], own_tokens), w_up[here], w_down[here]))
    weight_near = [gather_near(after(packed[0], token_parts[3], project_swapped, out_near))]

    segments = segment_ids[0]
    length = segments.shape[0]
    starts = jnp.sum((segments[None, :] < segments[:, None]).astype(jnp.int32), axis=1)
    positions = (jnp.arange(length, dtype=jnp.int32) - starts).astype(f32)
    half = HEAD_SIZE // 2
    frequency = rope_base ** (-(2.0 * jnp.arange(half, dtype=f32)) / HEAD_SIZE)
    angles = positions[:, None] * frequency[None, :]
    cos_half, sin_half = jnp.cos(angles), jnp.sin(angles)
    cosine = jnp.concatenate([cos_half] * 4, axis=1)
    sine = jnp.concatenate([-sin_half, sin_half] * 2, axis=1)
    first_blocks = starts[::tok] // tok
    place = jnp.stack([row, chip, core])
    meta = jnp.concatenate([place.astype(jnp.int32), first_blocks.astype(jnp.int32)])

    queries, key_rows, value_rows, normed, project_w = project(
        meta, token_parts, project_found, project_swapped, gain_attn, cosine, sine, q_cols, k_cols
    )
    cot_same[1] = after(cot_same[1], queries)
    attended, lse = attend(after(meta, cot_same[1]), queries, key_rows, value_rows, starts[:, None], tok)
    cot_other = [core_swap(rows) for rows in cot_same]
    for d in range(2, chips):
        cot_same.append(chip_shift(cot_same[-1], 1))
    attended, out_near = after((attended, out_near), weight_near[0], cot_same[3], cot_other)
    own_heads = lax.all_to_all(attended, "rows", 0, 0, tiled=True)
    out_mine = jnp.stack(gather_far(out_half, *out_near)).reshape(4, chips, sixth, width)
    out_parts = cores_in_order(out_mine, core_swap(out_mine), core, 2).reshape(4, tok, width)
    weight_near[0] = after(weight_near[0], own_heads)
    weight_parts = [gather_far(packed[0], *weight_near[0])]
    mixed_rows, moe_rows, gates = mix(
        meta,
        own_heads,
        out_parts,
        own_tokens,
        member,
        gain_moe,
        router_full,
        experts,
    )
    for group in range(1, groups):
        weight_near.append(gather_near(after(packed[group], weight_parts[0][3], moe_rows)))
    moe_same = [moe_rows, chip_shift(moe_rows, 1)]
    moe_other = [core_swap(rows) for rows in moe_same]
    moe_same.append(chip_shift(moe_same[1], 1))
    cot_other += [core_swap(rows) for rows in cot_same[2:]]

    moe_meta = jnp.stack([row, column * own_experts]).astype(jnp.int32)
    ffe = w_down.shape[1]
    kept = [[] for _ in range(groups)]
    pieces = [None] * chips
    grads = []

    def piece(d, start, stop):
        return add_low(pieces[d][0][:, start:stop], pieces[d][1][:, start:stop])

    both = 2 * width + LANES
    pairs = [(d, d + 1) for d in range(0, chips, 2)]
    early = [[] for _ in pairs]
    held = ()
    far, near, late, sums = [], [], [], []

    def make_grads(group, first_rows):
        chunks = kept[group]
        parts = weight_grads(
            [first_rows] + [k[0] for k in chunks[1:]],
            [k[3] for k in chunks],
            [k[2] for k in chunks],
            [k[1] for k in chunks],
        )
        grads.append([two_halves(part) for part in parts])
        for store, sent in zip((far, near), reduce_first(grads[-1])):
            store.append(sent)

    for group in range(groups):
        final = group == groups - 1
        for index, pair in enumerate(pairs):
            result = list(
                run_experts(
                    after(moe_meta, held),
                    [rows for d in pair for rows in (moe_same[d], moe_other[d])],
                    [rows for d in pair for rows in (cot_same[d], cot_other[d])],
                    early[index],
                    weight_parts[group],
                    ffe,
                    experts,
                    slots,
                    group * group_size,
                    final,
                )
            )
            held = result[0]
            if len(moe_other) == 2:
                moe_same[2] = after(moe_same[2], held)
                for d in range(3, chips):
                    moe_same.append(chip_shift(moe_same[-1], 1))
                moe_other += [core_swap(rows) for rows in moe_same[2:]]
                for later in range(1, groups):
                    weight_near[later] = after(weight_near[later], held)
                    weight_parts.append(gather_far(packed[later], *weight_near[later]))
            if not final:
                kept[group].append(result[:4])
                early[index] = result[4:]
                continue
            if index > 0:
                result = after(result, near, dx_hop)
            kept[group].append(result[4:8])
            for place, d in enumerate(pair):
                pieces[d] = (result[2 * place], core_swap(result[2 * place + 1]))
            if index == 0:
                dx_ring = piece(1, width, both)
                if groups > 1:
                    sums.append(reduce_second(grads[0], after(far[0], result[0])))
                    late.append([rows_swap(*sent) for sent in zip(sums[0], (1, 2))])
                held = (dx_ring, sums)
                dx_hop = chip_shift(dx_ring, 1)
                continue
            for d in pair:
                came = dx_hop if d == 2 else chip_shift(dx_ring, 1)
                if d == chips - 1:
                    came = after(came, grads[-1], late)
                    outs = [piece(at, 0, width) for at in range(chips - 1)]
                dx_ring = add_low(came, piece(d, width, both))
                if d == chips - 2:
                    make_grads(group, after(kept[group][0][0], dx_ring))
        if not final:
            make_grads(group, kept[group][0][0])
            held = grads[-1]
    outs.append(piece(chips - 1, 0, width))
    last_piece = piece(0, width, both)
    dx_came = after(chip_shift(dx_ring, 1), outs, last_piece)
    out_hop = chip_shift(after(outs[1], dx_came), 1)

    grad_mixed, grad_heads, wide_mine, wide_other = unmix(
        after(meta, far[-1]),
        dx_came,
        last_piece,
        mixed_rows,
        cotangent[0],
        gates,
        gain_moe,
        router_full,
        out_parts,
        own_heads,
        experts,
        chips,
    )
    grad_attended = lax.all_to_all(after(grad_heads, near[-1]), "rows", 0, 0, tiled=True)

    out_ring = add_low(after(out_hop, grad_attended), outs[2])
    wide_chip = add_low(wide_mine, core_swap(wide_other))
    wide_row = add_low_all(lax.all_to_all(wide_chip, "rows", 0, 0, tiled=True))
    wide_sum = jnp.sum(chips_exchange(wide_row).astype(f32), axis=0)
    grad_out_w = wide_sum[:, :width]
    grad_router_w = wide_sum[:, width : width + experts]
    grad_gain_moe_w = wide_sum[:, width + experts]

    sums.append(after(reduce_second(grads[-1], far[-1]), grad_attended))
    late.append([rows_swap(*sent) for sent in zip(sums[-1], (1, 2))])
    grad_lin = attend_back(
        after(meta, wide_chip, sums),
        queries,
        grad_attended,
        lse.T,
        starts[None, :],
        key_rows,
        value_rows,
        cosine,
        sine,
        tok,
    )
    grad_lin = after(grad_lin, late)
    normed_parts = [None] * 4
    for j in (3, 1, 2, 0):
        normed_parts[j] = dot_nt(grad_lin[j], project_w).astype(bf16)
    normed_sums = reduce_add(normed_parts, *after(reduce_far(normed_parts), wide_row))
    grad_normed = add_wide([normed_parts[0], *reduce_near(*normed_sums)])
    grad_project = dot_tn(normed.reshape(length, width), grad_lin.reshape(length, qkv_cols))
    project_pairs = grad_project.astype(bf16).reshape(chips, 2, width // columns, qkv_cols)
    project_chip = add_low(
        lax.dynamic_index_in_dim(project_pairs, core, 1, keepdims=False),
        core_swap(lax.dynamic_index_in_dim(project_pairs, 1 - core, 1, keepdims=False)),
    )
    project_sum = jnp.sum(chips_exchange(project_chip).astype(f32), axis=0)

    for d in range(3, chips):
        out_ring = add_low(after(chip_shift(out_ring, 1), grad_lin), outs[d])
    moe_out = add_wide([after(chip_shift(out_ring, 1), *normed_sums), outs[0]])
    block_out = mixed_rows + res_scale * moe_out

    totals = []
    for parts, soon, last in zip(grads, near, late):
        total = reduce_total([after(parts[0], *normed_sums)], soon, last)
        for array in join_halves(total, group_size):
            totals.append(unpack_weights(array, width // 4, ffe))
    grad_gate_w, grad_up_w, grad_down_w = (
        jnp.concatenate(arrays, axis=0) for arrays in zip(*totals)
    )

    own_w = jnp.concatenate([w_query, key_matrix, value_matrix], axis=1).astype(f32)
    own_gain = lax.dynamic_slice_in_dim(gain_attn[0], column * own_w.shape[0], own_w.shape[0], 0)
    gain_rows = (jnp.sum(project_sum * own_w, axis=1) / own_gain).reshape(4, -1)
    gain_sum = jnp.sum(lax.all_to_all(gain_rows, "rows", 0, 0, tiled=True), axis=0)
    grad_gain_attn = lax.ppermute(
        gain_sum,
        ("rows", "cols"),
        [(r * columns + c, 4 * c + r) for r in range(4) for c in range(columns)],
    )

    own_float = own_tokens.astype(f32)
    scale_attn = rms_scale(own_float)
    unit_attn = own_float * scale_attn
    grad_unit = grad_normed * gain_attn
    grad_tokens = grad_mixed + scale_attn * (
        grad_unit - unit_attn * jnp.mean(grad_unit * unit_attn, axis=-1, keepdims=True)
    )
    return (
        block_out[None],
        grad_tokens[None],
        project_sum[:, :q_cols],
        project_sum[:, q_cols : q_cols + k_cols],
        project_sum[:, q_cols + k_cols :],
        grad_out_w,
        grad_gain_attn,
        grad_gain_moe_w,
        grad_router_w,
        grad_gate_w,
        grad_up_w,
        grad_down_w,
    )


def solution(mesh):
    placed = (
        P("cols", "rows", None),
        P("cols", None),
        P("cols", "rows", None),
        P("cols", "rows"),
        P("cols", "rows"),
        P("cols", "rows"),
        P(("rows", "cols"), None),
        P(("rows", "cols")),
        P(("rows", "cols")),
        P(("rows", "cols"), None),
        P("cols", "rows", None),
        P("cols", "rows", None),
        P("cols", None, "rows"),
        P("cols", "rows", None),
    )
    return jax.shard_map(
        per_device,
        mesh=mesh,
        in_specs=placed,
        out_specs=(
            P("cols", "rows", None),
            P("cols", "rows", None),
            P("cols", "rows"),
            P("cols", "rows"),
            P("cols", "rows"),
            P(("rows", "cols"), None),
            P(("rows", "cols")),
            P(("rows", "cols")),
            P(("rows", "cols"), None),
            P("cols", "rows", None),
            P("cols", "rows", None),
            P("cols", None, "rows"),
        ),
        check_vma=False,
    )
```

time: 2120 us -> 777 us (0.37)
  waiting for transfers between devices: 1050 us -> 248 us
  local copies, waits for them, and re-layouts: 387 us -> 80.4 us
  matrix products: 319 us -> 13.6 us
  Pallas kernels: 0 us -> 219 us
  blocking collectives: 149 us -> 0 us
  starting transfers between devices: 36.9 us -> 95.2 us
  other arithmetic: 139 us -> 104 us
    all_to_all x6 -> x9, waiting for transfers between devices: 854 us -> 65.4 us  [the longest x4 23.1 us: chips_exchange(): lax.all_to_all(array, 'cols', 0, 0, axis_index_groups=alike, tiled=True)]
    dot_general x46 -> x5, matrix products: 316 us -> 13.6 us  [the longest x1 6.96 us: dot_tn(): lax.dot_general(left, right, (((0,), (0,)), ((), ())), preferred_element_...]
    pallas_call x0 -> x11, Pallas kernels: none -> 219 us  [the longest x4 115 us: run_experts(): pl.pallas_call(partial(experts_kernel, experts=experts, slots=slots, loca...]
    reduce_scatter x7 -> x0, waiting for transfers between devices: 189 us -> none  [the longest x1 140 us: per_device(): lax.psum_scatter(grad_out_w, ('rows', 'cols'), scatter_dimension=0, tiled...]
    ppermute x0 -> x61, waiting for transfers between devices: none -> 183 us  [the longest x12 117 us: chip_shift(): lax.ppermute(array, 'cols', [(i, (i + 2 * distance) % count) for i in ran...]
    gather x8 -> x0, local copies, waits for them, and re-layouts: 119 us -> none  [the longest x1 28.7 us: per_device(): grad_send = pair_padded[pair_table]]
    unnamed x2 -> x0, blocking collectives: 80.6 us -> none
    convert_element_type x5 -> x2, local copies, waits for them, and re-layouts: 70.3 us -> 0.01 us  [the longest x1 0.01 us: per_device(): gain_attn = small_full[:, experts].astype(f32)[None, :]]
  transfers between devices with their start and end apart: 21 -> 70, of which waited for: 8 -> 28; matrix products, arithmetic and copies ran while one was open for 33% -> 21% of each run, Pallas kernels for 0% -> 23%
where the time goes in v1:
time: 777 us; the launch traced here: 763 us
  waiting for transfers between devices  248 us (32%)
  Pallas kernels  219 us (28%)
  other arithmetic  104 us (13%)
  starting transfers between devices  95.2 us (12%)
  local copies, waits for them, and re-layouts  80.4 us (10%)
  matrix products  13.6 us (2%)
    ppermute x12, waiting for transfers between devices, chip_shift(): lax.ppermute(array, 'cols', [(i, (i + 2 * distance) % count) for i in ran...  117 us
    pallas_call x4, Pallas kernels, run_experts(): pl.pallas_call(partial(experts_kernel, experts=experts, slots=slots, loca...  115 us
    ppermute x32, waiting for transfers between devices, rows_swap(): return lax.ppermute(array, 'rows', [(i, i ^ distance) for i in range(4)])  62.8 us
    unnamed x195, local copies, waits for them, and re-layouts  46.1 us
    convert_element_type x18, other arithmetic, add_low(): return (left.astype(f32) + right.astype(f32)).astype(bf16)  44.8 us
    pallas_call x2, Pallas kernels, weight_grads(): pl.pallas_call(partial(weight_grad_kernel, chunks=chunks, own_count=own),...  32.4 us
    pallas_call x1, Pallas kernels, attend_back(): pl.pallas_call(partial(attend_back_kernel, bands=min(blocks, LONGEST_DOC...  29.3 us
    ppermute x32, starting transfers between devices, rows_swap(): return lax.ppermute(array, 'rows', [(i, i ^ distance) for i in range(4)])  29.1 us
  transfers between devices with their start and end apart: 70, of which 28 were waited for; matrix products, arithmetic and copies ran while one was open for 21% of the time, Pallas kernels for 23%

profile of v1, /device:TPU:6, one launch (start us, length us, event | category | flops | bytes accessed | tf_op | source)
XLA Modules:
  0.0 763.1 jit_solution(14022742671927395666)
XLA Ops:
  4.9 5.3 all-to-all-start
  35.8 4.2 all-to-all-start.1
  42.4 4.4 fusion.22
  49.2 6.2 all-to-all-done.1
  58.8 6.5 all-to-all-start.2
  65.3 5.2 pad_maximum_fusion.5
  74.8 21.0 %all-to-all-done.2 = bf16[32,48,128]{2,1,0:T(8,128)(2,1)} async-done(((bf16[32,48,128]{2,1,0:T(8,128)(2,1)}), bf16[32,48,128]{2,1,0:T(8,128)(2,1)}, u32[]{:S(2)}, u32[]{:S(2)}) %all-to-all-start.2) | async-done | bytes 393248 | tf_op jit(solution)/shard_map/all_to_all | solution.py:939
  102.5 9.3 %project.1 = (bf16[1536,384]{1,0:T(8,128)(2,1)S(1)}, bf16[1536,128]{1,0:T(8,128)(2,1)S(1)}, bf16[1536,128]{1,0:T(8,128)(2,1)S(1)}, bf16[4,384,1536]{2,1,0:T(8,128)(2,1)S(1)}, bf16[1536,640]{1,0:T(8,128)(2,1)S(1)}) custom-call(s32[7]{0:T(128)S(1)} %pad_add_fusion.meta, bf16[384,1536]{1,0:T(8,128)(2,1)S(1)} %bitcast.62, bf16[384,1536]{1,0:T(8,128)(2,1)S(1)} %copy-done.7, ...), custom_call_target="tpu_custom_call" | custom-call | flops 1150000000 | tf_op jit(solution)/shard_map/project/pallas_call | solution.py:209
  118.3 27.6 %collective-permute-done.10.refs_4_ = bf16[384,1664]{1,0:T(8,128)(2,1)S(1)} collective-permute-done((bf16[384,1664]{1,0:T(8,128)(2,1)}, bf16[384,1664]{1,0:T(8,128)(2,1)S(1)}, u32[]{:S(2)}, u32[]{:S(2)}) %collective-permute-start.10) | collective-permute-done | bytes 1277984 | tf_op jit(solution)/shard_map/ppermute | solution.py:119
  146.2 15.8 %attend.1 = (bf16[4,384,384]{2,1,0:T(8,128)(2,1)S(1)}, f32[1536,8]{1,0:T(8,128)S(1)}) custom-call(s32[7]{0:T(128)S(1)} %pad_add_fusion.meta, bf16[1536,384]{1,0:T(8,128)(2,1)S(1)} %get-tuple-element.125.queries, bf16[1536,128]{1,0:T(8,128)(2,1)S(1)} %get-tuple-element.128.keys, bf16[1536,128]{1,0:T(8,128)(2,1)S(1)} %get-tuple-element.129.values, ...), custom_call_target="tpu_custom_call" | custom-call | flops 1150000000 | tf_op jit(solution)/shard_map/attend/pallas_call | solution.py:276
  164.6 5.2 collective-permute-done.9.refs_10_
  170.0 7.7 %collective-permute-done.11.refs_6_ = bf16[384,1664]{1,0:T(8,128)(2,1)S(1)} collective-permute-done((bf16[384,1664]{1,0:T(8,128)(2,1)S(1)}, bf16[384,1664]{1,0:T(8,128)(2,1)S(1)}, u32[]{:S(2)}, u32[]{:S(2)}) %collective-permute-start.11) | collective-permute-done | bytes 1277984 | tf_op jit(solution)/shard_map/ppermute | solution.py:119
  180.5 7.4 collective-permute-done.14
  188.1 3.3 pad_maximum_fusion.1
  192.6 15.6 %all-to-all-start.3 = ((bf16[4,384,384]{2,1,0:T(8,128)(2,1)}), bf16[4,384,384]{2,1,0:T(8,128)(2,1)}, u32[]{:S(2)}, u32[]{:S(2)}) async-start(bf16[4,384,384]{2,1,0:T(8,128)(2,1)} %copy-done.18), calls=%async_computation.3 | async-start | bytes 2359296 | tf_op jit(solution)/shard_map/all_to_all | solution.py:986
  213.3 9.5 %all-to-all-done.3.heads = bf16[4,384,384]{2,1,0:T(8,128)(2,1)} async-done(((bf16[4,384,384]{2,1,0:T(8,128)(2,1)}), bf16[4,384,384]{2,1,0:T(8,128)(2,1)}, u32[]{:S(2)}, u32[]{:S(2)}) %all-to-all-start.3) | async-done | bytes 1179680 | tf_op jit(solution)/shard_map/all_to_all | solution.py:986
  225.1 6.4 mix.1
  237.1 26.2 %collective-permute-done.18.refs_2_ = bf16[384,1664]{1,0:T(8,128)(2,1)} collective-permute-done((bf16[384,1664]{1,0:T(8,128)(2,1)}, bf16[384,1664]{1,0:T(8,128)(2,1)}, u32[]{:S(2)}, u32[]{:S(2)}) %collective-permute-start.18) | collective-permute-done | bytes 1277984 | tf_op jit(solution)/shard_map/ppermute | solution.py:119
  270.7 24.0 %experts.4 = (bf16[2,512,1536]{2,1,0:T(8,128)(2,1)}, bf16[2,512,1536]{2,1,0:T(8,128)(2,1)}, bf16[2,512,512]{2,1,0:T(8,128)(2,1)}, bf16[2,512,1024]{2,1,0:T(8,128...) custom-call(s32[2]{0:T(128)} %pad_add_fusion.1.meta, ...), custom_call_target="tpu_custom_call" | custom-call | flops 29899999232 | tf_op jit(solution)/shard_map/experts/pallas_call | solution.py:757
  294.8 8.0 %collective-permute-done.22.refs_0_ = bf16[384,1664]{1,0:T(8,128)(2,1)} collective-permute-done((bf16[384,1664]{1,0:T(8,128)(2,1)}, bf16[384,1664]{1,0:T(8,128)(2,1)}, u32[]{:S(2)}, u32[]{:S(2)}) %collective-permute-start.22) | collective-permute-done | bytes 1277984 | tf_op jit(solution)/shard_map/ppermute | solution.py:119
  302.8 19.8 %collective-permute-done.29.refs_13_ = bf16[2,4608,128]{2,1,0:T(8,128)(2,1)} collective-permute-done((bf16[2,4608,128]{2,1,0:T(8,128)(2,1)}, bf16[2,4608,128]{2,1,0:T(8,128)(2,1)}, u32[]{:S(2)}, u32[]{:S(2)}) %collective-permute-start.29) | collective-permute-done | bytes 2359328 | tf_op jit(solution)/shard_map/ppermute | solution.py:42
  329.2 23.3 %collective-permute-done.30 = bf16[1,4608,128]{2,1,0:T(8,128)(2,1)S(1)} collective-permute-done((bf16[1,4608,128]{2,1,0:T(8,128)(2,1)S(1)}, bf16[1,4608,128]{2,1,0:T(8,128)(2,1)S(1)}, u32[]{:S(2)}, u32[]{:S(2)}) %collective-permute-start.30) | collective-permute-done | bytes 1179680 | tf_op jit(solution)/shard_map/ppermute | solution.py:42
  358.4 24.4 %experts.5 = (bf16[2,512,1536]{2,1,0:T(8,128)(2,1)}, bf16[2,512,1536]{2,1,0:T(8,128)(2,1)}, bf16[2,512,512]{2,1,0:T(8,128)(2,1)}, bf16[2,512,1024]{2,1,0:T(8,128...) custom-call(s32[2]{0:T(128)} %pad_add_fusion.1.meta, ...), custom_call_target="tpu_custom_call" | custom-call | flops 29899999232 | tf_op jit(solution)/shard_map/experts/pallas_call | solution.py:757
  382.9 16.2 %weight_grads.2 = (bf16[1,4608,128]{2,1,0:T(8,128)(2,1)}, bf16[1,4608,128]{2,1,0:T(8,128)(2,1)}, bf16[1,4608,128]{2,1,0:T(8,128)(2,1)}, bf16[1,4608,128]{2,1,0:T...) custom-call(bf16[2,512,1536]{2,1,0:T(8,128)(2,1)} %get-tuple-element, ...), custom_call_target="tpu_custom_call" | custom-call | flops 14949999616 | tf_op jit(solution)/shard_map/weight_grads/pallas_call | solution.py:836
  401.1 32.9 %experts.6 = (bf16[384,3200]{1,0:T(8,128)(2,1)}, bf16[384,3200]{1,0:T(8,128)(2,1)}, bf16[384,3200]{1,0:T(8,128)(2,1)}, bf16[384,3200]{1,0:T(8,128)(2,1)}, bf16[2...) custom-call(s32[2]{0:T(128)} %pad_add_fusion.1.meta, ...), custom_call_target="tpu_custom_call" | custom-call | flops 29899999232 | tf_op jit(solution)/shard_map/experts/pallas_call | solution.py:757
  443.8 33.3 %experts.7 = (bf16[384,3200]{1,0:T(8,128)(2,1)}, bf16[384,3200]{1,0:T(8,128)(2,1)}, bf16[384,3200]{1,0:T(8,128)(2,1)}, bf16[384,3200]{1,0:T(8,128)(2,1)}, bf16[2...) custom-call(s32[2]{0:T(128)} %pad_add_fusion.1.meta, ...), custom_call_target="tpu_custom_call" | custom-call | flops 29899999232 | tf_op jit(solution)/shard_map/experts/pallas_call | solution.py:757
  484.6 3.1 add_convert_fusion.13
  487.6 3.3 add_convert_fusion.4
  490.9 16.2 %weight_grads.3 = (bf16[1,4608,128]{2,1,0:T(8,128)(2,1)}, bf16[1,4608,128]{2,1,0:T(8,128)(2,1)}, bf16[1,4608,128]{2,1,0:T(8,128)(2,1)}, bf16[1,4608,128]{2,1,0:T...) custom-call(bf16[2,512,1536]{2,1,0:T(8,128)(2,1)} %get-tuple-element, ...), custom_call_target="tpu_custom_call" | custom-call | flops 14949999616 | tf_op jit(solution)/shard_map/weight_grads/pallas_call | solution.py:836
  509.3 14.1 %collective-permute-done.39 = bf16[384,1664]{1,0:T(8,128)(2,1)} collective-permute-done((bf16[384,1664]{1,0:T(8,128)(2,1)}, bf16[384,1664]{1,0:T(8,128)(2,1)}, u32[]{:S(2)}, u32[]{:S(2)}) %collective-permute-start.39) | collective-permute-done | bytes 1277984 | tf_op jit(solution)/shard_map/ppermute | solution.py:119
  537.7 20.2 %collective-permute-done.43.came = bf16[384,1664]{1,0:T(8,128)(2,1)S(1)} collective-permute-done((bf16[384,1664]{1,0:T(8,128)(2,1)S(1)}, bf16[384,1664]{1,0:T(8,128)(2,1)S(1)}, u32[]{:S(2)}, u32[]{:S(2)}) %collective-permute-start.43) | collective-permute-done | bytes 1277984 | tf_op jit(solution)/shard_map/ppermute | solution.py:119
  557.9 11.3 %unmix.1 = (f32[384,1536]{1,0:T(8,128)S(1)}, bf16[4,384,384]{2,1,0:T(8,128)(2,1)S(1)}, bf16[4,4,48,1664]{3,2,1,0:T(8,128)(2,1)S(1)}, bf16[4,4,48,1664]{3,2,1,0:T(8,128)(2,1)}) custom-call(s32[7]{0:T(128)S(1)} %pad_add_fusion.meta, bf16[384,1664]{1,0:T(8,128)(2,1)S(1)} %collective-permute-done.43.came, bf16[384,1664]{1,0:T(8,128)(2,1)S(1)} %add_convert_fusion.1.last, ...), custom_call_target="tpu_custom_call" | custom-call | flops 13799999488 | tf_op jit(solution)/shard_map/unmix/pallas_call | solution.py:500
  573.5 5.8 all-to-all-start.4
  582.2 11.6 %all-to-all-done.4.grads = bf16[4,384,384]{2,1,0:T(8,128)(2,1)} async-done(((bf16[4,384,384]{2,1,0:T(8,128)(2,1)}), bf16[4,384,384]{2,1,0:T(8,128)(2,1)}, u32[]{:S(2)}, u32[]{:S(2)}) %all-to-all-start.4) | async-done | bytes 1179680 | tf_op jit(solution)/shard_map/all_to_all | solution.py:1108
  595.8 13.6 %collective-permute-done.45 = bf16[384,1536]{1,0:T(8,128)(2,1)} collective-permute-done((bf16[384,1536]{1,0:T(8,128)(2,1)}, bf16[384,1536]{1,0:T(8,128)(2,1)}, u32[]{:S(2)}, u32[]{:S(2)}) %collective-permute-start.45) | collective-permute-done | bytes 1179680 | tf_op jit(solution)/shard_map/ppermute | solution.py:119
  612.3 3.8 add_convert_fusion
  616.1 5.0 all-to-all-start.5
  623.4 29.3 %attend_back.1 = bf16[4,384,640]{2,1,0:T(8,128)(2,1)S(1)} custom-call(s32[7]{0:T(128)S(1)} %pad_add_fusion.meta, bf16[1536,384]{1,0:T(8,128)(2,1)S(1)} %copy-done.26, bf16[4,384,384]{2,1,0:T(8,128)(2,1)} %all-to-all-done.4.grads, f32[8,1536]{1,0:T(8,128)S(1)} %bitcast.70, s32[1,1536]{1,0:T(1,128)S(1)} %broadcast_in_dim.47.starts, ...), custom_call_target="tpu_custom_call" | custom-call | flops 33350000640 | tf_op jit(solution)/shard_map/attend_back/pallas_call | solution.py:380
  652.7 7.0 bitcast_convert_fusion
  670.8 5.6 all-to-all-start.6
  676.4 3.1 reduce_sum.79
  707.3 13.7 %all-to-all-done.6 = bf16[4,192,640]{2,1,0:T(8,128)(2,1)} async-done(((bf16[4,192,640]{2,1,0:T(8,128)(2,1)}), bf16[4,192,640]{2,1,0:T(8,128)(2,1)}, u32[]{:S(2)}, u32[]{:S(2)}) %all-to-all-start.6) | async-done | bytes 983072 | tf_op jit(solution)/shard_map/all_to_all | solution.py:132
  724.1 5.8 all-to-all-start.8
  732.1 4.4 all-to-all-start.7
  736.6 3.3 maximum_maximum_fusion.2
  740.3 3.2 add_bitcast_fusion
  743.5 3.9 collective-permute-start.60
  756.9 3.3 fusion.6
  (412 shorter events, 201.8 us)
Async XLA Ops:
  0.7 46.2 %collective-permute-start.2 = (bf16[384,1536]{1,0:T(8,128)(2,1)}, bf16[384,1536]{1,0:T(8,128)(2,1)S(1)}, u32[]{:S(2)}, u32[]{:S(2)}) collective-permute-start(bf16[384,1536]{1,0:T(8,128)(2,1)} %bitcast.60), channel_id=1, source_target_pairs={{0,16},{8,24},{16,0},{24,8},{1,17},{9,25},{17,1},{25,9},{2,18},{10... | collective-permute-start | bytes 3538952 | tf_op jit(solution)/shard_map/ppermute | solution.py:42
  1.2 54.2 %collective-permute-start.1 = (bf16[384,1536]{1,0:T(8,128)(2,1)}, bf16[384,1536]{1,0:T(8,128)(2,1)S(1)}, u32[]{:S(2)}, u32[]{:S(2)}) collective-permute-start(bf16[384,1536]{1,0:T(8,128)(2,1)} %bitcast.61), channel_id=1, source_target_pairs={{0,8},{8,0},{16,24},{24,16},{1,9},{9,1},{17,25},{25,17},{2,10},{10... | collective-permute-start | bytes 3538952 | tf_op jit(solution)/shard_map/ppermute | solution.py:42
  4.9 29.1 %all-to-all-start = ((bf16[4,192,640]{2,1,0:T(8,128)(2,1)}), bf16[4,192,640]{2,1,0:T(8,128)(2,1)S(1)}, u32[]{:S(2)}, u32[]{:S(2)}) async-start(bf16[4,192,640]{2,1,0:T(8,128)(2,1)} %broadcast_in_dim.40), calls=%async_computation | async-start | bytes 1966080 | tf_op jit(solution)/shard_map/all_to_all | solution.py:132
  55.4 57.7 %collective-permute-start = (bf16[384,1664]{1,0:T(8,128)(2,1)}, bf16[384,1664]{1,0:T(8,128)(2,1)}, u32[]{:S(2)}, u32[]{:S(2)}) collective-permute-start(bf16[384,1664]{1,0:T(8,128)(2,1)} %pad_maximum_fusion.2.refs_4_), channel_id=1, source_target_pairs={{0,2},{1,3},{2,4},{3,5},{4,6},{5,7},{6,0},{7,1},{8,10},{9,11},{10,... | collective-permute-start | bytes 3833864 | tf_op jit(solution)/shard_map/ppermute | solution.py:119
  57.9 39.7 %collective-permute-start.5 = (bf16[4,192,640]{2,1,0:T(8,128)(2,1)S(1)}, bf16[4,192,640]{2,1,0:T(8,128)(2,1)}, u32[]{:S(2)}, u32[]{:S(2)}) collective-permute-start(bf16[4,192,640]{2,1,0:T(8,128)(2,1)S(1)} %all-to-all-done.refs_4_), channel_id=1, source_target_pairs={{0,1},{1,0},{2,3},{3,2},{4,5},{5,4},{6,7},{7,6},{8,9},{9,8},{10,11... | collective-permute-start | bytes 2949128 | tf_op jit(solution)/shard_map/ppermute | solution.py:126
  58.8 37.1 %all-to-all-start.2 = ((bf16[32,48,128]{2,1,0:T(8,128)(2,1)}), bf16[32,48,128]{2,1,0:T(8,128)(2,1)}, u32[]{:S(2)}, u32[]{:S(2)}) async-start(bf16[32,48,128]{2,1,0:T(8,128)(2,1)} %tile.2), calls=%async_computation.2 | async-start | bytes 786432 | tf_op jit(solution)/shard_map/all_to_all | solution.py:939
  71.7 44.9 %collective-permute-start.7 = (bf16[192,1536]{1,0:T(8,128)(2,1)}, bf16[192,1536]{1,0:T(8,128)(2,1)}, u32[]{:S(2)}, u32[]{:S(2)}) collective-permute-start(bf16[192,1536]{1,0:T(8,128)(2,1)} %bitcast.5), channel_id=1, source_target_pairs={{0,16},{8,24},{16,0},{24,8},{1,17},{9,25},{17,1},{25,9},{2,18},{10... | collective-permute-start | bytes 1769480 | tf_op jit(solution)/shard_map/ppermute | solution.py:42
  72.3 44.3 %collective-permute-start.6 = (bf16[192,1536]{1,0:T(8,128)(2,1)}, bf16[192,1536]{1,0:T(8,128)(2,1)}, u32[]{:S(2)}, u32[]{:S(2)}) collective-permute-start(bf16[192,1536]{1,0:T(8,128)(2,1)} %bitcast.5), channel_id=1, source_target_pairs={{0,8},{8,0},{16,24},{24,16},{1,9},{9,1},{17,25},{25,17},{2,10},{10... | collective-permute-start | bytes 1769480 | tf_op jit(solution)/shard_map/ppermute | solution.py:42
  113.1 32.8 %collective-permute-start.10 = (bf16[384,1664]{1,0:T(8,128)(2,1)}, bf16[384,1664]{1,0:T(8,128)(2,1)S(1)}, u32[]{:S(2)}, u32[]{:S(2)}) collective-permute-start(bf16[384,1664]{1,0:T(8,128)(2,1)} %collective-permute-done.refs_6_), channel_id=1, source_target_pairs={{0,2},{1,3},{2,4},{3,5},{4,6},{5,7},{6,0},{7,1},{8,10},{9,11},{10,... | collective-permute-start | bytes 3833864 | tf_op jit(solution)/shard_map/ppermute | solution.py:119
  116.6 53.2 %collective-permute-start.9 = (bf16[2,4608,128]{2,1,0:T(8,128)(2,1)S(1)}, bf16[2,4608,128]{2,1,0:T(8,128)(2,1)S(1)}, u32[]{:S(2)}, u32[]{:S(2)}) collective-permute-start(bf16[2,4608,128]{2,1,0:T(8,128)(2,1)S(1)} %get-tuple-element.133.refs_8_), channel_id=1, source_target_pairs={{0,16},{8,24},{16,0},{24,8},{1,17},{9,25},{17,1},{25,9},{2,18},{10... | collective-permute-start | bytes 7077896 | tf_op jit(solution)/shard_map/ppermute | solution.py:42
  117.3 52.7 %collective-permute-start.8 = (bf16[2,4608,128]{2,1,0:T(8,128)(2,1)S(1)}, bf16[2,4608,128]{2,1,0:T(8,128)(2,1)S(1)}, u32[]{:S(2)}, u32[]{:S(2)}) collective-permute-start(bf16[2,4608,128]{2,1,0:T(8,128)(2,1)S(1)} %get-tuple-element.133.refs_8_), channel_id=1, source_target_pairs={{0,8},{8,0},{16,24},{24,16},{1,9},{9,1},{17,25},{25,17},{2,10},{10... | collective-permute-start | bytes 7077896 | tf_op jit(solution)/shard_map/ppermute | solution.py:42
  117.8 46.8 %collective-permute-start.12 = (bf16[384,1664]{1,0:T(8,128)(2,1)S(1)}, bf16[384,1664]{1,0:T(8,128)(2,1)S(1)}, u32[]{:S(2)}, u32[]{:S(2)}) collective-permute-start(bf16[384,1664]{1,0:T(8,128)(2,1)S(1)} %copy-done.48), channel_id=1, source_target_pairs={{0,1},{1,0},{2,3},{3,2},{4,5},{5,4},{6,7},{7,6},{8,9},{9,8},{10,11... | collective-permute-start | bytes 3833864 | tf_op jit(solution)/shard_map/ppermute | solution.py:126
  117.8 46.8 %collective-permute-start.13 = (bf16[384,1664]{1,0:T(8,128)(2,1)}, bf16[384,1664]{1,0:T(8,128)(2,1)S(1)}, u32[]{:S(2)}, u32[]{:S(2)}) collective-permute-start(bf16[384,1664]{1,0:T(8,128)(2,1)} %collective-permute-done.refs_6_), channel_id=1, source_target_pairs={{0,1},{1,0},{2,3},{3,2},{4,5},{5,4},{6,7},{7,6},{8,9},{9,8},{10,11... | collective-permute-start | bytes 3833864 | tf_op jit(solution)/shard_map/ppermute | solution.py:126
  146.0 31.8 %collective-permute-start.11 = (bf16[384,1664]{1,0:T(8,128)(2,1)S(1)}, bf16[384,1664]{1,0:T(8,128)(2,1)S(1)}, u32[]{:S(2)}, u32[]{:S(2)}) collective-permute-start(bf16[384,1664]{1,0:T(8,128)(2,1)S(1)} %collective-permute-done.10.refs_4_), channel_id=1, source_target_pairs={{0,2},{1,3},{2,4},{3,5},{4,6},{5,7},{6,0},{7,1},{8,10},{9,11},{10,... | collective-permute-start | bytes 3833864 | tf_op jit(solution)/shard_map/ppermute | solution.py:119
  192.6 30.1 %all-to-all-start.3 = ((bf16[4,384,384]{2,1,0:T(8,128)(2,1)}), bf16[4,384,384]{2,1,0:T(8,128)(2,1)}, u32[]{:S(2)}, u32[]{:S(2)}) async-start(bf16[4,384,384]{2,1,0:T(8,128)(2,1)} %copy-done.18), calls=%async_computation.3 | async-start | bytes 2359296 | tf_op jit(solution)/shard_map/all_to_all | solution.py:986
  231.5 31.8 %collective-permute-start.18 = (bf16[384,1664]{1,0:T(8,128)(2,1)}, bf16[384,1664]{1,0:T(8,128)(2,1)}, u32[]{:S(2)}, u32[]{:S(2)}) collective-permute-start(bf16[384,1664]{1,0:T(8,128)(2,1)} %get-tuple-element.138.refs_0_), channel_id=1, source_target_pairs={{0,2},{1,3},{2,4},{3,5},{4,6},{5,7},{6,0},{7,1},{8,10},{9,11},{10,... | collective-permute-start | bytes 3833864 | tf_op jit(solution)/shard_map/ppermute | solution.py:119
  232.6 31.3 %collective-permute-start.20 = (bf16[1,4608,128]{2,1,0:T(8,128)(2,1)}, bf16[1,4608,128]{2,1,0:T(8,128)(2,1)}, u32[]{:S(2)}, u32[]{:S(2)}) collective-permute-start(bf16[1,4608,128]{2,1,0:T(8,128)(2,1)} %slice.370), channel_id=1, source_target_pairs={{0,8},{8,0},{16,24},{24,16},{1,9},{9,1},{17,25},{25,17},{2,10},{10... | collective-permute-start | bytes 3538952 | tf_op jit(solution)/shard_map/ppermute | solution.py:42
  235.6 30.6 %collective-permute-start.21 = (bf16[1,4608,128]{2,1,0:T(8,128)(2,1)}, bf16[1,4608,128]{2,1,0:T(8,128)(2,1)}, u32[]{:S(2)}, u32[]{:S(2)}) collective-permute-start(bf16[1,4608,128]{2,1,0:T(8,128)(2,1)} %slice.371), channel_id=1, source_target_pairs={{0,16},{8,24},{16,0},{24,8},{1,17},{9,25},{17,1},{25,9},{2,18},{10... | collective-permute-start | bytes 3538952 | tf_op jit(solution)/shard_map/ppermute | solution.py:42
  237.1 33.7 %collective-permute-start.17 = (bf16[384,1664]{1,0:T(8,128)(2,1)}, bf16[384,1664]{1,0:T(8,128)(2,1)}, u32[]{:S(2)}, u32[]{:S(2)}) collective-permute-start(bf16[384,1664]{1,0:T(8,128)(2,1)} %get-tuple-element.138.refs_0_), channel_id=1, source_target_pairs={{0,1},{1,0},{2,3},{3,2},{4,5},{5,4},{6,7},{7,6},{8,9},{9,8},{10,11... | collective-permute-start | bytes 3833864 | tf_op jit(solution)/shard_map/ppermute | solution.py:126
  268.6 54.0 %collective-permute-start.29 = (bf16[2,4608,128]{2,1,0:T(8,128)(2,1)}, bf16[2,4608,128]{2,1,0:T(8,128)(2,1)}, u32[]{:S(2)}, u32[]{:S(2)}) collective-permute-start(bf16[2,4608,128]{2,1,0:T(8,128)(2,1)} %get-tuple-element.164.refs_11_), channel_id=1, source_target_pairs={{0,16},{8,24},{16,0},{24,8},{1,17},{9,25},{17,1},{25,9},{2,18},{10... | collective-permute-start | bytes 7077896 | tf_op jit(solution)/shard_map/ppermute | solution.py:42
  270.1 53.7 %collective-permute-start.28 = (bf16[2,4608,128]{2,1,0:T(8,128)(2,1)}, bf16[2,4608,128]{2,1,0:T(8,128)(2,1)}, u32[]{:S(2)}, u32[]{:S(2)}) collective-permute-start(bf16[2,4608,128]{2,1,0:T(8,128)(2,1)} %get-tuple-element.164.refs_11_), channel_id=1, source_target_pairs={{0,8},{8,0},{16,24},{24,16},{1,9},{9,1},{17,25},{25,17},{2,10},{10... | collective-permute-start | bytes 7077896 | tf_op jit(solution)/shard_map/ppermute | solution.py:42
  270.7 32.0 %collective-permute-start.22 = (bf16[384,1664]{1,0:T(8,128)(2,1)}, bf16[384,1664]{1,0:T(8,128)(2,1)}, u32[]{:S(2)}, u32[]{:S(2)}) collective-permute-start(bf16[384,1664]{1,0:T(8,128)(2,1)} %collective-permute-done.18.refs_2_), channel_id=1, source_target_pairs={{0,2},{1,3},{2,4},{3,5},{4,6},{5,7},{6,0},{7,1},{8,10},{9,11},{10,... | collective-permute-start | bytes 3833864 | tf_op jit(solution)/shard_map/ppermute | solution.py:119
  302.8 49.7 %collective-permute-start.24 = (bf16[384,1664]{1,0:T(8,128)(2,1)}, bf16[384,1664]{1,0:T(8,128)(2,1)S(1)}, u32[]{:S(2)}, u32[]{:S(2)}) collective-permute-start(bf16[384,1664]{1,0:T(8,128)(2,1)} %collective-permute-done.22.refs_0_), channel_id=1, source_target_pairs={{0,2},{1,3},{2,4},{3,5},{4,6},{5,7},{6,0},{7,1},{8,10},{9,11},{10,... | collective-permute-start | bytes 3833864 | tf_op jit(solution)/shard_map/ppermute | solution.py:119
  399.1 37.1 %collective-permute-start.34 = (bf16[1,4608,128]{2,1,0:T(8,128)(2,1)}, bf16[1,4608,128]{2,1,0:T(8,128)(2,1)}, u32[]{:S(2)}, u32[]{:S(2)}) collective-permute-start(bf16[1,4608,128]{2,1,0:T(8,128)(2,1)} %get-tuple-element.157), channel_id=1, source_target_pairs={{0,8},{8,0},{16,24},{24,16},{1,9},{9,1},{17,25},{25,17},{2,10},{10... | collective-permute-start | bytes 3538952 | tf_op jit(solution)/shard_map/ppermute | solution.py:42
  400.5 35.7 %collective-permute-start.35 = (bf16[1,4608,128]{2,1,0:T(8,128)(2,1)}, bf16[1,4608,128]{2,1,0:T(8,128)(2,1)}, u32[]{:S(2)}, u32[]{:S(2)}) collective-permute-start(bf16[1,4608,128]{2,1,0:T(8,128)(2,1)} %get-tuple-element.158), channel_id=1, source_target_pairs={{0,16},{8,24},{16,0},{24,8},{1,17},{9,25},{17,1},{25,9},{2,18},{10... | collective-permute-start | bytes 3538952 | tf_op jit(solution)/shard_map/ppermute | solution.py:42
  434.1 43.0 %collective-permute-start.36 = (bf16[1,4608,128]{2,1,0:T(8,128)(2,1)}, bf16[1,4608,128]{2,1,0:T(8,128)(2,1)}, u32[]{:S(2)}, u32[]{:S(2)}) collective-permute-start(bf16[1,4608,128]{2,1,0:T(8,128)(2,1)} %get-tuple-element.153), channel_id=1, source_target_pairs={{0,8},{8,0},{16,24},{24,16},{1,9},{9,1},{17,25},{25,17},{2,10},{10... | collective-permute-start | bytes 3538952 | tf_op jit(solution)/shard_map/ppermute | solution.py:42
  435.6 41.5 %collective-permute-start.37 = (bf16[1,4608,128]{2,1,0:T(8,128)(2,1)}, bf16[1,4608,128]{2,1,0:T(8,128)(2,1)}, u32[]{:S(2)}, u32[]{:S(2)}) collective-permute-start(bf16[1,4608,128]{2,1,0:T(8,128)(2,1)} %get-tuple-element.156), channel_id=1, source_target_pairs={{0,16},{8,24},{16,0},{24,8},{1,17},{9,25},{17,1},{25,9},{2,18},{10... | collective-permute-start | bytes 3538952 | tf_op jit(solution)/shard_map/ppermute | solution.py:42
  436.2 48.3 %collective-permute-start.44 = (bf16[384,3200]{1,0:T(8,128)(2,1)}, bf16[384,3200]{1,0:T(8,128)(2,1)}, u32[]{:S(2)}, u32[]{:S(2)}) collective-permute-start(bf16[384,3200]{1,0:T(8,128)(2,1)} %get-tuple-element.206), channel_id=1, source_target_pairs={{0,1},{1,0},{2,3},{3,2},{4,5},{5,4},{6,7},{7,6},{8,9},{9,8},{10,11... | collective-permute-start | bytes 7372808 | tf_op jit(solution)/shard_map/ppermute | solution.py:126
  443.8 33.3 %collective-permute-start.33 = (bf16[384,1664]{1,0:T(8,128)(2,1)}, bf16[384,1664]{1,0:T(8,128)(2,1)}, u32[]{:S(2)}, u32[]{:S(2)}) collective-permute-start(bf16[384,1664]{1,0:T(8,128)(2,1)} %add_convert_fusion.6), channel_id=1, source_target_pairs={{0,2},{1,3},{2,4},{3,5},{4,6},{5,7},{6,0},{7,1},{8,10},{9,11},{10,... | collective-permute-start | bytes 3833864 | tf_op jit(solution)/shard_map/ppermute | solution.py:119
  479.6 29.1 %collective-permute-start.41 = (bf16[1,4608,128]{2,1,0:T(8,128)(2,1)}, bf16[1,4608,128]{2,1,0:T(8,128)(2,1)}, u32[]{:S(2)}, u32[]{:S(2)}) collective-permute-start(bf16[1,4608,128]{2,1,0:T(8,128)(2,1)} %add_convert_fusion.14), channel_id=1, source_target_pairs={{0,16},{8,24},{16,0},{24,8},{1,17},{9,25},{17,1},{25,9},{2,18},{10... | collective-permute-start | bytes 3538952 | tf_op jit(solution)/shard_map/ppermute | solution.py:42
  481.1 28.2 %collective-permute-start.40 = (bf16[1,4608,128]{2,1,0:T(8,128)(2,1)}, bf16[1,4608,128]{2,1,0:T(8,128)(2,1)}, u32[]{:S(2)}, u32[]{:S(2)}) collective-permute-start(bf16[1,4608,128]{2,1,0:T(8,128)(2,1)} %add_convert_fusion.15), channel_id=1, source_target_pairs={{0,8},{8,0},{16,24},{24,16},{1,9},{9,1},{17,25},{25,17},{2,10},{10... | collective-permute-start | bytes 3538952 | tf_op jit(solution)/shard_map/ppermute | solution.py:42
  484.6 38.8 %collective-permute-start.42 = (bf16[384,3200]{1,0:T(8,128)(2,1)}, bf16[384,3200]{1,0:T(8,128)(2,1)}, u32[]{:S(2)}, u32[]{:S(2)}) collective-permute-start(bf16[384,3200]{1,0:T(8,128)(2,1)} %get-tuple-element.205), channel_id=1, source_target_pairs={{0,1},{1,0},{2,3},{3,2},{4,5},{5,4},{6,7},{7,6},{8,9},{9,8},{10,11... | collective-permute-start | bytes 7372808 | tf_op jit(solution)/shard_map/ppermute | solution.py:126
  490.9 32.5 %collective-permute-start.39 = (bf16[384,1664]{1,0:T(8,128)(2,1)}, bf16[384,1664]{1,0:T(8,128)(2,1)}, u32[]{:S(2)}, u32[]{:S(2)}) collective-permute-start(bf16[384,1664]{1,0:T(8,128)(2,1)} %add_convert_fusion.4), channel_id=1, source_target_pairs={{0,2},{1,3},{2,4},{3,5},{4,6},{5,7},{6,0},{7,1},{8,10},{9,11},{10,... | collective-permute-start | bytes 3833864 | tf_op jit(solution)/shard_map/ppermute | solution.py:119
  507.1 29.5 %collective-permute-start.46 = (bf16[1,4608,128]{2,1,0:T(8,128)(2,1)}, bf16[1,4608,128]{2,1,0:T(8,128)(2,1)S(1)}, u32[]{:S(2)}, u32[]{:S(2)}) collective-permute-start(bf16[1,4608,128]{2,1,0:T(8,128)(2,1)} %get-tuple-element.201), channel_id=1, source_target_pairs={{0,8},{8,0},{16,24},{24,16},{1,9},{9,1},{17,25},{25,17},{2,10},{10... | collective-permute-start | bytes 3538952 | tf_op jit(solution)/shard_map/ppermute | solution.py:42
  508.6 29.0 %collective-permute-start.47 = (bf16[1,4608,128]{2,1,0:T(8,128)(2,1)}, bf16[1,4608,128]{2,1,0:T(8,128)(2,1)S(1)}, u32[]{:S(2)}, u32[]{:S(2)}) collective-permute-start(bf16[1,4608,128]{2,1,0:T(8,128)(2,1)} %get-tuple-element.202), channel_id=1, source_target_pairs={{0,16},{8,24},{16,0},{24,8},{1,17},{9,25},{17,1},{25,9},{2,18},{10... | collective-permute-start | bytes 3538952 | tf_op jit(solution)/shard_map/ppermute | solution.py:42
  526.1 31.8 %collective-permute-start.43 = (bf16[384,1664]{1,0:T(8,128)(2,1)S(1)}, bf16[384,1664]{1,0:T(8,128)(2,1)S(1)}, u32[]{:S(2)}, u32[]{:S(2)}) collective-permute-start(bf16[384,1664]{1,0:T(8,128)(2,1)S(1)} %add_convert_fusion.2), channel_id=1, source_target_pairs={{0,2},{1,3},{2,4},{3,5},{4,6},{5,7},{6,0},{7,1},{8,10},{9,11},{10,... | collective-permute-start | bytes 3833864 | tf_op jit(solution)/shard_map/ppermute | solution.py:119
  528.4 45.0 %collective-permute-start.48 = (bf16[1,4608,128]{2,1,0:T(8,128)(2,1)}, bf16[1,4608,128]{2,1,0:T(8,128)(2,1)}, u32[]{:S(2)}, u32[]{:S(2)}) collective-permute-start(bf16[1,4608,128]{2,1,0:T(8,128)(2,1)} %get-tuple-element.197), channel_id=1, source_target_pairs={{0,8},{8,0},{16,24},{24,16},{1,9},{9,1},{17,25},{25,17},{2,10},{10... | collective-permute-start | bytes 3538952 | tf_op jit(solution)/shard_map/ppermute | solution.py:42
  530.0 43.5 %collective-permute-start.49 = (bf16[1,4608,128]{2,1,0:T(8,128)(2,1)S(1)}, bf16[1,4608,128]{2,1,0:T(8,128)(2,1)}, u32[]{:S(2)}, u32[]{:S(2)}) collective-permute-start(bf16[1,4608,128]{2,1,0:T(8,128)(2,1)S(1)} %copy-done.84), channel_id=1, source_target_pairs={{0,16},{8,24},{16,0},{24,8},{1,17},{9,25},{17,1},{25,9},{2,18},{10... | collective-permute-start | bytes 3538952 | tf_op jit(solution)/shard_map/ppermute | solution.py:42
  572.1 40.2 %collective-permute-start.51 = (bf16[4,4,48,1664]{3,2,1,0:T(8,128)(2,1)}, bf16[4,4,48,1664]{3,2,1,0:T(8,128)(2,1)}, u32[]{:S(2)}, u32[]{:S(2)}) collective-permute-start(bf16[4,4,48,1664]{3,2,1,0:T(8,128)(2,1)} %get-tuple-element.215), channel_id=1, source_target_pairs={{0,1},{1,0},{2,3},{3,2},{4,5},{5,4},{6,7},{7,6},{8,9},{9,8},{10,11... | collective-permute-start | bytes 7667720 | tf_op jit(solution)/shard_map/ppermute | solution.py:126
  579.2 30.1 %collective-permute-start.45 = (bf16[384,1536]{1,0:T(8,128)(2,1)}, bf16[384,1536]{1,0:T(8,128)(2,1)}, u32[]{:S(2)}, u32[]{:S(2)}) collective-permute-start(bf16[384,1536]{1,0:T(8,128)(2,1)} %add_convert_fusion.16), channel_id=1, source_target_pairs={{0,2},{1,3},{2,4},{3,5},{4,6},{5,7},{6,0},{7,1},{8,10},{9,11},{10,... | collective-permute-start | bytes 3538952 | tf_op jit(solution)/shard_map/ppermute | solution.py:119
  593.7 59.0 %collective-permute-start.52 = (bf16[1,4608,128]{2,1,0:T(8,128)(2,1)}, bf16[1,4608,128]{2,1,0:T(8,128)(2,1)}, u32[]{:S(2)}, u32[]{:S(2)}) collective-permute-start(bf16[1,4608,128]{2,1,0:T(8,128)(2,1)} %add_convert_fusion.9), channel_id=1, source_target_pairs={{0,8},{8,0},{16,24},{24,16},{1,9},{9,1},{17,25},{25,17},{2,10},{10... | collective-permute-start | bytes 3538952 | tf_op jit(solution)/shard_map/ppermute | solution.py:42
  595.3 57.5 %collective-permute-start.53 = (bf16[1,4608,128]{2,1,0:T(8,128)(2,1)}, bf16[1,4608,128]{2,1,0:T(8,128)(2,1)}, u32[]{:S(2)}, u32[]{:S(2)}) collective-permute-start(bf16[1,4608,128]{2,1,0:T(8,128)(2,1)} %add_convert_fusion.8), channel_id=1, source_target_pairs={{0,16},{8,24},{16,0},{24,8},{1,17},{9,25},{17,1},{25,9},{2,18},{10... | collective-permute-start | bytes 3538952 | tf_op jit(solution)/shard_map/ppermute | solution.py:42
  612.3 47.4 %collective-permute-start.50 = (bf16[384,1536]{1,0:T(8,128)(2,1)}, bf16[384,1536]{1,0:T(8,128)(2,1)}, u32[]{:S(2)}, u32[]{:S(2)}) collective-permute-start(bf16[384,1536]{1,0:T(8,128)(2,1)} %add_convert_fusion.10), channel_id=1, source_target_pairs={{0,2},{1,3},{2,4},{3,5},{4,6},{5,7},{6,0},{7,1},{8,10},{9,11},{10,... | collective-permute-start | bytes 3538952 | tf_op jit(solution)/shard_map/ppermute | solution.py:119
  616.1 54.7 %all-to-all-start.5 = ((bf16[4,4,48,1664]{3,2,1,0:T(8,128)(2,1)}), bf16[4,4,48,1664]{3,2,1,0:T(8,128)(2,1)}, u32[]{:S(2)}, u32[]{:S(2)}) async-start(bf16[4,4,48,1664]{3,2,1,0:T(8,128)(2,1)} %add_convert_fusion), calls=%async_computation.5 | async-start | bytes 5111808 | tf_op jit(solution)/shard_map/all_to_all | solution.py:1112
  669.6 70.3 %collective-permute-start.54 = (bf16[384,1536]{1,0:T(8,128)(2,1)}, bf16[384,1536]{1,0:T(8,128)(2,1)}, u32[]{:S(2)}, u32[]{:S(2)}) collective-permute-start(bf16[384,1536]{1,0:T(8,128)(2,1)} %add_convert_fusion.7), channel_id=1, source_target_pairs={{0,2},{1,3},{2,4},{3,5},{4,6},{5,7},{6,0},{7,1},{8,10},{9,11},{10,... | collective-permute-start | bytes 3538952 | tf_op jit(solution)/shard_map/ppermute | solution.py:119
  670.8 50.3 %all-to-all-start.6 = ((bf16[4,192,640]{2,1,0:T(8,128)(2,1)}), bf16[4,192,640]{2,1,0:T(8,128)(2,1)}, u32[]{:S(2)}, u32[]{:S(2)}) async-start(bf16[4,192,640]{2,1,0:T(8,128)(2,1)} %fusion.12), calls=%async_computation.6 | async-start | bytes 1966080 | tf_op jit(solution)/shard_map/all_to_all | solution.py:132
  694.5 62.3 %collective-permute-start.57 = (bf16[384,1536]{1,0:T(8,128)(2,1)}, bf16[384,1536]{1,0:T(8,128)(2,1)}, u32[]{:S(2)}, u32[]{:S(2)}) collective-permute-start(bf16[384,1536]{1,0:T(8,128)(2,1)} %pad_maximum_fusion.3), channel_id=1, source_target_pairs={{0,8},{8,0},{16,24},{24,16},{1,9},{9,1},{17,25},{25,17},{2,10},{10... | collective-permute-start | bytes 3538952 | tf_op jit(solution)/shard_map/ppermute | solution.py:42
  694.9 62.0 %collective-permute-start.58 = (bf16[384,1536]{1,0:T(8,128)(2,1)}, bf16[384,1536]{1,0:T(8,128)(2,1)}, u32[]{:S(2)}, u32[]{:S(2)}) collective-permute-start(bf16[384,1536]{1,0:T(8,128)(2,1)} %pad_maximum_fusion.4), channel_id=1, source_target_pairs={{0,16},{8,24},{16,0},{24,8},{1,17},{9,25},{17,1},{25,9},{2,18},{10... | collective-permute-start | bytes 3538952 | tf_op jit(solution)/shard_map/ppermute | solution.py:42
  (111 other events, 1467.2 us)

commit v2 on v1

--- a/solution.py
+++ b/solution.py
@@ -86,20 +86,18 @@
 
 
 def reduce_first(pieces):
-    far = rows_swap(pieces[3][0], 1), rows_swap(pieces[3][1], 2)
-    near = rows_swap(pieces[1][0], 1), rows_swap(pieces[2][1], 2)
-    return far, near
+    return rows_swap(pieces[3][0], 1), rows_swap(pieces[3][1], 2)
 
 
 def reduce_second(pieces, far):
-    return add_low(pieces[1][1], far[1]), add_low(pieces[2][0], far[0])
-
-
-def reduce_total(pieces, near, late):
-    return [
-        add_wide([pieces[0][0], near[0], late[1]]),
-        add_wide([pieces[0][1], late[0], near[1]]),
-    ]
+    return (
+        jnp.concatenate([pieces[1][0], add_low(pieces[1][1], far[1])], axis=0),
+        jnp.concatenate([add_low(pieces[2][0], far[0]), pieces[2][1]], axis=0),
+    )
+
+
+def reduce_total(pieces, late):
+    return add_wide([jnp.concatenate(pieces[0], axis=0), *late])
 
 
 def add_wide(arrays):
@@ -126,15 +124,28 @@
     return lax.ppermute(array, "cols", [(i, i ^ 1) for i in range(count)])
 
 
+def chips_gather(array):
+    chips = lax.axis_size("cols") // 2
+    return [array] + [chip_shift(array, d) for d in range(1, chips)]
+
+
+def chips_in_order(array, chip):
+    chips = array.shape[0]
+    twice = jnp.concatenate([array[::-1]] * 2, axis=0)
+    return lax.dynamic_slice_in_dim(twice, chips - 1 - chip, chips, 0)
+
+
+def cores_sum(array):
+    count = lax.axis_size("cols")
+    pairs = [[i, i + 1] for i in range(0, count, 2)]
+    came = lax.all_to_all(array, "cols", 0, 0, axis_index_groups=pairs, tiled=True)
+    return add_low(came[0], came[1])
+
+
 def chips_exchange(array):
     count = lax.axis_size("cols")
     alike = [list(range(core, count, 2)) for core in range(2)]
     return lax.all_to_all(array, "cols", 0, 0, axis_index_groups=alike, tiled=True)
-
-
-def chips_spread(array):
-    chips = lax.axis_size("cols") // 2
-    return chips_exchange(jnp.broadcast_to(array, (chips,) + array.shape))
 
 
 def cores_in_order(mine, other, core, axis):
@@ -166,15 +177,17 @@
     q_out, k_out, v_out, n_out, w_out = refs[9:]
     step = pl.program_id(0)
     chips, rows, _ = found.shape
+    chip = meta[1]
 
     @pl.when(step == 0)
     def _():
         first_core = meta[2] == 0
-        for chip in range(chips):
-            mine, other = found[chip], swapped[chip]
-            at = 2 * rows * chip
-            w_out[at : at + rows, :] = jnp.where(first_core, mine, other)
-            w_out[at + rows : at + 2 * rows, :] = jnp.where(first_core, other, mine)
+        for d in range(chips):
+            mine, other = found[d], swapped[d]
+            here = pl.multiple_of(lax.rem(chip + chips - d, chips) * (2 * rows), 2 * rows)
+            w_out[pl.ds(here, 2 * rows), :] = jnp.concatenate(
+                [jnp.where(first_core, mine, other), jnp.where(first_core, other, mine)], axis=0
+            )
 
     for index, part in enumerate(parts):
 
@@ -229,7 +242,7 @@
             jax.ShapeDtypeStruct((width, q_cols + 2 * k_cols), bf16),
         ],
         compiler_params=call_params(32),
-        cost_estimate=cost(1),
+        cost_estimate=cost(10),
         name="project",
     )(meta, *parts, found, swapped, gain, cosine, sine)
 
@@ -294,7 +307,7 @@
             jax.ShapeDtypeStruct((length, 8), f32),
         ],
         compiler_params=call_params(32),
-        cost_estimate=cost(1),
+        cost_estimate=cost(16),
         name="attend",
     )(meta, queries, keys, values, starts)
 
@@ -857,8 +870,8 @@
     return arrays if len(arrays) == 2 else list(halves(arrays[0])[1:])
 
 
-def join_halves(arrays, own):
-    return arrays if own == 2 else [jnp.concatenate(arrays, axis=1)]
+def join_halves(array, own):
+    return array.reshape(own, 2 * array.shape[1] // own, array.shape[2])
 
 
 def pack_weights(gate, up, down):
@@ -922,11 +935,13 @@
     q_cols, k_cols = w_query.shape[1], key_matrix.shape[1]
 
     token_near = gather_near(own_tokens)
-    project_rows = jnp.concatenate([w_query, key_matrix, value_matrix], axis=1)
-    project_found = chips_spread(project_rows)
-    project_swapped = core_swap(project_found)
+    qkv_cols = q_cols + 2 * k_cols
     sixth = w_out.shape[0]
-    out_half = chips_spread(after(w_out, project_found)).reshape(chips * sixth, width)
+    found = chips_gather(
+        jnp.concatenate(
+            [w_query, key_matrix, value_matrix, w_out.reshape(4 * sixth, width // 4)], axis=1
+        )
+    )
     small = jnp.concatenate(
         [
             w_router,
@@ -937,20 +952,25 @@
         axis=1,
     )
     small_full = lax.all_to_all(
-        jnp.tile(after(small, out_half), (4 * columns, 1)), ("rows", "cols"), 0, 0, tiled=True
+        jnp.tile(small, (4 * columns, 1)), ("rows", "cols"), 0, 0, tiled=True
     )
     gain_attn = small_full[:, experts].astype(f32)[None, :]
     gain_moe = small_full[:, experts + 1].astype(f32)[None, :]
     router_full = jnp.where(jnp.arange(LANES) < experts, small_full, 0)
     token_parts = gather_far(own_tokens, *token_near)
-    qkv_cols = q_cols + 2 * k_cols
-    out_near = gather_near(after(out_half, token_near))
+    found = after(found, token_near)
+    project_found = jnp.stack([rows[:, :qkv_cols] for rows in found])
+    project_swapped = core_swap(project_found)
+
+    out_half = jnp.stack([rows[:, qkv_cols:].reshape(sixth, width) for rows in found])
+    out_half = chips_in_order(out_half, chip).reshape(chips * sixth, width)
+    out_near = gather_near(after(out_half, token_parts[3]))
 
     expert_rows = expert_ids[0]
     lane_range = jnp.arange(LANES, dtype=jnp.int32)
     member = jnp.any(expert_rows[:, :, None] == lane_range[None, None, :], axis=1).astype(bf16)
     cot_rows = jnp.concatenate([cotangent[0], member], axis=1)
-    cot_same = [cot_rows, chip_shift(after(cot_rows, out_half), 1)]
+    cot_same = [cot_rows, chip_shift(after(cot_rows, found[1:], token_parts[3]), 1)]
 
     groups = 2 if own_experts % 2 == 0 else 1
     group_size = own_experts // groups
@@ -958,7 +978,7 @@
     for group in range(groups):
         here = slice(group * group_size, (group + 1) * group_size)
         packed.append(pack_weights(after(w_gate[here], own_tokens), w_up[here], w_down[here]))
-    weight_near = [gather_near(after(packed[0], token_parts[3], project_swapped, out_near))]
+    weight_near = [gather_near(after(packed[0], token_parts[3], project_swapped, out_half))]
 
     segments = segment_ids[0]
     length = segments.shape[0]
@@ -977,12 +997,12 @@
     queries, key_rows, value_rows, normed, project_w = project(
         meta, token_parts, project_found, project_swapped, gain_attn, cosine, sine, q_cols, k_cols
     )
-    cot_same[1] = after(cot_same[1], queries)
-    attended, lse = attend(after(meta, cot_same[1]), queries, key_rows, value_rows, starts[:, None], tok)
+    attended, lse = attend(meta, queries, key_rows, value_rows, starts[:, None], tok)
+    cot_same[1], out_near = after((cot_same[1], out_near), attended)
     cot_other = [core_swap(rows) for rows in cot_same]
     for d in range(2, chips):
         cot_same.append(chip_shift(cot_same[-1], 1))
-    attended, out_near = after((attended, out_near), weight_near[0], cot_same[3], cot_other)
+    attended, out_near = after((attended, out_near), weight_near[0], cot_same[2], cot_other)
     own_heads = lax.all_to_all(attended, "rows", 0, 0, tiled=True)
     out_mine = jnp.stack(gather_far(out_half, *out_near)).reshape(4, chips, sixth, width)
     out_parts = cores_in_order(out_mine, core_swap(out_mine), core, 2).reshape(4, tok, width)
@@ -1000,7 +1020,7 @@
     )
     for group in range(1, groups):
         weight_near.append(gather_near(after(packed[group], weight_parts[0][3], moe_rows)))
-    moe_same = [moe_rows, chip_shift(moe_rows, 1)]
+    moe_same = [moe_rows, chip_shift(after(moe_rows, cot_same[3]), 1)]
     moe_other = [core_swap(rows) for rows in moe_same]
     moe_same.append(chip_shift(moe_same[1], 1))
     cot_other += [core_swap(rows) for rows in cot_same[2:]]
@@ -1018,7 +1038,7 @@
     pairs = [(d, d + 1) for d in range(0, chips, 2)]
     early = [[] for _ in pairs]
     held = ()
-    far, near, late, sums = [], [], [], []
+    far, late, sums = [], [], []
 
     def make_grads(group, first_rows):
         chunks = kept[group]
@@ -1029,12 +1049,14 @@
             [k[1] for k in chunks],
         )
         grads.append([two_halves(part) for part in parts])
-        for store, sent in zip((far, near), reduce_first(grads[-1])):
-            store.append(sent)
-
-    for group in range(groups):
-        final = group == groups - 1
-        for index, pair in enumerate(pairs):
+
+    for index, pair in enumerate(pairs):
+        for group in range(groups):
+            final = group == groups - 1
+            if final and index == len(pairs) - 1 and groups > 1:
+                make_grads(0, kept[0][0][0])
+                far.append(reduce_first(grads[0]))
+                held = grads[0]
             result = list(
                 run_experts(
                     after(moe_meta, held),
@@ -1052,6 +1074,7 @@
             held = result[0]
             if len(moe_other) == 2:
                 moe_same[2] = after(moe_same[2], held)
+                held = (held, moe_same[2])
                 for d in range(3, chips):
                     moe_same.append(chip_shift(moe_same[-1], 1))
                 moe_other += [core_swap(rows) for rows in moe_same[2:]]
@@ -1062,39 +1085,42 @@
                 kept[group].append(result[:4])
                 early[index] = result[4:]
                 continue
-            if index > 0:
-                result = after(result, near, dx_hop)
+            if index == 0:
+                result = after(result, moe_same[3])
+            if index == len(pairs) - 1:
+                result = after(result, dx_hop, far if groups > 1 else ())
             kept[group].append(result[4:8])
             for place, d in enumerate(pair):
                 pieces[d] = (result[2 * place], core_swap(result[2 * place + 1]))
             if index == 0:
                 dx_ring = piece(1, width, both)
-                if groups > 1:
-                    sums.append(reduce_second(grads[0], after(far[0], result[0])))
-                    late.append([rows_swap(*sent) for sent in zip(sums[0], (1, 2))])
-                held = (dx_ring, sums)
+                held = dx_ring
                 dx_hop = chip_shift(dx_ring, 1)
                 continue
             for d in pair:
                 came = dx_hop if d == 2 else chip_shift(dx_ring, 1)
                 if d == chips - 1:
-                    came = after(came, grads[-1], late)
-                    outs = [piece(at, 0, width) for at in range(chips - 1)]
-                dx_ring = add_low(came, piece(d, width, both))
-                if d == chips - 2:
-                    make_grads(group, after(kept[group][0][0], dx_ring))
-        if not final:
-            make_grads(group, kept[group][0][0])
-            held = grads[-1]
+                    came = after(came, grads[-1])
+                    far.append(reduce_first(after(grads[-1], came)))
+                dx_ring = add_low(came, last_pieces[0] if d == chips - 1 else piece(d, width, both))
+                if d != chips - 2:
+                    continue
+                last_pieces = [piece(chips - 1, width, both), piece(0, width, both)]
+                if groups > 1:
+                    sums.append(reduce_second(grads[0], after(far[0], dx_ring)))
+                    late.append([rows_swap(*sent) for sent in zip(sums[0], (1, 2))])
+                make_grads(group, after(kept[group][0][0], dx_ring, sums, last_pieces))
+    for d in range(chips):
+        pieces[d] = after(pieces[d], dx_ring)
+    outs = [piece(d, 0, width) for d in range(chips - 1)]
     outs.append(piece(chips - 1, 0, width))
-    last_piece = piece(0, width, both)
-    dx_came = after(chip_shift(dx_ring, 1), outs, last_piece)
+    dx_came = after(chip_shift(dx_ring, 1), outs)
     out_hop = chip_shift(after(outs[1], dx_came), 1)
 
     grad_mixed, grad_heads, wide_mine, wide_other = unmix(
-        after(meta, far[-1]),
+        after(meta, late[:1]),
         dx_came,
-        last_piece,
+        last_pieces[1],
         mixed_rows,
         cotangent[0],
         gates,
@@ -1105,20 +1131,13 @@
         experts,
         chips,
     )
-    grad_attended = lax.all_to_all(after(grad_heads, near[-1]), "rows", 0, 0, tiled=True)
-
-    out_ring = add_low(after(out_hop, grad_attended), outs[2])
-    wide_chip = add_low(wide_mine, core_swap(wide_other))
-    wide_row = add_low_all(lax.all_to_all(wide_chip, "rows", 0, 0, tiled=True))
-    wide_sum = jnp.sum(chips_exchange(wide_row).astype(f32), axis=0)
-    grad_out_w = wide_sum[:, :width]
-    grad_router_w = wide_sum[:, width : width + experts]
-    grad_gain_moe_w = wide_sum[:, width + experts]
-
-    sums.append(after(reduce_second(grads[-1], far[-1]), grad_attended))
-    late.append([rows_swap(*sent) for sent in zip(sums[-1], (1, 2))])
+    grad_attended = lax.all_to_all(grad_heads, "rows", 0, 0, tiled=True)
+
+    wide_chip = add_low(wide_mine, core_swap(after(wide_other, far[-1])))
+    wide_came = lax.all_to_all(wide_chip, "rows", 0, 0, tiled=True)
+
     grad_lin = attend_back(
-        after(meta, wide_chip, sums),
+        after(meta, wide_chip),
         queries,
         grad_attended,
         lse.T,
@@ -1129,30 +1148,39 @@
         sine,
         tok,
     )
-    grad_lin = after(grad_lin, late)
+    grad_lin = after(grad_lin, late[:1], wide_came)
     normed_parts = [None] * 4
     for j in (3, 1, 2, 0):
         normed_parts[j] = dot_nt(grad_lin[j], project_w).astype(bf16)
-    normed_sums = reduce_add(normed_parts, *after(reduce_far(normed_parts), wide_row))
-    grad_normed = add_wide([normed_parts[0], *reduce_near(*normed_sums)])
-    grad_project = dot_tn(normed.reshape(length, width), grad_lin.reshape(length, qkv_cols))
-    project_pairs = grad_project.astype(bf16).reshape(chips, 2, width // columns, qkv_cols)
-    project_chip = add_low(
-        lax.dynamic_index_in_dim(project_pairs, core, 1, keepdims=False),
-        core_swap(lax.dynamic_index_in_dim(project_pairs, 1 - core, 1, keepdims=False)),
-    )
-    project_sum = jnp.sum(chips_exchange(project_chip).astype(f32), axis=0)
-
+    normed_sums = reduce_add(normed_parts, *reduce_far(normed_parts))
+    normed_near = reduce_near(*normed_sums)
+    sums.append(reduce_second(grads[-1], after(far[-1], *normed_sums)))
+    late.append([rows_swap(*sent) for sent in zip(sums[-1], (1, 2))])
+    grad_project = dot_tn(
+        after(normed, *normed_parts).reshape(length, width), grad_lin.reshape(length, qkv_cols)
+    )
+    project_pairs = after(grad_project.astype(bf16), *normed_sums)
+    project_pairs = project_pairs.reshape(chips, 2, width // columns, qkv_cols)
+    project_chip = cores_sum(project_pairs.transpose(1, 0, 2, 3))
+    project_came = chips_exchange(project_chip)
+    project_sum = jnp.sum(after(project_came, late[-1]).astype(f32), axis=0)
+    grad_normed = add_wide([normed_parts[0], *after(normed_near, project_sum)])
+    wide_row = add_low_all(after(wide_came, project_came))
+    wide_sum = jnp.sum(chips_exchange(wide_row).astype(f32), axis=0)
+    grad_out_w = wide_sum[:, :width]
+    grad_router_w = wide_sum[:, width : width + experts]
+    grad_gain_moe_w = wide_sum[:, width + experts]
+
+    out_ring = add_low(after(out_hop, grad_lin), outs[2])
     for d in range(3, chips):
-        out_ring = add_low(after(chip_shift(out_ring, 1), grad_lin), outs[d])
-    moe_out = add_wide([after(chip_shift(out_ring, 1), *normed_sums), outs[0]])
+        out_ring = add_low(after(chip_shift(out_ring, 1), *normed_sums), outs[d])
+    moe_out = add_wide([after(chip_shift(out_ring, 1), project_chip), outs[0]])
     block_out = mixed_rows + res_scale * moe_out
 
     totals = []
-    for parts, soon, last in zip(grads, near, late):
-        total = reduce_total([after(parts[0], *normed_sums)], soon, last)
-        for array in join_halves(total, group_size):
-            totals.append(unpack_weights(array, width // 4, ffe))
+    for parts, came in zip(grads, late):
+        total = reduce_total([after(parts[0], *normed_sums, project_chip)], came)
+        totals.append(unpack_weights(join_halves(total, group_size), width // 4, ffe))
     grad_gate_w, grad_up_w, grad_down_w = (
         jnp.concatenate(arrays, axis=0) for arrays in zip(*totals)
     )

time: 777 us -> 755 us (0.972)
  waiting for transfers between devices: 248 us -> 231 us
  Pallas kernels: 219 us -> 208 us
  local copies, waits for them, and re-layouts: 80.4 us -> 89.2 us
    ppermute x12 -> x15, waiting for transfers between devices: 117 us -> 77.3 us  [chip_shift(): lax.ppermute(array, 'cols', [(i, (i + 2 * distance) % count) for i in ran...]
    ppermute x32 -> x28, waiting for transfers between devices: 62.8 us -> 92.2 us  [rows_swap(): return lax.ppermute(array, 'rows', [(i, i ^ distance) for i in range(4)])]
    all_to_all x3, waiting for transfers between devices: 32.6 us -> 9.18 us  [the longest x1 5.49 us: per_device(): lax.all_to_all(jnp.tile(small, (4 * columns, 1)), ('rows', 'cols'), 0, 0,...]
    ppermute x12 -> x15, starting transfers between devices: 1.75 us -> 19.1 us  [chip_shift(): lax.ppermute(array, 'cols', [(i, (i + 2 * distance) % count) for i in ran...]
    all_to_all x1, starting transfers between devices: 15.6 us -> 6.2 us  [per_device(): own_heads = lax.all_to_all(attended, 'rows', 0, 0, tiled=True)]
    all_to_all x4 -> x2, waiting for transfers between devices: 23.1 us -> 31.9 us  [chips_exchange(): lax.all_to_all(array, 'cols', 0, 0, axis_index_groups=alike, tiled=True)]
    concatenate x0 -> x5, other arithmetic: none -> 7.89 us  [the longest x2 3.22 us: reduce_second(): jnp.concatenate([pieces[1][0], add_low(pieces[1][1], far[1])], axis=0)]
    all_to_all x4 -> x2, starting transfers between devices: 19.5 us -> 13.3 us  [chips_exchange(): lax.all_to_all(array, 'cols', 0, 0, axis_index_groups=alike, tiled=True)]
  transfers between devices with their start and end apart: 70 -> 66, of which waited for: 28 -> 31; matrix products, arithmetic and copies ran while one was open for 21% -> 23% of each run, Pallas kernels for 23% -> 28%
where the time goes in v2:
time: 755 us; the launch traced here: 744 us
  waiting for transfers between devices  231 us (31%)
  Pallas kernels  208 us (28%)
  other arithmetic  105 us (14%)
  starting transfers between devices  91.3 us (12%)
  local copies, waits for them, and re-layouts  89.2 us (12%)
  matrix products  11.3 us (1%)
    pallas_call x4, Pallas kernels, run_experts(): pl.pallas_call(partial(experts_kernel, experts=experts, slots=slots, loca...  114 us
    ppermute x28, waiting for transfers between devices, rows_swap(): return lax.ppermute(array, 'rows', [(i, i ^ distance) for i in range(4)])  92.2 us
    ppermute x15, waiting for transfers between devices, chip_shift(): lax.ppermute(array, 'cols', [(i, (i + 2 * distance) % count) for i in ran...  77.3 us
    unnamed x238, local copies, waits for them, and re-layouts  44.9 us
    convert_element_type x19, other arithmetic, add_low(): return (left.astype(f32) + right.astype(f32)).astype(bf16)  42.1 us
    pallas_call x2, Pallas kernels, weight_grads(): pl.pallas_call(partial(weight_grad_kernel, chunks=chunks, own_count=own),...  32.4 us
    all_to_all x2, waiting for transfers between devices, chips_exchange(): lax.all_to_all(array, 'cols', 0, 0, axis_index_groups=alike, tiled=True)  31.9 us
    ppermute x28, starting transfers between devices, rows_swap(): return lax.ppermute(array, 'rows', [(i, i ^ distance) for i in range(4)])  25.3 us
  transfers between devices with their start and end apart: 66, of which 31 were waited for; matrix products, arithmetic and copies ran while one was open for 23% of the time, Pallas kernels for 28%

profile of v2, /device:TPU:6, one launch (start us, length us, event | category | flops | bytes accessed | tf_op | source)
XLA Modules:
  0.0 744.2 jit_solution(7275787197122602884)
XLA Ops:
  16.7 4.7 all-to-all-start
  49.5 5.5 all-to-all-done
  72.2 6.3 collective-permute-done.3
  84.3 9.4 %project.1 = (bf16[1536,384]{1,0:T(8,128)(2,1)S(1)}, bf16[1536,128]{1,0:T(8,128)(2,1)S(1)}, bf16[1536,128]{1,0:T(8,128)(2,1)S(1)}, bf16[4,384,1536]{2,1,0:T(8,128)(2,1)S(1)}, bf16[1536,640]{1,0:T(8,128)(2,1)S(1)}) custom-call(s32[7]{0:T(128)S(1)} %pad_add_fusion.meta, bf16[384,1536]{1,0:T(8,128)(2,1)S(1)} %bitcast.69, bf16[384,1536]{1,0:T(8,128)(2,1)S(1)} %copy-done.22, ...), custom_call_target="tpu_custom_call" | custom-call | flops 11500000256 | tf_op jit(solution)/shard_map/project/pallas_call | solution.py:222
  93.8 13.2 %attend.1 = (bf16[4,384,384]{2,1,0:T(8,128)(2,1)}, f32[1536,8]{1,0:T(8,128)S(1)}) custom-call(s32[7]{0:T(128)S(1)} %pad_add_fusion.meta, bf16[1536,384]{1,0:T(8,128)(2,1)S(1)} %get-tuple-element.152.queries, bf16[1536,128]{1,0:T(8,128)(2,1)S(1)} %get-tuple-element.153.keys, bf16[1536,128]{1,0:T(8,128)(2,1)S(1)} %get-tuple-element.154.values, ...), custom_call_target="tpu_custom_call" | custom-call | flops 18400000000 | tf_op jit(solution)/shard_map/attend/pallas_call | solution.py:289
  109.0 3.3 collective-permute-done.8.refs_6_
  112.6 29.8 %collective-permute-done.13.refs_4_ = bf16[384,1664]{1,0:T(8,128)(2,1)S(1)} collective-permute-done((bf16[384,1664]{1,0:T(8,128)(2,1)S(1)}, bf16[384,1664]{1,0:T(8,128)(2,1)S(1)}, u32[]{:S(2)}, u32[]{:S(2)}) %collective-permute-start.13) | collective-permute-done | bytes 1277984 | tf_op jit(solution)/shard_map/ppermute | solution.py:117
  147.9 5.8 collective-permute-done.17
  156.6 6.2 all-to-all-start.1
  167.5 9.7 %all-to-all-done.1.heads = bf16[4,384,384]{2,1,0:T(8,128)(2,1)S(1)} async-done(((bf16[4,384,384]{2,1,0:T(8,128)(2,1)}), bf16[4,384,384]{2,1,0:T(8,128)(2,1)S(1)}, u32[]{:S(2)}, u32[]{:S(2)}) %all-to-all-start.1) | async-done | bytes 1179680 | tf_op jit(solution)/shard_map/all_to_all | solution.py:1006
  183.8 5.4 mix.1
  194.5 26.6 %collective-permute-done.21.refs_2_ = bf16[384,1664]{1,0:T(8,128)(2,1)} collective-permute-done((bf16[384,1664]{1,0:T(8,128)(2,1)}, bf16[384,1664]{1,0:T(8,128)(2,1)}, u32[]{:S(2)}, u32[]{:S(2)}) %collective-permute-start.21) | collective-permute-done | bytes 1277984 | tf_op jit(solution)/shard_map/ppermute | solution.py:117
  229.4 24.0 %experts.4 = (bf16[2,512,1536]{2,1,0:T(8,128)(2,1)}, bf16[2,512,1536]{2,1,0:T(8,128)(2,1)}, bf16[2,512,512]{2,1,0:T(8,128)(2,1)}, bf16[2,512,1024]{2,1,0:T(8,128...) custom-call(s32[2]{0:T(128)} %pad_add_fusion.1.meta, ...), custom_call_target="tpu_custom_call" | custom-call | flops 29899999232 | tf_op jit(solution)/shard_map/experts/pallas_call | solution.py:770
  253.4 8.0 %collective-permute-done.25.refs_0_ = bf16[384,1664]{1,0:T(8,128)(2,1)} collective-permute-done((bf16[384,1664]{1,0:T(8,128)(2,1)}, bf16[384,1664]{1,0:T(8,128)(2,1)}, u32[]{:S(2)}, u32[]{:S(2)}) %collective-permute-start.25) | collective-permute-done | bytes 1277984 | tf_op jit(solution)/shard_map/ppermute | solution.py:117
  261.4 19.0 %collective-permute-done.26.refs_12_ = bf16[2,4608,128]{2,1,0:T(8,128)(2,1)} collective-permute-done((bf16[2,4608,128]{2,1,0:T(8,128)(2,1)}, bf16[2,4608,128]{2,1,0:T(8,128)(2,1)}, u32[]{:S(2)}, u32[]{:S(2)}) %collective-permute-start.26) | collective-permute-done | bytes 2359328 | tf_op jit(solution)/shard_map/ppermute | solution.py:42
  286.5 23.8 %collective-permute-done.28 = bf16[1,4608,128]{2,1,0:T(8,128)(2,1)S(1)} collective-permute-done((bf16[1,4608,128]{2,1,0:T(8,128)(2,1)S(1)}, bf16[1,4608,128]{2,1,0:T(8,128)(2,1)S(1)}, u32[]{:S(2)}, u32[]{:S(2)}) %collective-permute-start.28) | collective-permute-done | bytes 1179680 | tf_op jit(solution)/shard_map/ppermute | solution.py:42
  313.7 33.0 %experts.5 = (bf16[384,3200]{1,0:T(8,128)(2,1)}, bf16[384,3200]{1,0:T(8,128)(2,1)}, bf16[384,3200]{1,0:T(8,128)(2,1)}, bf16[384,3200]{1,0:T(8,128)(2,1)}, bf16[2...) custom-call(s32[2]{0:T(128)} %pad_add_fusion.1.meta, ...), custom_call_target="tpu_custom_call" | custom-call | flops 29899999232 | tf_op jit(solution)/shard_map/experts/pallas_call | solution.py:770
  347.9 6.5 collective-permute-done.31
  359.1 24.0 %experts.6 = (bf16[2,512,1536]{2,1,0:T(8,128)(2,1)}, bf16[2,512,1536]{2,1,0:T(8,128)(2,1)}, bf16[2,512,512]{2,1,0:T(8,128)(2,1)}, bf16[2,512,1024]{2,1,0:T(8,128...) custom-call(s32[2]{0:T(128)} %pad_add_fusion.1.meta, ...), custom_call_target="tpu_custom_call" | custom-call | flops 29899999232 | tf_op jit(solution)/shard_map/experts/pallas_call | solution.py:770
  383.2 16.2 %weight_grads.2 = (bf16[1,4608,128]{2,1,0:T(8,128)(2,1)}, bf16[1,4608,128]{2,1,0:T(8,128)(2,1)}, bf16[1,4608,128]{2,1,0:T(8,128)(2,1)}, bf16[1,4608,128]{2,1,0:T...) custom-call(bf16[2,512,1536]{2,1,0:T(8,128)(2,1)} %get-tuple-element, ...), custom_call_target="tpu_custom_call" | custom-call | flops 14949999616 | tf_op jit(solution)/shard_map/weight_grads/pallas_call | solution.py:849
  402.3 33.1 %experts.7 = (bf16[384,3200]{1,0:T(8,128)(2,1)}, bf16[384,3200]{1,0:T(8,128)(2,1)}, bf16[384,3200]{1,0:T(8,128)(2,1)}, bf16[384,3200]{1,0:T(8,128)(2,1)}, bf16[2...) custom-call(s32[2]{0:T(128)} %pad_add_fusion.1.meta, ...), custom_call_target="tpu_custom_call" | custom-call | flops 29899999232 | tf_op jit(solution)/shard_map/experts/pallas_call | solution.py:770
  435.6 3.2 add_convert_fusion.2.last
  440.4 3.8 add_convert_fusion.4
  454.8 16.1 %weight_grads.3 = (bf16[1,4608,128]{2,1,0:T(8,128)(2,1)}, bf16[1,4608,128]{2,1,0:T(8,128)(2,1)}, bf16[1,4608,128]{2,1,0:T(8,128)(2,1)}, bf16[1,4608,128]{2,1,0:T...) custom-call(bf16[2,512,1536]{2,1,0:T(8,128)(2,1)} %get-tuple-element, ...), custom_call_target="tpu_custom_call" | custom-call | flops 14949999616 | tf_op jit(solution)/shard_map/weight_grads/pallas_call | solution.py:849
  470.9 5.5 collective-permute-done.40
  492.1 9.8 %collective-permute-done.45 = bf16[2,4608,128]{2,1,0:T(8,128)(2,1)} collective-permute-done((bf16[2,4608,128]{2,1,0:T(8,128)(2,1)}, bf16[2,4608,128]{2,1,0:T(8,128)(2,1)}, u32[]{:S(2)}, u32[]{:S(2)}) %collective-permute-start.45) | collective-permute-done | bytes 2359328 | tf_op jit(solution)/shard_map/ppermute | solution.py:42
  501.9 3.9 collective-permute-done.46
  505.8 4.1 collective-permute-done.43.came
  510.0 10.2 %unmix.1 = (f32[384,1536]{1,0:T(8,128)S(1)}, bf16[4,384,384]{2,1,0:T(8,128)(2,1)S(1)}, bf16[4,4,48,1664]{3,2,1,0:T(8,128)(2,1)S(1)}, bf16[4,4,48,1664]{3,2,1,0:T(8,128)(2,1)}) custom-call(s32[7]{0:T(128)S(1)} %pad_add_fusion.meta, bf16[384,1664]{1,0:T(8,128)(2,1)S(1)} %collective-permute-done.43.came, bf16[384,1664]{1,0:T(8,128)(2,1)S(1)} %copy-done.5, ...), custom_call_target="tpu_custom_call" | custom-call | flops 13799999488 | tf_op jit(solution)/shard_map/unmix/pallas_call | solution.py:513
  526.3 3.6 collective-permute-done.48
  531.3 5.6 all-to-all-start.2
  542.2 4.6 add_convert_fusion
  546.8 3.7 all-to-all-done.2.grads
  550.5 6.0 all-to-all-start.3
  562.8 23.6 %attend_back.1 = bf16[4,384,640]{2,1,0:T(8,128)(2,1)S(1)} custom-call(s32[7]{0:T(128)S(1)} %pad_add_fusion.meta, bf16[1536,384]{1,0:T(8,128)(2,1)S(1)} %copy-done.30, bf16[4,384,384]{2,1,0:T(8,128)(2,1)} %all-to-all-done.2.grads, f32[8,1536]{1,0:T(8,128)S(1)} %bitcast.77, s32[1,1536]{1,0:T(1,128)S(1)} %broadcast_in_dim.39.starts, ...), custom_call_target="tpu_custom_call" | custom-call | flops 33350000640 | tf_op jit(solution)/shard_map/attend_back/pallas_call | solution.py:393
  597.7 7.3 collective-permute-start.50
  606.0 4.0 bitcast_convert_fusion
  610.0 7.7 %collective-permute-done.51 = bf16[192,1536]{1,0:T(8,128)(2,1)S(1)} collective-permute-done((bf16[192,1536]{1,0:T(8,128)(2,1)S(1)}, bf16[192,1536]{1,0:T(8,128)(2,1)S(1)}, u32[]{:S(2)}, u32[]{:S(2)}) %collective-permute-start.51) | collective-permute-done | bytes 589856 | tf_op jit(solution)/shard_map/ppermute | solution.py:42
  621.8 5.3 all_to_all.48
  628.3 6.5 all-to-all-start.5
  647.3 3.1 convert_add_fusion.1
  653.3 31.4 %all-to-all-done.5 = bf16[4,192,640]{2,1,0:T(8,128)(2,1)} async-done(((bf16[4,192,640]{2,1,0:T(8,128)(2,1)}), bf16[4,192,640]{2,1,0:T(8,128)(2,1)}, u32[]{:S(2)}, u32[]{:S(2)}) %all-to-all-start.5) | async-done | bytes 983072 | tf_op jit(solution)/shard_map/all_to_all | solution.py:148
  687.9 3.8 add_bitcast_fusion
  695.6 3.1 convert_add_fusion
  705.5 5.2 all-to-all-start.7
  718.8 6.9 all-to-all-start.6
  725.6 4.3 fusion.6
  732.6 3.8 maximum_maximum_fusion.2
  (461 shorter events, 232.4 us)
Async XLA Ops:
  0.7 45.9 %collective-permute-start = (bf16[384,1536]{1,0:T(8,128)(2,1)}, bf16[384,1536]{1,0:T(8,128)(2,1)S(1)}, u32[]{:S(2)}, u32[]{:S(2)}) collective-permute-start(bf16[384,1536]{1,0:T(8,128)(2,1)} %bitcast.67), channel_id=1, source_target_pairs={{0,8},{8,0},{16,24},{24,16},{1,9},{9,1},{17,25},{25,17},{2,10},{10... | collective-permute-start | bytes 3538952 | tf_op jit(solution)/shard_map/ppermute | solution.py:42
  1.3 42.8 %collective-permute-start.1 = (bf16[384,1536]{1,0:T(8,128)(2,1)}, bf16[384,1536]{1,0:T(8,128)(2,1)}, u32[]{:S(2)}, u32[]{:S(2)}) collective-permute-start(bf16[384,1536]{1,0:T(8,128)(2,1)} %bitcast.68), channel_id=1, source_target_pairs={{0,16},{8,24},{16,0},{24,8},{1,17},{9,25},{17,1},{25,9},{2,18},{10... | collective-permute-start | bytes 3538952 | tf_op jit(solution)/shard_map/ppermute | solution.py:42
  7.4 39.1 %collective-permute-start.4 = (bf16[192,1024]{1,0:T(8,128)(2,1)}, bf16[192,1024]{1,0:T(8,128)(2,1)}, u32[]{:S(2)}, u32[]{:S(2)}) collective-permute-start(bf16[192,1024]{1,0:T(8,128)(2,1)} %constant_dynamic-update-slice_fusion.2), channel_id=1, source_target_pairs={{0,2},{1,3},{2,4},{3,5},{4,6},{5,7},{6,0},{7,1},{8,10},{9,11},{10,... | collective-permute-start | bytes 1179656 | tf_op jit(solution)/shard_map/ppermute | solution.py:117
  9.5 37.1 %collective-permute-start.5 = (bf16[192,1024]{1,0:T(8,128)(2,1)}, bf16[192,1024]{1,0:T(8,128)(2,1)}, u32[]{:S(2)}, u32[]{:S(2)}) collective-permute-start(bf16[192,1024]{1,0:T(8,128)(2,1)} %constant_dynamic-update-slice_fusion.2), channel_id=1, source_target_pairs={{0,4},{1,5},{2,6},{3,7},{4,0},{5,1},{6,2},{7,3},{8,12},{9,13},{10,... | collective-permute-start | bytes 1179656 | tf_op jit(solution)/shard_map/ppermute | solution.py:117
  12.1 34.5 %collective-permute-start.6 = (bf16[192,1024]{1,0:T(8,128)(2,1)}, bf16[192,1024]{1,0:T(8,128)(2,1)}, u32[]{:S(2)}, u32[]{:S(2)}) collective-permute-start(bf16[192,1024]{1,0:T(8,128)(2,1)} %constant_dynamic-update-slice_fusion.2), channel_id=1, source_target_pairs={{0,6},{1,7},{2,0},{3,1},{4,2},{5,3},{6,4},{7,5},{8,14},{9,15},{10,... | collective-permute-start | bytes 1179656 | tf_op jit(solution)/shard_map/ppermute | solution.py:117
  16.7 38.3 %all-to-all-start = ((bf16[32,48,128]{2,1,0:T(8,128)(2,1)}), bf16[32,48,128]{2,1,0:T(8,128)(2,1)S(1)}, u32[]{:S(2)}, u32[]{:S(2)}) async-start(bf16[32,48,128]{2,1,0:T(8,128)(2,1)} %tile.2), calls=%async_computation | async-start | bytes 786432 | tf_op jit(solution)/shard_map/all_to_all | solution.py:954
  46.0 25.1 %collective-permute-start.2 = (bf16[192,1536]{1,0:T(8,128)(2,1)}, bf16[192,1536]{1,0:T(8,128)(2,1)}, u32[]{:S(2)}, u32[]{:S(2)}) collective-permute-start(bf16[192,1536]{1,0:T(8,128)(2,1)} %slice.414), channel_id=1, source_target_pairs={{0,8},{8,0},{16,24},{24,16},{1,9},{9,1},{17,25},{25,17},{2,10},{10... | collective-permute-start | bytes 1769480 | tf_op jit(solution)/shard_map/ppermute | solution.py:42
  49.4 32.3 %collective-permute-start.7 = (bf16[4,192,640]{2,1,0:T(8,128)(2,1)S(1)}, bf16[4,192,640]{2,1,0:T(8,128)(2,1)}, u32[]{:S(2)}, u32[]{:S(2)}) collective-permute-start(bf16[4,192,640]{2,1,0:T(8,128)(2,1)S(1)} %pad_maximum_fusion.9.refs_4_), channel_id=1, source_target_pairs={{0,1},{1,0},{2,3},{3,2},{4,5},{5,4},{6,7},{7,6},{8,9},{9,8},{10,11... | collective-permute-start | bytes 2949128 | tf_op jit(solution)/shard_map/ppermute | solution.py:124
  79.6 27.4 %collective-permute-start.9 = (bf16[192,1536]{1,0:T(8,128)(2,1)S(1)}, bf16[192,1536]{1,0:T(8,128)(2,1)S(1)}, u32[]{:S(2)}, u32[]{:S(2)}) collective-permute-start(bf16[192,1536]{1,0:T(8,128)(2,1)S(1)} %bitcast.90), channel_id=1, source_target_pairs={{0,8},{8,0},{16,24},{24,16},{1,9},{9,1},{17,25},{25,17},{2,10},{10... | collective-permute-start | bytes 1769480 | tf_op jit(solution)/shard_map/ppermute | solution.py:42
  80.3 28.7 %collective-permute-start.10 = (bf16[192,1536]{1,0:T(8,128)(2,1)S(1)}, bf16[192,1536]{1,0:T(8,128)(2,1)S(1)}, u32[]{:S(2)}, u32[]{:S(2)}) collective-permute-start(bf16[192,1536]{1,0:T(8,128)(2,1)S(1)} %bitcast.91), channel_id=1, source_target_pairs={{0,16},{8,24},{16,0},{24,8},{1,17},{9,25},{17,1},{25,9},{2,18},{10... | collective-permute-start | bytes 1769480 | tf_op jit(solution)/shard_map/ppermute | solution.py:42
  80.8 31.5 %collective-permute-start.8 = (bf16[384,1664]{1,0:T(8,128)(2,1)}, bf16[384,1664]{1,0:T(8,128)(2,1)S(1)}, u32[]{:S(2)}, u32[]{:S(2)}) collective-permute-start(bf16[384,1664]{1,0:T(8,128)(2,1)} %pad_maximum_fusion.6.refs_4_), channel_id=1, source_target_pairs={{0,2},{1,3},{2,4},{3,5},{4,6},{5,7},{6,0},{7,1},{8,10},{9,11},{10,... | collective-permute-start | bytes 3833864 | tf_op jit(solution)/shard_map/ppermute | solution.py:117
  81.7 63.8 %collective-permute-start.11 = (bf16[2,4608,128]{2,1,0:T(8,128)(2,1)}, bf16[2,4608,128]{2,1,0:T(8,128)(2,1)S(1)}, u32[]{:S(2)}, u32[]{:S(2)}) collective-permute-start(bf16[2,4608,128]{2,1,0:T(8,128)(2,1)} %get-tuple-element.161.refs_8_), channel_id=1, source_target_pairs={{0,8},{8,0},{16,24},{24,16},{1,9},{9,1},{17,25},{25,17},{2,10},{10... | collective-permute-start | bytes 7077896 | tf_op jit(solution)/shard_map/ppermute | solution.py:42
  82.8 62.8 %collective-permute-start.12 = (bf16[2,4608,128]{2,1,0:T(8,128)(2,1)}, bf16[2,4608,128]{2,1,0:T(8,128)(2,1)S(1)}, u32[]{:S(2)}, u32[]{:S(2)}) collective-permute-start(bf16[2,4608,128]{2,1,0:T(8,128)(2,1)} %get-tuple-element.161.refs_8_), channel_id=1, source_target_pairs={{0,16},{8,24},{16,0},{24,8},{1,17},{9,25},{17,1},{25,9},{2,18},{10... | collective-permute-start | bytes 7077896 | tf_op jit(solution)/shard_map/ppermute | solution.py:42
  112.3 30.1 %collective-permute-start.13 = (bf16[384,1664]{1,0:T(8,128)(2,1)S(1)}, bf16[384,1664]{1,0:T(8,128)(2,1)S(1)}, u32[]{:S(2)}, u32[]{:S(2)}) collective-permute-start(bf16[384,1664]{1,0:T(8,128)(2,1)S(1)} %collective-permute-done.8.refs_6_), channel_id=1, source_target_pairs={{0,2},{1,3},{2,4},{3,5},{4,6},{5,7},{6,0},{7,1},{8,10},{9,11},{10,... | collective-permute-start | bytes 3833864 | tf_op jit(solution)/shard_map/ppermute | solution.py:117
  112.5 29.9 %collective-permute-start.15 = (bf16[384,1664]{1,0:T(8,128)(2,1)S(1)}, bf16[384,1664]{1,0:T(8,128)(2,1)S(1)}, u32[]{:S(2)}, u32[]{:S(2)}) collective-permute-start(bf16[384,1664]{1,0:T(8,128)(2,1)S(1)} %collective-permute-done.8.refs_6_), channel_id=1, source_target_pairs={{0,1},{1,0},{2,3},{3,2},{4,5},{5,4},{6,7},{7,6},{8,9},{9,8},{10,11... | collective-permute-start | bytes 3833864 | tf_op jit(solution)/shard_map/ppermute | solution.py:124
  156.6 32.6 %collective-permute-start.20 = (bf16[384,1664]{1,0:T(8,128)(2,1)}, bf16[384,1664]{1,0:T(8,128)(2,1)}, u32[]{:S(2)}, u32[]{:S(2)}) collective-permute-start(bf16[384,1664]{1,0:T(8,128)(2,1)} %copy-done.98), channel_id=1, source_target_pairs={{0,2},{1,3},{2,4},{3,5},{4,6},{5,7},{6,0},{7,1},{8,10},{9,11},{10,... | collective-permute-start | bytes 3833864 | tf_op jit(solution)/shard_map/ppermute | solution.py:117
  156.6 20.7 %all-to-all-start.1 = ((bf16[4,384,384]{2,1,0:T(8,128)(2,1)}), bf16[4,384,384]{2,1,0:T(8,128)(2,1)S(1)}, u32[]{:S(2)}, u32[]{:S(2)}) async-start(bf16[4,384,384]{2,1,0:T(8,128)(2,1)} %get-tuple-element.163), calls=%async_computation.1 | async-start | bytes 2359296 | tf_op jit(solution)/shard_map/all_to_all | solution.py:1006
  189.2 31.9 %collective-permute-start.21 = (bf16[384,1664]{1,0:T(8,128)(2,1)}, bf16[384,1664]{1,0:T(8,128)(2,1)}, u32[]{:S(2)}, u32[]{:S(2)}) collective-permute-start(bf16[384,1664]{1,0:T(8,128)(2,1)} %get-tuple-element.168.refs_0_), channel_id=1, source_target_pairs={{0,2},{1,3},{2,4},{3,5},{4,6},{5,7},{6,0},{7,1},{8,10},{9,11},{10,... | collective-permute-start | bytes 3833864 | tf_op jit(solution)/shard_map/ppermute | solution.py:117
  190.3 31.4 %collective-permute-start.23 = (bf16[1,4608,128]{2,1,0:T(8,128)(2,1)}, bf16[1,4608,128]{2,1,0:T(8,128)(2,1)}, u32[]{:S(2)}, u32[]{:S(2)}) collective-permute-start(bf16[1,4608,128]{2,1,0:T(8,128)(2,1)} %slice.342), channel_id=1, source_target_pairs={{0,8},{8,0},{16,24},{24,16},{1,9},{9,1},{17,25},{25,17},{2,10},{10... | collective-permute-start | bytes 3538952 | tf_op jit(solution)/shard_map/ppermute | solution.py:42
  192.9 31.1 %collective-permute-start.24 = (bf16[1,4608,128]{2,1,0:T(8,128)(2,1)}, bf16[1,4608,128]{2,1,0:T(8,128)(2,1)}, u32[]{:S(2)}, u32[]{:S(2)}) collective-permute-start(bf16[1,4608,128]{2,1,0:T(8,128)(2,1)} %slice.343), channel_id=1, source_target_pairs={{0,16},{8,24},{16,0},{24,8},{1,17},{9,25},{17,1},{25,9},{2,18},{10... | collective-permute-start | bytes 3538952 | tf_op jit(solution)/shard_map/ppermute | solution.py:42
  194.5 34.9 %collective-permute-start.19 = (bf16[384,1664]{1,0:T(8,128)(2,1)}, bf16[384,1664]{1,0:T(8,128)(2,1)}, u32[]{:S(2)}, u32[]{:S(2)}) collective-permute-start(bf16[384,1664]{1,0:T(8,128)(2,1)} %get-tuple-element.168.refs_0_), channel_id=1, source_target_pairs={{0,1},{1,0},{2,3},{3,2},{4,5},{5,4},{6,7},{7,6},{8,9},{9,8},{10,11... | collective-permute-start | bytes 3833864 | tf_op jit(solution)/shard_map/ppermute | solution.py:124
  226.4 54.0 %collective-permute-start.26 = (bf16[2,4608,128]{2,1,0:T(8,128)(2,1)}, bf16[2,4608,128]{2,1,0:T(8,128)(2,1)}, u32[]{:S(2)}, u32[]{:S(2)}) collective-permute-start(bf16[2,4608,128]{2,1,0:T(8,128)(2,1)} %get-tuple-element.178.refs_11_), channel_id=1, source_target_pairs={{0,8},{8,0},{16,24},{24,16},{1,9},{9,1},{17,25},{25,17},{2,10},{10... | collective-permute-start | bytes 7077896 | tf_op jit(solution)/shard_map/ppermute | solution.py:42
  227.9 53.7 %collective-permute-start.27 = (bf16[2,4608,128]{2,1,0:T(8,128)(2,1)}, bf16[2,4608,128]{2,1,0:T(8,128)(2,1)}, u32[]{:S(2)}, u32[]{:S(2)}) collective-permute-start(bf16[2,4608,128]{2,1,0:T(8,128)(2,1)} %get-tuple-element.178.refs_11_), channel_id=1, source_target_pairs={{0,16},{8,24},{16,0},{24,8},{1,17},{9,25},{17,1},{25,9},{2,18},{10... | collective-permute-start | bytes 7077896 | tf_op jit(solution)/shard_map/ppermute | solution.py:42
  229.4 32.0 %collective-permute-start.25 = (bf16[384,1664]{1,0:T(8,128)(2,1)}, bf16[384,1664]{1,0:T(8,128)(2,1)}, u32[]{:S(2)}, u32[]{:S(2)}) collective-permute-start(bf16[384,1664]{1,0:T(8,128)(2,1)} %collective-permute-done.21.refs_2_), channel_id=1, source_target_pairs={{0,2},{1,3},{2,4},{3,5},{4,6},{5,7},{6,0},{7,1},{8,10},{9,11},{10,... | collective-permute-start | bytes 3833864 | tf_op jit(solution)/shard_map/ppermute | solution.py:117
  283.0 27.3 %collective-permute-start.28 = (bf16[1,4608,128]{2,1,0:T(8,128)(2,1)S(1)}, bf16[1,4608,128]{2,1,0:T(8,128)(2,1)S(1)}, u32[]{:S(2)}, u32[]{:S(2)}) collective-permute-start(bf16[1,4608,128]{2,1,0:T(8,128)(2,1)S(1)} %slice.356), channel_id=1, source_target_pairs={{0,8},{8,0},{16,24},{24,16},{1,9},{9,1},{17,25},{25,17},{2,10},{10... | collective-permute-start | bytes 3538952 | tf_op jit(solution)/shard_map/ppermute | solution.py:42
  284.9 27.2 %collective-permute-start.29 = (bf16[1,4608,128]{2,1,0:T(8,128)(2,1)S(1)}, bf16[1,4608,128]{2,1,0:T(8,128)(2,1)S(1)}, u32[]{:S(2)}, u32[]{:S(2)}) collective-permute-start(bf16[1,4608,128]{2,1,0:T(8,128)(2,1)S(1)} %slice.357), channel_id=1, source_target_pairs={{0,16},{8,24},{16,0},{24,8},{1,17},{9,25},{17,1},{25,9},{2,18},{10... | collective-permute-start | bytes 3538952 | tf_op jit(solution)/shard_map/ppermute | solution.py:42
  286.5 60.2 %collective-permute-start.30 = (bf16[384,1664]{1,0:T(8,128)(2,1)}, bf16[384,1664]{1,0:T(8,128)(2,1)}, u32[]{:S(2)}, u32[]{:S(2)}) collective-permute-start(bf16[384,1664]{1,0:T(8,128)(2,1)} %collective-permute-done.25.refs_0_), channel_id=1, source_target_pairs={{0,2},{1,3},{2,4},{3,5},{4,6},{5,7},{6,0},{7,1},{8,10},{9,11},{10,... | collective-permute-start | bytes 3833864 | tf_op jit(solution)/shard_map/ppermute | solution.py:117
  354.4 81.1 %collective-permute-start.42 = (bf16[384,3200]{1,0:T(8,128)(2,1)}, bf16[384,3200]{1,0:T(8,128)(2,1)}, u32[]{:S(2)}, u32[]{:S(2)}) collective-permute-start(bf16[384,3200]{1,0:T(8,128)(2,1)} %get-tuple-element.227), channel_id=1, source_target_pairs={{0,1},{1,0},{2,3},{3,2},{4,5},{5,4},{6,7},{7,6},{8,9},{9,8},{10,11... | collective-permute-start | bytes 7372808 | tf_op jit(solution)/shard_map/ppermute | solution.py:124
  358.6 76.9 %collective-permute-start.32 = (bf16[384,1664]{1,0:T(8,128)(2,1)}, bf16[384,1664]{1,0:T(8,128)(2,1)}, u32[]{:S(2)}, u32[]{:S(2)}) collective-permute-start(bf16[384,1664]{1,0:T(8,128)(2,1)} %add_convert_fusion.6), channel_id=1, source_target_pairs={{0,2},{1,3},{2,4},{3,5},{4,6},{5,7},{6,0},{7,1},{8,10},{9,11},{10,... | collective-permute-start | bytes 3833864 | tf_op jit(solution)/shard_map/ppermute | solution.py:117
  399.4 36.0 %collective-permute-start.37 = (bf16[1,4608,128]{2,1,0:T(8,128)(2,1)}, bf16[1,4608,128]{2,1,0:T(8,128)(2,1)}, u32[]{:S(2)}, u32[]{:S(2)}) collective-permute-start(bf16[1,4608,128]{2,1,0:T(8,128)(2,1)} %get-tuple-element.205), channel_id=1, source_target_pairs={{0,8},{8,0},{16,24},{24,16},{1,9},{9,1},{17,25},{25,17},{2,10},{10... | collective-permute-start | bytes 3538952 | tf_op jit(solution)/shard_map/ppermute | solution.py:42
  400.9 34.6 %collective-permute-start.38 = (bf16[1,4608,128]{2,1,0:T(8,128)(2,1)}, bf16[1,4608,128]{2,1,0:T(8,128)(2,1)}, u32[]{:S(2)}, u32[]{:S(2)}) collective-permute-start(bf16[1,4608,128]{2,1,0:T(8,128)(2,1)} %get-tuple-element.206), channel_id=1, source_target_pairs={{0,16},{8,24},{16,0},{24,8},{1,17},{9,25},{17,1},{25,9},{2,18},{10... | collective-permute-start | bytes 3538952 | tf_op jit(solution)/shard_map/ppermute | solution.py:42
  444.2 32.2 %collective-permute-start.40 = (bf16[384,1664]{1,0:T(8,128)(2,1)}, bf16[384,1664]{1,0:T(8,128)(2,1)}, u32[]{:S(2)}, u32[]{:S(2)}) collective-permute-start(bf16[384,1664]{1,0:T(8,128)(2,1)} %add_convert_fusion.4), channel_id=1, source_target_pairs={{0,2},{1,3},{2,4},{3,5},{4,6},{5,7},{6,0},{7,1},{8,10},{9,11},{10,... | collective-permute-start | bytes 3833864 | tf_op jit(solution)/shard_map/ppermute | solution.py:117
  447.5 54.4 %collective-permute-start.45 = (bf16[2,4608,128]{2,1,0:T(8,128)(2,1)}, bf16[2,4608,128]{2,1,0:T(8,128)(2,1)}, u32[]{:S(2)}, u32[]{:S(2)}) collective-permute-start(bf16[2,4608,128]{2,1,0:T(8,128)(2,1)} %pad_maximum_fusion.2), channel_id=1, source_target_pairs={{0,8},{8,0},{16,24},{24,16},{1,9},{9,1},{17,25},{25,17},{2,10},{10... | collective-permute-start | bytes 7077896 | tf_op jit(solution)/shard_map/ppermute | solution.py:42
  451.4 54.4 %collective-permute-start.46 = (bf16[2,4608,128]{2,1,0:T(8,128)(2,1)}, bf16[2,4608,128]{2,1,0:T(8,128)(2,1)}, u32[]{:S(2)}, u32[]{:S(2)}) collective-permute-start(bf16[2,4608,128]{2,1,0:T(8,128)(2,1)} %pad_maximum_fusion.3), channel_id=1, source_target_pairs={{0,16},{8,24},{16,0},{24,8},{1,17},{9,25},{17,1},{25,9},{2,18},{10... | collective-permute-start | bytes 7077896 | tf_op jit(solution)/shard_map/ppermute | solution.py:42
  478.6 31.3 %collective-permute-start.43 = (bf16[384,1664]{1,0:T(8,128)(2,1)S(1)}, bf16[384,1664]{1,0:T(8,128)(2,1)S(1)}, u32[]{:S(2)}, u32[]{:S(2)}) collective-permute-start(bf16[384,1664]{1,0:T(8,128)(2,1)S(1)} %add_convert_fusion.1), channel_id=1, source_target_pairs={{0,2},{1,3},{2,4},{3,5},{4,6},{5,7},{6,0},{7,1},{8,10},{9,11},{10,... | collective-permute-start | bytes 3833864 | tf_op jit(solution)/shard_map/ppermute | solution.py:117
  478.8 47.5 %collective-permute-start.47 = (bf16[1,4608,128]{2,1,0:T(8,128)(2,1)S(1)}, bf16[1,4608,128]{2,1,0:T(8,128)(2,1)S(1)}, u32[]{:S(2)}, u32[]{:S(2)}) collective-permute-start(bf16[1,4608,128]{2,1,0:T(8,128)(2,1)S(1)} %copy-done.103), channel_id=1, source_target_pairs={{0,8},{8,0},{16,24},{24,16},{1,9},{9,1},{17,25},{25,17},{2,10},{10... | collective-permute-start | bytes 3538952 | tf_op jit(solution)/shard_map/ppermute | solution.py:42
  479.5 50.4 %collective-permute-start.48 = (bf16[1,4608,128]{2,1,0:T(8,128)(2,1)S(1)}, bf16[1,4608,128]{2,1,0:T(8,128)(2,1)S(1)}, u32[]{:S(2)}, u32[]{:S(2)}) collective-permute-start(bf16[1,4608,128]{2,1,0:T(8,128)(2,1)S(1)} %copy-done.102), channel_id=1, source_target_pairs={{0,16},{8,24},{16,0},{24,8},{1,17},{9,25},{17,1},{25,9},{2,18},{10... | collective-permute-start | bytes 3538952 | tf_op jit(solution)/shard_map/ppermute | solution.py:42
  531.3 19.2 %all-to-all-start.2 = ((bf16[4,384,384]{2,1,0:T(8,128)(2,1)}), bf16[4,384,384]{2,1,0:T(8,128)(2,1)}, u32[]{:S(2)}, u32[]{:S(2)}) async-start(bf16[4,384,384]{2,1,0:T(8,128)(2,1)} %copy-done.11), calls=%async_computation.2 | async-start | bytes 2359296 | tf_op jit(solution)/shard_map/all_to_all | solution.py:1134
  540.7 54.3 %collective-permute-start.44 = (bf16[384,1536]{1,0:T(8,128)(2,1)}, bf16[384,1536]{1,0:T(8,128)(2,1)}, u32[]{:S(2)}, u32[]{:S(2)}) collective-permute-start(bf16[384,1536]{1,0:T(8,128)(2,1)} %add_convert_fusion.14), channel_id=1, source_target_pairs={{0,2},{1,3},{2,4},{3,5},{4,6},{5,7},{6,0},{7,1},{8,10},{9,11},{10,... | collective-permute-start | bytes 3538952 | tf_op jit(solution)/shard_map/ppermute | solution.py:117
  550.5 37.2 %all-to-all-start.3 = ((bf16[4,4,48,1664]{3,2,1,0:T(8,128)(2,1)}), bf16[4,4,48,1664]{3,2,1,0:T(8,128)(2,1)}, u32[]{:S(2)}, u32[]{:S(2)}) async-start(bf16[4,4,48,1664]{3,2,1,0:T(8,128)(2,1)} %add_convert_fusion), calls=%async_computation.3 | async-start | bytes 5111808 | tf_op jit(solution)/shard_map/all_to_all | solution.py:1137
  597.7 43.9 %collective-permute-start.50 = (bf16[384,1536]{1,0:T(8,128)(2,1)}, bf16[384,1536]{1,0:T(8,128)(2,1)}, u32[]{:S(2)}, u32[]{:S(2)}) collective-permute-start(bf16[384,1536]{1,0:T(8,128)(2,1)} %add_convert_fusion.10), channel_id=1, source_target_pairs={{0,2},{1,3},{2,4},{3,5},{4,6},{5,7},{6,0},{7,1},{8,10},{9,11},{10,... | collective-permute-start | bytes 3538952 | tf_op jit(solution)/shard_map/ppermute | solution.py:117
  618.9 84.7 %collective-permute-start.54 = (bf16[384,1536]{1,0:T(8,128)(2,1)}, bf16[384,1536]{1,0:T(8,128)(2,1)}, u32[]{:S(2)}, u32[]{:S(2)}) collective-permute-start(bf16[384,1536]{1,0:T(8,128)(2,1)} %pad_maximum_fusion.7), channel_id=1, source_target_pairs={{0,8},{8,0},{16,24},{24,16},{1,9},{9,1},{17,25},{25,17},{2,10},{10... | collective-permute-start | bytes 3538952 | tf_op jit(solution)/shard_map/ppermute | solution.py:42
  620.7 82.9 %collective-permute-start.55 = (bf16[384,1536]{1,0:T(8,128)(2,1)}, bf16[384,1536]{1,0:T(8,128)(2,1)}, u32[]{:S(2)}, u32[]{:S(2)}) collective-permute-start(bf16[384,1536]{1,0:T(8,128)(2,1)} %pad_maximum_fusion.8), channel_id=1, source_target_pairs={{0,16},{8,24},{16,0},{24,8},{1,17},{9,25},{17,1},{25,9},{2,18},{10... | collective-permute-start | bytes 3538952 | tf_op jit(solution)/shard_map/ppermute | solution.py:42
  628.3 56.5 %all-to-all-start.5 = ((bf16[4,192,640]{2,1,0:T(8,128)(2,1)}), bf16[4,192,640]{2,1,0:T(8,128)(2,1)}, u32[]{:S(2)}, u32[]{:S(2)}) async-start(bf16[4,192,640]{2,1,0:T(8,128)(2,1)} %fusion.9), calls=%async_computation.5 | async-start | bytes 1966080 | tf_op jit(solution)/shard_map/all_to_all | solution.py:148
  638.4 55.6 %collective-permute-start.56 = (bf16[2,4608,128]{2,1,0:T(8,128)(2,1)}, bf16[2,4608,128]{2,1,0:T(8,128)(2,1)}, u32[]{:S(2)}, u32[]{:S(2)}) collective-permute-start(bf16[2,4608,128]{2,1,0:T(8,128)(2,1)} %pad_maximum_fusion.4), channel_id=1, source_target_pairs={{0,8},{8,0},{16,24},{24,16},{1,9},{9,1},{17,25},{25,17},{2,10},{10... | collective-permute-start | bytes 7077896 | tf_op jit(solution)/shard_map/ppermute | solution.py:42
  641.4 54.2 %collective-permute-start.57 = (bf16[2,4608,128]{2,1,0:T(8,128)(2,1)}, bf16[2,4608,128]{2,1,0:T(8,128)(2,1)}, u32[]{:S(2)}, u32[]{:S(2)}) collective-permute-start(bf16[2,4608,128]{2,1,0:T(8,128)(2,1)} %pad_maximum_fusion.5), channel_id=1, source_target_pairs={{0,16},{8,24},{16,0},{24,8},{1,17},{9,25},{17,1},{25,9},{2,18},{10... | collective-permute-start | bytes 7077896 | tf_op jit(solution)/shard_map/ppermute | solution.py:42
  644.3 43.6 %collective-permute-start.53 = (bf16[384,1536]{1,0:T(8,128)(2,1)}, bf16[384,1536]{1,0:T(8,128)(2,1)}, u32[]{:S(2)}, u32[]{:S(2)}) collective-permute-start(bf16[384,1536]{1,0:T(8,128)(2,1)} %add_convert_fusion.9), channel_id=1, source_target_pairs={{0,2},{1,3},{2,4},{3,5},{4,6},{5,7},{6,0},{7,1},{8,10},{9,11},{10,... | collective-permute-start | bytes 3538952 | tf_op jit(solution)/shard_map/ppermute | solution.py:117
  718.8 21.4 %all-to-all-start.6 = ((bf16[4,48,1664]{2,1,0:T(8,128)(2,1)}), bf16[4,48,1664]{2,1,0:T(8,128)(2,1)}, u32[]{:S(2)}, u32[]{:S(2)}) async-start(bf16[4,48,1664]{2,1,0:T(8,128)(2,1)} %reduce_sum.82), calls=%async_computation.6 | async-start | bytes 1277952 | tf_op jit(solution)/shard_map/all_to_all | solution.py:148
  (126 other events, 1280.5 us)

commit v3 on v2

--- a/solution.py
+++ b/solution.py
@@ -56,11 +56,18 @@
     return rows_swap(array, 1), rows_swap(array, 2)
 
 
+def far_halves(from_x, from_y):
+    _, first_y, _ = halves(from_y)
+    _, _, second_x = halves(from_x)
+    return rows_swap(first_y, 1), rows_swap(second_x, 2)
+
+
+def join_far(array, from_x, from_y, far):
+    return [array, from_x, from_y, jnp.concatenate(far, axis=halves(array)[0])]
+
+
 def gather_far(array, from_x, from_y):
-    axis, first_y, _ = halves(from_y)
-    _, _, second_x = halves(from_x)
-    far = jnp.concatenate([rows_swap(first_y, 1), rows_swap(second_x, 2)], axis=axis)
-    return [array, from_x, from_y, far]
+    return join_far(array, from_x, from_y, far_halves(from_x, from_y))
 
 
 def rows_exchange(pieces):
@@ -958,7 +965,7 @@
     gain_moe = small_full[:, experts + 1].astype(f32)[None, :]
     router_full = jnp.where(jnp.arange(LANES) < experts, small_full, 0)
     token_parts = gather_far(own_tokens, *token_near)
-    found = after(found, token_near)
+    found = after(found, token_parts[3])
     project_found = jnp.stack([rows[:, :qkv_cols] for rows in found])
     project_swapped = core_swap(project_found)
 
@@ -999,15 +1006,15 @@
     )
     attended, lse = attend(meta, queries, key_rows, value_rows, starts[:, None], tok)
     cot_same[1], out_near = after((cot_same[1], out_near), attended)
-    cot_other = [core_swap(rows) for rows in cot_same]
     for d in range(2, chips):
         cot_same.append(chip_shift(cot_same[-1], 1))
-    attended, out_near = after((attended, out_near), weight_near[0], cot_same[2], cot_other)
+    attended = after(attended, weight_near[0])
     own_heads = lax.all_to_all(attended, "rows", 0, 0, tiled=True)
     out_mine = jnp.stack(gather_far(out_half, *out_near)).reshape(4, chips, sixth, width)
+    out_mine = after(out_mine, cot_same[2])
     out_parts = cores_in_order(out_mine, core_swap(out_mine), core, 2).reshape(4, tok, width)
     weight_near[0] = after(weight_near[0], own_heads)
-    weight_parts = [gather_far(packed[0], *weight_near[0])]
+    first_far = far_halves(*weight_near[0])
     mixed_rows, moe_rows, gates = mix(
         meta,
         own_heads,
@@ -1018,12 +1025,13 @@
         router_full,
         experts,
     )
+    weight_parts = [join_far(packed[0], *weight_near[0], after(first_far, moe_rows))]
     for group in range(1, groups):
-        weight_near.append(gather_near(after(packed[group], weight_parts[0][3], moe_rows)))
-    moe_same = [moe_rows, chip_shift(after(moe_rows, cot_same[3]), 1)]
+        weight_near.append(gather_near(after(packed[group], weight_parts[0][3])))
+    moe_same = [moe_rows, chip_shift(after(moe_rows, cot_same[3], weight_parts[0][3]), 1)]
     moe_other = [core_swap(rows) for rows in moe_same]
     moe_same.append(chip_shift(moe_same[1], 1))
-    cot_other += [core_swap(rows) for rows in cot_same[2:]]
+    cot_other = [core_swap(after(rows, moe_rows)) for rows in cot_same]
 
     moe_meta = jnp.stack([row, column * own_experts]).astype(jnp.int32)
     ffe = w_down.shape[1]
@@ -1188,6 +1196,7 @@
     own_w = jnp.concatenate([w_query, key_matrix, value_matrix], axis=1).astype(f32)
     own_gain = lax.dynamic_slice_in_dim(gain_attn[0], column * own_w.shape[0], own_w.shape[0], 0)
     gain_rows = (jnp.sum(project_sum * own_w, axis=1) / own_gain).reshape(4, -1)
+    gain_rows = after(gain_rows, wide_sum)
     gain_sum = jnp.sum(lax.all_to_all(gain_rows, "rows", 0, 0, tiled=True), axis=0)
     grad_gain_attn = lax.ppermute(
         gain_sum,

time: 755 us -> 790 us (1.046)
  waiting for transfers between devices: 231 us -> 263 us
    ppermute x28, waiting for transfers between devices: 92.2 us -> 161 us  [rows_swap(): return lax.ppermute(array, 'rows', [(i, i ^ distance) for i in range(4)])]
    ppermute x15, waiting for transfers between devices: 77.3 us -> 44.1 us  [chip_shift(): lax.ppermute(array, 'cols', [(i, (i + 2 * distance) % count) for i in ran...]
    unnamed x238 -> x230, local copies, waits for them, and re-layouts: 44.9 us -> 52.3 us
  transfers between devices with their start and end apart: 66 -> 66, of which waited for: 31 -> 29; matrix products, arithmetic and copies ran while one was open for 23% -> 22% of each run, Pallas kernels for 28% -> 27%
where the time goes in v3:
time: 790 us; the launch traced here: 778 us
  waiting for transfers between devices  263 us (33%)
  Pallas kernels  208 us (26%)
  other arithmetic  105 us (13%)
  local copies, waits for them, and re-layouts  90.5 us (11%)
  starting transfers between devices  90.2 us (11%)
  matrix products  11.4 us (1%)
    ppermute x28, waiting for transfers between devices, rows_swap(): return lax.ppermute(array, 'rows', [(i, i ^ distance) for i in range(4)])  161 us
    pallas_call x4, Pallas kernels, run_experts(): pl.pallas_call(partial(experts_kernel, experts=experts, slots=slots, loca...  114 us
    unnamed x230, local copies, waits for them, and re-layouts  52.3 us
    ppermute x15, waiting for transfers between devices, chip_shift(): lax.ppermute(array, 'cols', [(i, (i + 2 * distance) % count) for i in ran...  44.1 us
    convert_element_type x19, other arithmetic, add_low(): return (left.astype(f32) + right.astype(f32)).astype(bf16)  42.1 us
    pallas_call x2, Pallas kernels, weight_grads(): pl.pallas_call(partial(weight_grad_kernel, chunks=chunks, own_count=own),...  32.3 us
    all_to_all x2, waiting for transfers between devices, chips_exchange(): lax.all_to_all(array, 'cols', 0, 0, axis_index_groups=alike, tiled=True)  29.7 us
    ppermute x28, starting transfers between devices, rows_swap(): return lax.ppermute(array, 'rows', [(i, i ^ distance) for i in range(4)])  25.5 us
  transfers between devices with their start and end apart: 66, of which 29 were waited for; matrix products, arithmetic and copies ran while one was open for 22% of the time, Pallas kernels for 27%

profile of v3, /device:TPU:6, one launch (start us, length us, event | category | flops | bytes accessed | tf_op | source)
XLA Modules:
  0.0 777.5 jit_solution(16128933698867692160)
XLA Ops:
  16.7 5.3 all-to-all-start
  39.0 4.4 fusion.19
  51.3 9.8 %collective-permute-done.2 = bf16[192,1536]{1,0:T(8,128)(2,1)} collective-permute-done((bf16[192,1536]{1,0:T(8,128)(2,1)}, bf16[192,1536]{1,0:T(8,128)(2,1)}, u32[]{:S(2)}, u32[]{:S(2)}) %collective-permute-start.2) | collective-permute-done | bytes 589856 | tf_op jit(solution)/shard_map/ppermute | solution.py:42
  88.8 9.0 %project.1 = (bf16[1536,384]{1,0:T(8,128)(2,1)S(1)}, bf16[1536,128]{1,0:T(8,128)(2,1)S(1)}, bf16[1536,128]{1,0:T(8,128)(2,1)S(1)}, bf16[4,384,1536]{2,1,0:T(8,128)(2,1)S(1)}, bf16[1536,640]{1,0:T(8,128)(2,1)S(1)}) custom-call(s32[7]{0:T(128)S(1)} %pad_add_fusion.meta, bf16[384,1536]{1,0:T(8,128)(2,1)S(1)} %bitcast.69, bf16[384,1536]{1,0:T(8,128)(2,1)S(1)} %copy-done.22, ...), custom_call_target="tpu_custom_call" | custom-call | flops 11500000256 | tf_op jit(solution)/shard_map/project/pallas_call | solution.py:229
  100.1 13.7 %attend.1 = (bf16[4,384,384]{2,1,0:T(8,128)(2,1)}, f32[1536,8]{1,0:T(8,128)S(1)}) custom-call(s32[7]{0:T(128)S(1)} %pad_add_fusion.meta, bf16[1536,384]{1,0:T(8,128)(2,1)S(1)} %get-tuple-element.158.queries, bf16[1536,128]{1,0:T(8,128)(2,1)S(1)} %get-tuple-element.159.keys, bf16[1536,128]{1,0:T(8,128)(2,1)S(1)} %get-tuple-element.160.values, ...), custom_call_target="tpu_custom_call" | custom-call | flops 18400000000 | tf_op jit(solution)/shard_map/attend/pallas_call | solution.py:296
  121.5 56.7 %collective-permute-done.14 = bf16[96,1536]{1,0:T(8,128)(2,1)S(1)} collective-permute-done((bf16[96,1536]{1,0:T(8,128)(2,1)S(1)}, bf16[96,1536]{1,0:T(8,128)(2,1)S(1)}, u32[]{:S(2)}, u32[]{:S(2)}) %collective-permute-start.14) | collective-permute-done | bytes 294944 | tf_op jit(solution)/shard_map/ppermute | solution.py:42
  181.0 5.7 all-to-all-start.1
  191.1 9.8 %all-to-all-done.1.heads = bf16[4,384,384]{2,1,0:T(8,128)(2,1)S(1)} async-done(((bf16[4,384,384]{2,1,0:T(8,128)(2,1)}), bf16[4,384,384]{2,1,0:T(8,128)(2,1)S(1)}, u32[]{:S(2)}, u32[]{:S(2)}) %all-to-all-start.1) | async-done | bytes 1179680 | tf_op jit(solution)/shard_map/all_to_all | solution.py:1012
  210.2 5.4 mix.1
  215.6 14.4 %collective-permute-done.19 = bf16[1,4608,128]{2,1,0:T(8,128)(2,1)S(1)} collective-permute-done((bf16[1,4608,128]{2,1,0:T(8,128)(2,1)S(1)}, bf16[1,4608,128]{2,1,0:T(8,128)(2,1)S(1)}, u32[]{:S(2)}, u32[]{:S(2)}) %collective-permute-start.19) | collective-permute-done | bytes 1179680 | tf_op jit(solution)/shard_map/ppermute | solution.py:42
  236.1 28.7 %collective-permute-done.21.refs_2_ = bf16[384,1664]{1,0:T(8,128)(2,1)} collective-permute-done((bf16[384,1664]{1,0:T(8,128)(2,1)}, bf16[384,1664]{1,0:T(8,128)(2,1)}, u32[]{:S(2)}, u32[]{:S(2)}) %collective-permute-start.21) | collective-permute-done | bytes 1277984 | tf_op jit(solution)/shard_map/ppermute | solution.py:124
  268.2 24.0 %experts.4 = (bf16[2,512,1536]{2,1,0:T(8,128)(2,1)}, bf16[2,512,1536]{2,1,0:T(8,128)(2,1)}, bf16[2,512,512]{2,1,0:T(8,128)(2,1)}, bf16[2,512,1024]{2,1,0:T(8,128...) custom-call(s32[2]{0:T(128)} %pad_add_fusion.1.meta, ...), custom_call_target="tpu_custom_call" | custom-call | flops 29899999232 | tf_op jit(solution)/shard_map/experts/pallas_call | solution.py:777
  292.2 7.0 collective-permute-done.25.refs_0_
  299.2 20.2 %collective-permute-done.26.refs_12_ = bf16[2,4608,128]{2,1,0:T(8,128)(2,1)} collective-permute-done((bf16[2,4608,128]{2,1,0:T(8,128)(2,1)}, bf16[2,4608,128]{2,1,0:T(8,128)(2,1)}, u32[]{:S(2)}, u32[]{:S(2)}) %collective-permute-start.26) | collective-permute-done | bytes 2359328 | tf_op jit(solution)/shard_map/ppermute | solution.py:42
  324.5 23.9 %collective-permute-done.28 = bf16[1,4608,128]{2,1,0:T(8,128)(2,1)S(1)} collective-permute-done((bf16[1,4608,128]{2,1,0:T(8,128)(2,1)S(1)}, bf16[1,4608,128]{2,1,0:T(8,128)(2,1)S(1)}, u32[]{:S(2)}, u32[]{:S(2)}) %collective-permute-start.28) | collective-permute-done | bytes 1179680 | tf_op jit(solution)/shard_map/ppermute | solution.py:42
  352.5 33.0 %experts.5 = (bf16[384,3200]{1,0:T(8,128)(2,1)}, bf16[384,3200]{1,0:T(8,128)(2,1)}, bf16[384,3200]{1,0:T(8,128)(2,1)}, bf16[384,3200]{1,0:T(8,128)(2,1)}, bf16[2...) custom-call(s32[2]{0:T(128)} %pad_add_fusion.1.meta, ...), custom_call_target="tpu_custom_call" | custom-call | flops 29899999232 | tf_op jit(solution)/shard_map/experts/pallas_call | solution.py:777
  386.7 6.5 collective-permute-done.31
  398.0 24.0 %experts.6 = (bf16[2,512,1536]{2,1,0:T(8,128)(2,1)}, bf16[2,512,1536]{2,1,0:T(8,128)(2,1)}, bf16[2,512,512]{2,1,0:T(8,128)(2,1)}, bf16[2,512,1024]{2,1,0:T(8,128...) custom-call(s32[2]{0:T(128)} %pad_add_fusion.1.meta, ...), custom_call_target="tpu_custom_call" | custom-call | flops 29899999232 | tf_op jit(solution)/shard_map/experts/pallas_call | solution.py:777
  422.0 16.2 %weight_grads.2 = (bf16[1,4608,128]{2,1,0:T(8,128)(2,1)}, bf16[1,4608,128]{2,1,0:T(8,128)(2,1)}, bf16[1,4608,128]{2,1,0:T(8,128)(2,1)}, bf16[1,4608,128]{2,1,0:T...) custom-call(bf16[2,512,1536]{2,1,0:T(8,128)(2,1)} %get-tuple-element, ...), custom_call_target="tpu_custom_call" | custom-call | flops 14949999616 | tf_op jit(solution)/shard_map/weight_grads/pallas_call | solution.py:856
  440.0 33.1 %experts.7 = (bf16[384,3200]{1,0:T(8,128)(2,1)}, bf16[384,3200]{1,0:T(8,128)(2,1)}, bf16[384,3200]{1,0:T(8,128)(2,1)}, bf16[384,3200]{1,0:T(8,128)(2,1)}, bf16[2...) custom-call(s32[2]{0:T(128)} %pad_add_fusion.1.meta, ...), custom_call_target="tpu_custom_call" | custom-call | flops 29899999232 | tf_op jit(solution)/shard_map/experts/pallas_call | solution.py:777
  473.2 3.2 add_convert_fusion.2.last
  478.1 3.8 add_convert_fusion.4
  493.5 16.1 %weight_grads.3 = (bf16[1,4608,128]{2,1,0:T(8,128)(2,1)}, bf16[1,4608,128]{2,1,0:T(8,128)(2,1)}, bf16[1,4608,128]{2,1,0:T(8,128)(2,1)}, bf16[1,4608,128]{2,1,0:T...) custom-call(bf16[2,512,1536]{2,1,0:T(8,128)(2,1)} %get-tuple-element, ...), custom_call_target="tpu_custom_call" | custom-call | flops 14949999616 | tf_op jit(solution)/shard_map/weight_grads/pallas_call | solution.py:856
  509.6 4.5 collective-permute-done.40
  530.9 8.7 %collective-permute-done.45 = bf16[2,4608,128]{2,1,0:T(8,128)(2,1)} collective-permute-done((bf16[2,4608,128]{2,1,0:T(8,128)(2,1)}, bf16[2,4608,128]{2,1,0:T(8,128)(2,1)}, u32[]{:S(2)}, u32[]{:S(2)}) %collective-permute-start.45) | collective-permute-done | bytes 2359328 | tf_op jit(solution)/shard_map/ppermute | solution.py:42
  539.6 4.1 collective-permute-done.46
  543.7 3.8 collective-permute-done.43.came
  547.6 10.2 %unmix.1 = (f32[384,1536]{1,0:T(8,128)S(1)}, bf16[4,384,384]{2,1,0:T(8,128)(2,1)S(1)}, bf16[4,4,48,1664]{3,2,1,0:T(8,128)(2,1)S(1)}, bf16[4,4,48,1664]{3,2,1,0:T(8,128)(2,1)}) custom-call(s32[7]{0:T(128)S(1)} %pad_add_fusion.meta, bf16[384,1664]{1,0:T(8,128)(2,1)S(1)} %collective-permute-done.43.came, bf16[384,1664]{1,0:T(8,128)(2,1)S(1)} %copy-done.5, ...), custom_call_target="tpu_custom_call" | custom-call | flops 13799999488 | tf_op jit(solution)/shard_map/unmix/pallas_call | solution.py:520
  564.0 3.8 collective-permute-done.48
  569.1 5.8 all-to-all-start.2
  580.7 4.6 add_convert_fusion
  585.3 3.2 all-to-all-done.2.grads
  588.5 6.0 all-to-all-start.3
  600.8 23.6 %attend_back.1 = bf16[4,384,640]{2,1,0:T(8,128)(2,1)S(1)} custom-call(s32[7]{0:T(128)S(1)} %pad_add_fusion.meta, bf16[1536,384]{1,0:T(8,128)(2,1)S(1)} %copy-done.34, bf16[4,384,384]{2,1,0:T(8,128)(2,1)} %all-to-all-done.2.grads, f32[8,1536]{1,0:T(8,128)S(1)} %bitcast.77, s32[1,1536]{1,0:T(1,128)S(1)} %broadcast_in_dim.39.starts, ...), custom_call_target="tpu_custom_call" | custom-call | flops 33350000640 | tf_op jit(solution)/shard_map/attend_back/pallas_call | solution.py:400
  638.7 4.0 bitcast_convert_fusion
  642.7 9.7 %collective-permute-done.51 = bf16[192,1536]{1,0:T(8,128)(2,1)S(1)} collective-permute-done((bf16[192,1536]{1,0:T(8,128)(2,1)S(1)}, bf16[192,1536]{1,0:T(8,128)(2,1)S(1)}, u32[]{:S(2)}, u32[]{:S(2)}) %collective-permute-start.51) | collective-permute-done | bytes 589856 | tf_op jit(solution)/shard_map/ppermute | solution.py:42
  656.3 6.2 all_to_all.48
  663.7 7.2 all-to-all-start.5
  682.3 3.1 collective-permute-start.53
  685.5 3.1 convert_add_fusion.1
  691.5 29.7 %all-to-all-done.5 = bf16[4,192,640]{2,1,0:T(8,128)(2,1)} async-done(((bf16[4,192,640]{2,1,0:T(8,128)(2,1)}), bf16[4,192,640]{2,1,0:T(8,128)(2,1)}, u32[]{:S(2)}, u32[]{:S(2)}) %all-to-all-start.5) | async-done | bytes 983072 | tf_op jit(solution)/shard_map/all_to_all | solution.py:155
  724.3 4.2 all-to-all-start.6
  728.6 3.8 add_bitcast_fusion
  734.5 3.1 convert_add_fusion
  746.8 3.4 maximum_maximum_fusion
  755.6 4.0 fusion.6
  760.8 4.7 all-to-all-start.7
  772.3 4.5 collective-permute-done.58
  (453 shorter events, 232.3 us)
Async XLA Ops:
  0.7 44.2 %collective-permute-start = (bf16[384,1536]{1,0:T(8,128)(2,1)}, bf16[384,1536]{1,0:T(8,128)(2,1)S(1)}, u32[]{:S(2)}, u32[]{:S(2)}) collective-permute-start(bf16[384,1536]{1,0:T(8,128)(2,1)} %bitcast.67), channel_id=1, source_target_pairs={{0,8},{8,0},{16,24},{24,16},{1,9},{9,1},{17,25},{25,17},{2,10},{10... | collective-permute-start | bytes 3538952 | tf_op jit(solution)/shard_map/ppermute | solution.py:42
  1.3 42.2 %collective-permute-start.1 = (bf16[384,1536]{1,0:T(8,128)(2,1)}, bf16[384,1536]{1,0:T(8,128)(2,1)S(1)}, u32[]{:S(2)}, u32[]{:S(2)}) collective-permute-start(bf16[384,1536]{1,0:T(8,128)(2,1)} %bitcast.68), channel_id=1, source_target_pairs={{0,16},{8,24},{16,0},{24,8},{1,17},{9,25},{17,1},{25,9},{2,18},{10... | collective-permute-start | bytes 3538952 | tf_op jit(solution)/shard_map/ppermute | solution.py:42
  7.5 56.1 %collective-permute-start.4 = (bf16[192,1024]{1,0:T(8,128)(2,1)}, bf16[192,1024]{1,0:T(8,128)(2,1)}, u32[]{:S(2)}, u32[]{:S(2)}) collective-permute-start(bf16[192,1024]{1,0:T(8,128)(2,1)} %constant_dynamic-update-slice_fusion.2), channel_id=1, source_target_pairs={{0,2},{1,3},{2,4},{3,5},{4,6},{5,7},{6,0},{7,1},{8,10},{9,11},{10,... | collective-permute-start | bytes 1179656 | tf_op jit(solution)/shard_map/ppermute | solution.py:124
  9.5 54.1 %collective-permute-start.5 = (bf16[192,1024]{1,0:T(8,128)(2,1)}, bf16[192,1024]{1,0:T(8,128)(2,1)}, u32[]{:S(2)}, u32[]{:S(2)}) collective-permute-start(bf16[192,1024]{1,0:T(8,128)(2,1)} %constant_dynamic-update-slice_fusion.2), channel_id=1, source_target_pairs={{0,4},{1,5},{2,6},{3,7},{4,0},{5,1},{6,2},{7,3},{8,12},{9,13},{10,... | collective-permute-start | bytes 1179656 | tf_op jit(solution)/shard_map/ppermute | solution.py:124
  12.1 51.5 %collective-permute-start.6 = (bf16[192,1024]{1,0:T(8,128)(2,1)}, bf16[192,1024]{1,0:T(8,128)(2,1)}, u32[]{:S(2)}, u32[]{:S(2)}) collective-permute-start(bf16[192,1024]{1,0:T(8,128)(2,1)} %constant_dynamic-update-slice_fusion.2), channel_id=1, source_target_pairs={{0,6},{1,7},{2,0},{3,1},{4,2},{5,3},{6,4},{7,5},{8,14},{9,15},{10,... | collective-permute-start | bytes 1179656 | tf_op jit(solution)/shard_map/ppermute | solution.py:124
  16.7 52.3 %all-to-all-start = ((bf16[32,48,128]{2,1,0:T(8,128)(2,1)}), bf16[32,48,128]{2,1,0:T(8,128)(2,1)}, u32[]{:S(2)}, u32[]{:S(2)}) async-start(bf16[32,48,128]{2,1,0:T(8,128)(2,1)} %tile.2), calls=%async_computation | async-start | bytes 786432 | tf_op jit(solution)/shard_map/all_to_all | solution.py:961
  79.3 34.5 %collective-permute-start.11 = (bf16[192,1536]{1,0:T(8,128)(2,1)S(1)}, bf16[192,1536]{1,0:T(8,128)(2,1)S(1)}, u32[]{:S(2)}, u32[]{:S(2)}) collective-permute-start(bf16[192,1536]{1,0:T(8,128)(2,1)S(1)} %bitcast.85), channel_id=1, source_target_pairs={{0,8},{8,0},{16,24},{24,16},{1,9},{9,1},{17,25},{25,17},{2,10},{10... | collective-permute-start | bytes 1769480 | tf_op jit(solution)/shard_map/ppermute | solution.py:42
  80.7 33.1 %collective-permute-start.12 = (bf16[192,1536]{1,0:T(8,128)(2,1)S(1)}, bf16[192,1536]{1,0:T(8,128)(2,1)S(1)}, u32[]{:S(2)}, u32[]{:S(2)}) collective-permute-start(bf16[192,1536]{1,0:T(8,128)(2,1)S(1)} %bitcast.86), channel_id=1, source_target_pairs={{0,16},{8,24},{16,0},{24,8},{1,17},{9,25},{17,1},{25,9},{2,18},{10... | collective-permute-start | bytes 1769480 | tf_op jit(solution)/shard_map/ppermute | solution.py:42
  81.2 32.6 %collective-permute-start.10 = (bf16[384,1664]{1,0:T(8,128)(2,1)}, bf16[384,1664]{1,0:T(8,128)(2,1)}, u32[]{:S(2)}, u32[]{:S(2)}) collective-permute-start(bf16[384,1664]{1,0:T(8,128)(2,1)} %pad_maximum_fusion.6.refs_4_), channel_id=1, source_target_pairs={{0,2},{1,3},{2,4},{3,5},{4,6},{5,7},{6,0},{7,1},{8,10},{9,11},{10,... | collective-permute-start | bytes 3833864 | tf_op jit(solution)/shard_map/ppermute | solution.py:124
  113.8 66.1 %collective-permute-start.15 = (bf16[384,1664]{1,0:T(8,128)(2,1)}, bf16[384,1664]{1,0:T(8,128)(2,1)S(1)}, u32[]{:S(2)}, u32[]{:S(2)}) collective-permute-start(bf16[384,1664]{1,0:T(8,128)(2,1)} %collective-permute-done.10.refs_6_), channel_id=1, source_target_pairs={{0,2},{1,3},{2,4},{3,5},{4,6},{5,7},{6,0},{7,1},{8,10},{9,11},{10,... | collective-permute-start | bytes 3833864 | tf_op jit(solution)/shard_map/ppermute | solution.py:124
  117.0 63.0 %collective-permute-start.8 = (bf16[2,4608,128]{2,1,0:T(8,128)(2,1)S(1)}, bf16[2,4608,128]{2,1,0:T(8,128)(2,1)}, u32[]{:S(2)}, u32[]{:S(2)}) collective-permute-start(bf16[2,4608,128]{2,1,0:T(8,128)(2,1)S(1)} %get-tuple-element.163.refs_8_), channel_id=1, source_target_pairs={{0,8},{8,0},{16,24},{24,16},{1,9},{9,1},{17,25},{25,17},{2,10},{10... | collective-permute-start | bytes 7077896 | tf_op jit(solution)/shard_map/ppermute | solution.py:42
  117.8 63.2 %collective-permute-start.9 = (bf16[2,4608,128]{2,1,0:T(8,128)(2,1)S(1)}, bf16[2,4608,128]{2,1,0:T(8,128)(2,1)}, u32[]{:S(2)}, u32[]{:S(2)}) collective-permute-start(bf16[2,4608,128]{2,1,0:T(8,128)(2,1)S(1)} %get-tuple-element.163.refs_8_), channel_id=1, source_target_pairs={{0,16},{8,24},{16,0},{24,8},{1,17},{9,25},{17,1},{25,9},{2,18},{10... | collective-permute-start | bytes 7077896 | tf_op jit(solution)/shard_map/ppermute | solution.py:42
  119.3 58.8 %collective-permute-start.14 = (bf16[96,1536]{1,0:T(8,128)(2,1)S(1)}, bf16[96,1536]{1,0:T(8,128)(2,1)S(1)}, u32[]{:S(2)}, u32[]{:S(2)}) collective-permute-start(bf16[96,1536]{1,0:T(8,128)(2,1)S(1)} %slice.340), channel_id=1, source_target_pairs={{0,16},{8,24},{16,0},{24,8},{1,17},{9,25},{17,1},{25,9},{2,18},{10... | collective-permute-start | bytes 884744 | tf_op jit(solution)/shard_map/ppermute | solution.py:42
  120.0 58.2 %collective-permute-start.13 = (bf16[96,1536]{1,0:T(8,128)(2,1)S(1)}, bf16[96,1536]{1,0:T(8,128)(2,1)S(1)}, u32[]{:S(2)}, u32[]{:S(2)}) collective-permute-start(bf16[96,1536]{1,0:T(8,128)(2,1)S(1)} %slice.339), channel_id=1, source_target_pairs={{0,8},{8,0},{16,24},{24,16},{1,9},{9,1},{17,25},{25,17},{2,10},{10... | collective-permute-start | bytes 884744 | tf_op jit(solution)/shard_map/ppermute | solution.py:42
  179.9 26.2 %collective-permute-start.16 = (bf16[4,4,48,1536]{3,2,1,0:T(8,128)(2,1)}, bf16[4,4,48,1536]{3,2,1,0:T(8,128)(2,1)}, u32[]{:S(2)}, u32[]{:S(2)}) collective-permute-start(bf16[4,4,48,1536]{3,2,1,0:T(8,128)(2,1)} %pad_maximum_fusion.1), channel_id=1, source_target_pairs={{0,1},{1,0},{2,3},{3,2},{4,5},{5,4},{6,7},{7,6},{8,9},{9,8},{10,11... | collective-permute-start | bytes 7077896 | tf_op jit(solution)/shard_map/ppermute | solution.py:131
  188.5 44.3 %collective-permute-start.18 = (bf16[384,1664]{1,0:T(8,128)(2,1)}, bf16[384,1664]{1,0:T(8,128)(2,1)}, u32[]{:S(2)}, u32[]{:S(2)}) collective-permute-start(bf16[384,1664]{1,0:T(8,128)(2,1)} %copy-done.97), channel_id=1, source_target_pairs={{0,2},{1,3},{2,4},{3,5},{4,6},{5,7},{6,0},{7,1},{8,10},{9,11},{10,... | collective-permute-start | bytes 3833864 | tf_op jit(solution)/shard_map/ppermute | solution.py:124
  202.6 27.4 %collective-permute-start.19 = (bf16[1,4608,128]{2,1,0:T(8,128)(2,1)S(1)}, bf16[1,4608,128]{2,1,0:T(8,128)(2,1)S(1)}, u32[]{:S(2)}, u32[]{:S(2)}) collective-permute-start(bf16[1,4608,128]{2,1,0:T(8,128)(2,1)S(1)} %slice.342), channel_id=1, source_target_pairs={{0,8},{8,0},{16,24},{24,16},{1,9},{9,1},{17,25},{25,17},{2,10},{10... | collective-permute-start | bytes 3538952 | tf_op jit(solution)/shard_map/ppermute | solution.py:42
  205.5 27.0 %collective-permute-start.20 = (bf16[1,4608,128]{2,1,0:T(8,128)(2,1)S(1)}, bf16[1,4608,128]{2,1,0:T(8,128)(2,1)S(1)}, u32[]{:S(2)}, u32[]{:S(2)}) collective-permute-start(bf16[1,4608,128]{2,1,0:T(8,128)(2,1)S(1)} %slice.343), channel_id=1, source_target_pairs={{0,16},{8,24},{16,0},{24,8},{1,17},{9,25},{17,1},{25,9},{2,18},{10... | collective-permute-start | bytes 3538952 | tf_op jit(solution)/shard_map/ppermute | solution.py:42
  234.2 30.6 %collective-permute-start.21 = (bf16[384,1664]{1,0:T(8,128)(2,1)}, bf16[384,1664]{1,0:T(8,128)(2,1)}, u32[]{:S(2)}, u32[]{:S(2)}) collective-permute-start(bf16[384,1664]{1,0:T(8,128)(2,1)} %get-tuple-element.177.refs_0_), channel_id=1, source_target_pairs={{0,2},{1,3},{2,4},{3,5},{4,6},{5,7},{6,0},{7,1},{8,10},{9,11},{10,... | collective-permute-start | bytes 3833864 | tf_op jit(solution)/shard_map/ppermute | solution.py:124
  235.6 30.4 %collective-permute-start.17 = (bf16[384,1664]{1,0:T(8,128)(2,1)}, bf16[384,1664]{1,0:T(8,128)(2,1)}, u32[]{:S(2)}, u32[]{:S(2)}) collective-permute-start(bf16[384,1664]{1,0:T(8,128)(2,1)} %get-tuple-element.177.refs_0_), channel_id=1, source_target_pairs={{0,1},{1,0},{2,3},{3,2},{4,5},{5,4},{6,7},{7,6},{8,9},{9,8},{10,11... | collective-permute-start | bytes 3833864 | tf_op jit(solution)/shard_map/ppermute | solution.py:131
  235.6 31.6 %collective-permute-start.23 = (bf16[384,1664]{1,0:T(8,128)(2,1)}, bf16[384,1664]{1,0:T(8,128)(2,1)}, u32[]{:S(2)}, u32[]{:S(2)}) collective-permute-start(bf16[384,1664]{1,0:T(8,128)(2,1)} %pad_maximum_fusion.6.refs_4_), channel_id=1, source_target_pairs={{0,1},{1,0},{2,3},{3,2},{4,5},{5,4},{6,7},{7,6},{8,9},{9,8},{10,11... | collective-permute-start | bytes 3833864 | tf_op jit(solution)/shard_map/ppermute | solution.py:131
  236.1 31.1 %collective-permute-start.24 = (bf16[384,1664]{1,0:T(8,128)(2,1)}, bf16[384,1664]{1,0:T(8,128)(2,1)}, u32[]{:S(2)}, u32[]{:S(2)}) collective-permute-start(bf16[384,1664]{1,0:T(8,128)(2,1)} %collective-permute-done.10.refs_6_), channel_id=1, source_target_pairs={{0,1},{1,0},{2,3},{3,2},{4,5},{5,4},{6,7},{7,6},{8,9},{9,8},{10,11... | collective-permute-start | bytes 3833864 | tf_op jit(solution)/shard_map/ppermute | solution.py:131
  265.4 54.0 %collective-permute-start.26 = (bf16[2,4608,128]{2,1,0:T(8,128)(2,1)}, bf16[2,4608,128]{2,1,0:T(8,128)(2,1)}, u32[]{:S(2)}, u32[]{:S(2)}) collective-permute-start(bf16[2,4608,128]{2,1,0:T(8,128)(2,1)} %get-tuple-element.187.refs_11_), channel_id=1, source_target_pairs={{0,8},{8,0},{16,24},{24,16},{1,9},{9,1},{17,25},{25,17},{2,10},{10... | collective-permute-start | bytes 7077896 | tf_op jit(solution)/shard_map/ppermute | solution.py:42
  265.9 53.7 %collective-permute-start.27 = (bf16[2,4608,128]{2,1,0:T(8,128)(2,1)}, bf16[2,4608,128]{2,1,0:T(8,128)(2,1)}, u32[]{:S(2)}, u32[]{:S(2)}) collective-permute-start(bf16[2,4608,128]{2,1,0:T(8,128)(2,1)} %get-tuple-element.187.refs_11_), channel_id=1, source_target_pairs={{0,16},{8,24},{16,0},{24,8},{1,17},{9,25},{17,1},{25,9},{2,18},{10... | collective-permute-start | bytes 7077896 | tf_op jit(solution)/shard_map/ppermute | solution.py:42
  267.2 32.0 %collective-permute-start.25 = (bf16[384,1664]{1,0:T(8,128)(2,1)}, bf16[384,1664]{1,0:T(8,128)(2,1)}, u32[]{:S(2)}, u32[]{:S(2)}) collective-permute-start(bf16[384,1664]{1,0:T(8,128)(2,1)} %collective-permute-done.21.refs_2_), channel_id=1, source_target_pairs={{0,2},{1,3},{2,4},{3,5},{4,6},{5,7},{6,0},{7,1},{8,10},{9,11},{10,... | collective-permute-start | bytes 3833864 | tf_op jit(solution)/shard_map/ppermute | solution.py:124
  321.0 27.4 %collective-permute-start.28 = (bf16[1,4608,128]{2,1,0:T(8,128)(2,1)S(1)}, bf16[1,4608,128]{2,1,0:T(8,128)(2,1)S(1)}, u32[]{:S(2)}, u32[]{:S(2)}) collective-permute-start(bf16[1,4608,128]{2,1,0:T(8,128)(2,1)S(1)} %slice.356), channel_id=1, source_target_pairs={{0,8},{8,0},{16,24},{24,16},{1,9},{9,1},{17,25},{25,17},{2,10},{10... | collective-permute-start | bytes 3538952 | tf_op jit(solution)/shard_map/ppermute | solution.py:42
  323.9 27.1 %collective-permute-start.29 = (bf16[1,4608,128]{2,1,0:T(8,128)(2,1)S(1)}, bf16[1,4608,128]{2,1,0:T(8,128)(2,1)S(1)}, u32[]{:S(2)}, u32[]{:S(2)}) collective-permute-start(bf16[1,4608,128]{2,1,0:T(8,128)(2,1)S(1)} %slice.357), channel_id=1, source_target_pairs={{0,16},{8,24},{16,0},{24,8},{1,17},{9,25},{17,1},{25,9},{2,18},{10... | collective-permute-start | bytes 3538952 | tf_op jit(solution)/shard_map/ppermute | solution.py:42
  324.5 61.0 %collective-permute-start.30 = (bf16[384,1664]{1,0:T(8,128)(2,1)}, bf16[384,1664]{1,0:T(8,128)(2,1)}, u32[]{:S(2)}, u32[]{:S(2)}) collective-permute-start(bf16[384,1664]{1,0:T(8,128)(2,1)} %collective-permute-done.25.refs_0_), channel_id=1, source_target_pairs={{0,2},{1,3},{2,4},{3,5},{4,6},{5,7},{6,0},{7,1},{8,10},{9,11},{10,... | collective-permute-start | bytes 3833864 | tf_op jit(solution)/shard_map/ppermute | solution.py:124
  393.2 79.9 %collective-permute-start.42 = (bf16[384,3200]{1,0:T(8,128)(2,1)}, bf16[384,3200]{1,0:T(8,128)(2,1)}, u32[]{:S(2)}, u32[]{:S(2)}) collective-permute-start(bf16[384,3200]{1,0:T(8,128)(2,1)} %get-tuple-element.238), channel_id=1, source_target_pairs={{0,1},{1,0},{2,3},{3,2},{4,5},{5,4},{6,7},{7,6},{8,9},{9,8},{10,11... | collective-permute-start | bytes 7372808 | tf_op jit(solution)/shard_map/ppermute | solution.py:131
  397.4 75.7 %collective-permute-start.32 = (bf16[384,1664]{1,0:T(8,128)(2,1)}, bf16[384,1664]{1,0:T(8,128)(2,1)}, u32[]{:S(2)}, u32[]{:S(2)}) collective-permute-start(bf16[384,1664]{1,0:T(8,128)(2,1)} %add_convert_fusion.6), channel_id=1, source_target_pairs={{0,2},{1,3},{2,4},{3,5},{4,6},{5,7},{6,0},{7,1},{8,10},{9,11},{10,... | collective-permute-start | bytes 3833864 | tf_op jit(solution)/shard_map/ppermute | solution.py:124
  438.2 34.9 %collective-permute-start.37 = (bf16[1,4608,128]{2,1,0:T(8,128)(2,1)}, bf16[1,4608,128]{2,1,0:T(8,128)(2,1)}, u32[]{:S(2)}, u32[]{:S(2)}) collective-permute-start(bf16[1,4608,128]{2,1,0:T(8,128)(2,1)} %get-tuple-element.216), channel_id=1, source_target_pairs={{0,8},{8,0},{16,24},{24,16},{1,9},{9,1},{17,25},{25,17},{2,10},{10... | collective-permute-start | bytes 3538952 | tf_op jit(solution)/shard_map/ppermute | solution.py:42
  438.9 34.2 %collective-permute-start.38 = (bf16[1,4608,128]{2,1,0:T(8,128)(2,1)}, bf16[1,4608,128]{2,1,0:T(8,128)(2,1)}, u32[]{:S(2)}, u32[]{:S(2)}) collective-permute-start(bf16[1,4608,128]{2,1,0:T(8,128)(2,1)} %get-tuple-element.217), channel_id=1, source_target_pairs={{0,16},{8,24},{16,0},{24,8},{1,17},{9,25},{17,1},{25,9},{2,18},{10... | collective-permute-start | bytes 3538952 | tf_op jit(solution)/shard_map/ppermute | solution.py:42
  481.9 32.2 %collective-permute-start.40 = (bf16[384,1664]{1,0:T(8,128)(2,1)}, bf16[384,1664]{1,0:T(8,128)(2,1)}, u32[]{:S(2)}, u32[]{:S(2)}) collective-permute-start(bf16[384,1664]{1,0:T(8,128)(2,1)} %add_convert_fusion.4), channel_id=1, source_target_pairs={{0,2},{1,3},{2,4},{3,5},{4,6},{5,7},{6,0},{7,1},{8,10},{9,11},{10,... | collective-permute-start | bytes 3833864 | tf_op jit(solution)/shard_map/ppermute | solution.py:124
  485.2 54.4 %collective-permute-start.45 = (bf16[2,4608,128]{2,1,0:T(8,128)(2,1)}, bf16[2,4608,128]{2,1,0:T(8,128)(2,1)}, u32[]{:S(2)}, u32[]{:S(2)}) collective-permute-start(bf16[2,4608,128]{2,1,0:T(8,128)(2,1)} %pad_maximum_fusion.2), channel_id=1, source_target_pairs={{0,8},{8,0},{16,24},{24,16},{1,9},{9,1},{17,25},{25,17},{2,10},{10... | collective-permute-start | bytes 7077896 | tf_op jit(solution)/shard_map/ppermute | solution.py:42
  489.3 54.4 %collective-permute-start.46 = (bf16[2,4608,128]{2,1,0:T(8,128)(2,1)}, bf16[2,4608,128]{2,1,0:T(8,128)(2,1)}, u32[]{:S(2)}, u32[]{:S(2)}) collective-permute-start(bf16[2,4608,128]{2,1,0:T(8,128)(2,1)} %pad_maximum_fusion.3), channel_id=1, source_target_pairs={{0,16},{8,24},{16,0},{24,8},{1,17},{9,25},{17,1},{25,9},{2,18},{10... | collective-permute-start | bytes 7077896 | tf_op jit(solution)/shard_map/ppermute | solution.py:42
  516.2 31.3 %collective-permute-start.43 = (bf16[384,1664]{1,0:T(8,128)(2,1)S(1)}, bf16[384,1664]{1,0:T(8,128)(2,1)S(1)}, u32[]{:S(2)}, u32[]{:S(2)}) collective-permute-start(bf16[384,1664]{1,0:T(8,128)(2,1)S(1)} %add_convert_fusion.1), channel_id=1, source_target_pairs={{0,2},{1,3},{2,4},{3,5},{4,6},{5,7},{6,0},{7,1},{8,10},{9,11},{10,... | collective-permute-start | bytes 3833864 | tf_op jit(solution)/shard_map/ppermute | solution.py:124
  516.5 47.5 %collective-permute-start.47 = (bf16[1,4608,128]{2,1,0:T(8,128)(2,1)S(1)}, bf16[1,4608,128]{2,1,0:T(8,128)(2,1)S(1)}, u32[]{:S(2)}, u32[]{:S(2)}) collective-permute-start(bf16[1,4608,128]{2,1,0:T(8,128)(2,1)S(1)} %copy-done.99), channel_id=1, source_target_pairs={{0,8},{8,0},{16,24},{24,16},{1,9},{9,1},{17,25},{25,17},{2,10},{10... | collective-permute-start | bytes 3538952 | tf_op jit(solution)/shard_map/ppermute | solution.py:42
  517.4 50.3 %collective-permute-start.48 = (bf16[1,4608,128]{2,1,0:T(8,128)(2,1)S(1)}, bf16[1,4608,128]{2,1,0:T(8,128)(2,1)S(1)}, u32[]{:S(2)}, u32[]{:S(2)}) collective-permute-start(bf16[1,4608,128]{2,1,0:T(8,128)(2,1)S(1)} %copy-done.98), channel_id=1, source_target_pairs={{0,16},{8,24},{16,0},{24,8},{1,17},{9,25},{17,1},{25,9},{2,18},{10... | collective-permute-start | bytes 3538952 | tf_op jit(solution)/shard_map/ppermute | solution.py:42
  578.7 54.4 %collective-permute-start.44 = (bf16[384,1536]{1,0:T(8,128)(2,1)}, bf16[384,1536]{1,0:T(8,128)(2,1)}, u32[]{:S(2)}, u32[]{:S(2)}) collective-permute-start(bf16[384,1536]{1,0:T(8,128)(2,1)} %add_convert_fusion.14), channel_id=1, source_target_pairs={{0,2},{1,3},{2,4},{3,5},{4,6},{5,7},{6,0},{7,1},{8,10},{9,11},{10,... | collective-permute-start | bytes 3538952 | tf_op jit(solution)/shard_map/ppermute | solution.py:124
  588.5 37.2 %all-to-all-start.3 = ((bf16[4,4,48,1664]{3,2,1,0:T(8,128)(2,1)}), bf16[4,4,48,1664]{3,2,1,0:T(8,128)(2,1)}, u32[]{:S(2)}, u32[]{:S(2)}) async-start(bf16[4,4,48,1664]{3,2,1,0:T(8,128)(2,1)} %add_convert_fusion), calls=%async_computation.3 | async-start | bytes 5111808 | tf_op jit(solution)/shard_map/all_to_all | solution.py:1145
  635.8 43.9 %collective-permute-start.50 = (bf16[384,1536]{1,0:T(8,128)(2,1)}, bf16[384,1536]{1,0:T(8,128)(2,1)}, u32[]{:S(2)}, u32[]{:S(2)}) collective-permute-start(bf16[384,1536]{1,0:T(8,128)(2,1)} %add_convert_fusion.10), channel_id=1, source_target_pairs={{0,2},{1,3},{2,4},{3,5},{4,6},{5,7},{6,0},{7,1},{8,10},{9,11},{10,... | collective-permute-start | bytes 3538952 | tf_op jit(solution)/shard_map/ppermute | solution.py:124
  653.7 89.6 %collective-permute-start.54 = (bf16[384,1536]{1,0:T(8,128)(2,1)}, bf16[384,1536]{1,0:T(8,128)(2,1)}, u32[]{:S(2)}, u32[]{:S(2)}) collective-permute-start(bf16[384,1536]{1,0:T(8,128)(2,1)} %pad_maximum_fusion.7), channel_id=1, source_target_pairs={{0,8},{8,0},{16,24},{24,16},{1,9},{9,1},{17,25},{25,17},{2,10},{10... | collective-permute-start | bytes 3538952 | tf_op jit(solution)/shard_map/ppermute | solution.py:42
  655.5 87.8 %collective-permute-start.55 = (bf16[384,1536]{1,0:T(8,128)(2,1)}, bf16[384,1536]{1,0:T(8,128)(2,1)}, u32[]{:S(2)}, u32[]{:S(2)}) collective-permute-start(bf16[384,1536]{1,0:T(8,128)(2,1)} %pad_maximum_fusion.8), channel_id=1, source_target_pairs={{0,16},{8,24},{16,0},{24,8},{1,17},{9,25},{17,1},{25,9},{2,18},{10... | collective-permute-start | bytes 3538952 | tf_op jit(solution)/shard_map/ppermute | solution.py:42
  663.7 57.5 %all-to-all-start.5 = ((bf16[4,192,640]{2,1,0:T(8,128)(2,1)}), bf16[4,192,640]{2,1,0:T(8,128)(2,1)}, u32[]{:S(2)}, u32[]{:S(2)}) async-start(bf16[4,192,640]{2,1,0:T(8,128)(2,1)} %fusion.9), calls=%async_computation.5 | async-start | bytes 1966080 | tf_op jit(solution)/shard_map/all_to_all | solution.py:155
  674.6 57.8 %collective-permute-start.56 = (bf16[2,4608,128]{2,1,0:T(8,128)(2,1)}, bf16[2,4608,128]{2,1,0:T(8,128)(2,1)}, u32[]{:S(2)}, u32[]{:S(2)}) collective-permute-start(bf16[2,4608,128]{2,1,0:T(8,128)(2,1)} %pad_maximum_fusion.4), channel_id=1, source_target_pairs={{0,8},{8,0},{16,24},{24,16},{1,9},{9,1},{17,25},{25,17},{2,10},{10... | collective-permute-start | bytes 7077896 | tf_op jit(solution)/shard_map/ppermute | solution.py:42
  678.3 56.3 %collective-permute-start.57 = (bf16[2,4608,128]{2,1,0:T(8,128)(2,1)}, bf16[2,4608,128]{2,1,0:T(8,128)(2,1)}, u32[]{:S(2)}, u32[]{:S(2)}) collective-permute-start(bf16[2,4608,128]{2,1,0:T(8,128)(2,1)} %pad_maximum_fusion.5), channel_id=1, source_target_pairs={{0,16},{8,24},{16,0},{24,8},{1,17},{9,25},{17,1},{25,9},{2,18},{10... | collective-permute-start | bytes 7077896 | tf_op jit(solution)/shard_map/ppermute | solution.py:42
  682.3 46.3 %collective-permute-start.53 = (bf16[384,1536]{1,0:T(8,128)(2,1)}, bf16[384,1536]{1,0:T(8,128)(2,1)}, u32[]{:S(2)}, u32[]{:S(2)}) collective-permute-start(bf16[384,1536]{1,0:T(8,128)(2,1)} %add_convert_fusion.9), channel_id=1, source_target_pairs={{0,2},{1,3},{2,4},{3,5},{4,6},{5,7},{6,0},{7,1},{8,10},{9,11},{10,... | collective-permute-start | bytes 3538952 | tf_op jit(solution)/shard_map/ppermute | solution.py:124
  724.3 35.3 %all-to-all-start.6 = ((bf16[4,48,1664]{2,1,0:T(8,128)(2,1)}), bf16[4,48,1664]{2,1,0:T(8,128)(2,1)}, u32[]{:S(2)}, u32[]{:S(2)}) async-start(bf16[4,48,1664]{2,1,0:T(8,128)(2,1)} %reduce_sum.82), calls=%async_computation.6 | async-start | bytes 1277952 | tf_op jit(solution)/shard_map/all_to_all | solution.py:155
  (122 other events, 984.6 us)

commit v4 on v3

--- a/solution.py
+++ b/solution.py
@@ -792,7 +792,7 @@
         ),
         out_shape=out_shapes,
         compiler_params=call_params(60),
-        cost_estimate=cost(26),
+        cost_estimate=cost(4),
         name="experts",
     )(meta, *x_blocks, *g_blocks, *early, *parts)
 
@@ -1006,12 +1006,12 @@
     )
     attended, lse = attend(meta, queries, key_rows, value_rows, starts[:, None], tok)
     cot_same[1], out_near = after((cot_same[1], out_near), attended)
+    cot_other = [core_swap(rows) for rows in cot_same]
     for d in range(2, chips):
         cot_same.append(chip_shift(cot_same[-1], 1))
-    attended = after(attended, weight_near[0])
+    attended, out_near = after((attended, out_near), weight_near[0], cot_same[2], cot_other)
     own_heads = lax.all_to_all(attended, "rows", 0, 0, tiled=True)
     out_mine = jnp.stack(gather_far(out_half, *out_near)).reshape(4, chips, sixth, width)
-    out_mine = after(out_mine, cot_same[2])
     out_parts = cores_in_order(out_mine, core_swap(out_mine), core, 2).reshape(4, tok, width)
     weight_near[0] = after(weight_near[0], own_heads)
     first_far = far_halves(*weight_near[0])
@@ -1031,7 +1031,7 @@
     moe_same = [moe_rows, chip_shift(after(moe_rows, cot_same[3], weight_parts[0][3]), 1)]
     moe_other = [core_swap(rows) for rows in moe_same]
     moe_same.append(chip_shift(moe_same[1], 1))
-    cot_other = [core_swap(after(rows, moe_rows)) for rows in cot_same]
+    cot_other += [core_swap(rows) for rows in cot_same[2:]]
 
     moe_meta = jnp.stack([row, column * own_experts]).astype(jnp.int32)
     ffe = w_down.shape[1]

time: 790 us -> 745 us (0.943)
  waiting for transfers between devices: 263 us -> 236 us
    ppermute x28, waiting for transfers between devices: 161 us -> 94.2 us  [rows_swap(): return lax.ppermute(array, 'rows', [(i, i ^ distance) for i in range(4)])]
    ppermute x15, waiting for transfers between devices: 44.1 us -> 75.2 us  [chip_shift(): lax.ppermute(array, 'cols', [(i, (i + 2 * distance) % count) for i in ran...]
    unnamed x230 -> x258, local copies, waits for them, and re-layouts: 52.3 us -> 44.4 us
  transfers between devices with their start and end apart: 66 -> 66, of which waited for: 29 -> 31; matrix products, arithmetic and copies ran while one was open for 22% -> 22% of each run, Pallas kernels for 27% -> 28%
where the time goes in v4:
time: 745 us; the launch traced here: 736 us
  waiting for transfers between devices  236 us (32%)
  Pallas kernels  207 us (28%)
  other arithmetic  103 us (14%)
  starting transfers between devices  87.1 us (12%)
  local copies, waits for them, and re-layouts  84.4 us (11%)
  matrix products  11.4 us (2%)
    pallas_call x4, Pallas kernels, run_experts(): pl.pallas_call(partial(experts_kernel, experts=experts, slots=slots, loca...  114 us
    ppermute x28, waiting for transfers between devices, rows_swap(): return lax.ppermute(array, 'rows', [(i, i ^ distance) for i in range(4)])  94.2 us
    ppermute x15, waiting for transfers between devices, chip_shift(): lax.ppermute(array, 'cols', [(i, (i + 2 * distance) % count) for i in ran...  75.2 us
    unnamed x258, local copies, waits for them, and re-layouts  44.4 us
    convert_element_type x19, other arithmetic, add_low(): return (left.astype(f32) + right.astype(f32)).astype(bf16)  38.9 us
    pallas_call x2, Pallas kernels, weight_grads(): pl.pallas_call(partial(weight_grad_kernel, chunks=chunks, own_count=own),...  32.4 us
    all_to_all x2, waiting for transfers between devices, chips_exchange(): lax.all_to_all(array, 'cols', 0, 0, axis_index_groups=alike, tiled=True)  30.4 us
    ppermute x28, starting transfers between devices, rows_swap(): return lax.ppermute(array, 'rows', [(i, i ^ distance) for i in range(4)])  24.7 us
  transfers between devices with their start and end apart: 66, of which 31 were waited for; matrix products, arithmetic and copies ran while one was open for 22% of the time, Pallas kernels for 28%

profile of v4, /device:TPU:6, one launch (start us, length us, event | category | flops | bytes accessed | tf_op | source)
XLA Modules:
  0.0 736.5 jit_solution(14664976564444142795)
XLA Ops:
  16.7 5.3 all-to-all-start
  35.4 4.4 fusion.19
  47.6 10.1 %collective-permute-done.2 = bf16[192,1536]{1,0:T(8,128)(2,1)} collective-permute-done((bf16[192,1536]{1,0:T(8,128)(2,1)}, bf16[192,1536]{1,0:T(8,128)(2,1)}, u32[]{:S(2)}, u32[]{:S(2)}) %collective-permute-start.2) | collective-permute-done | bytes 589856 | tf_op jit(solution)/shard_map/ppermute | solution.py:42
  92.9 9.0 %project.1 = (bf16[1536,384]{1,0:T(8,128)(2,1)S(1)}, bf16[1536,128]{1,0:T(8,128)(2,1)S(1)}, bf16[1536,128]{1,0:T(8,128)(2,1)S(1)}, bf16[4,384,1536]{2,1,0:T(8,128)(2,1)S(1)}, bf16[1536,640]{1,0:T(8,128)(2,1)S(1)}) custom-call(s32[7]{0:T(128)S(1)} %pad_add_fusion.meta, bf16[384,1536]{1,0:T(8,128)(2,1)S(1)} %bitcast.69, bf16[384,1536]{1,0:T(8,128)(2,1)S(1)} %copy-done.23, ...), custom_call_target="tpu_custom_call" | custom-call | flops 11500000256 | tf_op jit(solution)/shard_map/project/pallas_call | solution.py:229
  104.1 13.2 %attend.1 = (bf16[4,384,384]{2,1,0:T(8,128)(2,1)}, f32[1536,8]{1,0:T(8,128)S(1)}) custom-call(s32[7]{0:T(128)S(1)} %pad_add_fusion.meta, bf16[1536,384]{1,0:T(8,128)(2,1)S(1)} %get-tuple-element.155.queries, bf16[1536,128]{1,0:T(8,128)(2,1)S(1)} %get-tuple-element.156.keys, bf16[1536,128]{1,0:T(8,128)(2,1)S(1)} %get-tuple-element.157.values, ...), custom_call_target="tpu_custom_call" | custom-call | flops 18400000000 | tf_op jit(solution)/shard_map/attend/pallas_call | solution.py:296
  122.4 29.5 %collective-permute-done.13.refs_4_ = bf16[384,1664]{1,0:T(8,128)(2,1)S(1)} collective-permute-done((bf16[384,1664]{1,0:T(8,128)(2,1)S(1)}, bf16[384,1664]{1,0:T(8,128)(2,1)S(1)}, u32[]{:S(2)}, u32[]{:S(2)}) %collective-permute-start.13) | collective-permute-done | bytes 1277984 | tf_op jit(solution)/shard_map/ppermute | solution.py:124
  154.0 6.5 collective-permute-done.17
  162.9 5.3 all-to-all-start.1
  170.5 12.1 %all-to-all-done.1.heads = bf16[4,384,384]{2,1,0:T(8,128)(2,1)S(1)} async-done(((bf16[4,384,384]{2,1,0:T(8,128)(2,1)}), bf16[4,384,384]{2,1,0:T(8,128)(2,1)S(1)}, u32[]{:S(2)}, u32[]{:S(2)}) %all-to-all-start.1) | async-done | bytes 1179680 | tf_op jit(solution)/shard_map/all_to_all | solution.py:1013
  190.0 4.3 mix.1
  194.4 17.9 %collective-permute-done.21 = bf16[1,4608,128]{2,1,0:T(8,128)(2,1)S(1)} collective-permute-done((bf16[1,4608,128]{2,1,0:T(8,128)(2,1)S(1)}, bf16[1,4608,128]{2,1,0:T(8,128)(2,1)S(1)}, u32[]{:S(2)}, u32[]{:S(2)}) %collective-permute-start.21) | collective-permute-done | bytes 1179680 | tf_op jit(solution)/shard_map/ppermute | solution.py:42
  217.1 27.4 %collective-permute-done.23.refs_2_ = bf16[384,1664]{1,0:T(8,128)(2,1)} collective-permute-done((bf16[384,1664]{1,0:T(8,128)(2,1)S(1)}, bf16[384,1664]{1,0:T(8,128)(2,1)}, u32[]{:S(2)}, u32[]{:S(2)}) %collective-permute-start.23) | collective-permute-done | bytes 1277984 | tf_op jit(solution)/shard_map/ppermute | solution.py:124
  247.8 24.0 %experts.4 = (bf16[2,512,1536]{2,1,0:T(8,128)(2,1)}, bf16[2,512,1536]{2,1,0:T(8,128)(2,1)}, bf16[2,512,512]{2,1,0:T(8,128)(2,1)}, bf16[2,512,1024]{2,1,0:T(8,128...) custom-call(s32[2]{0:T(128)} %pad_add_fusion.1.meta, ...), custom_call_target="tpu_custom_call" | custom-call | flops 4600000000 | tf_op jit(solution)/shard_map/experts/pallas_call | solution.py:777
  271.8 5.2 collective-permute-done.25.refs_0_
  281.9 24.2 %collective-permute-done.28 = bf16[1,4608,128]{2,1,0:T(8,128)(2,1)S(1)} collective-permute-done((bf16[1,4608,128]{2,1,0:T(8,128)(2,1)S(1)}, bf16[1,4608,128]{2,1,0:T(8,128)(2,1)S(1)}, u32[]{:S(2)}, u32[]{:S(2)}) %collective-permute-start.28) | collective-permute-done | bytes 1179680 | tf_op jit(solution)/shard_map/ppermute | solution.py:42
  309.9 33.0 %experts.5 = (bf16[384,3200]{1,0:T(8,128)(2,1)}, bf16[384,3200]{1,0:T(8,128)(2,1)}, bf16[384,3200]{1,0:T(8,128)(2,1)}, bf16[384,3200]{1,0:T(8,128)(2,1)}, bf16[2...) custom-call(s32[2]{0:T(128)} %pad_add_fusion.1.meta, ...), custom_call_target="tpu_custom_call" | custom-call | flops 4600000000 | tf_op jit(solution)/shard_map/experts/pallas_call | solution.py:777
  344.1 3.8 collective-permute-done.31
  347.9 3.6 add_convert_fusion.6
  355.3 24.1 %experts.6 = (bf16[2,512,1536]{2,1,0:T(8,128)(2,1)}, bf16[2,512,1536]{2,1,0:T(8,128)(2,1)}, bf16[2,512,512]{2,1,0:T(8,128)(2,1)}, bf16[2,512,1024]{2,1,0:T(8,128...) custom-call(s32[2]{0:T(128)} %pad_add_fusion.1.meta, ...), custom_call_target="tpu_custom_call" | custom-call | flops 4600000000 | tf_op jit(solution)/shard_map/experts/pallas_call | solution.py:777
  379.4 16.2 %weight_grads.2 = (bf16[1,4608,128]{2,1,0:T(8,128)(2,1)}, bf16[1,4608,128]{2,1,0:T(8,128)(2,1)}, bf16[1,4608,128]{2,1,0:T(8,128)(2,1)}, bf16[1,4608,128]{2,1,0:T...) custom-call(bf16[2,512,1536]{2,1,0:T(8,128)(2,1)} %get-tuple-element, ...), custom_call_target="tpu_custom_call" | custom-call | flops 14949999616 | tf_op jit(solution)/shard_map/weight_grads/pallas_call | solution.py:856
  397.6 33.1 %experts.7 = (bf16[384,3200]{1,0:T(8,128)(2,1)}, bf16[384,3200]{1,0:T(8,128)(2,1)}, bf16[384,3200]{1,0:T(8,128)(2,1)}, bf16[384,3200]{1,0:T(8,128)(2,1)}, bf16[2...) custom-call(s32[2]{0:T(128)} %pad_add_fusion.1.meta, ...), custom_call_target="tpu_custom_call" | custom-call | flops 4600000000 | tf_op jit(solution)/shard_map/experts/pallas_call | solution.py:777
  431.3 3.2 add_convert_fusion.2.last
  435.8 3.8 add_convert_fusion.4
  448.5 16.2 %weight_grads.3 = (bf16[1,4608,128]{2,1,0:T(8,128)(2,1)}, bf16[1,4608,128]{2,1,0:T(8,128)(2,1)}, bf16[1,4608,128]{2,1,0:T(8,128)(2,1)}, bf16[1,4608,128]{2,1,0:T...) custom-call(bf16[2,512,1536]{2,1,0:T(8,128)(2,1)} %get-tuple-element, ...), custom_call_target="tpu_custom_call" | custom-call | flops 14949999616 | tf_op jit(solution)/shard_map/weight_grads/pallas_call | solution.py:856
  464.7 7.4 %collective-permute-done.40 = bf16[384,1664]{1,0:T(8,128)(2,1)} collective-permute-done((bf16[384,1664]{1,0:T(8,128)(2,1)}, bf16[384,1664]{1,0:T(8,128)(2,1)}, u32[]{:S(2)}, u32[]{:S(2)}) %collective-permute-start.40) | collective-permute-done | bytes 1277984 | tf_op jit(solution)/shard_map/ppermute | solution.py:124
  488.5 8.5 %collective-permute-done.45 = bf16[2,4608,128]{2,1,0:T(8,128)(2,1)} collective-permute-done((bf16[2,4608,128]{2,1,0:T(8,128)(2,1)}, bf16[2,4608,128]{2,1,0:T(8,128)(2,1)}, u32[]{:S(2)}, u32[]{:S(2)}) %collective-permute-start.45) | collective-permute-done | bytes 2359328 | tf_op jit(solution)/shard_map/ppermute | solution.py:42
  499.8 5.6 collective-permute-done.43.came
  505.5 10.2 %unmix.1 = (f32[384,1536]{1,0:T(8,128)S(1)}, bf16[4,384,384]{2,1,0:T(8,128)(2,1)S(1)}, bf16[4,4,48,1664]{3,2,1,0:T(8,128)(2,1)S(1)}, bf16[4,4,48,1664]{3,2,1,0:T(8,128)(2,1)}) custom-call(s32[7]{0:T(128)S(1)} %pad_add_fusion.meta, bf16[384,1664]{1,0:T(8,128)(2,1)S(1)} %collective-permute-done.43.came, bf16[384,1664]{1,0:T(8,128)(2,1)S(1)} %copy-done.8, ...), custom_call_target="tpu_custom_call" | custom-call | flops 13799999488 | tf_op jit(solution)/shard_map/unmix/pallas_call | solution.py:520
  525.8 5.8 all-to-all-start.2
  535.5 4.6 add_convert_fusion
  540.0 5.2 all-to-all-done.2.grads
  545.3 6.0 all-to-all-start.3
  557.6 23.6 %attend_back.1 = bf16[4,384,640]{2,1,0:T(8,128)(2,1)S(1)} custom-call(s32[7]{0:T(128)S(1)} %pad_add_fusion.meta, bf16[1536,384]{1,0:T(8,128)(2,1)S(1)} %copy-done.35, bf16[4,384,384]{2,1,0:T(8,128)(2,1)} %all-to-all-done.2.grads, f32[8,1536]{1,0:T(8,128)S(1)} %bitcast.77, s32[1,1536]{1,0:T(1,128)S(1)} %broadcast_in_dim.39.starts, ...), custom_call_target="tpu_custom_call" | custom-call | flops 33350000640 | tf_op jit(solution)/shard_map/attend_back/pallas_call | solution.py:400
  592.6 4.5 collective-permute-start.50
  598.0 4.0 bitcast_convert_fusion
  602.1 10.5 %collective-permute-done.51 = bf16[192,1536]{1,0:T(8,128)(2,1)S(1)} collective-permute-done((bf16[192,1536]{1,0:T(8,128)(2,1)S(1)}, bf16[192,1536]{1,0:T(8,128)(2,1)S(1)}, u32[]{:S(2)}, u32[]{:S(2)}) %collective-permute-start.51) | collective-permute-done | bytes 589856 | tf_op jit(solution)/shard_map/ppermute | solution.py:42
  616.2 5.3 all_to_all.48
  622.7 4.8 all-to-all-start.5
  641.1 3.1 convert_add_fusion.1
  647.2 30.4 %all-to-all-done.5 = bf16[4,192,640]{2,1,0:T(8,128)(2,1)} async-done(((bf16[4,192,640]{2,1,0:T(8,128)(2,1)}), bf16[4,192,640]{2,1,0:T(8,128)(2,1)}, u32[]{:S(2)}, u32[]{:S(2)}) %all-to-all-start.5) | async-done | bytes 983072 | tf_op jit(solution)/shard_map/all_to_all | solution.py:155
  680.6 4.2 all-to-all-start.6
  684.8 3.8 add_bitcast_fusion
  688.6 3.3 collective-permute-done.56
  693.5 3.1 convert_add_fusion
  705.7 3.4 maximum_maximum_fusion
  714.6 4.0 fusion.6
  719.8 4.7 all-to-all-start.7
  730.0 5.7 collective-permute-done.58
  (481 shorter events, 227.0 us)
Async XLA Ops:
  0.7 40.6 %collective-permute-start = (bf16[384,1536]{1,0:T(8,128)(2,1)}, bf16[384,1536]{1,0:T(8,128)(2,1)S(1)}, u32[]{:S(2)}, u32[]{:S(2)}) collective-permute-start(bf16[384,1536]{1,0:T(8,128)(2,1)} %bitcast.67), channel_id=1, source_target_pairs={{0,8},{8,0},{16,24},{24,16},{1,9},{9,1},{17,25},{25,17},{2,10},{10... | collective-permute-start | bytes 3538952 | tf_op jit(solution)/shard_map/ppermute | solution.py:42
  1.3 38.5 %collective-permute-start.1 = (bf16[384,1536]{1,0:T(8,128)(2,1)}, bf16[384,1536]{1,0:T(8,128)(2,1)S(1)}, u32[]{:S(2)}, u32[]{:S(2)}) collective-permute-start(bf16[384,1536]{1,0:T(8,128)(2,1)} %bitcast.68), channel_id=1, source_target_pairs={{0,16},{8,24},{16,0},{24,8},{1,17},{9,25},{17,1},{25,9},{2,18},{10... | collective-permute-start | bytes 3538952 | tf_op jit(solution)/shard_map/ppermute | solution.py:42
  7.5 52.6 %collective-permute-start.4 = (bf16[192,1024]{1,0:T(8,128)(2,1)}, bf16[192,1024]{1,0:T(8,128)(2,1)}, u32[]{:S(2)}, u32[]{:S(2)}) collective-permute-start(bf16[192,1024]{1,0:T(8,128)(2,1)} %constant_dynamic-update-slice_fusion.2), channel_id=1, source_target_pairs={{0,2},{1,3},{2,4},{3,5},{4,6},{5,7},{6,0},{7,1},{8,10},{9,11},{10,... | collective-permute-start | bytes 1179656 | tf_op jit(solution)/shard_map/ppermute | solution.py:124
  9.5 50.6 %collective-permute-start.5 = (bf16[192,1024]{1,0:T(8,128)(2,1)}, bf16[192,1024]{1,0:T(8,128)(2,1)}, u32[]{:S(2)}, u32[]{:S(2)}) collective-permute-start(bf16[192,1024]{1,0:T(8,128)(2,1)} %constant_dynamic-update-slice_fusion.2), channel_id=1, source_target_pairs={{0,4},{1,5},{2,6},{3,7},{4,0},{5,1},{6,2},{7,3},{8,12},{9,13},{10,... | collective-permute-start | bytes 1179656 | tf_op jit(solution)/shard_map/ppermute | solution.py:124
  12.1 48.0 %collective-permute-start.6 = (bf16[192,1024]{1,0:T(8,128)(2,1)}, bf16[192,1024]{1,0:T(8,128)(2,1)}, u32[]{:S(2)}, u32[]{:S(2)}) collective-permute-start(bf16[192,1024]{1,0:T(8,128)(2,1)} %constant_dynamic-update-slice_fusion.2), channel_id=1, source_target_pairs={{0,6},{1,7},{2,0},{3,1},{4,2},{5,3},{6,4},{7,5},{8,14},{9,15},{10,... | collective-permute-start | bytes 1179656 | tf_op jit(solution)/shard_map/ppermute | solution.py:124
  16.7 48.9 %all-to-all-start = ((bf16[32,48,128]{2,1,0:T(8,128)(2,1)}), bf16[32,48,128]{2,1,0:T(8,128)(2,1)}, u32[]{:S(2)}, u32[]{:S(2)}) async-start(bf16[32,48,128]{2,1,0:T(8,128)(2,1)} %tile.2), calls=%async_computation | async-start | bytes 786432 | tf_op jit(solution)/shard_map/all_to_all | solution.py:961
  62.9 21.7 %collective-permute-start.7 = (bf16[4,192,640]{2,1,0:T(8,128)(2,1)S(1)}, bf16[4,192,640]{2,1,0:T(8,128)(2,1)}, u32[]{:S(2)}, u32[]{:S(2)}) collective-permute-start(bf16[4,192,640]{2,1,0:T(8,128)(2,1)S(1)} %pad_maximum_fusion.9.refs_4_), channel_id=1, source_target_pairs={{0,1},{1,0},{2,3},{3,2},{4,5},{5,4},{6,7},{7,6},{8,9},{9,8},{10,11... | collective-permute-start | bytes 2949128 | tf_op jit(solution)/shard_map/ppermute | solution.py:131
  81.0 36.3 %collective-permute-start.9 = (bf16[192,1536]{1,0:T(8,128)(2,1)S(1)}, bf16[192,1536]{1,0:T(8,128)(2,1)S(1)}, u32[]{:S(2)}, u32[]{:S(2)}) collective-permute-start(bf16[192,1536]{1,0:T(8,128)(2,1)S(1)} %bitcast.88), channel_id=1, source_target_pairs={{0,8},{8,0},{16,24},{24,16},{1,9},{9,1},{17,25},{25,17},{2,10},{10... | collective-permute-start | bytes 1769480 | tf_op jit(solution)/shard_map/ppermute | solution.py:42
  82.2 37.3 %collective-permute-start.10 = (bf16[192,1536]{1,0:T(8,128)(2,1)S(1)}, bf16[192,1536]{1,0:T(8,128)(2,1)S(1)}, u32[]{:S(2)}, u32[]{:S(2)}) collective-permute-start(bf16[192,1536]{1,0:T(8,128)(2,1)S(1)} %bitcast.89), channel_id=1, source_target_pairs={{0,16},{8,24},{16,0},{24,8},{1,17},{9,25},{17,1},{25,9},{2,18},{10... | collective-permute-start | bytes 1769480 | tf_op jit(solution)/shard_map/ppermute | solution.py:42
  82.7 36.8 %collective-permute-start.8 = (bf16[384,1664]{1,0:T(8,128)(2,1)}, bf16[384,1664]{1,0:T(8,128)(2,1)S(1)}, u32[]{:S(2)}, u32[]{:S(2)}) collective-permute-start(bf16[384,1664]{1,0:T(8,128)(2,1)} %pad_maximum_fusion.6.refs_4_), channel_id=1, source_target_pairs={{0,2},{1,3},{2,4},{3,5},{4,6},{5,7},{6,0},{7,1},{8,10},{9,11},{10,... | collective-permute-start | bytes 3833864 | tf_op jit(solution)/shard_map/ppermute | solution.py:124
  84.7 67.3 %collective-permute-start.11 = (bf16[2,4608,128]{2,1,0:T(8,128)(2,1)}, bf16[2,4608,128]{2,1,0:T(8,128)(2,1)S(1)}, u32[]{:S(2)}, u32[]{:S(2)}) collective-permute-start(bf16[2,4608,128]{2,1,0:T(8,128)(2,1)} %copy-done.48), channel_id=1, source_target_pairs={{0,8},{8,0},{16,24},{24,16},{1,9},{9,1},{17,25},{25,17},{2,10},{10... | collective-permute-start | bytes 7077896 | tf_op jit(solution)/shard_map/ppermute | solution.py:42
  85.5 66.4 %collective-permute-start.12 = (bf16[2,4608,128]{2,1,0:T(8,128)(2,1)}, bf16[2,4608,128]{2,1,0:T(8,128)(2,1)S(1)}, u32[]{:S(2)}, u32[]{:S(2)}) collective-permute-start(bf16[2,4608,128]{2,1,0:T(8,128)(2,1)} %copy-done.48), channel_id=1, source_target_pairs={{0,16},{8,24},{16,0},{24,8},{1,17},{9,25},{17,1},{25,9},{2,18},{10... | collective-permute-start | bytes 7077896 | tf_op jit(solution)/shard_map/ppermute | solution.py:42
  119.5 32.4 %collective-permute-start.13 = (bf16[384,1664]{1,0:T(8,128)(2,1)S(1)}, bf16[384,1664]{1,0:T(8,128)(2,1)S(1)}, u32[]{:S(2)}, u32[]{:S(2)}) collective-permute-start(bf16[384,1664]{1,0:T(8,128)(2,1)S(1)} %collective-permute-done.8.refs_6_), channel_id=1, source_target_pairs={{0,2},{1,3},{2,4},{3,5},{4,6},{5,7},{6,0},{7,1},{8,10},{9,11},{10,... | collective-permute-start | bytes 3833864 | tf_op jit(solution)/shard_map/ppermute | solution.py:124
  122.2 29.7 %collective-permute-start.15 = (bf16[384,1664]{1,0:T(8,128)(2,1)S(1)}, bf16[384,1664]{1,0:T(8,128)(2,1)S(1)}, u32[]{:S(2)}, u32[]{:S(2)}) collective-permute-start(bf16[384,1664]{1,0:T(8,128)(2,1)S(1)} %collective-permute-done.8.refs_6_), channel_id=1, source_target_pairs={{0,1},{1,0},{2,3},{3,2},{4,5},{5,4},{6,7},{7,6},{8,9},{9,8},{10,11... | collective-permute-start | bytes 3833864 | tf_op jit(solution)/shard_map/ppermute | solution.py:131
  162.8 24.0 %collective-permute-start.18 = (bf16[4,4,48,1536]{3,2,1,0:T(8,128)(2,1)}, bf16[4,4,48,1536]{3,2,1,0:T(8,128)(2,1)}, u32[]{:S(2)}, u32[]{:S(2)}) collective-permute-start(bf16[4,4,48,1536]{3,2,1,0:T(8,128)(2,1)} %pad_maximum_fusion.1), channel_id=1, source_target_pairs={{0,1},{1,0},{2,3},{3,2},{4,5},{5,4},{6,7},{7,6},{8,9},{9,8},{10,11... | collective-permute-start | bytes 7077896 | tf_op jit(solution)/shard_map/ppermute | solution.py:131
  162.9 19.8 %all-to-all-start.1 = ((bf16[4,384,384]{2,1,0:T(8,128)(2,1)}), bf16[4,384,384]{2,1,0:T(8,128)(2,1)S(1)}, u32[]{:S(2)}, u32[]{:S(2)}) async-start(bf16[4,384,384]{2,1,0:T(8,128)(2,1)} %get-tuple-element.166), calls=%async_computation.1 | async-start | bytes 2359296 | tf_op jit(solution)/shard_map/all_to_all | solution.py:1013
  169.3 44.7 %collective-permute-start.20 = (bf16[384,1664]{1,0:T(8,128)(2,1)}, bf16[384,1664]{1,0:T(8,128)(2,1)}, u32[]{:S(2)}, u32[]{:S(2)}) collective-permute-start(bf16[384,1664]{1,0:T(8,128)(2,1)} %copy-done.52), channel_id=1, source_target_pairs={{0,2},{1,3},{2,4},{3,5},{4,6},{5,7},{6,0},{7,1},{8,10},{9,11},{10,... | collective-permute-start | bytes 3833864 | tf_op jit(solution)/shard_map/ppermute | solution.py:124
  184.5 27.7 %collective-permute-start.21 = (bf16[1,4608,128]{2,1,0:T(8,128)(2,1)S(1)}, bf16[1,4608,128]{2,1,0:T(8,128)(2,1)S(1)}, u32[]{:S(2)}, u32[]{:S(2)}) collective-permute-start(bf16[1,4608,128]{2,1,0:T(8,128)(2,1)S(1)} %slice.342), channel_id=1, source_target_pairs={{0,8},{8,0},{16,24},{24,16},{1,9},{9,1},{17,25},{25,17},{2,10},{10... | collective-permute-start | bytes 3538952 | tf_op jit(solution)/shard_map/ppermute | solution.py:42
  186.2 27.5 %collective-permute-start.22 = (bf16[1,4608,128]{2,1,0:T(8,128)(2,1)S(1)}, bf16[1,4608,128]{2,1,0:T(8,128)(2,1)S(1)}, u32[]{:S(2)}, u32[]{:S(2)}) collective-permute-start(bf16[1,4608,128]{2,1,0:T(8,128)(2,1)S(1)} %slice.343), channel_id=1, source_target_pairs={{0,16},{8,24},{16,0},{24,8},{1,17},{9,25},{17,1},{25,9},{2,18},{10... | collective-permute-start | bytes 3538952 | tf_op jit(solution)/shard_map/ppermute | solution.py:42
  213.9 30.5 %collective-permute-start.23 = (bf16[384,1664]{1,0:T(8,128)(2,1)S(1)}, bf16[384,1664]{1,0:T(8,128)(2,1)}, u32[]{:S(2)}, u32[]{:S(2)}) collective-permute-start(bf16[384,1664]{1,0:T(8,128)(2,1)S(1)} %get-tuple-element.175.refs_0_), channel_id=1, source_target_pairs={{0,2},{1,3},{2,4},{3,5},{4,6},{5,7},{6,0},{7,1},{8,10},{9,11},{10,... | collective-permute-start | bytes 3833864 | tf_op jit(solution)/shard_map/ppermute | solution.py:124
  215.2 61.9 %collective-permute-start.26 = (bf16[2,4608,128]{2,1,0:T(8,128)(2,1)}, bf16[2,4608,128]{2,1,0:T(8,128)(2,1)}, u32[]{:S(2)}, u32[]{:S(2)}) collective-permute-start(bf16[2,4608,128]{2,1,0:T(8,128)(2,1)} %get-tuple-element.183.refs_11_), channel_id=1, source_target_pairs={{0,8},{8,0},{16,24},{24,16},{1,9},{9,1},{17,25},{25,17},{2,10},{10... | collective-permute-start | bytes 7077896 | tf_op jit(solution)/shard_map/ppermute | solution.py:42
  216.0 61.1 %collective-permute-start.27 = (bf16[2,4608,128]{2,1,0:T(8,128)(2,1)}, bf16[2,4608,128]{2,1,0:T(8,128)(2,1)}, u32[]{:S(2)}, u32[]{:S(2)}) collective-permute-start(bf16[2,4608,128]{2,1,0:T(8,128)(2,1)} %get-tuple-element.183.refs_11_), channel_id=1, source_target_pairs={{0,16},{8,24},{16,0},{24,8},{1,17},{9,25},{17,1},{25,9},{2,18},{10... | collective-permute-start | bytes 7077896 | tf_op jit(solution)/shard_map/ppermute | solution.py:42
  217.1 28.0 %collective-permute-start.19 = (bf16[384,1664]{1,0:T(8,128)(2,1)S(1)}, bf16[384,1664]{1,0:T(8,128)(2,1)}, u32[]{:S(2)}, u32[]{:S(2)}) collective-permute-start(bf16[384,1664]{1,0:T(8,128)(2,1)S(1)} %get-tuple-element.175.refs_0_), channel_id=1, source_target_pairs={{0,1},{1,0},{2,3},{3,2},{4,5},{5,4},{6,7},{7,6},{8,9},{9,8},{10,11... | collective-permute-start | bytes 3833864 | tf_op jit(solution)/shard_map/ppermute | solution.py:131
  244.5 32.6 %collective-permute-start.25 = (bf16[384,1664]{1,0:T(8,128)(2,1)}, bf16[384,1664]{1,0:T(8,128)(2,1)}, u32[]{:S(2)}, u32[]{:S(2)}) collective-permute-start(bf16[384,1664]{1,0:T(8,128)(2,1)} %collective-permute-done.23.refs_2_), channel_id=1, source_target_pairs={{0,2},{1,3},{2,4},{3,5},{4,6},{5,7},{6,0},{7,1},{8,10},{9,11},{10,... | collective-permute-start | bytes 3833864 | tf_op jit(solution)/shard_map/ppermute | solution.py:124
  278.4 27.7 %collective-permute-start.28 = (bf16[1,4608,128]{2,1,0:T(8,128)(2,1)S(1)}, bf16[1,4608,128]{2,1,0:T(8,128)(2,1)S(1)}, u32[]{:S(2)}, u32[]{:S(2)}) collective-permute-start(bf16[1,4608,128]{2,1,0:T(8,128)(2,1)S(1)} %slice.356), channel_id=1, source_target_pairs={{0,8},{8,0},{16,24},{24,16},{1,9},{9,1},{17,25},{25,17},{2,10},{10... | collective-permute-start | bytes 3538952 | tf_op jit(solution)/shard_map/ppermute | solution.py:42
  281.0 27.4 %collective-permute-start.29 = (bf16[1,4608,128]{2,1,0:T(8,128)(2,1)S(1)}, bf16[1,4608,128]{2,1,0:T(8,128)(2,1)S(1)}, u32[]{:S(2)}, u32[]{:S(2)}) collective-permute-start(bf16[1,4608,128]{2,1,0:T(8,128)(2,1)S(1)} %slice.357), channel_id=1, source_target_pairs={{0,16},{8,24},{16,0},{24,8},{1,17},{9,25},{17,1},{25,9},{2,18},{10... | collective-permute-start | bytes 3538952 | tf_op jit(solution)/shard_map/ppermute | solution.py:42
  281.9 61.0 %collective-permute-start.30 = (bf16[384,1664]{1,0:T(8,128)(2,1)}, bf16[384,1664]{1,0:T(8,128)(2,1)}, u32[]{:S(2)}, u32[]{:S(2)}) collective-permute-start(bf16[384,1664]{1,0:T(8,128)(2,1)} %collective-permute-done.25.refs_0_), channel_id=1, source_target_pairs={{0,2},{1,3},{2,4},{3,5},{4,6},{5,7},{6,0},{7,1},{8,10},{9,11},{10,... | collective-permute-start | bytes 3833864 | tf_op jit(solution)/shard_map/ppermute | solution.py:124
  351.5 79.3 %collective-permute-start.32 = (bf16[384,1664]{1,0:T(8,128)(2,1)}, bf16[384,1664]{1,0:T(8,128)(2,1)}, u32[]{:S(2)}, u32[]{:S(2)}) collective-permute-start(bf16[384,1664]{1,0:T(8,128)(2,1)} %add_convert_fusion.6), channel_id=1, source_target_pairs={{0,2},{1,3},{2,4},{3,5},{4,6},{5,7},{6,0},{7,1},{8,10},{9,11},{10,... | collective-permute-start | bytes 3833864 | tf_op jit(solution)/shard_map/ppermute | solution.py:124
  395.6 35.1 %collective-permute-start.37 = (bf16[1,4608,128]{2,1,0:T(8,128)(2,1)}, bf16[1,4608,128]{2,1,0:T(8,128)(2,1)S(1)}, u32[]{:S(2)}, u32[]{:S(2)}) collective-permute-start(bf16[1,4608,128]{2,1,0:T(8,128)(2,1)} %get-tuple-element.210), channel_id=1, source_target_pairs={{0,8},{8,0},{16,24},{24,16},{1,9},{9,1},{17,25},{25,17},{2,10},{10... | collective-permute-start | bytes 3538952 | tf_op jit(solution)/shard_map/ppermute | solution.py:42
  396.6 34.1 %collective-permute-start.38 = (bf16[1,4608,128]{2,1,0:T(8,128)(2,1)}, bf16[1,4608,128]{2,1,0:T(8,128)(2,1)S(1)}, u32[]{:S(2)}, u32[]{:S(2)}) collective-permute-start(bf16[1,4608,128]{2,1,0:T(8,128)(2,1)} %get-tuple-element.211), channel_id=1, source_target_pairs={{0,16},{8,24},{16,0},{24,8},{1,17},{9,25},{17,1},{25,9},{2,18},{10... | collective-permute-start | bytes 3538952 | tf_op jit(solution)/shard_map/ppermute | solution.py:42
  397.6 33.7 %collective-permute-start.42 = (bf16[384,3200]{1,0:T(8,128)(2,1)}, bf16[384,3200]{1,0:T(8,128)(2,1)}, u32[]{:S(2)}, u32[]{:S(2)}) collective-permute-start(bf16[384,3200]{1,0:T(8,128)(2,1)} %get-tuple-element.232), channel_id=1, source_target_pairs={{0,1},{1,0},{2,3},{3,2},{4,5},{5,4},{6,7},{7,6},{8,9},{9,8},{10,11... | collective-permute-start | bytes 7372808 | tf_op jit(solution)/shard_map/ppermute | solution.py:131
  439.6 32.5 %collective-permute-start.40 = (bf16[384,1664]{1,0:T(8,128)(2,1)}, bf16[384,1664]{1,0:T(8,128)(2,1)}, u32[]{:S(2)}, u32[]{:S(2)}) collective-permute-start(bf16[384,1664]{1,0:T(8,128)(2,1)} %add_convert_fusion.4), channel_id=1, source_target_pairs={{0,2},{1,3},{2,4},{3,5},{4,6},{5,7},{6,0},{7,1},{8,10},{9,11},{10,... | collective-permute-start | bytes 3833864 | tf_op jit(solution)/shard_map/ppermute | solution.py:124
  442.5 54.4 %collective-permute-start.45 = (bf16[2,4608,128]{2,1,0:T(8,128)(2,1)}, bf16[2,4608,128]{2,1,0:T(8,128)(2,1)}, u32[]{:S(2)}, u32[]{:S(2)}) collective-permute-start(bf16[2,4608,128]{2,1,0:T(8,128)(2,1)} %pad_maximum_fusion.2), channel_id=1, source_target_pairs={{0,8},{8,0},{16,24},{24,16},{1,9},{9,1},{17,25},{25,17},{2,10},{10... | collective-permute-start | bytes 7077896 | tf_op jit(solution)/shard_map/ppermute | solution.py:42
  445.5 54.4 %collective-permute-start.46 = (bf16[2,4608,128]{2,1,0:T(8,128)(2,1)}, bf16[2,4608,128]{2,1,0:T(8,128)(2,1)}, u32[]{:S(2)}, u32[]{:S(2)}) collective-permute-start(bf16[2,4608,128]{2,1,0:T(8,128)(2,1)} %pad_maximum_fusion.3), channel_id=1, source_target_pairs={{0,16},{8,24},{16,0},{24,8},{1,17},{9,25},{17,1},{25,9},{2,18},{10... | collective-permute-start | bytes 7077896 | tf_op jit(solution)/shard_map/ppermute | solution.py:42
  473.9 31.6 %collective-permute-start.43 = (bf16[384,1664]{1,0:T(8,128)(2,1)S(1)}, bf16[384,1664]{1,0:T(8,128)(2,1)S(1)}, u32[]{:S(2)}, u32[]{:S(2)}) collective-permute-start(bf16[384,1664]{1,0:T(8,128)(2,1)S(1)} %add_convert_fusion.1), channel_id=1, source_target_pairs={{0,2},{1,3},{2,4},{3,5},{4,6},{5,7},{6,0},{7,1},{8,10},{9,11},{10,... | collective-permute-start | bytes 3833864 | tf_op jit(solution)/shard_map/ppermute | solution.py:124
  474.1 47.4 %collective-permute-start.47 = (bf16[1,4608,128]{2,1,0:T(8,128)(2,1)S(1)}, bf16[1,4608,128]{2,1,0:T(8,128)(2,1)S(1)}, u32[]{:S(2)}, u32[]{:S(2)}) collective-permute-start(bf16[1,4608,128]{2,1,0:T(8,128)(2,1)S(1)} %copy-done.113), channel_id=1, source_target_pairs={{0,8},{8,0},{16,24},{24,16},{1,9},{9,1},{17,25},{25,17},{2,10},{10... | collective-permute-start | bytes 3538952 | tf_op jit(solution)/shard_map/ppermute | solution.py:42
  475.2 49.3 %collective-permute-start.48 = (bf16[1,4608,128]{2,1,0:T(8,128)(2,1)S(1)}, bf16[1,4608,128]{2,1,0:T(8,128)(2,1)S(1)}, u32[]{:S(2)}, u32[]{:S(2)}) collective-permute-start(bf16[1,4608,128]{2,1,0:T(8,128)(2,1)S(1)} %copy-done.112), channel_id=1, source_target_pairs={{0,16},{8,24},{16,0},{24,8},{1,17},{9,25},{17,1},{25,9},{2,18},{10... | collective-permute-start | bytes 3538952 | tf_op jit(solution)/shard_map/ppermute | solution.py:42
  525.8 19.5 %all-to-all-start.2 = ((bf16[4,384,384]{2,1,0:T(8,128)(2,1)}), bf16[4,384,384]{2,1,0:T(8,128)(2,1)}, u32[]{:S(2)}, u32[]{:S(2)}) async-start(bf16[4,384,384]{2,1,0:T(8,128)(2,1)} %copy-done.14), calls=%async_computation.2 | async-start | bytes 2359296 | tf_op jit(solution)/shard_map/all_to_all | solution.py:1142
  535.5 54.5 %collective-permute-start.44 = (bf16[384,1536]{1,0:T(8,128)(2,1)}, bf16[384,1536]{1,0:T(8,128)(2,1)}, u32[]{:S(2)}, u32[]{:S(2)}) collective-permute-start(bf16[384,1536]{1,0:T(8,128)(2,1)} %add_convert_fusion.14), channel_id=1, source_target_pairs={{0,2},{1,3},{2,4},{3,5},{4,6},{5,7},{6,0},{7,1},{8,10},{9,11},{10,... | collective-permute-start | bytes 3538952 | tf_op jit(solution)/shard_map/ppermute | solution.py:124
  545.3 37.2 %all-to-all-start.3 = ((bf16[4,4,48,1664]{3,2,1,0:T(8,128)(2,1)}), bf16[4,4,48,1664]{3,2,1,0:T(8,128)(2,1)}, u32[]{:S(2)}, u32[]{:S(2)}) async-start(bf16[4,4,48,1664]{3,2,1,0:T(8,128)(2,1)} %add_convert_fusion), calls=%async_computation.3 | async-start | bytes 5111808 | tf_op jit(solution)/shard_map/all_to_all | solution.py:1145
  592.6 43.8 %collective-permute-start.50 = (bf16[384,1536]{1,0:T(8,128)(2,1)}, bf16[384,1536]{1,0:T(8,128)(2,1)}, u32[]{:S(2)}, u32[]{:S(2)}) collective-permute-start(bf16[384,1536]{1,0:T(8,128)(2,1)} %add_convert_fusion.10), channel_id=1, source_target_pairs={{0,2},{1,3},{2,4},{3,5},{4,6},{5,7},{6,0},{7,1},{8,10},{9,11},{10,... | collective-permute-start | bytes 3538952 | tf_op jit(solution)/shard_map/ppermute | solution.py:124
  613.9 88.3 %collective-permute-start.54 = (bf16[384,1536]{1,0:T(8,128)(2,1)}, bf16[384,1536]{1,0:T(8,128)(2,1)}, u32[]{:S(2)}, u32[]{:S(2)}) collective-permute-start(bf16[384,1536]{1,0:T(8,128)(2,1)} %pad_maximum_fusion.7), channel_id=1, source_target_pairs={{0,8},{8,0},{16,24},{24,16},{1,9},{9,1},{17,25},{25,17},{2,10},{10... | collective-permute-start | bytes 3538952 | tf_op jit(solution)/shard_map/ppermute | solution.py:42
  615.7 86.5 %collective-permute-start.55 = (bf16[384,1536]{1,0:T(8,128)(2,1)}, bf16[384,1536]{1,0:T(8,128)(2,1)}, u32[]{:S(2)}, u32[]{:S(2)}) collective-permute-start(bf16[384,1536]{1,0:T(8,128)(2,1)} %pad_maximum_fusion.8), channel_id=1, source_target_pairs={{0,16},{8,24},{16,0},{24,8},{1,17},{9,25},{17,1},{25,9},{2,18},{10... | collective-permute-start | bytes 3538952 | tf_op jit(solution)/shard_map/ppermute | solution.py:42
  622.7 54.8 %all-to-all-start.5 = ((bf16[4,192,640]{2,1,0:T(8,128)(2,1)}), bf16[4,192,640]{2,1,0:T(8,128)(2,1)}, u32[]{:S(2)}, u32[]{:S(2)}) async-start(bf16[4,192,640]{2,1,0:T(8,128)(2,1)} %fusion.9), calls=%async_computation.5 | async-start | bytes 1966080 | tf_op jit(solution)/shard_map/all_to_all | solution.py:155
  631.2 60.7 %collective-permute-start.56 = (bf16[2,4608,128]{2,1,0:T(8,128)(2,1)}, bf16[2,4608,128]{2,1,0:T(8,128)(2,1)}, u32[]{:S(2)}, u32[]{:S(2)}) collective-permute-start(bf16[2,4608,128]{2,1,0:T(8,128)(2,1)} %pad_maximum_fusion.4), channel_id=1, source_target_pairs={{0,8},{8,0},{16,24},{24,16},{1,9},{9,1},{17,25},{25,17},{2,10},{10... | collective-permute-start | bytes 7077896 | tf_op jit(solution)/shard_map/ppermute | solution.py:42
  634.8 58.6 %collective-permute-start.57 = (bf16[2,4608,128]{2,1,0:T(8,128)(2,1)}, bf16[2,4608,128]{2,1,0:T(8,128)(2,1)}, u32[]{:S(2)}, u32[]{:S(2)}) collective-permute-start(bf16[2,4608,128]{2,1,0:T(8,128)(2,1)} %pad_maximum_fusion.5), channel_id=1, source_target_pairs={{0,16},{8,24},{16,0},{24,8},{1,17},{9,25},{17,1},{25,9},{2,18},{10... | collective-permute-start | bytes 7077896 | tf_op jit(solution)/shard_map/ppermute | solution.py:42
  638.9 46.0 %collective-permute-start.53 = (bf16[384,1536]{1,0:T(8,128)(2,1)}, bf16[384,1536]{1,0:T(8,128)(2,1)}, u32[]{:S(2)}, u32[]{:S(2)}) collective-permute-start(bf16[384,1536]{1,0:T(8,128)(2,1)} %add_convert_fusion.9), channel_id=1, source_target_pairs={{0,2},{1,3},{2,4},{3,5},{4,6},{5,7},{6,0},{7,1},{8,10},{9,11},{10,... | collective-permute-start | bytes 3538952 | tf_op jit(solution)/shard_map/ppermute | solution.py:124
  680.6 38.0 %all-to-all-start.6 = ((bf16[4,48,1664]{2,1,0:T(8,128)(2,1)}), bf16[4,48,1664]{2,1,0:T(8,128)(2,1)}, u32[]{:S(2)}, u32[]{:S(2)}) async-start(bf16[4,48,1664]{2,1,0:T(8,128)(2,1)} %reduce_sum.82), calls=%async_computation.6 | async-start | bytes 1277952 | tf_op jit(solution)/shard_map/all_to_all | solution.py:155
  (136 other events, 1260.5 us)

commit v5 on v4

--- a/solution.py
+++ b/solution.py
@@ -314,7 +314,7 @@
             jax.ShapeDtypeStruct((length, 8), f32),
         ],
         compiler_params=call_params(32),
-        cost_estimate=cost(16),
+        cost_estimate=cost(5),
         name="attend",
     )(meta, queries, keys, values, starts)
 
@@ -969,10 +969,6 @@
     project_found = jnp.stack([rows[:, :qkv_cols] for rows in found])
     project_swapped = core_swap(project_found)
 
-    out_half = jnp.stack([rows[:, qkv_cols:].reshape(sixth, width) for rows in found])
-    out_half = chips_in_order(out_half, chip).reshape(chips * sixth, width)
-    out_near = gather_near(after(out_half, token_parts[3]))
-
     expert_rows = expert_ids[0]
     lane_range = jnp.arange(LANES, dtype=jnp.int32)
     member = jnp.any(expert_rows[:, :, None] == lane_range[None, None, :], axis=1).astype(bf16)
@@ -985,7 +981,7 @@
     for group in range(groups):
         here = slice(group * group_size, (group + 1) * group_size)
         packed.append(pack_weights(after(w_gate[here], own_tokens), w_up[here], w_down[here]))
-    weight_near = [gather_near(after(packed[0], token_parts[3], project_swapped, out_half))]
+    weight_near = [gather_near(after(packed[0], token_parts[3], project_swapped))]
 
     segments = segment_ids[0]
     length = segments.shape[0]
@@ -1004,14 +1000,18 @@
     queries, key_rows, value_rows, normed, project_w = project(
         meta, token_parts, project_found, project_swapped, gain_attn, cosine, sine, q_cols, k_cols
     )
+    found = after(found, queries)
+    out_half = jnp.stack([rows[:, qkv_cols:].reshape(sixth, width) for rows in found])
+    out_half = chips_in_order(out_half, chip).reshape(chips * sixth, width)
+    out_near = gather_near(out_half)
     attended, lse = attend(meta, queries, key_rows, value_rows, starts[:, None], tok)
-    cot_same[1], out_near = after((cot_same[1], out_near), attended)
-    cot_other = [core_swap(rows) for rows in cot_same]
-    for d in range(2, chips):
-        cot_same.append(chip_shift(cot_same[-1], 1))
-    attended, out_near = after((attended, out_near), weight_near[0], cot_same[2], cot_other)
+    cot_same[1] = after(cot_same[1], attended)
+    cot_same.append(chip_shift(cot_same[1], 1))
+    out_near = after(out_near, weight_near[0], attended)
+    attended = after(attended, weight_near[0], cot_same[1])
     own_heads = lax.all_to_all(attended, "rows", 0, 0, tiled=True)
     out_mine = jnp.stack(gather_far(out_half, *out_near)).reshape(4, chips, sixth, width)
+    out_mine = after(out_mine, cot_same[2])
     out_parts = cores_in_order(out_mine, core_swap(out_mine), core, 2).reshape(4, tok, width)
     weight_near[0] = after(weight_near[0], own_heads)
     first_far = far_halves(*weight_near[0])
@@ -1028,10 +1028,15 @@
     weight_parts = [join_far(packed[0], *weight_near[0], after(first_far, moe_rows))]
     for group in range(1, groups):
         weight_near.append(gather_near(after(packed[group], weight_parts[0][3])))
-    moe_same = [moe_rows, chip_shift(after(moe_rows, cot_same[3], weight_parts[0][3]), 1)]
+    cot_other = [core_swap(after(rows, own_heads)) for rows in cot_same[:2]]
+    moe_same = [
+        moe_rows, chip_shift(after(moe_rows, cot_same[2], cot_other, weight_parts[0][3]), 1)
+    ]
+    for d in range(3, chips):
+        cot_same.append(chip_shift(after(cot_same[-1], moe_same[1]), 1))
     moe_other = [core_swap(rows) for rows in moe_same]
     moe_same.append(chip_shift(moe_same[1], 1))
-    cot_other += [core_swap(rows) for rows in cot_same[2:]]
+    cot_other += [core_swap(after(rows, moe_rows)) for rows in cot_same[2:]]
 
     moe_meta = jnp.stack([row, column * own_experts]).astype(jnp.int32)
     ffe = w_down.shape[1]
@@ -1094,7 +1099,7 @@
                 early[index] = result[4:]
                 continue
             if index == 0:
-                result = after(result, moe_same[3])
+                result = after(result, moe_same[3], cot_same[3])
             if index == len(pairs) - 1:
                 result = after(result, dx_hop, far if groups > 1 else ())
             kept[group].append(result[4:8])
@@ -1171,9 +1176,9 @@
     project_pairs = project_pairs.reshape(chips, 2, width // columns, qkv_cols)
     project_chip = cores_sum(project_pairs.transpose(1, 0, 2, 3))
     project_came = chips_exchange(project_chip)
-    project_sum = jnp.sum(after(project_came, late[-1]).astype(f32), axis=0)
+    project_sum = jnp.sum(project_came.astype(f32), axis=0)
     grad_normed = add_wide([normed_parts[0], *after(normed_near, project_sum)])
-    wide_row = add_low_all(after(wide_came, project_came))
+    wide_row = add_low_all(after(wide_came, project_came, late[-1]))
     wide_sum = jnp.sum(chips_exchange(wide_row).astype(f32), axis=0)
     grad_out_w = wide_sum[:, :width]
     grad_router_w = wide_sum[:, width : width + experts]
@@ -1182,7 +1187,7 @@
     out_ring = add_low(after(out_hop, grad_lin), outs[2])
     for d in range(3, chips):
         out_ring = add_low(after(chip_shift(out_ring, 1), *normed_sums), outs[d])
-    moe_out = add_wide([after(chip_shift(out_ring, 1), project_chip), outs[0]])
+    moe_out = add_wide([chip_shift(after(out_ring, project_came), 1), outs[0]])
     block_out = mixed_rows + res_scale * moe_out
 
     totals = []
@@ -1196,7 +1201,6 @@
     own_w = jnp.concatenate([w_query, key_matrix, value_matrix], axis=1).astype(f32)
     own_gain = lax.dynamic_slice_in_dim(gain_attn[0], column * own_w.shape[0], own_w.shape[0], 0)
     gain_rows = (jnp.sum(project_sum * own_w, axis=1) / own_gain).reshape(4, -1)
-    gain_rows = after(gain_rows, wide_sum)
     gain_sum = jnp.sum(lax.all_to_all(gain_rows, "rows", 0, 0, tiled=True), axis=0)
     grad_gain_attn = lax.ppermute(
         gain_sum,

time: 745 us -> 741 us (level)
    ppermute x15, waiting for transfers between devices: 75.2 us -> 51.1 us  [chip_shift(): lax.ppermute(array, 'cols', [(i, (i + 2 * distance) % count) for i in ran...]
    ppermute x28, waiting for transfers between devices: 94.2 us -> 114 us  [rows_swap(): return lax.ppermute(array, 'rows', [(i, i ^ distance) for i in range(4)])]
    all_to_all x1, waiting for transfers between devices: 1.51 us -> 15.1 us  [per_device(): lax.all_to_all(gain_rows, 'rows', 0, 0, tiled=True)]
    all_to_all x2, waiting for transfers between devices: 30.4 us -> 18.2 us  [chips_exchange(): lax.all_to_all(array, 'cols', 0, 0, axis_index_groups=alike, tiled=True)]
    ppermute x15, starting transfers between devices: 20.1 us -> 11.5 us  [chip_shift(): lax.ppermute(array, 'cols', [(i, (i + 2 * distance) % count) for i in ran...]
    unnamed x258 -> x230, local copies, waits for them, and re-layouts: 44.4 us -> 50.5 us
  transfers between devices with their start and end apart: 66 -> 66, of which waited for: 31 -> 33; matrix products, arithmetic and copies ran while one was open for 22% -> 21% of each run, Pallas kernels for 28% -> 28%
where the time goes in v5:
time: 741 us; the launch traced here: 731 us
  waiting for transfers between devices  235 us (32%)
  Pallas kernels  207 us (28%)
  other arithmetic  98 us (13%)
  starting transfers between devices  84.5 us (11%)
  local copies, waits for them, and re-layouts  83.8 us (11%)
  matrix products  11.4 us (2%)
  blocking collectives  8.32 us (1%)
    pallas_call x4, Pallas kernels, run_experts(): pl.pallas_call(partial(experts_kernel, experts=experts, slots=slots, loca...  114 us
    ppermute x28, waiting for transfers between devices, rows_swap(): return lax.ppermute(array, 'rows', [(i, i ^ distance) for i in range(4)])  114 us
    ppermute x15, waiting for transfers between devices, chip_shift(): lax.ppermute(array, 'cols', [(i, (i + 2 * distance) % count) for i in ran...  51.1 us
    unnamed x230, local copies, waits for them, and re-layouts  50.5 us
    convert_element_type x19, other arithmetic, add_low(): return (left.astype(f32) + right.astype(f32)).astype(bf16)  40.1 us
    pallas_call x2, Pallas kernels, weight_grads(): pl.pallas_call(partial(weight_grad_kernel, chunks=chunks, own_count=own),...  32.4 us
    ppermute x28, starting transfers between devices, rows_swap(): return lax.ppermute(array, 'rows', [(i, i ^ distance) for i in range(4)])  24.6 us
    pallas_call x1, Pallas kernels, attend_back(): pl.pallas_call(partial(attend_back_kernel, bands=min(blocks, LONGEST_DOC...  23.6 us
  transfers between devices with their start and end apart: 66, of which 33 were waited for; matrix products, arithmetic and copies ran while one was open for 21% of the time, Pallas kernels for 28%

profile of v5, /device:TPU:6, one launch (start us, length us, event | category | flops | bytes accessed | tf_op | source)
XLA Modules:
  0.0 730.9 jit_solution(11741139858511364359)
XLA Ops:
  14.2 4.7 all-to-all-start
  41.6 14.2 %collective-permute-done.2 = bf16[192,1536]{1,0:T(8,128)(2,1)S(1)} collective-permute-done((bf16[192,1536]{1,0:T(8,128)(2,1)S(1)}, bf16[192,1536]{1,0:T(8,128)(2,1)S(1)}, u32[]{:S(2)}, u32[]{:S(2)}) %collective-permute-start.2) | collective-permute-done | bytes 589856 | tf_op jit(solution)/shard_map/ppermute | solution.py:42
  74.2 9.4 %project.1 = (bf16[1536,384]{1,0:T(8,128)(2,1)S(1)}, bf16[1536,128]{1,0:T(8,128)(2,1)S(1)}, bf16[1536,128]{1,0:T(8,128)(2,1)S(1)}, bf16[4,384,1536]{2,1,0:T(8,128)(2,1)S(1)}, bf16[1536,640]{1,0:T(8,128)(2,1)S(1)}) custom-call(s32[7]{0:T(128)S(1)} %pad_add_fusion.meta, bf16[384,1536]{1,0:T(8,128)(2,1)S(1)} %bitcast.69, bf16[384,1536]{1,0:T(8,128)(2,1)S(1)} %copy-done.23, ...), custom_call_target="tpu_custom_call" | custom-call | flops 11500000256 | tf_op jit(solution)/shard_map/project/pallas_call | solution.py:229
  100.4 13.2 %attend.1 = (bf16[4,384,384]{2,1,0:T(8,128)(2,1)}, f32[1536,8]{1,0:T(8,128)S(1)}) custom-call(s32[7]{0:T(128)S(1)} %pad_add_fusion.meta, bf16[1536,384]{1,0:T(8,128)(2,1)S(1)} %copy-done.33, bf16[1536,128]{1,0:T(8,128)(2,1)S(1)} %get-tuple-element.161.keys, bf16[1536,128]{1,0:T(8,128)(2,1)S(1)} %copy-done.38, s32[1536,1]{1,0:T(8,128)S(1)} %reduce_sum.86.starts), custom_call_target="tpu_custom_call" | custom-call | flops 5750000128 | tf_op jit(solution)/shard_map/attend/pallas_call | solution.py:296
  115.3 18.3 %collective-permute-done.11 = bf16[192,1536]{1,0:T(8,128)(2,1)S(1)} collective-permute-done((bf16[192,1536]{1,0:T(8,128)(2,1)S(1)}, bf16[192,1536]{1,0:T(8,128)(2,1)S(1)}, u32[]{:S(2)}, u32[]{:S(2)}) %collective-permute-start.11) | collective-permute-done | bytes 589856 | tf_op jit(solution)/shard_map/ppermute | solution.py:42
  136.3 6.7 collective-permute-done.14
  147.9 4.9 all-to-all-start.1
  153.0 14.4 %all-to-all-done.1.heads = bf16[4,384,384]{2,1,0:T(8,128)(2,1)S(1)} async-done(((bf16[4,384,384]{2,1,0:T(8,128)(2,1)}), bf16[4,384,384]{2,1,0:T(8,128)(2,1)S(1)}, u32[]{:S(2)}, u32[]{:S(2)}) %all-to-all-start.1) | async-done | bytes 1179680 | tf_op jit(solution)/shard_map/all_to_all | solution.py:1012
  176.7 4.3 mix.1
  181.1 16.1 %collective-permute-done.20 = bf16[1,4608,128]{2,1,0:T(8,128)(2,1)S(1)} collective-permute-done((bf16[1,4608,128]{2,1,0:T(8,128)(2,1)S(1)}, bf16[1,4608,128]{2,1,0:T(8,128)(2,1)S(1)}, u32[]{:S(2)}, u32[]{:S(2)}) %collective-permute-start.20) | collective-permute-done | bytes 1179680 | tf_op jit(solution)/shard_map/ppermute | solution.py:42
  202.2 28.6 %collective-permute-done.22.refs_2_ = bf16[384,1664]{1,0:T(8,128)(2,1)} collective-permute-done((bf16[384,1664]{1,0:T(8,128)(2,1)S(1)}, bf16[384,1664]{1,0:T(8,128)(2,1)}, u32[]{:S(2)}, u32[]{:S(2)}) %collective-permute-start.22) | collective-permute-done | bytes 1277984 | tf_op jit(solution)/shard_map/ppermute | solution.py:124
  234.2 24.0 %experts.4 = (bf16[2,512,1536]{2,1,0:T(8,128)(2,1)}, bf16[2,512,1536]{2,1,0:T(8,128)(2,1)}, bf16[2,512,512]{2,1,0:T(8,128)(2,1)}, bf16[2,512,1024]{2,1,0:T(8,128...) custom-call(s32[2]{0:T(128)} %pad_add_fusion.1.meta, ...), custom_call_target="tpu_custom_call" | custom-call | flops 4600000000 | tf_op jit(solution)/shard_map/experts/pallas_call | solution.py:777
  258.3 5.2 collective-permute-done.24.refs_0_
  268.3 24.1 %collective-permute-done.27 = bf16[1,4608,128]{2,1,0:T(8,128)(2,1)S(1)} collective-permute-done((bf16[1,4608,128]{2,1,0:T(8,128)(2,1)S(1)}, bf16[1,4608,128]{2,1,0:T(8,128)(2,1)S(1)}, u32[]{:S(2)}, u32[]{:S(2)}) %collective-permute-start.27) | collective-permute-done | bytes 1179680 | tf_op jit(solution)/shard_map/ppermute | solution.py:42
  295.6 33.0 %experts.5 = (bf16[384,3200]{1,0:T(8,128)(2,1)}, bf16[384,3200]{1,0:T(8,128)(2,1)}, bf16[384,3200]{1,0:T(8,128)(2,1)}, bf16[384,3200]{1,0:T(8,128)(2,1)}, bf16[2...) custom-call(s32[2]{0:T(128)} %pad_add_fusion.1.meta, ...), custom_call_target="tpu_custom_call" | custom-call | flops 4600000000 | tf_op jit(solution)/shard_map/experts/pallas_call | solution.py:777
  329.9 3.8 collective-permute-done.31
  333.6 3.6 add_convert_fusion.6
  337.3 3.7 collective-permute-done.33.refs_1_
  342.1 24.0 %experts.6 = (bf16[2,512,1536]{2,1,0:T(8,128)(2,1)}, bf16[2,512,1536]{2,1,0:T(8,128)(2,1)}, bf16[2,512,512]{2,1,0:T(8,128)(2,1)}, bf16[2,512,1024]{2,1,0:T(8,128...) custom-call(s32[2]{0:T(128)} %pad_add_fusion.1.meta, ...), custom_call_target="tpu_custom_call" | custom-call | flops 4600000000 | tf_op jit(solution)/shard_map/experts/pallas_call | solution.py:777
  366.1 16.2 %weight_grads.2 = (bf16[1,4608,128]{2,1,0:T(8,128)(2,1)}, bf16[1,4608,128]{2,1,0:T(8,128)(2,1)}, bf16[1,4608,128]{2,1,0:T(8,128)(2,1)}, bf16[1,4608,128]{2,1,0:T...) custom-call(bf16[2,512,1536]{2,1,0:T(8,128)(2,1)} %get-tuple-element, ...), custom_call_target="tpu_custom_call" | custom-call | flops 14949999616 | tf_op jit(solution)/shard_map/weight_grads/pallas_call | solution.py:856
  384.4 33.3 %experts.7 = (bf16[384,3200]{1,0:T(8,128)(2,1)}, bf16[384,3200]{1,0:T(8,128)(2,1)}, bf16[384,3200]{1,0:T(8,128)(2,1)}, bf16[384,3200]{1,0:T(8,128)(2,1)}, bf16[2...) custom-call(s32[2]{0:T(128)} %pad_add_fusion.1.meta, ...), custom_call_target="tpu_custom_call" | custom-call | flops 4600000000 | tf_op jit(solution)/shard_map/experts/pallas_call | solution.py:777
  435.9 16.2 %weight_grads.3 = (bf16[1,4608,128]{2,1,0:T(8,128)(2,1)}, bf16[1,4608,128]{2,1,0:T(8,128)(2,1)}, bf16[1,4608,128]{2,1,0:T(8,128)(2,1)}, bf16[1,4608,128]{2,1,0:T...) custom-call(bf16[2,512,1536]{2,1,0:T(8,128)(2,1)} %get-tuple-element, ...), custom_call_target="tpu_custom_call" | custom-call | flops 14949999616 | tf_op jit(solution)/shard_map/weight_grads/pallas_call | solution.py:856
  452.2 5.8 collective-permute-done.40
  474.1 9.2 %collective-permute-done.45 = bf16[2,4608,128]{2,1,0:T(8,128)(2,1)} collective-permute-done((bf16[2,4608,128]{2,1,0:T(8,128)(2,1)}, bf16[2,4608,128]{2,1,0:T(8,128)(2,1)}, u32[]{:S(2)}, u32[]{:S(2)}) %collective-permute-start.45) | collective-permute-done | bytes 2359328 | tf_op jit(solution)/shard_map/ppermute | solution.py:42
  483.4 4.7 collective-permute-done.46
  488.0 3.2 collective-permute-done.43.came
  491.3 10.2 %unmix.1 = (f32[384,1536]{1,0:T(8,128)S(1)}, bf16[4,384,384]{2,1,0:T(8,128)(2,1)S(1)}, bf16[4,4,48,1664]{3,2,1,0:T(8,128)(2,1)S(1)}, bf16[4,4,48,1664]{3,2,1,0:T(8,128)(2,1)}) custom-call(s32[7]{0:T(128)S(1)} %pad_add_fusion.meta, bf16[384,1664]{1,0:T(8,128)(2,1)S(1)} %collective-permute-done.43.came, bf16[384,1664]{1,0:T(8,128)(2,1)S(1)} %copy-done.8, ...), custom_call_target="tpu_custom_call" | custom-call | flops 13799999488 | tf_op jit(solution)/shard_map/unmix/pallas_call | solution.py:520
  508.0 4.4 collective-permute-done.48
  513.7 5.7 all-to-all-start.2
  523.3 4.6 add_convert_fusion
  527.9 5.1 all-to-all-done.2.grads
  533.0 6.0 all-to-all-start.3
  545.3 23.6 %attend_back.1 = bf16[4,384,640]{2,1,0:T(8,128)(2,1)S(1)} custom-call(s32[7]{0:T(128)S(1)} %pad_add_fusion.meta, bf16[1536,384]{1,0:T(8,128)(2,1)S(1)} %copy-done.34, bf16[4,384,384]{2,1,0:T(8,128)(2,1)} %all-to-all-done.2.grads, f32[8,1536]{1,0:T(8,128)S(1)} %bitcast.77, s32[1,1536]{1,0:T(1,128)S(1)} %broadcast_in_dim.39.starts, ...), custom_call_target="tpu_custom_call" | custom-call | flops 33350000640 | tf_op jit(solution)/shard_map/attend_back/pallas_call | solution.py:400
  581.2 4.0 bitcast_convert_fusion
  585.2 7.7 %collective-permute-done.51 = bf16[192,1536]{1,0:T(8,128)(2,1)S(1)} collective-permute-done((bf16[192,1536]{1,0:T(8,128)(2,1)S(1)}, bf16[192,1536]{1,0:T(8,128)(2,1)S(1)}, u32[]{:S(2)}, u32[]{:S(2)}) %collective-permute-start.51) | collective-permute-done | bytes 589856 | tf_op jit(solution)/shard_map/ppermute | solution.py:42
  596.8 8.3 %all_to_all.48 = bf16[2,4,192,640]{3,2,1,0:T(8,128)(2,1)S(1)} all-to-all(bf16[2,4,192,640]{3,2,1,0:T(8,128)(2,1)S(1)} %bitcast.82), channel_id=1, replica_groups={{0,1},{2,3},{4,5},{6,7},{8,9},{10,11},{12,13},{14,15},{16,17},{18,19},{..., dimensions={0} | all-to-all | bytes 3932160 | tf_op jit(solution)/shard_map/all_to_all | solution.py:148
  606.4 9.2 %all-to-all-start.5 = ((bf16[4,192,640]{2,1,0:T(8,128)(2,1)}), bf16[4,192,640]{2,1,0:T(8,128)(2,1)}, u32[]{:S(2)}, u32[]{:S(2)}) async-start(bf16[4,192,640]{2,1,0:T(8,128)(2,1)} %fusion.9), calls=%async_computation.5 | async-start | bytes 1966080 | tf_op jit(solution)/shard_map/all_to_all | solution.py:155
  624.4 3.1 convert_add_fusion.1
  633.5 7.4 %all-to-all-done.5 = bf16[4,192,640]{2,1,0:T(8,128)(2,1)} async-done(((bf16[4,192,640]{2,1,0:T(8,128)(2,1)}), bf16[4,192,640]{2,1,0:T(8,128)(2,1)}, u32[]{:S(2)}, u32[]{:S(2)}) %all-to-all-start.5) | async-done | bytes 983072 | tf_op jit(solution)/shard_map/all_to_all | solution.py:155
  646.0 6.3 all-to-all-start.7
  655.4 4.1 fusion.6
  660.9 15.1 %all-to-all-done.7 = f32[4,1,48]{2,1,0:T(1,128)} async-done(((f32[4,1,48]{2,1,0:T(1,128)}), f32[4,1,48]{2,1,0:T(1,128)}, u32[]{:S(2)}, u32[]{:S(2)}) %all-to-all-start.7) | async-done | bytes 800 | tf_op jit(solution)/shard_map/all_to_all | solution.py:1204
  676.7 5.0 collective-permute-start.58
  683.1 5.3 collective-permute-done.58
  691.4 4.2 all-to-all-start.6
  695.6 3.5 convert_add_fusion
  707.6 5.3 collective-permute-done.53
  716.1 10.8 %all-to-all-done.6 = bf16[4,48,1664]{2,1,0:T(8,128)(2,1)} async-done(((bf16[4,48,1664]{2,1,0:T(8,128)(2,1)}), bf16[4,48,1664]{2,1,0:T(8,128)(2,1)}, u32[]{:S(2)}, u32[]{:S(2)}) %all-to-all-start.6) | async-done | bytes 639008 | tf_op jit(solution)/shard_map/all_to_all | solution.py:155
  (453 shorter events, 225.0 us)
Async XLA Ops:
  0.7 39.3 %collective-permute-start = (bf16[384,1536]{1,0:T(8,128)(2,1)}, bf16[384,1536]{1,0:T(8,128)(2,1)S(1)}, u32[]{:S(2)}, u32[]{:S(2)}) collective-permute-start(bf16[384,1536]{1,0:T(8,128)(2,1)} %bitcast.67), channel_id=1, source_target_pairs={{0,8},{8,0},{16,24},{24,16},{1,9},{9,1},{17,25},{25,17},{2,10},{10... | collective-permute-start | bytes 3538952 | tf_op jit(solution)/shard_map/ppermute | solution.py:42
  1.3 36.9 %collective-permute-start.1 = (bf16[384,1536]{1,0:T(8,128)(2,1)}, bf16[384,1536]{1,0:T(8,128)(2,1)}, u32[]{:S(2)}, u32[]{:S(2)}) collective-permute-start(bf16[384,1536]{1,0:T(8,128)(2,1)} %bitcast.68), channel_id=1, source_target_pairs={{0,16},{8,24},{16,0},{24,8},{1,17},{9,25},{17,1},{25,9},{2,18},{10... | collective-permute-start | bytes 3538952 | tf_op jit(solution)/shard_map/ppermute | solution.py:42
  4.9 51.3 %collective-permute-start.4 = (bf16[192,1024]{1,0:T(8,128)(2,1)S(1)}, bf16[192,1024]{1,0:T(8,128)(2,1)}, u32[]{:S(2)}, u32[]{:S(2)}) collective-permute-start(bf16[192,1024]{1,0:T(8,128)(2,1)S(1)} %constant_dynamic-update-slice_fusion.2), channel_id=1, source_target_pairs={{0,2},{1,3},{2,4},{3,5},{4,6},{5,7},{6,0},{7,1},{8,10},{9,11},{10,... | collective-permute-start | bytes 1179656 | tf_op jit(solution)/shard_map/ppermute | solution.py:124
  7.0 49.2 %collective-permute-start.5 = (bf16[192,1024]{1,0:T(8,128)(2,1)S(1)}, bf16[192,1024]{1,0:T(8,128)(2,1)}, u32[]{:S(2)}, u32[]{:S(2)}) collective-permute-start(bf16[192,1024]{1,0:T(8,128)(2,1)S(1)} %constant_dynamic-update-slice_fusion.2), channel_id=1, source_target_pairs={{0,4},{1,5},{2,6},{3,7},{4,0},{5,1},{6,2},{7,3},{8,12},{9,13},{10,... | collective-permute-start | bytes 1179656 | tf_op jit(solution)/shard_map/ppermute | solution.py:124
  9.6 46.7 %collective-permute-start.6 = (bf16[192,1024]{1,0:T(8,128)(2,1)S(1)}, bf16[192,1024]{1,0:T(8,128)(2,1)}, u32[]{:S(2)}, u32[]{:S(2)}) collective-permute-start(bf16[192,1024]{1,0:T(8,128)(2,1)S(1)} %constant_dynamic-update-slice_fusion.2), channel_id=1, source_target_pairs={{0,6},{1,7},{2,0},{3,1},{4,2},{5,3},{6,4},{7,5},{8,14},{9,15},{10,... | collective-permute-start | bytes 1179656 | tf_op jit(solution)/shard_map/ppermute | solution.py:124
  14.2 50.6 %all-to-all-start = ((bf16[32,48,128]{2,1,0:T(8,128)(2,1)}), bf16[32,48,128]{2,1,0:T(8,128)(2,1)S(1)}, u32[]{:S(2)}, u32[]{:S(2)}) async-start(bf16[32,48,128]{2,1,0:T(8,128)(2,1)} %tile.2), calls=%async_computation | async-start | bytes 786432 | tf_op jit(solution)/shard_map/all_to_all | solution.py:961
  65.3 48.2 %collective-permute-start.10 = (bf16[384,1664]{1,0:T(8,128)(2,1)}, bf16[384,1664]{1,0:T(8,128)(2,1)}, u32[]{:S(2)}, u32[]{:S(2)}) collective-permute-start(bf16[384,1664]{1,0:T(8,128)(2,1)} %pad_maximum_fusion.6.refs_4_), channel_id=1, source_target_pairs={{0,2},{1,3},{2,4},{3,5},{4,6},{5,7},{6,0},{7,1},{8,10},{9,11},{10,... | collective-permute-start | bytes 3833864 | tf_op jit(solution)/shard_map/ppermute | solution.py:124
  67.4 67.4 %collective-permute-start.8 = (bf16[2,4608,128]{2,1,0:T(8,128)(2,1)}, bf16[2,4608,128]{2,1,0:T(8,128)(2,1)}, u32[]{:S(2)}, u32[]{:S(2)}) collective-permute-start(bf16[2,4608,128]{2,1,0:T(8,128)(2,1)} %get-tuple-element.165.refs_8_), channel_id=1, source_target_pairs={{0,8},{8,0},{16,24},{24,16},{1,9},{9,1},{17,25},{25,17},{2,10},{10... | collective-permute-start | bytes 7077896 | tf_op jit(solution)/shard_map/ppermute | solution.py:42
  68.9 65.9 %collective-permute-start.9 = (bf16[2,4608,128]{2,1,0:T(8,128)(2,1)}, bf16[2,4608,128]{2,1,0:T(8,128)(2,1)}, u32[]{:S(2)}, u32[]{:S(2)}) collective-permute-start(bf16[2,4608,128]{2,1,0:T(8,128)(2,1)} %get-tuple-element.165.refs_8_), channel_id=1, source_target_pairs={{0,16},{8,24},{16,0},{24,8},{1,17},{9,25},{17,1},{25,9},{2,18},{10... | collective-permute-start | bytes 7077896 | tf_op jit(solution)/shard_map/ppermute | solution.py:42
  97.0 36.6 %collective-permute-start.11 = (bf16[192,1536]{1,0:T(8,128)(2,1)S(1)}, bf16[192,1536]{1,0:T(8,128)(2,1)S(1)}, u32[]{:S(2)}, u32[]{:S(2)}) collective-permute-start(bf16[192,1536]{1,0:T(8,128)(2,1)S(1)} %bitcast.87), channel_id=1, source_target_pairs={{0,8},{8,0},{16,24},{24,16},{1,9},{9,1},{17,25},{25,17},{2,10},{10... | collective-permute-start | bytes 1769480 | tf_op jit(solution)/shard_map/ppermute | solution.py:42
  97.6 37.2 %collective-permute-start.12 = (bf16[192,1536]{1,0:T(8,128)(2,1)S(1)}, bf16[192,1536]{1,0:T(8,128)(2,1)S(1)}, u32[]{:S(2)}, u32[]{:S(2)}) collective-permute-start(bf16[192,1536]{1,0:T(8,128)(2,1)S(1)} %bitcast.88), channel_id=1, source_target_pairs={{0,16},{8,24},{16,0},{24,8},{1,17},{9,25},{17,1},{25,9},{2,18},{10... | collective-permute-start | bytes 1769480 | tf_op jit(solution)/shard_map/ppermute | solution.py:42
  113.6 34.3 %collective-permute-start.15 = (bf16[384,1664]{1,0:T(8,128)(2,1)}, bf16[384,1664]{1,0:T(8,128)(2,1)}, u32[]{:S(2)}, u32[]{:S(2)}) collective-permute-start(bf16[384,1664]{1,0:T(8,128)(2,1)} %collective-permute-done.10.refs_6_), channel_id=1, source_target_pairs={{0,2},{1,3},{2,4},{3,5},{4,6},{5,7},{6,0},{7,1},{8,10},{9,11},{10,... | collective-permute-start | bytes 3833864 | tf_op jit(solution)/shard_map/ppermute | solution.py:124
  147.9 24.9 %collective-permute-start.16 = (bf16[4,4,48,1536]{3,2,1,0:T(8,128)(2,1)}, bf16[4,4,48,1536]{3,2,1,0:T(8,128)(2,1)}, u32[]{:S(2)}, u32[]{:S(2)}) collective-permute-start(bf16[4,4,48,1536]{3,2,1,0:T(8,128)(2,1)} %pad_maximum_fusion.1), channel_id=1, source_target_pairs={{0,1},{1,0},{2,3},{3,2},{4,5},{5,4},{6,7},{7,6},{8,9},{9,8},{10,11... | collective-permute-start | bytes 7077896 | tf_op jit(solution)/shard_map/ppermute | solution.py:131
  147.9 19.4 %all-to-all-start.1 = ((bf16[4,384,384]{2,1,0:T(8,128)(2,1)}), bf16[4,384,384]{2,1,0:T(8,128)(2,1)S(1)}, u32[]{:S(2)}, u32[]{:S(2)}) async-start(bf16[4,384,384]{2,1,0:T(8,128)(2,1)} %get-tuple-element.168), calls=%async_computation.1 | async-start | bytes 2359296 | tf_op jit(solution)/shard_map/all_to_all | solution.py:1012
  167.3 32.7 %collective-permute-start.18 = (bf16[384,1664]{1,0:T(8,128)(2,1)}, bf16[384,1664]{1,0:T(8,128)(2,1)S(1)}, u32[]{:S(2)}, u32[]{:S(2)}) collective-permute-start(bf16[384,1664]{1,0:T(8,128)(2,1)} %pad_maximum_fusion.6.refs_4_), channel_id=1, source_target_pairs={{0,1},{1,0},{2,3},{3,2},{4,5},{5,4},{6,7},{7,6},{8,9},{9,8},{10,11... | collective-permute-start | bytes 3833864 | tf_op jit(solution)/shard_map/ppermute | solution.py:131
  167.4 32.8 %collective-permute-start.19 = (bf16[384,1664]{1,0:T(8,128)(2,1)}, bf16[384,1664]{1,0:T(8,128)(2,1)S(1)}, u32[]{:S(2)}, u32[]{:S(2)}) collective-permute-start(bf16[384,1664]{1,0:T(8,128)(2,1)} %collective-permute-done.10.refs_6_), channel_id=1, source_target_pairs={{0,1},{1,0},{2,3},{3,2},{4,5},{5,4},{6,7},{7,6},{8,9},{9,8},{10,11... | collective-permute-start | bytes 3833864 | tf_op jit(solution)/shard_map/ppermute | solution.py:131
  169.2 27.9 %collective-permute-start.20 = (bf16[1,4608,128]{2,1,0:T(8,128)(2,1)S(1)}, bf16[1,4608,128]{2,1,0:T(8,128)(2,1)S(1)}, u32[]{:S(2)}, u32[]{:S(2)}) collective-permute-start(bf16[1,4608,128]{2,1,0:T(8,128)(2,1)S(1)} %slice.342), channel_id=1, source_target_pairs={{0,8},{8,0},{16,24},{24,16},{1,9},{9,1},{17,25},{25,17},{2,10},{10... | collective-permute-start | bytes 3538952 | tf_op jit(solution)/shard_map/ppermute | solution.py:42
  172.1 27.7 %collective-permute-start.21 = (bf16[1,4608,128]{2,1,0:T(8,128)(2,1)S(1)}, bf16[1,4608,128]{2,1,0:T(8,128)(2,1)S(1)}, u32[]{:S(2)}, u32[]{:S(2)}) collective-permute-start(bf16[1,4608,128]{2,1,0:T(8,128)(2,1)S(1)} %slice.343), channel_id=1, source_target_pairs={{0,16},{8,24},{16,0},{24,8},{1,17},{9,25},{17,1},{25,9},{2,18},{10... | collective-permute-start | bytes 3538952 | tf_op jit(solution)/shard_map/ppermute | solution.py:42
  200.1 30.8 %collective-permute-start.22 = (bf16[384,1664]{1,0:T(8,128)(2,1)S(1)}, bf16[384,1664]{1,0:T(8,128)(2,1)}, u32[]{:S(2)}, u32[]{:S(2)}) collective-permute-start(bf16[384,1664]{1,0:T(8,128)(2,1)S(1)} %get-tuple-element.184.refs_0_), channel_id=1, source_target_pairs={{0,2},{1,3},{2,4},{3,5},{4,6},{5,7},{6,0},{7,1},{8,10},{9,11},{10,... | collective-permute-start | bytes 3833864 | tf_op jit(solution)/shard_map/ppermute | solution.py:124
  200.2 63.3 %collective-permute-start.25 = (bf16[2,4608,128]{2,1,0:T(8,128)(2,1)}, bf16[2,4608,128]{2,1,0:T(8,128)(2,1)}, u32[]{:S(2)}, u32[]{:S(2)}) collective-permute-start(bf16[2,4608,128]{2,1,0:T(8,128)(2,1)} %get-tuple-element.192.refs_11_), channel_id=1, source_target_pairs={{0,8},{8,0},{16,24},{24,16},{1,9},{9,1},{17,25},{25,17},{2,10},{10... | collective-permute-start | bytes 7077896 | tf_op jit(solution)/shard_map/ppermute | solution.py:42
  200.8 62.7 %collective-permute-start.26 = (bf16[2,4608,128]{2,1,0:T(8,128)(2,1)}, bf16[2,4608,128]{2,1,0:T(8,128)(2,1)}, u32[]{:S(2)}, u32[]{:S(2)}) collective-permute-start(bf16[2,4608,128]{2,1,0:T(8,128)(2,1)} %get-tuple-element.192.refs_11_), channel_id=1, source_target_pairs={{0,16},{8,24},{16,0},{24,8},{1,17},{9,25},{17,1},{25,9},{2,18},{10... | collective-permute-start | bytes 7077896 | tf_op jit(solution)/shard_map/ppermute | solution.py:42
  202.2 29.3 %collective-permute-start.17 = (bf16[384,1664]{1,0:T(8,128)(2,1)S(1)}, bf16[384,1664]{1,0:T(8,128)(2,1)}, u32[]{:S(2)}, u32[]{:S(2)}) collective-permute-start(bf16[384,1664]{1,0:T(8,128)(2,1)S(1)} %get-tuple-element.184.refs_0_), channel_id=1, source_target_pairs={{0,1},{1,0},{2,3},{3,2},{4,5},{5,4},{6,7},{7,6},{8,9},{9,8},{10,11... | collective-permute-start | bytes 3833864 | tf_op jit(solution)/shard_map/ppermute | solution.py:131
  230.9 32.6 %collective-permute-start.24 = (bf16[384,1664]{1,0:T(8,128)(2,1)}, bf16[384,1664]{1,0:T(8,128)(2,1)}, u32[]{:S(2)}, u32[]{:S(2)}) collective-permute-start(bf16[384,1664]{1,0:T(8,128)(2,1)} %collective-permute-done.22.refs_2_), channel_id=1, source_target_pairs={{0,2},{1,3},{2,4},{3,5},{4,6},{5,7},{6,0},{7,1},{8,10},{9,11},{10,... | collective-permute-start | bytes 3833864 | tf_op jit(solution)/shard_map/ppermute | solution.py:124
  264.9 27.6 %collective-permute-start.27 = (bf16[1,4608,128]{2,1,0:T(8,128)(2,1)S(1)}, bf16[1,4608,128]{2,1,0:T(8,128)(2,1)S(1)}, u32[]{:S(2)}, u32[]{:S(2)}) collective-permute-start(bf16[1,4608,128]{2,1,0:T(8,128)(2,1)S(1)} %slice.356), channel_id=1, source_target_pairs={{0,8},{8,0},{16,24},{24,16},{1,9},{9,1},{17,25},{25,17},{2,10},{10... | collective-permute-start | bytes 3538952 | tf_op jit(solution)/shard_map/ppermute | solution.py:42
  266.8 27.3 %collective-permute-start.28 = (bf16[1,4608,128]{2,1,0:T(8,128)(2,1)S(1)}, bf16[1,4608,128]{2,1,0:T(8,128)(2,1)S(1)}, u32[]{:S(2)}, u32[]{:S(2)}) collective-permute-start(bf16[1,4608,128]{2,1,0:T(8,128)(2,1)S(1)} %slice.357), channel_id=1, source_target_pairs={{0,16},{8,24},{16,0},{24,8},{1,17},{9,25},{17,1},{25,9},{2,18},{10... | collective-permute-start | bytes 3538952 | tf_op jit(solution)/shard_map/ppermute | solution.py:42
  268.3 60.3 %collective-permute-start.30 = (bf16[384,1664]{1,0:T(8,128)(2,1)}, bf16[384,1664]{1,0:T(8,128)(2,1)}, u32[]{:S(2)}, u32[]{:S(2)}) collective-permute-start(bf16[384,1664]{1,0:T(8,128)(2,1)} %collective-permute-done.15.refs_4_), channel_id=1, source_target_pairs={{0,2},{1,3},{2,4},{3,5},{4,6},{5,7},{6,0},{7,1},{8,10},{9,11},{10,... | collective-permute-start | bytes 3833864 | tf_op jit(solution)/shard_map/ppermute | solution.py:124
  268.3 60.4 %collective-permute-start.29 = (bf16[384,1664]{1,0:T(8,128)(2,1)}, bf16[384,1664]{1,0:T(8,128)(2,1)}, u32[]{:S(2)}, u32[]{:S(2)}) collective-permute-start(bf16[384,1664]{1,0:T(8,128)(2,1)} %collective-permute-done.24.refs_0_), channel_id=1, source_target_pairs={{0,2},{1,3},{2,4},{3,5},{4,6},{5,7},{6,0},{7,1},{8,10},{9,11},{10,... | collective-permute-start | bytes 3833864 | tf_op jit(solution)/shard_map/ppermute | solution.py:124
  337.2 80.6 %collective-permute-start.32 = (bf16[384,1664]{1,0:T(8,128)(2,1)}, bf16[384,1664]{1,0:T(8,128)(2,1)}, u32[]{:S(2)}, u32[]{:S(2)}) collective-permute-start(bf16[384,1664]{1,0:T(8,128)(2,1)} %add_convert_fusion.6), channel_id=1, source_target_pairs={{0,2},{1,3},{2,4},{3,5},{4,6},{5,7},{6,0},{7,1},{8,10},{9,11},{10,... | collective-permute-start | bytes 3833864 | tf_op jit(solution)/shard_map/ppermute | solution.py:124
  382.3 35.4 %collective-permute-start.37 = (bf16[1,4608,128]{2,1,0:T(8,128)(2,1)}, bf16[1,4608,128]{2,1,0:T(8,128)(2,1)}, u32[]{:S(2)}, u32[]{:S(2)}) collective-permute-start(bf16[1,4608,128]{2,1,0:T(8,128)(2,1)} %get-tuple-element.222), channel_id=1, source_target_pairs={{0,8},{8,0},{16,24},{24,16},{1,9},{9,1},{17,25},{25,17},{2,10},{10... | collective-permute-start | bytes 3538952 | tf_op jit(solution)/shard_map/ppermute | solution.py:42
  383.9 33.9 %collective-permute-start.38 = (bf16[1,4608,128]{2,1,0:T(8,128)(2,1)}, bf16[1,4608,128]{2,1,0:T(8,128)(2,1)}, u32[]{:S(2)}, u32[]{:S(2)}) collective-permute-start(bf16[1,4608,128]{2,1,0:T(8,128)(2,1)} %get-tuple-element.223), channel_id=1, source_target_pairs={{0,16},{8,24},{16,0},{24,8},{1,17},{9,25},{17,1},{25,9},{2,18},{10... | collective-permute-start | bytes 3538952 | tf_op jit(solution)/shard_map/ppermute | solution.py:42
  384.4 33.9 %collective-permute-start.42 = (bf16[384,3200]{1,0:T(8,128)(2,1)}, bf16[384,3200]{1,0:T(8,128)(2,1)}, u32[]{:S(2)}, u32[]{:S(2)}) collective-permute-start(bf16[384,3200]{1,0:T(8,128)(2,1)} %get-tuple-element.244), channel_id=1, source_target_pairs={{0,1},{1,0},{2,3},{3,2},{4,5},{5,4},{6,7},{7,6},{8,9},{9,8},{10,11... | collective-permute-start | bytes 7372808 | tf_op jit(solution)/shard_map/ppermute | solution.py:131
  425.6 32.3 %collective-permute-start.40 = (bf16[384,1664]{1,0:T(8,128)(2,1)S(1)}, bf16[384,1664]{1,0:T(8,128)(2,1)}, u32[]{:S(2)}, u32[]{:S(2)}) collective-permute-start(bf16[384,1664]{1,0:T(8,128)(2,1)S(1)} %add_convert_fusion.4), channel_id=1, source_target_pairs={{0,2},{1,3},{2,4},{3,5},{4,6},{5,7},{6,0},{7,1},{8,10},{9,11},{10,... | collective-permute-start | bytes 3833864 | tf_op jit(solution)/shard_map/ppermute | solution.py:124
  429.0 54.4 %collective-permute-start.45 = (bf16[2,4608,128]{2,1,0:T(8,128)(2,1)}, bf16[2,4608,128]{2,1,0:T(8,128)(2,1)}, u32[]{:S(2)}, u32[]{:S(2)}) collective-permute-start(bf16[2,4608,128]{2,1,0:T(8,128)(2,1)} %pad_maximum_fusion.2), channel_id=1, source_target_pairs={{0,8},{8,0},{16,24},{24,16},{1,9},{9,1},{17,25},{25,17},{2,10},{10... | collective-permute-start | bytes 7077896 | tf_op jit(solution)/shard_map/ppermute | solution.py:42
  433.6 54.4 %collective-permute-start.46 = (bf16[2,4608,128]{2,1,0:T(8,128)(2,1)}, bf16[2,4608,128]{2,1,0:T(8,128)(2,1)}, u32[]{:S(2)}, u32[]{:S(2)}) collective-permute-start(bf16[2,4608,128]{2,1,0:T(8,128)(2,1)} %pad_maximum_fusion.3), channel_id=1, source_target_pairs={{0,16},{8,24},{16,0},{24,8},{1,17},{9,25},{17,1},{25,9},{2,18},{10... | collective-permute-start | bytes 7077896 | tf_op jit(solution)/shard_map/ppermute | solution.py:42
  459.7 31.6 %collective-permute-start.43 = (bf16[384,1664]{1,0:T(8,128)(2,1)S(1)}, bf16[384,1664]{1,0:T(8,128)(2,1)S(1)}, u32[]{:S(2)}, u32[]{:S(2)}) collective-permute-start(bf16[384,1664]{1,0:T(8,128)(2,1)S(1)} %add_convert_fusion.1), channel_id=1, source_target_pairs={{0,2},{1,3},{2,4},{3,5},{4,6},{5,7},{6,0},{7,1},{8,10},{9,11},{10,... | collective-permute-start | bytes 3833864 | tf_op jit(solution)/shard_map/ppermute | solution.py:124
  459.9 48.0 %collective-permute-start.47 = (bf16[1,4608,128]{2,1,0:T(8,128)(2,1)S(1)}, bf16[1,4608,128]{2,1,0:T(8,128)(2,1)S(1)}, u32[]{:S(2)}, u32[]{:S(2)}) collective-permute-start(bf16[1,4608,128]{2,1,0:T(8,128)(2,1)S(1)} %copy-done.99), channel_id=1, source_target_pairs={{0,8},{8,0},{16,24},{24,16},{1,9},{9,1},{17,25},{25,17},{2,10},{10... | collective-permute-start | bytes 3538952 | tf_op jit(solution)/shard_map/ppermute | solution.py:42
  461.4 50.9 %collective-permute-start.48 = (bf16[1,4608,128]{2,1,0:T(8,128)(2,1)S(1)}, bf16[1,4608,128]{2,1,0:T(8,128)(2,1)S(1)}, u32[]{:S(2)}, u32[]{:S(2)}) collective-permute-start(bf16[1,4608,128]{2,1,0:T(8,128)(2,1)S(1)} %copy-done.98), channel_id=1, source_target_pairs={{0,16},{8,24},{16,0},{24,8},{1,17},{9,25},{17,1},{25,9},{2,18},{10... | collective-permute-start | bytes 3538952 | tf_op jit(solution)/shard_map/ppermute | solution.py:42
  523.3 54.3 %collective-permute-start.44 = (bf16[384,1536]{1,0:T(8,128)(2,1)}, bf16[384,1536]{1,0:T(8,128)(2,1)}, u32[]{:S(2)}, u32[]{:S(2)}) collective-permute-start(bf16[384,1536]{1,0:T(8,128)(2,1)} %add_convert_fusion.14), channel_id=1, source_target_pairs={{0,2},{1,3},{2,4},{3,5},{4,6},{5,7},{6,0},{7,1},{8,10},{9,11},{10,... | collective-permute-start | bytes 3538952 | tf_op jit(solution)/shard_map/ppermute | solution.py:124
  533.0 37.2 %all-to-all-start.3 = ((bf16[4,4,48,1664]{3,2,1,0:T(8,128)(2,1)}), bf16[4,4,48,1664]{3,2,1,0:T(8,128)(2,1)}, u32[]{:S(2)}, u32[]{:S(2)}) async-start(bf16[4,4,48,1664]{3,2,1,0:T(8,128)(2,1)} %add_convert_fusion), calls=%async_computation.3 | async-start | bytes 5111808 | tf_op jit(solution)/shard_map/all_to_all | solution.py:1150
  580.3 50.2 %collective-permute-start.50 = (bf16[384,1536]{1,0:T(8,128)(2,1)}, bf16[384,1536]{1,0:T(8,128)(2,1)}, u32[]{:S(2)}, u32[]{:S(2)}) collective-permute-start(bf16[384,1536]{1,0:T(8,128)(2,1)} %add_convert_fusion.10), channel_id=1, source_target_pairs={{0,2},{1,3},{2,4},{3,5},{4,6},{5,7},{6,0},{7,1},{8,10},{9,11},{10,... | collective-permute-start | bytes 3538952 | tf_op jit(solution)/shard_map/ppermute | solution.py:124
  594.2 48.0 %collective-permute-start.54 = (bf16[384,1536]{1,0:T(8,128)(2,1)}, bf16[384,1536]{1,0:T(8,128)(2,1)}, u32[]{:S(2)}, u32[]{:S(2)}) collective-permute-start(bf16[384,1536]{1,0:T(8,128)(2,1)} %pad_maximum_fusion.7), channel_id=1, source_target_pairs={{0,8},{8,0},{16,24},{24,16},{1,9},{9,1},{17,25},{25,17},{2,10},{10... | collective-permute-start | bytes 3538952 | tf_op jit(solution)/shard_map/ppermute | solution.py:42
  596.0 46.2 %collective-permute-start.55 = (bf16[384,1536]{1,0:T(8,128)(2,1)}, bf16[384,1536]{1,0:T(8,128)(2,1)}, u32[]{:S(2)}, u32[]{:S(2)}) collective-permute-start(bf16[384,1536]{1,0:T(8,128)(2,1)} %pad_maximum_fusion.8), channel_id=1, source_target_pairs={{0,16},{8,24},{16,0},{24,8},{1,17},{9,25},{17,1},{25,9},{2,18},{10... | collective-permute-start | bytes 3538952 | tf_op jit(solution)/shard_map/ppermute | solution.py:42
  606.4 34.5 %all-to-all-start.5 = ((bf16[4,192,640]{2,1,0:T(8,128)(2,1)}), bf16[4,192,640]{2,1,0:T(8,128)(2,1)}, u32[]{:S(2)}, u32[]{:S(2)}) async-start(bf16[4,192,640]{2,1,0:T(8,128)(2,1)} %fusion.9), calls=%async_computation.5 | async-start | bytes 1966080 | tf_op jit(solution)/shard_map/all_to_all | solution.py:155
  619.2 69.1 %collective-permute-start.56 = (bf16[2,4608,128]{2,1,0:T(8,128)(2,1)}, bf16[2,4608,128]{2,1,0:T(8,128)(2,1)}, u32[]{:S(2)}, u32[]{:S(2)}) collective-permute-start(bf16[2,4608,128]{2,1,0:T(8,128)(2,1)} %pad_maximum_fusion.4), channel_id=1, source_target_pairs={{0,8},{8,0},{16,24},{24,16},{1,9},{9,1},{17,25},{25,17},{2,10},{10... | collective-permute-start | bytes 7077896 | tf_op jit(solution)/shard_map/ppermute | solution.py:42
  622.9 65.4 %collective-permute-start.57 = (bf16[2,4608,128]{2,1,0:T(8,128)(2,1)}, bf16[2,4608,128]{2,1,0:T(8,128)(2,1)}, u32[]{:S(2)}, u32[]{:S(2)}) collective-permute-start(bf16[2,4608,128]{2,1,0:T(8,128)(2,1)} %pad_maximum_fusion.5), channel_id=1, source_target_pairs={{0,16},{8,24},{16,0},{24,8},{1,17},{9,25},{17,1},{25,9},{2,18},{10... | collective-permute-start | bytes 7077896 | tf_op jit(solution)/shard_map/ppermute | solution.py:42
  646.0 30.0 %all-to-all-start.7 = ((f32[4,1,48]{2,1,0:T(1,128)}), f32[4,1,48]{2,1,0:T(1,128)}, u32[]{:S(2)}, u32[]{:S(2)}) async-start(f32[4,1,48]{2,1,0:T(1,128)} %all_to_all.38), calls=%async_computation.7 | async-start | bytes 4096 | tf_op jit(solution)/shard_map/all_to_all | solution.py:1204
  681.7 31.2 %collective-permute-start.53 = (bf16[384,1536]{1,0:T(8,128)(2,1)}, bf16[384,1536]{1,0:T(8,128)(2,1)}, u32[]{:S(2)}, u32[]{:S(2)}) collective-permute-start(bf16[384,1536]{1,0:T(8,128)(2,1)} %add_convert_fusion.9), channel_id=1, source_target_pairs={{0,2},{1,3},{2,4},{3,5},{4,6},{5,7},{6,0},{7,1},{8,10},{9,11},{10,... | collective-permute-start | bytes 3538952 | tf_op jit(solution)/shard_map/ppermute | solution.py:124
  691.4 35.4 %all-to-all-start.6 = ((bf16[4,48,1664]{2,1,0:T(8,128)(2,1)}), bf16[4,48,1664]{2,1,0:T(8,128)(2,1)}, u32[]{:S(2)}, u32[]{:S(2)}) async-start(bf16[4,48,1664]{2,1,0:T(8,128)(2,1)} %reduce_sum.82), calls=%async_computation.6 | async-start | bytes 1277952 | tf_op jit(solution)/shard_map/all_to_all | solution.py:155
  (122 other events, 1081.2 us)

commit v6 on v5

--- a/solution.py
+++ b/solution.py
@@ -1176,9 +1176,9 @@
     project_pairs = project_pairs.reshape(chips, 2, width // columns, qkv_cols)
     project_chip = cores_sum(project_pairs.transpose(1, 0, 2, 3))
     project_came = chips_exchange(project_chip)
-    project_sum = jnp.sum(project_came.astype(f32), axis=0)
+    project_sum = jnp.sum(after(project_came, late[-1]).astype(f32), axis=0)
     grad_normed = add_wide([normed_parts[0], *after(normed_near, project_sum)])
-    wide_row = add_low_all(after(wide_came, project_came, late[-1]))
+    wide_row = add_low_all(after(wide_came, project_came))
     wide_sum = jnp.sum(chips_exchange(wide_row).astype(f32), axis=0)
     grad_out_w = wide_sum[:, :width]
     grad_router_w = wide_sum[:, width : width + experts]
@@ -1201,6 +1201,7 @@
     own_w = jnp.concatenate([w_query, key_matrix, value_matrix], axis=1).astype(f32)
     own_gain = lax.dynamic_slice_in_dim(gain_attn[0], column * own_w.shape[0], own_w.shape[0], 0)
     gain_rows = (jnp.sum(project_sum * own_w, axis=1) / own_gain).reshape(4, -1)
+    gain_rows = after(gain_rows, wide_sum)
     gain_sum = jnp.sum(lax.all_to_all(gain_rows, "rows", 0, 0, tiled=True), axis=0)
     grad_gain_attn = lax.ppermute(
         gain_sum,

time: 741 us -> 741 us (level)
  Pallas kernels: 207 us -> 216 us
  starting transfers between devices: 84.5 us -> 76.8 us
    ppermute x28, waiting for transfers between devices: 114 us -> 140 us  [rows_swap(): return lax.ppermute(array, 'rows', [(i, i ^ distance) for i in range(4)])]
    all_to_all x1, waiting for transfers between devices: 15.1 us -> 0.77 us  [per_device(): lax.all_to_all(gain_rows, 'rows', 0, 0, tiled=True)]
    all_to_all x2, waiting for transfers between devices: 18.2 us -> 7.44 us  [chips_exchange(): lax.all_to_all(array, 'cols', 0, 0, axis_index_groups=alike, tiled=True)]
    ppermute x15, waiting for transfers between devices: 51.1 us -> 43.4 us  [chip_shift(): lax.ppermute(array, 'cols', [(i, (i + 2 * distance) % count) for i in ran...]
    unnamed x230 -> x238, local copies, waits for them, and re-layouts: 50.5 us -> 50.6 us
  transfers between devices with their start and end apart: 66 -> 66, of which waited for: 33 -> 33; matrix products, arithmetic and copies ran while one was open for 21% -> 22% of each run, Pallas kernels for 28% -> 30%
where the time goes in v6:
time: 741 us; the launch traced here: 728 us
  waiting for transfers between devices  228 us (31%)
  Pallas kernels  216 us (29%)
  other arithmetic  98.5 us (13%)
  local copies, waits for them, and re-layouts  89.3 us (12%)
  starting transfers between devices  76.8 us (10%)
  matrix products  11.4 us (2%)
    ppermute x28, waiting for transfers between devices, rows_swap(): return lax.ppermute(array, 'rows', [(i, i ^ distance) for i in range(4)])  140 us
    pallas_call x4, Pallas kernels, run_experts(): pl.pallas_call(partial(experts_kernel, experts=experts, slots=slots, loca...  114 us
    unnamed x238, local copies, waits for them, and re-layouts  50.6 us
    ppermute x15, waiting for transfers between devices, chip_shift(): lax.ppermute(array, 'cols', [(i, (i + 2 * distance) % count) for i in ran...  43.4 us
    convert_element_type x19, other arithmetic, add_low(): return (left.astype(f32) + right.astype(f32)).astype(bf16)  40.1 us
    pallas_call x2, Pallas kernels, weight_grads(): pl.pallas_call(partial(weight_grad_kernel, chunks=chunks, own_count=own),...  32.4 us
    pallas_call x1, Pallas kernels, attend_back(): pl.pallas_call(partial(attend_back_kernel, bands=min(blocks, LONGEST_DOC...  29.5 us
    ppermute x28, starting transfers between devices, rows_swap(): return lax.ppermute(array, 'rows', [(i, i ^ distance) for i in range(4)])  24.9 us
  transfers between devices with their start and end apart: 66, of which 33 were waited for; matrix products, arithmetic and copies ran while one was open for 22% of the time, Pallas kernels for 30%

profile of v6, /device:TPU:6, one launch (start us, length us, event | category | flops | bytes accessed | tf_op | source)
XLA Modules:
  0.0 727.5 jit_solution(15315999064100561324)
XLA Ops:
  14.2 4.7 all-to-all-start
  41.5 14.2 %collective-permute-done.2 = bf16[192,1536]{1,0:T(8,128)(2,1)S(1)} collective-permute-done((bf16[192,1536]{1,0:T(8,128)(2,1)S(1)}, bf16[192,1536]{1,0:T(8,128)(2,1)S(1)}, u32[]{:S(2)}, u32[]{:S(2)}) %collective-permute-start.2) | collective-permute-done | bytes 589856 | tf_op jit(solution)/shard_map/ppermute | solution.py:42
  74.2 9.4 %project.1 = (bf16[1536,384]{1,0:T(8,128)(2,1)S(1)}, bf16[1536,128]{1,0:T(8,128)(2,1)S(1)}, bf16[1536,128]{1,0:T(8,128)(2,1)S(1)}, bf16[4,384,1536]{2,1,0:T(8,128)(2,1)S(1)}, bf16[1536,640]{1,0:T(8,128)(2,1)S(1)}) custom-call(s32[7]{0:T(128)S(1)} %pad_add_fusion.meta, bf16[384,1536]{1,0:T(8,128)(2,1)S(1)} %bitcast.69, bf16[384,1536]{1,0:T(8,128)(2,1)S(1)} %copy-done.23, ...), custom_call_target="tpu_custom_call" | custom-call | flops 11500000256 | tf_op jit(solution)/shard_map/project/pallas_call | solution.py:229
  100.3 16.2 %attend.1 = (bf16[4,384,384]{2,1,0:T(8,128)(2,1)}, f32[1536,8]{1,0:T(8,128)S(1)}) custom-call(s32[7]{0:T(128)S(1)} %pad_add_fusion.meta, bf16[1536,384]{1,0:T(8,128)(2,1)S(1)} %copy-done.33, bf16[1536,128]{1,0:T(8,128)(2,1)S(1)} %get-tuple-element.163.keys, bf16[1536,128]{1,0:T(8,128)(2,1)S(1)} %copy-done.38, s32[1536,1]{1,0:T(8,128)S(1)} %reduce_sum.86.starts), custom_call_target="tpu_custom_call" | custom-call | flops 5750000128 | tf_op jit(solution)/shard_map/attend/pallas_call | solution.py:296
  116.7 16.9 %collective-permute-done.11 = bf16[192,1536]{1,0:T(8,128)(2,1)S(1)} collective-permute-done((bf16[192,1536]{1,0:T(8,128)(2,1)S(1)}, bf16[192,1536]{1,0:T(8,128)(2,1)S(1)}, u32[]{:S(2)}, u32[]{:S(2)}) %collective-permute-start.11) | collective-permute-done | bytes 589856 | tf_op jit(solution)/shard_map/ppermute | solution.py:42
  136.2 6.7 collective-permute-done.14
  146.6 4.9 all-to-all-start.1
  151.6 14.4 %all-to-all-done.1.heads = bf16[4,384,384]{2,1,0:T(8,128)(2,1)S(1)} async-done(((bf16[4,384,384]{2,1,0:T(8,128)(2,1)}), bf16[4,384,384]{2,1,0:T(8,128)(2,1)S(1)}, u32[]{:S(2)}, u32[]{:S(2)}) %all-to-all-start.1) | async-done | bytes 1179680 | tf_op jit(solution)/shard_map/all_to_all | solution.py:1012
  175.4 4.3 mix.1
  179.7 16.1 %collective-permute-done.20 = bf16[1,4608,128]{2,1,0:T(8,128)(2,1)S(1)} collective-permute-done((bf16[1,4608,128]{2,1,0:T(8,128)(2,1)S(1)}, bf16[1,4608,128]{2,1,0:T(8,128)(2,1)S(1)}, u32[]{:S(2)}, u32[]{:S(2)}) %collective-permute-start.20) | collective-permute-done | bytes 1179680 | tf_op jit(solution)/shard_map/ppermute | solution.py:42
  201.8 27.8 %collective-permute-done.22.refs_2_ = bf16[384,1664]{1,0:T(8,128)(2,1)} collective-permute-done((bf16[384,1664]{1,0:T(8,128)(2,1)S(1)}, bf16[384,1664]{1,0:T(8,128)(2,1)}, u32[]{:S(2)}, u32[]{:S(2)}) %collective-permute-start.22) | collective-permute-done | bytes 1277984 | tf_op jit(solution)/shard_map/ppermute | solution.py:124
  232.9 24.0 %experts.4 = (bf16[2,512,1536]{2,1,0:T(8,128)(2,1)}, bf16[2,512,1536]{2,1,0:T(8,128)(2,1)}, bf16[2,512,512]{2,1,0:T(8,128)(2,1)}, bf16[2,512,1024]{2,1,0:T(8,128...) custom-call(s32[2]{0:T(128)} %pad_add_fusion.1.meta, ...), custom_call_target="tpu_custom_call" | custom-call | flops 4600000000 | tf_op jit(solution)/shard_map/experts/pallas_call | solution.py:777
  256.9 5.2 collective-permute-done.24.refs_0_
  267.0 24.1 %collective-permute-done.27 = bf16[1,4608,128]{2,1,0:T(8,128)(2,1)S(1)} collective-permute-done((bf16[1,4608,128]{2,1,0:T(8,128)(2,1)S(1)}, bf16[1,4608,128]{2,1,0:T(8,128)(2,1)S(1)}, u32[]{:S(2)}, u32[]{:S(2)}) %collective-permute-start.27) | collective-permute-done | bytes 1179680 | tf_op jit(solution)/shard_map/ppermute | solution.py:42
  294.3 33.0 %experts.5 = (bf16[384,3200]{1,0:T(8,128)(2,1)}, bf16[384,3200]{1,0:T(8,128)(2,1)}, bf16[384,3200]{1,0:T(8,128)(2,1)}, bf16[384,3200]{1,0:T(8,128)(2,1)}, bf16[2...) custom-call(s32[2]{0:T(128)} %pad_add_fusion.1.meta, ...), custom_call_target="tpu_custom_call" | custom-call | flops 4600000000 | tf_op jit(solution)/shard_map/experts/pallas_call | solution.py:777
  328.6 3.8 collective-permute-done.31
  332.4 3.6 add_convert_fusion.6
  336.0 3.7 collective-permute-done.33.refs_1_
  340.8 24.0 %experts.6 = (bf16[2,512,1536]{2,1,0:T(8,128)(2,1)}, bf16[2,512,1536]{2,1,0:T(8,128)(2,1)}, bf16[2,512,512]{2,1,0:T(8,128)(2,1)}, bf16[2,512,1024]{2,1,0:T(8,128...) custom-call(s32[2]{0:T(128)} %pad_add_fusion.1.meta, ...), custom_call_target="tpu_custom_call" | custom-call | flops 4600000000 | tf_op jit(solution)/shard_map/experts/pallas_call | solution.py:777
  364.8 16.2 %weight_grads.2 = (bf16[1,4608,128]{2,1,0:T(8,128)(2,1)}, bf16[1,4608,128]{2,1,0:T(8,128)(2,1)}, bf16[1,4608,128]{2,1,0:T(8,128)(2,1)}, bf16[1,4608,128]{2,1,0:T...) custom-call(bf16[2,512,1536]{2,1,0:T(8,128)(2,1)} %get-tuple-element, ...), custom_call_target="tpu_custom_call" | custom-call | flops 14949999616 | tf_op jit(solution)/shard_map/weight_grads/pallas_call | solution.py:856
  383.1 33.2 %experts.7 = (bf16[384,3200]{1,0:T(8,128)(2,1)}, bf16[384,3200]{1,0:T(8,128)(2,1)}, bf16[384,3200]{1,0:T(8,128)(2,1)}, bf16[384,3200]{1,0:T(8,128)(2,1)}, bf16[2...) custom-call(s32[2]{0:T(128)} %pad_add_fusion.1.meta, ...), custom_call_target="tpu_custom_call" | custom-call | flops 4600000000 | tf_op jit(solution)/shard_map/experts/pallas_call | solution.py:777
  434.6 16.3 %weight_grads.3 = (bf16[1,4608,128]{2,1,0:T(8,128)(2,1)}, bf16[1,4608,128]{2,1,0:T(8,128)(2,1)}, bf16[1,4608,128]{2,1,0:T(8,128)(2,1)}, bf16[1,4608,128]{2,1,0:T...) custom-call(bf16[2,512,1536]{2,1,0:T(8,128)(2,1)} %get-tuple-element, ...), custom_call_target="tpu_custom_call" | custom-call | flops 14949999616 | tf_op jit(solution)/shard_map/weight_grads/pallas_call | solution.py:856
  450.8 5.7 collective-permute-done.40
  472.7 9.3 %collective-permute-done.45 = bf16[2,4608,128]{2,1,0:T(8,128)(2,1)} collective-permute-done((bf16[2,4608,128]{2,1,0:T(8,128)(2,1)}, bf16[2,4608,128]{2,1,0:T(8,128)(2,1)}, u32[]{:S(2)}, u32[]{:S(2)}) %collective-permute-start.45) | collective-permute-done | bytes 2359328 | tf_op jit(solution)/shard_map/ppermute | solution.py:42
  482.0 4.7 collective-permute-done.46
  486.7 3.2 collective-permute-done.43.came
  489.9 10.2 %unmix.1 = (f32[384,1536]{1,0:T(8,128)S(1)}, bf16[4,384,384]{2,1,0:T(8,128)(2,1)S(1)}, bf16[4,4,48,1664]{3,2,1,0:T(8,128)(2,1)S(1)}, bf16[4,4,48,1664]{3,2,1,0:T(8,128)(2,1)}) custom-call(s32[7]{0:T(128)S(1)} %pad_add_fusion.meta, bf16[384,1664]{1,0:T(8,128)(2,1)S(1)} %collective-permute-done.43.came, bf16[384,1664]{1,0:T(8,128)(2,1)S(1)} %copy-done.8, ...), custom_call_target="tpu_custom_call" | custom-call | flops 13799999488 | tf_op jit(solution)/shard_map/unmix/pallas_call | solution.py:520
  506.6 4.4 collective-permute-done.48
  512.3 5.8 all-to-all-start.2
  522.0 4.6 add_convert_fusion
  526.5 5.1 all-to-all-done.2.grads
  531.7 6.0 all-to-all-start.3
  544.0 29.5 %attend_back.1 = bf16[4,384,640]{2,1,0:T(8,128)(2,1)S(1)} custom-call(s32[7]{0:T(128)S(1)} %pad_add_fusion.meta, bf16[1536,384]{1,0:T(8,128)(2,1)S(1)} %copy-done.34, bf16[4,384,384]{2,1,0:T(8,128)(2,1)} %all-to-all-done.2.grads, f32[8,1536]{1,0:T(8,128)S(1)} %bitcast.77, s32[1,1536]{1,0:T(1,128)S(1)} %broadcast_in_dim.39.starts, ...), custom_call_target="tpu_custom_call" | custom-call | flops 33350000640 | tf_op jit(solution)/shard_map/attend_back/pallas_call | solution.py:400
  585.8 4.0 bitcast_convert_fusion
  589.8 7.6 %collective-permute-done.51 = bf16[192,1536]{1,0:T(8,128)(2,1)S(1)} collective-permute-done((bf16[192,1536]{1,0:T(8,128)(2,1)S(1)}, bf16[192,1536]{1,0:T(8,128)(2,1)S(1)}, u32[]{:S(2)}, u32[]{:S(2)}) %collective-permute-start.51) | collective-permute-done | bytes 589856 | tf_op jit(solution)/shard_map/ppermute | solution.py:42
  601.6 5.3 all_to_all.48
  608.1 6.0 all-to-all-start.5
  622.9 3.1 convert_add_fusion.1
  632.0 7.4 %all-to-all-done.5 = bf16[4,192,640]{2,1,0:T(8,128)(2,1)} async-done(((bf16[4,192,640]{2,1,0:T(8,128)(2,1)}), bf16[4,192,640]{2,1,0:T(8,128)(2,1)}, u32[]{:S(2)}, u32[]{:S(2)}) %all-to-all-start.5) | async-done | bytes 983072 | tf_op jit(solution)/shard_map/all_to_all | solution.py:155
  639.6 3.1 reduce_sum.82
  642.8 5.1 all-to-all-start.6
  647.9 25.9 %collective-permute-done.56 = bf16[2,4608,128]{2,1,0:T(8,128)(2,1)} collective-permute-done((bf16[2,4608,128]{2,1,0:T(8,128)(2,1)}, bf16[2,4608,128]{2,1,0:T(8,128)(2,1)}, u32[]{:S(2)}, u32[]{:S(2)}) %collective-permute-start.56) | collective-permute-done | bytes 2359328 | tf_op jit(solution)/shard_map/ppermute | solution.py:42
  675.2 3.8 convert_add_fusion
  689.7 3.4 maximum_maximum_fusion
  699.3 4.0 fusion.6
  705.3 4.6 all-to-all-start.7
  719.2 4.4 collective-permute-done.58
  723.7 3.1 add_bitcast_fusion
  (461 shorter events, 223.3 us)
Async XLA Ops:
  0.7 39.2 %collective-permute-start = (bf16[384,1536]{1,0:T(8,128)(2,1)}, bf16[384,1536]{1,0:T(8,128)(2,1)S(1)}, u32[]{:S(2)}, u32[]{:S(2)}) collective-permute-start(bf16[384,1536]{1,0:T(8,128)(2,1)} %bitcast.67), channel_id=1, source_target_pairs={{0,8},{8,0},{16,24},{24,16},{1,9},{9,1},{17,25},{25,17},{2,10},{10... | collective-permute-start | bytes 3538952 | tf_op jit(solution)/shard_map/ppermute | solution.py:42
  1.3 36.9 %collective-permute-start.1 = (bf16[384,1536]{1,0:T(8,128)(2,1)}, bf16[384,1536]{1,0:T(8,128)(2,1)}, u32[]{:S(2)}, u32[]{:S(2)}) collective-permute-start(bf16[384,1536]{1,0:T(8,128)(2,1)} %bitcast.68), channel_id=1, source_target_pairs={{0,16},{8,24},{16,0},{24,8},{1,17},{9,25},{17,1},{25,9},{2,18},{10... | collective-permute-start | bytes 3538952 | tf_op jit(solution)/shard_map/ppermute | solution.py:42
  4.9 51.3 %collective-permute-start.4 = (bf16[192,1024]{1,0:T(8,128)(2,1)S(1)}, bf16[192,1024]{1,0:T(8,128)(2,1)}, u32[]{:S(2)}, u32[]{:S(2)}) collective-permute-start(bf16[192,1024]{1,0:T(8,128)(2,1)S(1)} %constant_dynamic-update-slice_fusion.2), channel_id=1, source_target_pairs={{0,2},{1,3},{2,4},{3,5},{4,6},{5,7},{6,0},{7,1},{8,10},{9,11},{10,... | collective-permute-start | bytes 1179656 | tf_op jit(solution)/shard_map/ppermute | solution.py:124
  7.0 49.2 %collective-permute-start.5 = (bf16[192,1024]{1,0:T(8,128)(2,1)S(1)}, bf16[192,1024]{1,0:T(8,128)(2,1)}, u32[]{:S(2)}, u32[]{:S(2)}) collective-permute-start(bf16[192,1024]{1,0:T(8,128)(2,1)S(1)} %constant_dynamic-update-slice_fusion.2), channel_id=1, source_target_pairs={{0,4},{1,5},{2,6},{3,7},{4,0},{5,1},{6,2},{7,3},{8,12},{9,13},{10,... | collective-permute-start | bytes 1179656 | tf_op jit(solution)/shard_map/ppermute | solution.py:124
  9.6 46.6 %collective-permute-start.6 = (bf16[192,1024]{1,0:T(8,128)(2,1)S(1)}, bf16[192,1024]{1,0:T(8,128)(2,1)}, u32[]{:S(2)}, u32[]{:S(2)}) collective-permute-start(bf16[192,1024]{1,0:T(8,128)(2,1)S(1)} %constant_dynamic-update-slice_fusion.2), channel_id=1, source_target_pairs={{0,6},{1,7},{2,0},{3,1},{4,2},{5,3},{6,4},{7,5},{8,14},{9,15},{10,... | collective-permute-start | bytes 1179656 | tf_op jit(solution)/shard_map/ppermute | solution.py:124
  14.2 50.5 %all-to-all-start = ((bf16[32,48,128]{2,1,0:T(8,128)(2,1)}), bf16[32,48,128]{2,1,0:T(8,128)(2,1)S(1)}, u32[]{:S(2)}, u32[]{:S(2)}) async-start(bf16[32,48,128]{2,1,0:T(8,128)(2,1)} %tile.2), calls=%async_computation | async-start | bytes 786432 | tf_op jit(solution)/shard_map/all_to_all | solution.py:961
  65.3 51.2 %collective-permute-start.10 = (bf16[384,1664]{1,0:T(8,128)(2,1)}, bf16[384,1664]{1,0:T(8,128)(2,1)}, u32[]{:S(2)}, u32[]{:S(2)}) collective-permute-start(bf16[384,1664]{1,0:T(8,128)(2,1)} %pad_maximum_fusion.6.refs_4_), channel_id=1, source_target_pairs={{0,2},{1,3},{2,4},{3,5},{4,6},{5,7},{6,0},{7,1},{8,10},{9,11},{10,... | collective-permute-start | bytes 3833864 | tf_op jit(solution)/shard_map/ppermute | solution.py:124
  67.3 67.4 %collective-permute-start.8 = (bf16[2,4608,128]{2,1,0:T(8,128)(2,1)}, bf16[2,4608,128]{2,1,0:T(8,128)(2,1)}, u32[]{:S(2)}, u32[]{:S(2)}) collective-permute-start(bf16[2,4608,128]{2,1,0:T(8,128)(2,1)} %get-tuple-element.167.refs_8_), channel_id=1, source_target_pairs={{0,8},{8,0},{16,24},{24,16},{1,9},{9,1},{17,25},{25,17},{2,10},{10... | collective-permute-start | bytes 7077896 | tf_op jit(solution)/shard_map/ppermute | solution.py:42
  68.8 65.9 %collective-permute-start.9 = (bf16[2,4608,128]{2,1,0:T(8,128)(2,1)}, bf16[2,4608,128]{2,1,0:T(8,128)(2,1)}, u32[]{:S(2)}, u32[]{:S(2)}) collective-permute-start(bf16[2,4608,128]{2,1,0:T(8,128)(2,1)} %get-tuple-element.167.refs_8_), channel_id=1, source_target_pairs={{0,16},{8,24},{16,0},{24,8},{1,17},{9,25},{17,1},{25,9},{2,18},{10... | collective-permute-start | bytes 7077896 | tf_op jit(solution)/shard_map/ppermute | solution.py:42
  96.9 36.6 %collective-permute-start.11 = (bf16[192,1536]{1,0:T(8,128)(2,1)S(1)}, bf16[192,1536]{1,0:T(8,128)(2,1)S(1)}, u32[]{:S(2)}, u32[]{:S(2)}) collective-permute-start(bf16[192,1536]{1,0:T(8,128)(2,1)S(1)} %bitcast.87), channel_id=1, source_target_pairs={{0,8},{8,0},{16,24},{24,16},{1,9},{9,1},{17,25},{25,17},{2,10},{10... | collective-permute-start | bytes 1769480 | tf_op jit(solution)/shard_map/ppermute | solution.py:42
  97.6 37.2 %collective-permute-start.12 = (bf16[192,1536]{1,0:T(8,128)(2,1)S(1)}, bf16[192,1536]{1,0:T(8,128)(2,1)S(1)}, u32[]{:S(2)}, u32[]{:S(2)}) collective-permute-start(bf16[192,1536]{1,0:T(8,128)(2,1)S(1)} %bitcast.88), channel_id=1, source_target_pairs={{0,16},{8,24},{16,0},{24,8},{1,17},{9,25},{17,1},{25,9},{2,18},{10... | collective-permute-start | bytes 1769480 | tf_op jit(solution)/shard_map/ppermute | solution.py:42
  116.5 30.1 %collective-permute-start.15 = (bf16[384,1664]{1,0:T(8,128)(2,1)}, bf16[384,1664]{1,0:T(8,128)(2,1)}, u32[]{:S(2)}, u32[]{:S(2)}) collective-permute-start(bf16[384,1664]{1,0:T(8,128)(2,1)} %collective-permute-done.10.refs_6_), channel_id=1, source_target_pairs={{0,2},{1,3},{2,4},{3,5},{4,6},{5,7},{6,0},{7,1},{8,10},{9,11},{10,... | collective-permute-start | bytes 3833864 | tf_op jit(solution)/shard_map/ppermute | solution.py:124
  146.6 24.9 %collective-permute-start.16 = (bf16[4,4,48,1536]{3,2,1,0:T(8,128)(2,1)}, bf16[4,4,48,1536]{3,2,1,0:T(8,128)(2,1)}, u32[]{:S(2)}, u32[]{:S(2)}) collective-permute-start(bf16[4,4,48,1536]{3,2,1,0:T(8,128)(2,1)} %pad_maximum_fusion.1), channel_id=1, source_target_pairs={{0,1},{1,0},{2,3},{3,2},{4,5},{5,4},{6,7},{7,6},{8,9},{9,8},{10,11... | collective-permute-start | bytes 7077896 | tf_op jit(solution)/shard_map/ppermute | solution.py:131
  146.6 19.4 %all-to-all-start.1 = ((bf16[4,384,384]{2,1,0:T(8,128)(2,1)}), bf16[4,384,384]{2,1,0:T(8,128)(2,1)S(1)}, u32[]{:S(2)}, u32[]{:S(2)}) async-start(bf16[4,384,384]{2,1,0:T(8,128)(2,1)} %get-tuple-element.170), calls=%async_computation.1 | async-start | bytes 2359296 | tf_op jit(solution)/shard_map/all_to_all | solution.py:1012
  166.0 32.7 %collective-permute-start.18 = (bf16[384,1664]{1,0:T(8,128)(2,1)}, bf16[384,1664]{1,0:T(8,128)(2,1)S(1)}, u32[]{:S(2)}, u32[]{:S(2)}) collective-permute-start(bf16[384,1664]{1,0:T(8,128)(2,1)} %pad_maximum_fusion.6.refs_4_), channel_id=1, source_target_pairs={{0,1},{1,0},{2,3},{3,2},{4,5},{5,4},{6,7},{7,6},{8,9},{9,8},{10,11... | collective-permute-start | bytes 3833864 | tf_op jit(solution)/shard_map/ppermute | solution.py:131
  166.0 32.8 %collective-permute-start.19 = (bf16[384,1664]{1,0:T(8,128)(2,1)}, bf16[384,1664]{1,0:T(8,128)(2,1)S(1)}, u32[]{:S(2)}, u32[]{:S(2)}) collective-permute-start(bf16[384,1664]{1,0:T(8,128)(2,1)} %collective-permute-done.10.refs_6_), channel_id=1, source_target_pairs={{0,1},{1,0},{2,3},{3,2},{4,5},{5,4},{6,7},{7,6},{8,9},{9,8},{10,11... | collective-permute-start | bytes 3833864 | tf_op jit(solution)/shard_map/ppermute | solution.py:131
  167.9 27.9 %collective-permute-start.20 = (bf16[1,4608,128]{2,1,0:T(8,128)(2,1)S(1)}, bf16[1,4608,128]{2,1,0:T(8,128)(2,1)S(1)}, u32[]{:S(2)}, u32[]{:S(2)}) collective-permute-start(bf16[1,4608,128]{2,1,0:T(8,128)(2,1)S(1)} %slice.342), channel_id=1, source_target_pairs={{0,8},{8,0},{16,24},{24,16},{1,9},{9,1},{17,25},{25,17},{2,10},{10... | collective-permute-start | bytes 3538952 | tf_op jit(solution)/shard_map/ppermute | solution.py:42
  170.8 27.7 %collective-permute-start.21 = (bf16[1,4608,128]{2,1,0:T(8,128)(2,1)S(1)}, bf16[1,4608,128]{2,1,0:T(8,128)(2,1)S(1)}, u32[]{:S(2)}, u32[]{:S(2)}) collective-permute-start(bf16[1,4608,128]{2,1,0:T(8,128)(2,1)S(1)} %slice.343), channel_id=1, source_target_pairs={{0,16},{8,24},{16,0},{24,8},{1,17},{9,25},{17,1},{25,9},{2,18},{10... | collective-permute-start | bytes 3538952 | tf_op jit(solution)/shard_map/ppermute | solution.py:42
  198.8 30.8 %collective-permute-start.22 = (bf16[384,1664]{1,0:T(8,128)(2,1)S(1)}, bf16[384,1664]{1,0:T(8,128)(2,1)}, u32[]{:S(2)}, u32[]{:S(2)}) collective-permute-start(bf16[384,1664]{1,0:T(8,128)(2,1)S(1)} %get-tuple-element.186.refs_0_), channel_id=1, source_target_pairs={{0,2},{1,3},{2,4},{3,5},{4,6},{5,7},{6,0},{7,1},{8,10},{9,11},{10,... | collective-permute-start | bytes 3833864 | tf_op jit(solution)/shard_map/ppermute | solution.py:124
  199.8 62.4 %collective-permute-start.25 = (bf16[2,4608,128]{2,1,0:T(8,128)(2,1)}, bf16[2,4608,128]{2,1,0:T(8,128)(2,1)}, u32[]{:S(2)}, u32[]{:S(2)}) collective-permute-start(bf16[2,4608,128]{2,1,0:T(8,128)(2,1)} %get-tuple-element.194.refs_11_), channel_id=1, source_target_pairs={{0,8},{8,0},{16,24},{24,16},{1,9},{9,1},{17,25},{25,17},{2,10},{10... | collective-permute-start | bytes 7077896 | tf_op jit(solution)/shard_map/ppermute | solution.py:42
  200.3 61.8 %collective-permute-start.26 = (bf16[2,4608,128]{2,1,0:T(8,128)(2,1)}, bf16[2,4608,128]{2,1,0:T(8,128)(2,1)}, u32[]{:S(2)}, u32[]{:S(2)}) collective-permute-start(bf16[2,4608,128]{2,1,0:T(8,128)(2,1)} %get-tuple-element.194.refs_11_), channel_id=1, source_target_pairs={{0,16},{8,24},{16,0},{24,8},{1,17},{9,25},{17,1},{25,9},{2,18},{10... | collective-permute-start | bytes 7077896 | tf_op jit(solution)/shard_map/ppermute | solution.py:42
  201.8 28.4 %collective-permute-start.17 = (bf16[384,1664]{1,0:T(8,128)(2,1)S(1)}, bf16[384,1664]{1,0:T(8,128)(2,1)}, u32[]{:S(2)}, u32[]{:S(2)}) collective-permute-start(bf16[384,1664]{1,0:T(8,128)(2,1)S(1)} %get-tuple-element.186.refs_0_), channel_id=1, source_target_pairs={{0,1},{1,0},{2,3},{3,2},{4,5},{5,4},{6,7},{7,6},{8,9},{9,8},{10,11... | collective-permute-start | bytes 3833864 | tf_op jit(solution)/shard_map/ppermute | solution.py:131
  229.6 32.6 %collective-permute-start.24 = (bf16[384,1664]{1,0:T(8,128)(2,1)}, bf16[384,1664]{1,0:T(8,128)(2,1)}, u32[]{:S(2)}, u32[]{:S(2)}) collective-permute-start(bf16[384,1664]{1,0:T(8,128)(2,1)} %collective-permute-done.22.refs_2_), channel_id=1, source_target_pairs={{0,2},{1,3},{2,4},{3,5},{4,6},{5,7},{6,0},{7,1},{8,10},{9,11},{10,... | collective-permute-start | bytes 3833864 | tf_op jit(solution)/shard_map/ppermute | solution.py:124
  263.5 27.6 %collective-permute-start.27 = (bf16[1,4608,128]{2,1,0:T(8,128)(2,1)S(1)}, bf16[1,4608,128]{2,1,0:T(8,128)(2,1)S(1)}, u32[]{:S(2)}, u32[]{:S(2)}) collective-permute-start(bf16[1,4608,128]{2,1,0:T(8,128)(2,1)S(1)} %slice.356), channel_id=1, source_target_pairs={{0,8},{8,0},{16,24},{24,16},{1,9},{9,1},{17,25},{25,17},{2,10},{10... | collective-permute-start | bytes 3538952 | tf_op jit(solution)/shard_map/ppermute | solution.py:42
  265.5 27.3 %collective-permute-start.28 = (bf16[1,4608,128]{2,1,0:T(8,128)(2,1)S(1)}, bf16[1,4608,128]{2,1,0:T(8,128)(2,1)S(1)}, u32[]{:S(2)}, u32[]{:S(2)}) collective-permute-start(bf16[1,4608,128]{2,1,0:T(8,128)(2,1)S(1)} %slice.357), channel_id=1, source_target_pairs={{0,16},{8,24},{16,0},{24,8},{1,17},{9,25},{17,1},{25,9},{2,18},{10... | collective-permute-start | bytes 3538952 | tf_op jit(solution)/shard_map/ppermute | solution.py:42
  267.0 60.4 %collective-permute-start.30 = (bf16[384,1664]{1,0:T(8,128)(2,1)}, bf16[384,1664]{1,0:T(8,128)(2,1)}, u32[]{:S(2)}, u32[]{:S(2)}) collective-permute-start(bf16[384,1664]{1,0:T(8,128)(2,1)} %collective-permute-done.15.refs_4_), channel_id=1, source_target_pairs={{0,2},{1,3},{2,4},{3,5},{4,6},{5,7},{6,0},{7,1},{8,10},{9,11},{10,... | collective-permute-start | bytes 3833864 | tf_op jit(solution)/shard_map/ppermute | solution.py:124
  267.0 60.4 %collective-permute-start.29 = (bf16[384,1664]{1,0:T(8,128)(2,1)}, bf16[384,1664]{1,0:T(8,128)(2,1)}, u32[]{:S(2)}, u32[]{:S(2)}) collective-permute-start(bf16[384,1664]{1,0:T(8,128)(2,1)} %collective-permute-done.24.refs_0_), channel_id=1, source_target_pairs={{0,2},{1,3},{2,4},{3,5},{4,6},{5,7},{6,0},{7,1},{8,10},{9,11},{10,... | collective-permute-start | bytes 3833864 | tf_op jit(solution)/shard_map/ppermute | solution.py:124
  335.9 80.4 %collective-permute-start.32 = (bf16[384,1664]{1,0:T(8,128)(2,1)}, bf16[384,1664]{1,0:T(8,128)(2,1)}, u32[]{:S(2)}, u32[]{:S(2)}) collective-permute-start(bf16[384,1664]{1,0:T(8,128)(2,1)} %add_convert_fusion.6), channel_id=1, source_target_pairs={{0,2},{1,3},{2,4},{3,5},{4,6},{5,7},{6,0},{7,1},{8,10},{9,11},{10,... | collective-permute-start | bytes 3833864 | tf_op jit(solution)/shard_map/ppermute | solution.py:124
  381.0 35.4 %collective-permute-start.37 = (bf16[1,4608,128]{2,1,0:T(8,128)(2,1)}, bf16[1,4608,128]{2,1,0:T(8,128)(2,1)}, u32[]{:S(2)}, u32[]{:S(2)}) collective-permute-start(bf16[1,4608,128]{2,1,0:T(8,128)(2,1)} %get-tuple-element.224), channel_id=1, source_target_pairs={{0,8},{8,0},{16,24},{24,16},{1,9},{9,1},{17,25},{25,17},{2,10},{10... | collective-permute-start | bytes 3538952 | tf_op jit(solution)/shard_map/ppermute | solution.py:42
  382.6 33.8 %collective-permute-start.38 = (bf16[1,4608,128]{2,1,0:T(8,128)(2,1)}, bf16[1,4608,128]{2,1,0:T(8,128)(2,1)}, u32[]{:S(2)}, u32[]{:S(2)}) collective-permute-start(bf16[1,4608,128]{2,1,0:T(8,128)(2,1)} %get-tuple-element.225), channel_id=1, source_target_pairs={{0,16},{8,24},{16,0},{24,8},{1,17},{9,25},{17,1},{25,9},{2,18},{10... | collective-permute-start | bytes 3538952 | tf_op jit(solution)/shard_map/ppermute | solution.py:42
  383.1 33.9 %collective-permute-start.42 = (bf16[384,3200]{1,0:T(8,128)(2,1)}, bf16[384,3200]{1,0:T(8,128)(2,1)}, u32[]{:S(2)}, u32[]{:S(2)}) collective-permute-start(bf16[384,3200]{1,0:T(8,128)(2,1)} %get-tuple-element.246), channel_id=1, source_target_pairs={{0,1},{1,0},{2,3},{3,2},{4,5},{5,4},{6,7},{7,6},{8,9},{9,8},{10,11... | collective-permute-start | bytes 7372808 | tf_op jit(solution)/shard_map/ppermute | solution.py:131
  424.2 32.3 %collective-permute-start.40 = (bf16[384,1664]{1,0:T(8,128)(2,1)S(1)}, bf16[384,1664]{1,0:T(8,128)(2,1)}, u32[]{:S(2)}, u32[]{:S(2)}) collective-permute-start(bf16[384,1664]{1,0:T(8,128)(2,1)S(1)} %add_convert_fusion.4), channel_id=1, source_target_pairs={{0,2},{1,3},{2,4},{3,5},{4,6},{5,7},{6,0},{7,1},{8,10},{9,11},{10,... | collective-permute-start | bytes 3833864 | tf_op jit(solution)/shard_map/ppermute | solution.py:124
  427.6 54.4 %collective-permute-start.45 = (bf16[2,4608,128]{2,1,0:T(8,128)(2,1)}, bf16[2,4608,128]{2,1,0:T(8,128)(2,1)}, u32[]{:S(2)}, u32[]{:S(2)}) collective-permute-start(bf16[2,4608,128]{2,1,0:T(8,128)(2,1)} %pad_maximum_fusion.2), channel_id=1, source_target_pairs={{0,8},{8,0},{16,24},{24,16},{1,9},{9,1},{17,25},{25,17},{2,10},{10... | collective-permute-start | bytes 7077896 | tf_op jit(solution)/shard_map/ppermute | solution.py:42
  432.2 54.4 %collective-permute-start.46 = (bf16[2,4608,128]{2,1,0:T(8,128)(2,1)}, bf16[2,4608,128]{2,1,0:T(8,128)(2,1)}, u32[]{:S(2)}, u32[]{:S(2)}) collective-permute-start(bf16[2,4608,128]{2,1,0:T(8,128)(2,1)} %pad_maximum_fusion.3), channel_id=1, source_target_pairs={{0,16},{8,24},{16,0},{24,8},{1,17},{9,25},{17,1},{25,9},{2,18},{10... | collective-permute-start | bytes 7077896 | tf_op jit(solution)/shard_map/ppermute | solution.py:42
  458.3 31.6 %collective-permute-start.43 = (bf16[384,1664]{1,0:T(8,128)(2,1)S(1)}, bf16[384,1664]{1,0:T(8,128)(2,1)S(1)}, u32[]{:S(2)}, u32[]{:S(2)}) collective-permute-start(bf16[384,1664]{1,0:T(8,128)(2,1)S(1)} %add_convert_fusion.1), channel_id=1, source_target_pairs={{0,2},{1,3},{2,4},{3,5},{4,6},{5,7},{6,0},{7,1},{8,10},{9,11},{10,... | collective-permute-start | bytes 3833864 | tf_op jit(solution)/shard_map/ppermute | solution.py:124
  458.5 48.1 %collective-permute-start.47 = (bf16[1,4608,128]{2,1,0:T(8,128)(2,1)S(1)}, bf16[1,4608,128]{2,1,0:T(8,128)(2,1)S(1)}, u32[]{:S(2)}, u32[]{:S(2)}) collective-permute-start(bf16[1,4608,128]{2,1,0:T(8,128)(2,1)S(1)} %copy-done.103), channel_id=1, source_target_pairs={{0,8},{8,0},{16,24},{24,16},{1,9},{9,1},{17,25},{25,17},{2,10},{10... | collective-permute-start | bytes 3538952 | tf_op jit(solution)/shard_map/ppermute | solution.py:42
  460.0 50.9 %collective-permute-start.48 = (bf16[1,4608,128]{2,1,0:T(8,128)(2,1)S(1)}, bf16[1,4608,128]{2,1,0:T(8,128)(2,1)S(1)}, u32[]{:S(2)}, u32[]{:S(2)}) collective-permute-start(bf16[1,4608,128]{2,1,0:T(8,128)(2,1)S(1)} %copy-done.102), channel_id=1, source_target_pairs={{0,16},{8,24},{16,0},{24,8},{1,17},{9,25},{17,1},{25,9},{2,18},{10... | collective-permute-start | bytes 3538952 | tf_op jit(solution)/shard_map/ppermute | solution.py:42
  512.3 19.3 %all-to-all-start.2 = ((bf16[4,384,384]{2,1,0:T(8,128)(2,1)}), bf16[4,384,384]{2,1,0:T(8,128)(2,1)}, u32[]{:S(2)}, u32[]{:S(2)}) async-start(bf16[4,384,384]{2,1,0:T(8,128)(2,1)} %copy-done.14), calls=%async_computation.2 | async-start | bytes 2359296 | tf_op jit(solution)/shard_map/all_to_all | solution.py:1147
  521.9 60.3 %collective-permute-start.44 = (bf16[384,1536]{1,0:T(8,128)(2,1)}, bf16[384,1536]{1,0:T(8,128)(2,1)}, u32[]{:S(2)}, u32[]{:S(2)}) collective-permute-start(bf16[384,1536]{1,0:T(8,128)(2,1)} %add_convert_fusion.14), channel_id=1, source_target_pairs={{0,2},{1,3},{2,4},{3,5},{4,6},{5,7},{6,0},{7,1},{8,10},{9,11},{10,... | collective-permute-start | bytes 3538952 | tf_op jit(solution)/shard_map/ppermute | solution.py:124
  531.7 43.1 %all-to-all-start.3 = ((bf16[4,4,48,1664]{3,2,1,0:T(8,128)(2,1)}), bf16[4,4,48,1664]{3,2,1,0:T(8,128)(2,1)}, u32[]{:S(2)}, u32[]{:S(2)}) async-start(bf16[4,4,48,1664]{3,2,1,0:T(8,128)(2,1)} %add_convert_fusion), calls=%async_computation.3 | async-start | bytes 5111808 | tf_op jit(solution)/shard_map/all_to_all | solution.py:1150
  584.8 44.1 %collective-permute-start.50 = (bf16[384,1536]{1,0:T(8,128)(2,1)}, bf16[384,1536]{1,0:T(8,128)(2,1)}, u32[]{:S(2)}, u32[]{:S(2)}) collective-permute-start(bf16[384,1536]{1,0:T(8,128)(2,1)} %add_convert_fusion.10), channel_id=1, source_target_pairs={{0,2},{1,3},{2,4},{3,5},{4,6},{5,7},{6,0},{7,1},{8,10},{9,11},{10,... | collective-permute-start | bytes 3538952 | tf_op jit(solution)/shard_map/ppermute | solution.py:124
  598.6 86.3 %collective-permute-start.54 = (bf16[384,1536]{1,0:T(8,128)(2,1)}, bf16[384,1536]{1,0:T(8,128)(2,1)}, u32[]{:S(2)}, u32[]{:S(2)}) collective-permute-start(bf16[384,1536]{1,0:T(8,128)(2,1)} %pad_maximum_fusion.7), channel_id=1, source_target_pairs={{0,8},{8,0},{16,24},{24,16},{1,9},{9,1},{17,25},{25,17},{2,10},{10... | collective-permute-start | bytes 3538952 | tf_op jit(solution)/shard_map/ppermute | solution.py:42
  600.5 84.4 %collective-permute-start.55 = (bf16[384,1536]{1,0:T(8,128)(2,1)}, bf16[384,1536]{1,0:T(8,128)(2,1)}, u32[]{:S(2)}, u32[]{:S(2)}) collective-permute-start(bf16[384,1536]{1,0:T(8,128)(2,1)} %pad_maximum_fusion.8), channel_id=1, source_target_pairs={{0,16},{8,24},{16,0},{24,8},{1,17},{9,25},{17,1},{25,9},{2,18},{10... | collective-permute-start | bytes 3538952 | tf_op jit(solution)/shard_map/ppermute | solution.py:42
  608.1 31.3 %all-to-all-start.5 = ((bf16[4,192,640]{2,1,0:T(8,128)(2,1)}), bf16[4,192,640]{2,1,0:T(8,128)(2,1)}, u32[]{:S(2)}, u32[]{:S(2)}) async-start(bf16[4,192,640]{2,1,0:T(8,128)(2,1)} %fusion.9), calls=%async_computation.5 | async-start | bytes 1966080 | tf_op jit(solution)/shard_map/all_to_all | solution.py:155
  617.8 55.9 %collective-permute-start.56 = (bf16[2,4608,128]{2,1,0:T(8,128)(2,1)}, bf16[2,4608,128]{2,1,0:T(8,128)(2,1)}, u32[]{:S(2)}, u32[]{:S(2)}) collective-permute-start(bf16[2,4608,128]{2,1,0:T(8,128)(2,1)} %pad_maximum_fusion.4), channel_id=1, source_target_pairs={{0,8},{8,0},{16,24},{24,16},{1,9},{9,1},{17,25},{25,17},{2,10},{10... | collective-permute-start | bytes 7077896 | tf_op jit(solution)/shard_map/ppermute | solution.py:42
  621.5 53.8 %collective-permute-start.57 = (bf16[2,4608,128]{2,1,0:T(8,128)(2,1)}, bf16[2,4608,128]{2,1,0:T(8,128)(2,1)}, u32[]{:S(2)}, u32[]{:S(2)}) collective-permute-start(bf16[2,4608,128]{2,1,0:T(8,128)(2,1)} %pad_maximum_fusion.5), channel_id=1, source_target_pairs={{0,16},{8,24},{16,0},{24,8},{1,17},{9,25},{17,1},{25,9},{2,18},{10... | collective-permute-start | bytes 7077896 | tf_op jit(solution)/shard_map/ppermute | solution.py:42
  639.4 84.2 %collective-permute-start.53 = (bf16[384,1536]{1,0:T(8,128)(2,1)}, bf16[384,1536]{1,0:T(8,128)(2,1)}, u32[]{:S(2)}, u32[]{:S(2)}) collective-permute-start(bf16[384,1536]{1,0:T(8,128)(2,1)} %add_convert_fusion.9), channel_id=1, source_target_pairs={{0,2},{1,3},{2,4},{3,5},{4,6},{5,7},{6,0},{7,1},{8,10},{9,11},{10,... | collective-permute-start | bytes 3538952 | tf_op jit(solution)/shard_map/ppermute | solution.py:124
  642.8 60.5 %all-to-all-start.6 = ((bf16[4,48,1664]{2,1,0:T(8,128)(2,1)}), bf16[4,48,1664]{2,1,0:T(8,128)(2,1)}, u32[]{:S(2)}, u32[]{:S(2)}) async-start(bf16[4,48,1664]{2,1,0:T(8,128)(2,1)} %reduce_sum.82), calls=%async_computation.6 | async-start | bytes 1277952 | tf_op jit(solution)/shard_map/all_to_all | solution.py:155
  (126 other events, 1135.9 us)
